TPU v7x, 128 devices: a whole 4x4x4 slice. The times are simulated.
128 devices in a mesh: row: 8 (over z_hi, x), col: 16 (over y, z_lo, core).
Axes of the slice: x: 4, y: 4, z: 4 (z_hi: 2, z_lo: 2; z = z_hi * 2 + z_lo), core: 2. Of those that a mesh axis runs over, the one named last changes fastest.
Arguments:
- activations: bfloat16 [20480, 768], P(('row', 'col')), may hold values from -6 to 6
- signals: bfloat16 [20480, 768], P(('row', 'col')), may hold values from -6 to 6
- labels: int32 [20480], P(('row', 'col')), may hold values from 0 to 344
- coefficients: float32 [345, 20480], P(None, ('row', 'col')), may hold values from -6 to 6
Outputs:
- updated: float32 [345, 20480], P(None, ('row', 'col'))
All inputs are finite; a program needn't handle non-finite values.
Results may differ from a plain program's by a relative error of at most 0.0003.
Values may be sent and summed in bfloat16 or wider, within the bound.
No kernel may reach another device: no remote copies, remote signals or barrier semaphores. Data moves between devices by JAX's collectives and lax.ppermute only.
A program may use at most 128 MiB of HBM per device.

v0:
```python
import jax
import jax.numpy as jnp
from jax import lax
from jax.sharding import PartitionSpec as P

FEAT = 768


damping = 0.8
ridge = 0.1


def kernel_piece(left_act, left_sig, right_act, right_sig):
    dims = (((1,), (1,)), ((), ()))
    gram_a = lax.dot_general(left_act, right_act, dims, preferred_element_type=jnp.float32) / FEAT
    gram_s = lax.dot_general(left_sig, right_sig, dims, preferred_element_type=jnp.float32) / FEAT
    return gram_a * gram_s


def shards(activations, signals, labels, coefficients):
    block_act, block_sig = (
        lax.all_gather(activations, "row", axis=0, tiled=True),
        lax.all_gather(signals, "row", axis=0, tiled=True),
    )
    far_coefs = lax.all_gather(coefficients, "col", axis=1, tiled=True)
    kernel = kernel_piece(
        lax.all_gather(activations, "col", axis=0, tiled=True),
        lax.all_gather(signals, "col", axis=0, tiled=True),
        block_act,
        block_sig,
    )
    partial_sum = jnp.dot(
        far_coefs, kernel, precision=lax.Precision.HIGHEST, preferred_element_type=jnp.float32
    )
    product = lax.psum_scatter(partial_sum, "row", scatter_dimension=1, tiled=True)
    classes = jnp.arange(coefficients.shape[0], dtype=jnp.int32)
    targets = (labels[None, :] == classes[:, None]).astype(jnp.float32) - 1.0 / coefficients.shape[
        0
    ]
    return coefficients + damping * (targets - product - ridge * coefficients)


def solution(mesh):
    in_specs = (
        P(("row", "col"), None),
        P(("row", "col"), None),
        P(("row", "col")),
        P(None, ("row", "col")),
    )
    out_specs = P(None, ("row", "col"))
    return jax.shard_map(shards, mesh=mesh, in_specs=in_specs, out_specs=out_specs, check_vma=False)
```

profile of v0, /device:TPU:0, one launch (start us, length us, event | category | flops | bytes accessed | tf_op | source)
XLA Modules:
  0.0 340.5 jit_solution(3074554470234860550)
XLA Ops:
  6.5 0.0 all-gather.8.cloned.1.call-start
  6.5 0.7 all-gather.8.cloned.1.call-update
  7.3 0.0 all-gather.6.cloned.1.call-start
  7.3 0.7 all-gather.6.cloned.1.call-update
  8.0 0.0 all-gather.12.cloned.1.call-start
  8.1 0.7 all-gather.12.cloned.1.call-update
  8.7 0.0 all-gather.10.cloned.1.call-start
  8.8 0.5 all-gather.10.cloned.1.call-update
  9.3 0.0 all-gather.14.cloned.1.call-start
  9.4 0.5 all-gather.14.cloned.1.call-update
  9.9 0.0 reduce-scatter.4.cloned.1.call-start
  10.0 56.3 %all-gather.8.cloned.1.call-done = bf16[1280,768]{1,0:T(8,128)(2,1)} async-done(((bf16[160,768]{1,0:T(8,128)(2,1)}), bf16[1280,768]{1,0:T(8,128)(2,1)}) %all-gather.8.cloned.1.call-update) | async-done | bytes 1966096 | tf_op jit(solution)/shard_map/all_gather | solution.py:22
  66.2 37.3 %all-gather.6.cloned.1.call-done = bf16[2560,768]{1,0:T(8,128)(2,1)} async-done(((bf16[160,768]{1,0:T(8,128)(2,1)}), bf16[2560,768]{1,0:T(8,128)(2,1)}) %all-gather.6.cloned.1.call-update) | async-done | bytes 3932176 | tf_op jit(solution)/shard_map/all_gather | solution.py:27
  103.5 10.4 %convolution_multiply_fusion.1 = f32[2560,1280]{1,0:T(8,128)} fusion(bf16[2560,768]{1,0:T(8,128)(2,1)} %all-gather.6.cloned.1.call-done, bf16[1280,768]{1,0:T(8,128)(2,1)} %all-gather.8.cloned.1.call-done), kind=kOutput, calls=%fused_computation.2 | convolution fusion | flops 5036441600 | bytes 19005440 | tf_op jit(solution)/shard_map/dot_general | solution.py:15
  113.9 46.1 %all-gather.12.cloned.1.call-done = bf16[1280,768]{1,0:T(8,128)(2,1)} async-done(((bf16[160,768]{1,0:T(8,128)(2,1)}), bf16[1280,768]{1,0:T(8,128)(2,1)}) %all-gather.12.cloned.1.call-update) | async-done | bytes 1966096 | tf_op jit(solution)/shard_map/all_gather | solution.py:23
  159.9 37.1 %all-gather.10.cloned.1.call-done = bf16[2560,768]{1,0:T(8,128)(2,1)} async-done(((bf16[160,768]{1,0:T(8,128)(2,1)}), bf16[2560,768]{1,0:T(8,128)(2,1)}) %all-gather.10.cloned.1.call-update) | async-done | bytes 3932176 | tf_op jit(solution)/shard_map/all_gather | solution.py:28
  197.1 12.3 %fusion = f32[2560,1280]{1,0:T(8,128)} fusion(f32[2560,1280]{1,0:T(8,128)} %convolution_multiply_fusion.1, bf16[2560,768]{1,0:T(8,128)(2,1)} %all-gather.10.cloned.1.call-done, bf16[1280,768]{1,0:T(8,128)(2,1)} %all-gather.12.cloned.1.call-done), kind=kOutput, calls=%fused_computation.1 | convolution fusion | flops 5039718400 | bytes 32112640 | tf_op jit(solution)/shard_map/dot_general | solution.py:16
  209.4 26.2 %all-gather.14.cloned.1.call-done = f32[345,2560]{0,1:T(8,128)} async-done(((f32[345,160]{0,1:T(8,128)}), f32[345,2560]{0,1:T(8,128)}) %all-gather.14.cloned.1.call-update) | async-done | bytes 3532816 | tf_op jit(solution)/shard_map/all_gather | solution.py:25
  235.6 18.6 %convolution_bitcast_fusion = f32[345,1280]{1,0:T(8,128)S(1)} fusion(f32[2560,1280]{1,0:T(8,128)} %fusion, f32[345,2560]{0,1:T(8,128)} %all-gather.14.cloned.1.call-done), kind=kOutput, calls=%fused_computation.3 | convolution fusion | flops 13565952000 | bytes 18406400 | tf_op jit(solution)/shard_map/dot_general | solution.py:32
  254.2 0.0 copy-start
  254.2 0.0 copy-start.1
  254.3 1.8 copy.12
  256.1 0.0 reduce-scatter.4.cloned.1.call-update
  256.1 75.8 %reduce-scatter.4.cloned.1.call-done = f32[160,345]{1,0:T(8,128)} async-done(((f32[1280,345]{1,0:T(8,128)}), f32[160,345]{1,0:T(8,128)}) %reduce-scatter.4.cloned.1.call-update) | async-done | bytes 220816
  331.9 0.0 copy-done
  331.9 0.0 copy-done.1
  331.9 1.8 fusion.3
Async XLA Ops:
  6.5 59.7 %all-gather.8.cloned.1.call-start = ((), (), s32[]{:S(2)}) async-start(), calls=%async_computation.2 | async-start | bytes 2211840 | tf_op jit(solution)/shard_map/all_gather | solution.py:22
  7.3 96.2 %all-gather.6.cloned.1.call-start = ((), (), s32[]{:S(2)}) async-start(), calls=%async_computation.1 | async-start | bytes 4177920 | tf_op jit(solution)/shard_map/all_gather | solution.py:27
  8.0 151.9 %all-gather.12.cloned.1.call-start = ((), (), s32[]{:S(2)}) async-start(), calls=%async_computation.4 | async-start | bytes 2211840 | tf_op jit(solution)/shard_map/all_gather | solution.py:23
  8.7 188.3 %all-gather.10.cloned.1.call-start = ((), (), s32[]{:S(2)}) async-start(), calls=%async_computation.3 | async-start | bytes 4177920 | tf_op jit(solution)/shard_map/all_gather | solution.py:28
  9.3 226.3 %all-gather.14.cloned.1.call-start = ((), (), s32[]{:S(2)}) async-start(), calls=%async_computation.5 | async-start | bytes 4177920 | tf_op jit(solution)/shard_map/all_gather | solution.py:25
  9.9 322.0 %reduce-scatter.4.cloned.1.call-start = ((), (), s32[]{:S(2)}) async-start(), calls=%async_computation.6 | async-start | bytes 2211840
  254.2 77.7 %copy-start = (f32[345,160]{0,1:T(8,128)S(1)}, f32[345,160]{0,1:T(8,128)}, u32[]{:S(2)}) copy-start(f32[345,160]{0,1:T(8,128)} %param.7) | copy-start | bytes 662404
  254.2 77.6 %copy-start.1 = (s32[160]{0:T(256)S(1)}, s32[160]{0:T(256)}, u32[]{:S(2)}) copy-start(s32[160]{0:T(256)} %param.6) | copy-start | bytes 1924
Sparse Core Ops, SparseCore 0:
  9.7 56.5 all-gather.7
  67.9 35.5 all-gather.5
  105.8 54.0 all-gather.11
  161.5 35.5 all-gather.9
  198.6 36.9 all-gather.13
  256.2 75.6 reduce-scatter.3
where the time goes:
time: 341 us
  waiting for transfers between devices  282 us (83%)
  matrix products  41.4 us (12%)
  between operations  13.5 us (4%)
    unnamed x7, waiting for transfers between devices  78.9 us
    all_gather x1, waiting for transfers between devices, shards(): lax.all_gather(activations, 'row', axis=0, tiled=True)  56.3 us
    all_gather x1, waiting for transfers between devices, shards(): lax.all_gather(signals, 'row', axis=0, tiled=True)  46.1 us
    all_gather x1, waiting for transfers between devices, shards(): lax.all_gather(activations, 'col', axis=0, tiled=True)  37.3 us
    all_gather x1, waiting for transfers between devices, shards(): lax.all_gather(signals, 'col', axis=0, tiled=True)  37.1 us
    all_gather x1, waiting for transfers between devices, shards(): far_coefs = lax.all_gather(coefficients, 'col', axis=1, tiled=True)  26.2 us
    dot_general x1, matrix products, shards(): jnp.dot(far_coefs, kernel, precision=lax.Precision.HIGHEST, preferred_ele...  18.6 us
    dot_general x1, matrix products, kernel_piece(): lax.dot_general(left_sig, right_sig, dims, preferred_element_type=jnp.flo...  12.3 us
  transfers between devices with their start and end apart: 6, of which 6 were waited for; matrix products, arithmetic and copies ran while one was open for 7% of the time, Pallas kernels for 0%

commit v1 on v0

v1 whole, which is shorter than its diff:
```python
import functools

import jax
import jax.numpy as jnp
from jax import lax
from jax.experimental import pallas as pl
from jax.experimental.pallas import tpu as pltpu
from jax.sharding import PartitionSpec as P

FEAT = 768
CLASSES = 345
LANES = 384
OWN = 160
AXES = ("row", "col")

damping = 0.8
ridge = 0.1

f32, bf16 = jnp.float32, jnp.bfloat16
NT = (((1,), (1,)), ((), ()))
NN = (((1,), (0,)), ((), ()))


def encode(x, y, z, core):
    return ((((z >> 1) * 4 + x) * 4 + y) * 2 + (z & 1)) * 2 + core


def decode(index):
    return (index >> 4) & 3, (index >> 2) & 3, (index >> 6) * 2 + ((index >> 1) & 1), index & 1


def moves(dx=0, dy=0, far=0, near=0, other=0):
    pairs = []
    for index in range(128):
        x, y, z, core = decode(index)
        if far:
            z = 3 - z
        if near:
            z = z ^ 1
        pairs.append((index, encode((x + dx) % 4, (y + dy) % 4, z, core ^ other)))
    return pairs


def send(value, **move):
    return lax.ppermute(value, AXES, moves(**move))


def dot(a, b, dims):
    return lax.dot_general(a, b, dims, preferred_element_type=f32)


def gram_kernel(*refs):
    right_in, left_in, coef_in = refs[:8], refs[8:24], refs[24]
    outs = refs[25:33]
    right, left, coef, split, total, sems = refs[33:]
    col = lax.axis_index("col")
    copies = []
    for i in range(8):
        copies.append(pltpu.make_async_copy(right_in[i], right.at[pl.ds(i * OWN, OWN)], sems.at[i]))
    for i in range(16):
        copies.append(pltpu.make_async_copy(left_in[i], left.at[pl.ds(i * OWN, OWN)], sems.at[8 + i]))
    y, near, core = col // 4, (col // 2) % 2, col % 2
    for i, (dy, dn, dc) in enumerate(LEFT):
        at = (((y + dy) % 4) * 2 + (near + dn) % 2) * 2 + (core + dc) % 2
        copies.append(
            pltpu.make_async_copy(
                coef_in.at[pl.ds(pl.multiple_of(at * OWN, OWN), OWN)], coef.at[pl.ds(i * OWN, OWN)], sems.at[24 + i]
            )
        )
    for copy in copies:
        copy.start()
    for copy in copies:
        copy.wait()
    split[...] = jnp.zeros_like(split)
    values = coef[...]
    high = values.astype(bf16)
    split[:, :CLASSES] = high
    split[:, LANES : LANES + CLASSES] = (values - high.astype(f32)).astype(bf16)

    rows, cols = 640, 512

    @pl.loop(0, 1280 // rows)
    def _(step):
        n = pl.ds(pl.multiple_of(step * rows, rows), rows)
        part = None
        for j in range(2560 // cols):
            m = pl.ds(j * cols, cols)
            gram_a = dot(right[n, :FEAT], left[m, :FEAT], NT)
            gram_s = dot(right[n, FEAT:], left[m, FEAT:], NT)
            kernel = gram_a * gram_s
            high = kernel.astype(bf16)
            low = (kernel - high.astype(f32)).astype(bf16)
            both = dot(high, split[m, :], NN)
            new = both[:, :LANES] + both[:, LANES:] + dot(low, split[m, :LANES], NN)
            part = new if part is None else part + new
        total[n, :] = part

    for i in range(8):
        outs[i][...] = total[pl.ds(i * OWN, OWN), :CLASSES]


LEFT = tuple((dy, dn, dc) for dc in (0, 1) for dy, dn in ((0, 0), (0, 1), (1, 0), (3, 0), (1, 1), (3, 1), (2, 0), (2, 1)))


def partial_sums(right, left, coefs):
    spec = pl.BlockSpec(memory_space=pl.ANY)
    return pl.pallas_call(
        gram_kernel,
        out_shape=[jax.ShapeDtypeStruct((OWN, CLASSES), f32)] * 8,
        in_specs=[spec] * 25,
        out_specs=[pl.BlockSpec(memory_space=pltpu.VMEM)] * 8,
        scratch_shapes=[
            pltpu.VMEM((1280, 2 * FEAT), bf16),
            pltpu.VMEM((2560, 2 * FEAT), bf16),
            pltpu.VMEM((2560, CLASSES), f32),
            pltpu.VMEM((2560, 2 * LANES), bf16),
            pltpu.VMEM((1280, LANES), f32),
            pltpu.SemaphoreType.DMA((40,)),
        ],
        cost_estimate=pl.CostEstimate(flops=17_000_000_000, bytes_accessed=16_000_000, transcendentals=0),
        compiler_params=pltpu.CompilerParams(vmem_limit_bytes=48 << 20),
        name="gram_product",
    )(*right, *left, coefs)


def ring_gather(own, axis, pair):
    up, down = {axis: 1}, {axis: -1}
    mate = send(own, **{pair: 1})
    left, right = send(own, **up), send(own, **down)
    mate_left, mate_right = send(mate, **up), send(mate, **down)
    across = send(left, **up)
    mate_across = send(mate_right, **down)
    return [own, mate, right, left, mate_right, mate_left, across, mate_across]


def shards(activations, signals, labels, coefficients):
    coefs = coefficients.T
    all_coefs = lax.all_gather(coefs, "col", axis=0, tiled=True)
    own = jnp.concatenate([activations, signals], axis=1)
    right = ring_gather(own, "dx", "far")
    near = ring_gather(own, "dy", "near")
    left = near + [send(block, other=1) for block in near]
    sums = partial_sums(right, left, all_coefs)
    product = sums[0]
    for part, (dx, far) in zip(sums[1:], ((0, 1), (1, 0), (-1, 0), (1, 1), (-1, 1), (2, 0), (2, 1))):
        product = product + send(part, dx=dx, far=far)
    product = product * (1.0 / (FEAT * FEAT))
    classes = jnp.arange(CLASSES, dtype=jnp.int32)
    targets = (labels[:, None] == classes[None, :]).astype(f32) - 1.0 / CLASSES
    return (coefs + damping * (targets - product - ridge * coefs)).T


def solution(mesh):
    in_specs = (P(AXES, None), P(AXES, None), P(AXES), P(None, AXES))
    return jax.shard_map(shards, mesh=mesh, in_specs=in_specs, out_specs=P(None, AXES), check_vma=False)
```

time: 341 us -> 160 us (0.47)
  waiting for transfers between devices: 282 us -> 69.4 us
  starting transfers between devices: 0.19 us -> 43.4 us
  matrix products: 41.4 us -> 0 us
  Pallas kernels: 0 us -> 27.8 us
    all_gather x5 -> x1, waiting for transfers between devices: 203 us -> 0.01 us  [shards(): all_coefs = lax.all_gather(coefs, 'col', axis=0, tiled=True)]
    unnamed x7 -> x1, waiting for transfers between devices: 78.9 us -> 0.71 us
    ppermute x0 -> x29, waiting for transfers between devices: none -> 68.6 us  [send(): return lax.ppermute(value, AXES, moves(**move))]
    ppermute x0 -> x29, starting transfers between devices: none -> 43.4 us  [send(): return lax.ppermute(value, AXES, moves(**move))]
    dot_general x3 -> x0, matrix products: 41.4 us -> none  [the longest x1 18.6 us: shards(): jnp.dot(far_coefs, kernel, precision=lax.Precision.HIGHEST, preferred_ele...]
    pallas_call x0 -> x1, Pallas kernels: none -> 27.8 us  [partial_sums(): pl.pallas_call(gram_kernel, out_shape=[jax.ShapeDtypeStruct((OWN, CLASSES...]
  transfers between devices with their start and end apart: 6 -> 30, of which waited for: 6 -> 12; matrix products, arithmetic and copies ran while one was open for 7% -> 1% of each run, Pallas kernels for 0% -> 0%
where the time goes in v1:
time: 160 us; the launch traced here: 159 us
  waiting for transfers between devices  69.4 us (43%)
  starting transfers between devices  43.4 us (27%)
  Pallas kernels  27.8 us (17%)
  between operations  13.6 us (8%)
  local copies, waits for them, and re-layouts  3.8 us (2%)
    ppermute x29, waiting for transfers between devices, send(): return lax.ppermute(value, AXES, moves(**move))  68.6 us
    ppermute x29, starting transfers between devices, send(): return lax.ppermute(value, AXES, moves(**move))  43.4 us
    pallas_call x1, Pallas kernels, partial_sums(): pl.pallas_call(gram_kernel, out_shape=[jax.ShapeDtypeStruct((OWN, CLASSES...  27.8 us
  transfers between devices with their start and end apart: 30, of which 12 were waited for; matrix products, arithmetic and copies ran while one was open for 1% of the time, Pallas kernels for 0%

profile of v1, /device:TPU:0, one launch (start us, length us, event | category | flops | bytes accessed | tf_op | source)
XLA Modules:
  0.0 158.8 jit_solution(16178252594186580463)
XLA Ops:
  6.5 0.7 all-gather.2.cloned.1.call-update
  7.3 1.0 constant_dynamic-update-slice_fusion.1
  8.2 0.0 copy-start.3
  8.2 1.0 constant_dynamic-update-slice_fusion.refs_0_.refs_8_
  9.2 0.1 collective-permute-start.14
  9.3 1.7 %collective-permute-start.9 = (bf16[160,1536]{1,0:T(8,128)(2,1)S(1)}, bf16[160,1536]{1,0:T(8,128)(2,1)S(1)}, u32[]{:S(2)}, u32[]{:S(2)}) collective-permute-start(bf16[160,1536]{1,0:T(8,128)(2,1)S(1)} %constant_dynamic-update-slice_fusion.refs_0_.refs_8_), channel_id=1, source_target_pairs={{0,4},{1,5},{2,6},{3,7},{4,8},{5,9},{6,10},{7,11},{8,12},{9,13},{1... | collective-permute-start | bytes 1474568 | tf_op jit(solution)/shard_map/ppermute | solution.py:45
  11.0 1.6 collective-permute-start.8
  12.6 2.0 %collective-permute-start.7 = (bf16[160,1536]{1,0:T(8,128)(2,1)S(1)}, bf16[160,1536]{1,0:T(8,128)(2,1)S(1)}, u32[]{:S(2)}, u32[]{:S(2)}) collective-permute-start(bf16[160,1536]{1,0:T(8,128)(2,1)S(1)} %constant_dynamic-update-slice_fusion.refs_0_.refs_8_), channel_id=1, source_target_pairs={{0,2},{1,3},{2,0},{3,1},{4,6},{5,7},{6,4},{7,5},{8,10},{9,11},{10,... | collective-permute-start | bytes 1474568 | tf_op jit(solution)/shard_map/ppermute | solution.py:45
  14.6 1.5 collective-permute-start.2
  16.1 0.0 collective-permute-done.14.refs_16_
  16.1 1.7 %collective-permute-start.1 = (bf16[160,1536]{1,0:T(8,128)(2,1)S(1)}, bf16[160,1536]{1,0:T(8,128)(2,1)S(1)}, u32[]{:S(2)}, u32[]{:S(2)}) collective-permute-start(bf16[160,1536]{1,0:T(8,128)(2,1)S(1)} %constant_dynamic-update-slice_fusion.refs_0_.refs_8_), channel_id=1, source_target_pairs={{0,48},{1,49},{2,50},{3,51},{4,52},{5,53},{6,54},{7,55},{8,56},{9,... | collective-permute-start | bytes 1474568 | tf_op jit(solution)/shard_map/ppermute | solution.py:45
  17.8 6.4 %collective-permute-done.9.refs_11_ = bf16[160,1536]{1,0:T(8,128)(2,1)S(1)} collective-permute-done((bf16[160,1536]{1,0:T(8,128)(2,1)S(1)}, bf16[160,1536]{1,0:T(8,128)(2,1)S(1)}, u32[]{:S(2)}, u32[]{:S(2)}) %collective-permute-start.9) | collective-permute-done | bytes 491552 | tf_op jit(solution)/shard_map/ppermute | solution.py:45
  24.3 4.7 %collective-permute-start = (bf16[160,1536]{1,0:T(8,128)(2,1)S(1)}, bf16[160,1536]{1,0:T(8,128)(2,1)S(1)}, u32[]{:S(2)}, u32[]{:S(2)}) collective-permute-start(bf16[160,1536]{1,0:T(8,128)(2,1)S(1)} %constant_dynamic-update-slice_fusion.refs_0_.refs_8_), channel_id=1, source_target_pairs={{0,66},{1,67},{2,64},{3,65},{4,70},{5,71},{6,68},{7,69},{8,74},{9,... | collective-permute-start | bytes 1474568 | tf_op jit(solution)/shard_map/ppermute | solution.py:45
  29.0 0.0 collective-permute-done.8.refs_10_
  29.0 0.0 collective-permute-start.17
  29.0 1.8 %collective-permute-done.7.refs_9_ = bf16[160,1536]{1,0:T(8,128)(2,1)S(1)} collective-permute-done((bf16[160,1536]{1,0:T(8,128)(2,1)S(1)}, bf16[160,1536]{1,0:T(8,128)(2,1)S(1)}, u32[]{:S(2)}, u32[]{:S(2)}) %collective-permute-start.7) | collective-permute-done | bytes 491552 | tf_op jit(solution)/shard_map/ppermute | solution.py:45
  30.8 0.8 collective-permute-start.12
  31.6 0.0 collective-permute-done.2.refs_3_
  31.6 0.2 collective-permute-start.16
  31.7 0.0 collective-permute-done.1.refs_2_
  31.7 0.4 collective-permute-start.15
  32.1 7.3 %collective-permute-done.refs_1_ = bf16[160,1536]{1,0:T(8,128)(2,1)S(1)} collective-permute-done((bf16[160,1536]{1,0:T(8,128)(2,1)S(1)}, bf16[160,1536]{1,0:T(8,128)(2,1)S(1)}, u32[]{:S(2)}, u32[]{:S(2)}) %collective-permute-start) | collective-permute-done | bytes 491552 | tf_op jit(solution)/shard_map/ppermute | solution.py:45
  39.4 3.6 %collective-permute-start.10 = (bf16[160,1536]{1,0:T(8,128)(2,1)S(1)}, bf16[160,1536]{1,0:T(8,128)(2,1)S(1)}, u32[]{:S(2)}, u32[]{:S(2)}) collective-permute-start(bf16[160,1536]{1,0:T(8,128)(2,1)S(1)} %collective-permute-done.7.refs_9_), channel_id=1, source_target_pairs={{0,12},{1,13},{2,14},{3,15},{4,0},{5,1},{6,2},{7,3},{8,4},{9,5},{1... | collective-permute-start | bytes 1474568 | tf_op jit(solution)/shard_map/ppermute | solution.py:45
  43.0 0.0 collective-permute-done.17.refs_19_
  43.0 0.0 collective-permute-start.11
  43.1 10.3 %collective-permute-done.12.refs_14_ = bf16[160,1536]{1,0:T(8,128)(2,1)S(1)} collective-permute-done((bf16[160,1536]{1,0:T(8,128)(2,1)S(1)}, bf16[160,1536]{1,0:T(8,128)(2,1)S(1)}, u32[]{:S(2)}, u32[]{:S(2)}) %collective-permute-start.12) | collective-permute-done | bytes 491552 | tf_op jit(solution)/shard_map/ppermute | solution.py:45
  53.3 1.5 collective-permute-start.5
  54.8 0.0 collective-permute-done.16.refs_18_
  54.8 1.6 %collective-permute-start.4 = (bf16[160,1536]{1,0:T(8,128)(2,1)S(1)}, bf16[160,1536]{1,0:T(8,128)(2,1)S(1)}, u32[]{:S(2)}, u32[]{:S(2)}) collective-permute-start(bf16[160,1536]{1,0:T(8,128)(2,1)S(1)} %collective-permute-done.refs_1_), channel_id=1, source_target_pairs={{0,16},{1,17},{2,18},{3,19},{4,20},{5,21},{6,22},{7,23},{8,24},{9,... | collective-permute-start | bytes 1474568 | tf_op jit(solution)/shard_map/ppermute | solution.py:45
  56.4 0.0 collective-permute-done.15.refs_17_
  56.4 1.8 %collective-permute-start.3 = (bf16[160,1536]{1,0:T(8,128)(2,1)S(1)}, bf16[160,1536]{1,0:T(8,128)(2,1)S(1)}, u32[]{:S(2)}, u32[]{:S(2)}) collective-permute-start(bf16[160,1536]{1,0:T(8,128)(2,1)S(1)} %collective-permute-done.refs_1_), channel_id=1, source_target_pairs={{0,48},{1,49},{2,50},{3,51},{4,52},{5,53},{6,54},{7,55},{8,56},{9,... | collective-permute-start | bytes 1474568 | tf_op jit(solution)/shard_map/ppermute | solution.py:45
  58.2 0.0 collective-permute-done.10.refs_12_
  58.2 3.5 %collective-permute-start.13 = (bf16[160,1536]{1,0:T(8,128)(2,1)S(1)}, bf16[160,1536]{1,0:T(8,128)(2,1)S(1)}, u32[]{:S(2)}, u32[]{:S(2)}) collective-permute-start(bf16[160,1536]{1,0:T(8,128)(2,1)S(1)} %collective-permute-done.10.refs_12_), channel_id=1, source_target_pairs={{0,12},{1,13},{2,14},{3,15},{4,0},{5,1},{6,2},{7,3},{8,4},{9,5},{1... | collective-permute-start | bytes 1474568 | tf_op jit(solution)/shard_map/ppermute | solution.py:45
  61.7 2.9 %collective-permute-done.11.refs_13_ = bf16[160,1536]{1,0:T(8,128)(2,1)S(1)} collective-permute-done((bf16[160,1536]{1,0:T(8,128)(2,1)S(1)}, bf16[160,1536]{1,0:T(8,128)(2,1)S(1)}, u32[]{:S(2)}, u32[]{:S(2)}) %collective-permute-start.11) | collective-permute-done | bytes 491552 | tf_op jit(solution)/shard_map/ppermute | solution.py:45
  64.5 0.0 collective-permute-start.18
  64.5 4.1 %collective-permute-done.5.refs_6_ = bf16[160,1536]{1,0:T(8,128)(2,1)S(1)} collective-permute-done((bf16[160,1536]{1,0:T(8,128)(2,1)S(1)}, bf16[160,1536]{1,0:T(8,128)(2,1)S(1)}, u32[]{:S(2)}, u32[]{:S(2)}) %collective-permute-start.5) | collective-permute-done | bytes 491552 | tf_op jit(solution)/shard_map/ppermute | solution.py:45
  68.7 0.0 collective-permute-start.20
  68.7 9.0 %collective-permute-done.4.refs_5_ = bf16[160,1536]{1,0:T(8,128)(2,1)S(1)} collective-permute-done((bf16[160,1536]{1,0:T(8,128)(2,1)S(1)}, bf16[160,1536]{1,0:T(8,128)(2,1)S(1)}, u32[]{:S(2)}, u32[]{:S(2)}) %collective-permute-start.4) | collective-permute-done | bytes 491552 | tf_op jit(solution)/shard_map/ppermute | solution.py:45
  77.7 0.0 collective-permute-start.19
  77.7 0.0 collective-permute-done.3.refs_4_
  77.7 1.8 %collective-permute-start.6 = (bf16[160,1536]{1,0:T(8,128)(2,1)S(1)}, bf16[160,1536]{1,0:T(8,128)(2,1)S(1)}, u32[]{:S(2)}, u32[]{:S(2)}) collective-permute-start(bf16[160,1536]{1,0:T(8,128)(2,1)S(1)} %collective-permute-done.3.refs_4_), channel_id=1, source_target_pairs={{0,48},{1,49},{2,50},{3,51},{4,52},{5,53},{6,54},{7,55},{8,56},{9,... | collective-permute-start | bytes 1474568 | tf_op jit(solution)/shard_map/ppermute | solution.py:45
  79.5 0.0 collective-permute-done.13.refs_15_
  79.5 0.2 collective-permute-start.21
  79.6 0.0 collective-permute-done.20.refs_22_
  79.7 0.0 collective-permute-done.19.refs_21_
  79.7 0.0 collective-permute-done.18.refs_20_
  79.7 11.6 %collective-permute-done.6.refs_7_ = bf16[160,1536]{1,0:T(8,128)(2,1)S(1)} collective-permute-done((bf16[160,1536]{1,0:T(8,128)(2,1)S(1)}, bf16[160,1536]{1,0:T(8,128)(2,1)S(1)}, u32[]{:S(2)}, u32[]{:S(2)}) %collective-permute-start.6) | collective-permute-done | bytes 491552 | tf_op jit(solution)/shard_map/ppermute | solution.py:45
  91.4 0.8 copy-done
  92.2 0.0 collective-permute-done.21.refs_23_
  92.2 1.0 copy-done.1
  93.2 27.8 %gram_product.1 = (f32[160,345]{1,0:T(8,128)S(1)}, f32[160,345]{1,0:T(8,128)S(1)}, f32[160,345]{1,0:T(8,128)S(1)}, f32[160,345]{1,0:T(8,128)S(1)}, f32[160,345]{...) custom-call(bf16[160,1536]{1,0:T(8,128)(2,1)S(1)} %constant_dynamic-update-slice_fusion.ref, ...), custom_call_target="tpu_custom_call" | custom-call | flops 16999999488 | bytes 16000000 | tf_op jit(solution)/shard_map/gram_product/pallas_call | solution.py:107
  121.1 1.5 collective-permute-start.22
  122.6 0.3 collective-permute-start.23
  122.9 3.0 %collective-permute-start.24 = (f32[160,345]{1,0:T(8,128)S(1)}, f32[160,345]{1,0:T(8,128)S(1)}, u32[]{:S(2)}, u32[]{:S(2)}) collective-permute-start(f32[160,345]{1,0:T(8,128)S(1)} %get-tuple-element.16), channel_id=1, source_target_pairs={{0,48},{1,49},{2,50},{3,51},{4,52},{5,53},{6,54},{7,55},{8,56},{9,... | collective-permute-start | bytes 662408 | tf_op jit(solution)/shard_map/ppermute | solution.py:45
  125.8 0.3 collective-permute-start.25
  126.1 5.1 %collective-permute-start.26 = (f32[160,345]{1,0:T(8,128)S(1)}, f32[160,345]{1,0:T(8,128)S(1)}, u32[]{:S(2)}, u32[]{:S(2)}) collective-permute-start(f32[160,345]{1,0:T(8,128)S(1)} %get-tuple-element.18), channel_id=1, source_target_pairs={{0,114},{1,115},{2,112},{3,113},{4,118},{5,119},{6,116},{7,117},{8... | collective-permute-start | bytes 662408 | tf_op jit(solution)/shard_map/ppermute | solution.py:45
  131.2 1.1 collective-permute-start.27
  132.3 0.0 collective-permute-done.23
  132.3 3.6 %collective-permute-start.28 = (f32[160,345]{1,0:T(8,128)S(1)}, f32[160,345]{1,0:T(8,128)S(1)}, u32[]{:S(2)}, u32[]{:S(2)}) collective-permute-start(f32[160,345]{1,0:T(8,128)S(1)} %get-tuple-element.20), channel_id=1, source_target_pairs={{0,98},{1,99},{2,96},{3,97},{4,102},{5,103},{6,100},{7,101},{8,106... | collective-permute-start | bytes 662408 | tf_op jit(solution)/shard_map/ppermute | solution.py:45
  135.9 4.5 %collective-permute-done.25 = f32[160,345]{1,0:T(8,128)S(1)} collective-permute-done((f32[160,345]{1,0:T(8,128)S(1)}, f32[160,345]{1,0:T(8,128)S(1)}, u32[]{:S(2)}, u32[]{:S(2)}) %collective-permute-start.25) | collective-permute-done | bytes 220832 | tf_op jit(solution)/shard_map/ppermute | solution.py:45
  140.4 0.1 collective-permute-done.26
  140.5 5.8 %collective-permute-done.27 = f32[160,345]{1,0:T(8,128)S(1)} collective-permute-done((f32[160,345]{1,0:T(8,128)S(1)}, f32[160,345]{1,0:T(8,128)S(1)}, u32[]{:S(2)}, u32[]{:S(2)}) %collective-permute-start.27) | collective-permute-done | bytes 220832 | tf_op jit(solution)/shard_map/ppermute | solution.py:45
  146.4 4.8 %collective-permute-done.28 = f32[160,345]{1,0:T(8,128)S(1)} collective-permute-done((f32[160,345]{1,0:T(8,128)S(1)}, f32[160,345]{1,0:T(8,128)S(1)}, u32[]{:S(2)}, u32[]{:S(2)}) %collective-permute-start.28) | collective-permute-done | bytes 220832 | tf_op jit(solution)/shard_map/ppermute | solution.py:45
  151.1 0.9 add_bitcast_fusion
  (35 shorter events, 0.1 us)
Async XLA Ops:
  6.5 85.7 %all-gather.2.cloned.1.call-start = ((), (), s32[]{:S(2)}) async-start(), calls=%async_computation | async-start | bytes 4177920 | tf_op jit(solution)/shard_map/all_gather | solution.py:138
  8.2 142.9 %copy-start.3 = (s32[160]{0:T(256)S(1)}, s32[160]{0:T(256)}, u32[]{:S(2)}) copy-start(s32[160]{0:T(256)} %param.6) | copy-start | bytes 1924
  9.2 6.9 %collective-permute-start.14 = (bf16[160,1536]{1,0:T(8,128)(2,1)S(1)}, bf16[160,1536]{1,0:T(8,128)(2,1)}, u32[]{:S(2)}, u32[]{:S(2)}) collective-permute-start(bf16[160,1536]{1,0:T(8,128)(2,1)S(1)} %constant_dynamic-update-slice_fusion.refs_0_.refs_8_), channel_id=1, source_target_pairs={{0,1},{1,0},{2,3},{3,2},{4,5},{5,4},{6,7},{7,6},{8,9},{9,8},{10,11... | collective-permute-start | bytes 1474568 | tf_op jit(solution)/shard_map/ppermute | solution.py:45
  9.3 15.0 %collective-permute-start.9 = (bf16[160,1536]{1,0:T(8,128)(2,1)S(1)}, bf16[160,1536]{1,0:T(8,128)(2,1)S(1)}, u32[]{:S(2)}, u32[]{:S(2)}) collective-permute-start(bf16[160,1536]{1,0:T(8,128)(2,1)S(1)} %constant_dynamic-update-slice_fusion.refs_0_.refs_8_), channel_id=1, source_target_pairs={{0,4},{1,5},{2,6},{3,7},{4,8},{5,9},{6,10},{7,11},{8,12},{9,13},{1... | collective-permute-start | bytes 1474568 | tf_op jit(solution)/shard_map/ppermute | solution.py:45
  11.0 18.0 %collective-permute-start.8 = (bf16[160,1536]{1,0:T(8,128)(2,1)S(1)}, bf16[160,1536]{1,0:T(8,128)(2,1)S(1)}, u32[]{:S(2)}, u32[]{:S(2)}) collective-permute-start(bf16[160,1536]{1,0:T(8,128)(2,1)S(1)} %constant_dynamic-update-slice_fusion.refs_0_.refs_8_), channel_id=1, source_target_pairs={{0,12},{1,13},{2,14},{3,15},{4,0},{5,1},{6,2},{7,3},{8,4},{9,5},{1... | collective-permute-start | bytes 1474568 | tf_op jit(solution)/shard_map/ppermute | solution.py:45
  12.6 18.2 %collective-permute-start.7 = (bf16[160,1536]{1,0:T(8,128)(2,1)S(1)}, bf16[160,1536]{1,0:T(8,128)(2,1)S(1)}, u32[]{:S(2)}, u32[]{:S(2)}) collective-permute-start(bf16[160,1536]{1,0:T(8,128)(2,1)S(1)} %constant_dynamic-update-slice_fusion.refs_0_.refs_8_), channel_id=1, source_target_pairs={{0,2},{1,3},{2,0},{3,1},{4,6},{5,7},{6,4},{7,5},{8,10},{9,11},{10,... | collective-permute-start | bytes 1474568 | tf_op jit(solution)/shard_map/ppermute | solution.py:45
  14.6 17.0 %collective-permute-start.2 = (bf16[160,1536]{1,0:T(8,128)(2,1)S(1)}, bf16[160,1536]{1,0:T(8,128)(2,1)S(1)}, u32[]{:S(2)}, u32[]{:S(2)}) collective-permute-start(bf16[160,1536]{1,0:T(8,128)(2,1)S(1)} %constant_dynamic-update-slice_fusion.refs_0_.refs_8_), channel_id=1, source_target_pairs={{0,16},{1,17},{2,18},{3,19},{4,20},{5,21},{6,22},{7,23},{8,24},{9,... | collective-permute-start | bytes 1474568 | tf_op jit(solution)/shard_map/ppermute | solution.py:45
  16.1 15.6 %collective-permute-start.1 = (bf16[160,1536]{1,0:T(8,128)(2,1)S(1)}, bf16[160,1536]{1,0:T(8,128)(2,1)S(1)}, u32[]{:S(2)}, u32[]{:S(2)}) collective-permute-start(bf16[160,1536]{1,0:T(8,128)(2,1)S(1)} %constant_dynamic-update-slice_fusion.refs_0_.refs_8_), channel_id=1, source_target_pairs={{0,48},{1,49},{2,50},{3,51},{4,52},{5,53},{6,54},{7,55},{8,56},{9,... | collective-permute-start | bytes 1474568 | tf_op jit(solution)/shard_map/ppermute | solution.py:45
  24.3 18.8 %copy-start.4 = (bf16[160,1536]{1,0:T(8,128)(2,1)}, bf16[160,1536]{1,0:T(8,128)(2,1)S(1)}, u32[]{:S(2)}) copy-start(bf16[160,1536]{1,0:T(8,128)(2,1)S(1)} %collective-permute-done.9.refs_11_) | copy-start | bytes 1474564
  24.3 15.1 %collective-permute-start = (bf16[160,1536]{1,0:T(8,128)(2,1)S(1)}, bf16[160,1536]{1,0:T(8,128)(2,1)S(1)}, u32[]{:S(2)}, u32[]{:S(2)}) collective-permute-start(bf16[160,1536]{1,0:T(8,128)(2,1)S(1)} %constant_dynamic-update-slice_fusion.refs_0_.refs_8_), channel_id=1, source_target_pairs={{0,66},{1,67},{2,64},{3,65},{4,70},{5,71},{6,68},{7,69},{8,74},{9,... | collective-permute-start | bytes 1474568 | tf_op jit(solution)/shard_map/ppermute | solution.py:45
  29.0 25.8 %copy-start.5 = (bf16[160,1536]{1,0:T(8,128)(2,1)}, bf16[160,1536]{1,0:T(8,128)(2,1)S(1)}, u32[]{:S(2)}) copy-start(bf16[160,1536]{1,0:T(8,128)(2,1)S(1)} %collective-permute-done.8.refs_10_) | copy-start | bytes 1474564
  29.0 14.0 %collective-permute-start.17 = (bf16[160,1536]{1,0:T(8,128)(2,1)S(1)}, bf16[160,1536]{1,0:T(8,128)(2,1)S(1)}, u32[]{:S(2)}, u32[]{:S(2)}) collective-permute-start(bf16[160,1536]{1,0:T(8,128)(2,1)S(1)} %collective-permute-done.9.refs_11_), channel_id=1, source_target_pairs={{0,1},{1,0},{2,3},{3,2},{4,5},{5,4},{6,7},{7,6},{8,9},{9,8},{10,11... | collective-permute-start | bytes 1474568 | tf_op jit(solution)/shard_map/ppermute | solution.py:45
  30.8 46.9 %copy-start.6 = (bf16[160,1536]{1,0:T(8,128)(2,1)}, bf16[160,1536]{1,0:T(8,128)(2,1)S(1)}, u32[]{:S(2)}) copy-start(bf16[160,1536]{1,0:T(8,128)(2,1)S(1)} %collective-permute-done.7.refs_9_) | copy-start | bytes 1474564
  30.8 22.6 %collective-permute-start.12 = (bf16[160,1536]{1,0:T(8,128)(2,1)S(1)}, bf16[160,1536]{1,0:T(8,128)(2,1)S(1)}, u32[]{:S(2)}, u32[]{:S(2)}) collective-permute-start(bf16[160,1536]{1,0:T(8,128)(2,1)S(1)} %collective-permute-done.9.refs_11_), channel_id=1, source_target_pairs={{0,4},{1,5},{2,6},{3,7},{4,8},{5,9},{6,10},{7,11},{8,12},{9,13},{1... | collective-permute-start | bytes 1474568 | tf_op jit(solution)/shard_map/ppermute | solution.py:45
  31.6 23.2 %collective-permute-start.16 = (bf16[160,1536]{1,0:T(8,128)(2,1)S(1)}, bf16[160,1536]{1,0:T(8,128)(2,1)S(1)}, u32[]{:S(2)}, u32[]{:S(2)}) collective-permute-start(bf16[160,1536]{1,0:T(8,128)(2,1)S(1)} %collective-permute-done.8.refs_10_), channel_id=1, source_target_pairs={{0,1},{1,0},{2,3},{3,2},{4,5},{5,4},{6,7},{7,6},{8,9},{9,8},{10,11... | collective-permute-start | bytes 1474568 | tf_op jit(solution)/shard_map/ppermute | solution.py:45
  31.7 24.7 %collective-permute-start.15 = (bf16[160,1536]{1,0:T(8,128)(2,1)S(1)}, bf16[160,1536]{1,0:T(8,128)(2,1)S(1)}, u32[]{:S(2)}, u32[]{:S(2)}) collective-permute-start(bf16[160,1536]{1,0:T(8,128)(2,1)S(1)} %collective-permute-done.7.refs_9_), channel_id=1, source_target_pairs={{0,1},{1,0},{2,3},{3,2},{4,5},{5,4},{6,7},{7,6},{8,9},{9,8},{10,11... | collective-permute-start | bytes 1474568 | tf_op jit(solution)/shard_map/ppermute | solution.py:45
  39.4 18.8 %collective-permute-start.10 = (bf16[160,1536]{1,0:T(8,128)(2,1)S(1)}, bf16[160,1536]{1,0:T(8,128)(2,1)S(1)}, u32[]{:S(2)}, u32[]{:S(2)}) collective-permute-start(bf16[160,1536]{1,0:T(8,128)(2,1)S(1)} %collective-permute-done.7.refs_9_), channel_id=1, source_target_pairs={{0,12},{1,13},{2,14},{3,15},{4,0},{5,1},{6,2},{7,3},{8,4},{9,5},{1... | collective-permute-start | bytes 1474568 | tf_op jit(solution)/shard_map/ppermute | solution.py:45
  43.0 13.4 %copy-start.7 = (bf16[160,1536]{1,0:T(8,128)(2,1)}, bf16[160,1536]{1,0:T(8,128)(2,1)S(1)}, u32[]{:S(2)}) copy-start(bf16[160,1536]{1,0:T(8,128)(2,1)S(1)} %collective-permute-done.17.refs_19_) | copy-start | bytes 1474564
  43.0 21.5 %collective-permute-start.11 = (bf16[160,1536]{1,0:T(8,128)(2,1)S(1)}, bf16[160,1536]{1,0:T(8,128)(2,1)S(1)}, u32[]{:S(2)}, u32[]{:S(2)}) collective-permute-start(bf16[160,1536]{1,0:T(8,128)(2,1)S(1)} %collective-permute-done.7.refs_9_), channel_id=1, source_target_pairs={{0,4},{1,5},{2,6},{3,7},{4,8},{5,9},{6,10},{7,11},{8,12},{9,13},{1... | collective-permute-start | bytes 1474568 | tf_op jit(solution)/shard_map/ppermute | solution.py:45
  53.3 38.0 %copy-start.8 = (bf16[160,1536]{1,0:T(8,128)(2,1)}, bf16[160,1536]{1,0:T(8,128)(2,1)S(1)}, u32[]{:S(2)}) copy-start(bf16[160,1536]{1,0:T(8,128)(2,1)S(1)} %collective-permute-done.12.refs_14_) | copy-start | bytes 1474564
  53.3 15.4 %collective-permute-start.5 = (bf16[160,1536]{1,0:T(8,128)(2,1)S(1)}, bf16[160,1536]{1,0:T(8,128)(2,1)S(1)}, u32[]{:S(2)}, u32[]{:S(2)}) collective-permute-start(bf16[160,1536]{1,0:T(8,128)(2,1)S(1)} %collective-permute-done.2.refs_3_), channel_id=1, source_target_pairs={{0,16},{1,17},{2,18},{3,19},{4,20},{5,21},{6,22},{7,23},{8,24},{9,... | collective-permute-start | bytes 1474568 | tf_op jit(solution)/shard_map/ppermute | solution.py:45
  54.8 36.5 %copy-start.9 = (bf16[160,1536]{1,0:T(8,128)(2,1)}, bf16[160,1536]{1,0:T(8,128)(2,1)S(1)}, u32[]{:S(2)}) copy-start(bf16[160,1536]{1,0:T(8,128)(2,1)S(1)} %collective-permute-done.16.refs_18_) | copy-start | bytes 1474564
  54.8 22.9 %collective-permute-start.4 = (bf16[160,1536]{1,0:T(8,128)(2,1)S(1)}, bf16[160,1536]{1,0:T(8,128)(2,1)S(1)}, u32[]{:S(2)}, u32[]{:S(2)}) collective-permute-start(bf16[160,1536]{1,0:T(8,128)(2,1)S(1)} %collective-permute-done.refs_1_), channel_id=1, source_target_pairs={{0,16},{1,17},{2,18},{3,19},{4,20},{5,21},{6,22},{7,23},{8,24},{9,... | collective-permute-start | bytes 1474568 | tf_op jit(solution)/shard_map/ppermute | solution.py:45
  56.4 34.9 %copy-start.10 = (bf16[160,1536]{1,0:T(8,128)(2,1)}, bf16[160,1536]{1,0:T(8,128)(2,1)S(1)}, u32[]{:S(2)}) copy-start(bf16[160,1536]{1,0:T(8,128)(2,1)S(1)} %collective-permute-done.15.refs_17_) | copy-start | bytes 1474564
  56.4 21.3 %collective-permute-start.3 = (bf16[160,1536]{1,0:T(8,128)(2,1)S(1)}, bf16[160,1536]{1,0:T(8,128)(2,1)S(1)}, u32[]{:S(2)}, u32[]{:S(2)}) collective-permute-start(bf16[160,1536]{1,0:T(8,128)(2,1)S(1)} %collective-permute-done.refs_1_), channel_id=1, source_target_pairs={{0,48},{1,49},{2,50},{3,51},{4,52},{5,53},{6,54},{7,55},{8,56},{9,... | collective-permute-start | bytes 1474568 | tf_op jit(solution)/shard_map/ppermute | solution.py:45
  58.2 33.1 %copy-start.11 = (bf16[160,1536]{1,0:T(8,128)(2,1)}, bf16[160,1536]{1,0:T(8,128)(2,1)S(1)}, u32[]{:S(2)}) copy-start(bf16[160,1536]{1,0:T(8,128)(2,1)S(1)} %collective-permute-done.10.refs_12_) | copy-start | bytes 1474564
  58.2 21.3 %collective-permute-start.13 = (bf16[160,1536]{1,0:T(8,128)(2,1)S(1)}, bf16[160,1536]{1,0:T(8,128)(2,1)S(1)}, u32[]{:S(2)}, u32[]{:S(2)}) collective-permute-start(bf16[160,1536]{1,0:T(8,128)(2,1)S(1)} %collective-permute-done.10.refs_12_), channel_id=1, source_target_pairs={{0,12},{1,13},{2,14},{3,15},{4,0},{5,1},{6,2},{7,3},{8,4},{9,5},{1... | collective-permute-start | bytes 1474568 | tf_op jit(solution)/shard_map/ppermute | solution.py:45
  64.5 26.8 %copy-start.12 = (bf16[160,1536]{1,0:T(8,128)(2,1)}, bf16[160,1536]{1,0:T(8,128)(2,1)S(1)}, u32[]{:S(2)}) copy-start(bf16[160,1536]{1,0:T(8,128)(2,1)S(1)} %collective-permute-done.11.refs_13_) | copy-start | bytes 1474564
  64.5 15.1 %collective-permute-start.18 = (bf16[160,1536]{1,0:T(8,128)(2,1)S(1)}, bf16[160,1536]{1,0:T(8,128)(2,1)S(1)}, u32[]{:S(2)}, u32[]{:S(2)}) collective-permute-start(bf16[160,1536]{1,0:T(8,128)(2,1)S(1)} %collective-permute-done.10.refs_12_), channel_id=1, source_target_pairs={{0,1},{1,0},{2,3},{3,2},{4,5},{5,4},{6,7},{7,6},{8,9},{9,8},{10,11... | collective-permute-start | bytes 1474568 | tf_op jit(solution)/shard_map/ppermute | solution.py:45
  68.7 11.0 %collective-permute-start.20 = (bf16[160,1536]{1,0:T(8,128)(2,1)S(1)}, bf16[160,1536]{1,0:T(8,128)(2,1)S(1)}, u32[]{:S(2)}, u32[]{:S(2)}) collective-permute-start(bf16[160,1536]{1,0:T(8,128)(2,1)S(1)} %collective-permute-done.12.refs_14_), channel_id=1, source_target_pairs={{0,1},{1,0},{2,3},{3,2},{4,5},{5,4},{6,7},{7,6},{8,9},{9,8},{10,11... | collective-permute-start | bytes 1474568 | tf_op jit(solution)/shard_map/ppermute | solution.py:45
  77.7 2.0 %collective-permute-start.19 = (bf16[160,1536]{1,0:T(8,128)(2,1)S(1)}, bf16[160,1536]{1,0:T(8,128)(2,1)S(1)}, u32[]{:S(2)}, u32[]{:S(2)}) collective-permute-start(bf16[160,1536]{1,0:T(8,128)(2,1)S(1)} %collective-permute-done.11.refs_13_), channel_id=1, source_target_pairs={{0,1},{1,0},{2,3},{3,2},{4,5},{5,4},{6,7},{7,6},{8,9},{9,8},{10,11... | collective-permute-start | bytes 1474568 | tf_op jit(solution)/shard_map/ppermute | solution.py:45
  77.7 13.6 %collective-permute-start.6 = (bf16[160,1536]{1,0:T(8,128)(2,1)S(1)}, bf16[160,1536]{1,0:T(8,128)(2,1)S(1)}, u32[]{:S(2)}, u32[]{:S(2)}) collective-permute-start(bf16[160,1536]{1,0:T(8,128)(2,1)S(1)} %collective-permute-done.3.refs_4_), channel_id=1, source_target_pairs={{0,48},{1,49},{2,50},{3,51},{4,52},{5,53},{6,54},{7,55},{8,56},{9,... | collective-permute-start | bytes 1474568 | tf_op jit(solution)/shard_map/ppermute | solution.py:45
  79.5 11.9 %copy-start.13 = (bf16[160,1536]{1,0:T(8,128)(2,1)}, bf16[160,1536]{1,0:T(8,128)(2,1)S(1)}, u32[]{:S(2)}) copy-start(bf16[160,1536]{1,0:T(8,128)(2,1)S(1)} %collective-permute-done.13.refs_15_) | copy-start | bytes 1474564
  79.5 12.7 %collective-permute-start.21 = (bf16[160,1536]{1,0:T(8,128)(2,1)S(1)}, bf16[160,1536]{1,0:T(8,128)(2,1)}, u32[]{:S(2)}, u32[]{:S(2)}) collective-permute-start(bf16[160,1536]{1,0:T(8,128)(2,1)S(1)} %collective-permute-done.13.refs_15_), channel_id=1, source_target_pairs={{0,1},{1,0},{2,3},{3,2},{4,5},{5,4},{6,7},{7,6},{8,9},{9,8},{10,11... | collective-permute-start | bytes 1474568 | tf_op jit(solution)/shard_map/ppermute | solution.py:45
  79.7 11.7 %copy-start.15 = (bf16[160,1536]{1,0:T(8,128)(2,1)}, bf16[160,1536]{1,0:T(8,128)(2,1)S(1)}, u32[]{:S(2)}) copy-start(bf16[160,1536]{1,0:T(8,128)(2,1)S(1)} %collective-permute-done.20.refs_22_) | copy-start | bytes 1474564
  79.7 11.7 %copy-start.16 = (bf16[160,1536]{1,0:T(8,128)(2,1)}, bf16[160,1536]{1,0:T(8,128)(2,1)S(1)}, u32[]{:S(2)}) copy-start(bf16[160,1536]{1,0:T(8,128)(2,1)S(1)} %collective-permute-done.19.refs_21_) | copy-start | bytes 1474564
  79.7 11.7 %copy-start.14 = (bf16[160,1536]{1,0:T(8,128)(2,1)}, bf16[160,1536]{1,0:T(8,128)(2,1)S(1)}, u32[]{:S(2)}) copy-start(bf16[160,1536]{1,0:T(8,128)(2,1)S(1)} %collective-permute-done.18.refs_20_) | copy-start | bytes 1474564
  91.4 0.8 copy-start
  92.2 1.0 copy-start.1
  93.2 57.9 %copy-start.2 = (f32[345,160]{0,1:T(8,128)S(1)}, f32[345,160]{0,1:T(8,128)}, u32[]{:S(2)}) copy-start(f32[345,160]{0,1:T(8,128)} %param.7) | copy-start | bytes 662404
  121.1 10.1 %collective-permute-start.22 = (f32[160,345]{1,0:T(8,128)S(1)}, f32[160,345]{1,0:T(8,128)S(1)}, u32[]{:S(2)}, u32[]{:S(2)}) collective-permute-start(f32[160,345]{1,0:T(8,128)S(1)} %get-tuple-element.14), channel_id=1, source_target_pairs={{0,66},{1,67},{2,64},{3,65},{4,70},{5,71},{6,68},{7,69},{8,74},{9,... | collective-permute-start | bytes 662408 | tf_op jit(solution)/shard_map/ppermute | solution.py:45
  122.6 9.7 %collective-permute-start.23 = (f32[160,345]{1,0:T(8,128)S(1)}, f32[160,345]{1,0:T(8,128)S(1)}, u32[]{:S(2)}, u32[]{:S(2)}) collective-permute-start(f32[160,345]{1,0:T(8,128)S(1)} %get-tuple-element.15), channel_id=1, source_target_pairs={{0,16},{1,17},{2,18},{3,19},{4,20},{5,21},{6,22},{7,23},{8,24},{9,... | collective-permute-start | bytes 662408 | tf_op jit(solution)/shard_map/ppermute | solution.py:45
  122.9 13.1 %collective-permute-start.24 = (f32[160,345]{1,0:T(8,128)S(1)}, f32[160,345]{1,0:T(8,128)S(1)}, u32[]{:S(2)}, u32[]{:S(2)}) collective-permute-start(f32[160,345]{1,0:T(8,128)S(1)} %get-tuple-element.16), channel_id=1, source_target_pairs={{0,48},{1,49},{2,50},{3,51},{4,52},{5,53},{6,54},{7,55},{8,56},{9,... | collective-permute-start | bytes 662408 | tf_op jit(solution)/shard_map/ppermute | solution.py:45
  125.8 14.6 %collective-permute-start.25 = (f32[160,345]{1,0:T(8,128)S(1)}, f32[160,345]{1,0:T(8,128)S(1)}, u32[]{:S(2)}, u32[]{:S(2)}) collective-permute-start(f32[160,345]{1,0:T(8,128)S(1)} %get-tuple-element.17), channel_id=1, source_target_pairs={{0,82},{1,83},{2,80},{3,81},{4,86},{5,87},{6,84},{7,85},{8,90},{9,... | collective-permute-start | bytes 662408 | tf_op jit(solution)/shard_map/ppermute | solution.py:45
  126.1 14.4 %collective-permute-start.26 = (f32[160,345]{1,0:T(8,128)S(1)}, f32[160,345]{1,0:T(8,128)S(1)}, u32[]{:S(2)}, u32[]{:S(2)}) collective-permute-start(f32[160,345]{1,0:T(8,128)S(1)} %get-tuple-element.18), channel_id=1, source_target_pairs={{0,114},{1,115},{2,112},{3,113},{4,118},{5,119},{6,116},{7,117},{8... | collective-permute-start | bytes 662408 | tf_op jit(solution)/shard_map/ppermute | solution.py:45
  131.2 15.2 %collective-permute-start.27 = (f32[160,345]{1,0:T(8,128)S(1)}, f32[160,345]{1,0:T(8,128)S(1)}, u32[]{:S(2)}, u32[]{:S(2)}) collective-permute-start(f32[160,345]{1,0:T(8,128)S(1)} %get-tuple-element.19), channel_id=1, source_target_pairs={{0,32},{1,33},{2,34},{3,35},{4,36},{5,37},{6,38},{7,39},{8,40},{9,... | collective-permute-start | bytes 662408 | tf_op jit(solution)/shard_map/ppermute | solution.py:45
  132.3 18.8 %collective-permute-start.28 = (f32[160,345]{1,0:T(8,128)S(1)}, f32[160,345]{1,0:T(8,128)S(1)}, u32[]{:S(2)}, u32[]{:S(2)}) collective-permute-start(f32[160,345]{1,0:T(8,128)S(1)} %get-tuple-element.20), channel_id=1, source_target_pairs={{0,98},{1,99},{2,96},{3,97},{4,102},{5,103},{6,100},{7,101},{8,106... | collective-permute-start | bytes 662408 | tf_op jit(solution)/shard_map/ppermute | solution.py:45
Sparse Core Ops, SparseCore 0:
  9.1 47.9 all-gather.1

commit v2 on v0

v2 whole, which is shorter than its diff:
```python
import functools

import jax
import jax.numpy as jnp
from jax import lax
from jax.experimental import pallas as pl
from jax.experimental.pallas import tpu as pltpu
from jax.sharding import PartitionSpec as P

FEAT = 768
CLASSES = 345
LANES = 384
OWN = 160
AXES = ("row", "col")

damping = 0.8
ridge = 0.1

f32, bf16 = jnp.float32, jnp.bfloat16
NT = (((1,), (1,)), ((), ()))
NN = (((1,), (0,)), ((), ()))
VMEM = pl.BlockSpec(memory_space=pltpu.VMEM)


def encode(x, y, z, core):
    return ((((z >> 1) * 4 + x) * 4 + y) * 2 + (z & 1)) * 2 + core


def decode(index):
    return (index >> 4) & 3, (index >> 2) & 3, (index >> 6) * 2 + ((index >> 1) & 1), index & 1


def moves(group, dims):
    pairs = []
    for index in range(128):
        x, y, z, core = decode(index)
        place = {"x": x, "y": y, "z": z}
        for dim in dims:
            if dim == "c":
                core ^= 1
            else:
                place[dim] = 3 - place[dim] if group == "far" else place[dim] ^ 1
        pairs.append((index, encode(place["x"], place["y"], place["z"], core)))
    return pairs


def send(value, group, dims):
    return lax.ppermute(value, AXES, moves(group, dims))


def after(value, *others):
    return lax.optimization_barrier((value, *others))[0]


def dot(a, b, dims):
    return lax.dot_general(a, b, dims, preferred_element_type=f32)


def split_kernel(coef, split):
    split[...] = jnp.zeros_like(split)
    values = coef[...]
    high = values.astype(bf16)
    split[:, :CLASSES] = high
    split[:, LANES : LANES + CLASSES] = (values - high.astype(f32)).astype(bf16)


def split_coefs(coefs):
    return pl.pallas_call(
        split_kernel,
        out_shape=pltpu.VMEM((OWN, 2 * LANES), bf16),
        in_specs=[VMEM],
        out_specs=VMEM,
        compiler_params=pltpu.CompilerParams(vmem_limit_bytes=4 << 20),
        name="split_coefs",
    )(coefs)


def arrange_kernel(plan, n_in, *refs):
    for out, pieces in zip(refs[n_in:], plan):
        for source, row, out_row, out_col in pieces:
            out[out_row * OWN : (out_row + 1) * OWN, out_col * FEAT : (out_col + 1) * FEAT] = refs[source][
                row * OWN : (row + 1) * OWN, :
            ]


def arrange(outputs, name):
    arrays, plan, shapes = [], [], []

    def place(array):
        for i, known in enumerate(arrays):
            if known is array:
                return i
        arrays.append(array)
        return len(arrays) - 1

    for columns in outputs:
        plan.append(
            [
                (place(array), block, out_row, out_col)
                for out_col, column in enumerate(columns)
                for out_row, (array, block) in enumerate(column)
            ]
        )
        shapes.append(pltpu.VMEM((len(columns[0]) * OWN, len(columns) * FEAT), bf16))
    return pl.pallas_call(
        functools.partial(arrange_kernel, plan, len(arrays)),
        out_shape=shapes,
        in_specs=[VMEM] * len(arrays),
        out_specs=[VMEM] * len(shapes),
        compiler_params=pltpu.CompilerParams(vmem_limit_bytes=8 << 20),
        name=name,
    )(*arrays)


def block_kernel(plan, n_in, with_total, apart, rows, *refs):
    inputs, refs = refs[:n_in], refs[n_in:]
    total_in, refs = (refs[0], refs[1:]) if with_total else (None, refs)
    outs, (right, left, split) = refs[:-3], refs[-3:]
    targets = (right, left, split)
    for target, out_row, out_col, source, row, col in plan:
        targets[target][out_row * OWN : (out_row + 1) * OWN, out_col * FEAT : (out_col + 1) * FEAT] = inputs[source][
            row * OWN : (row + 1) * OWN, col * FEAT : (col + 1) * FEAT
        ]
    n_right, n_left = right.shape[0], left.shape[0]
    for start in range(0, n_right, rows):
        n = slice(start, start + rows)
        part = total_in[n, :] if with_total else None
        at = 0
        while at < n_left:
            size = min(512, n_left - at)
            m = slice(at, at + size)
            at += size
            gram_a = dot(right[n, :FEAT], left[m, :FEAT], NT)
            gram_s = dot(right[n, FEAT:], left[m, FEAT:], NT)
            kernel = gram_a * gram_s
            high = kernel.astype(bf16)
            low = (kernel - high.astype(f32)).astype(bf16)
            both = dot(high, split[m, :], NN)
            new = both[:, :LANES] + both[:, LANES:] + dot(low, split[m, :LANES], NN)
            part = new if part is None else part + new
        if apart:
            for i in range(rows // OWN):
                outs[start // OWN + i][...] = part[i * OWN : (i + 1) * OWN, :CLASSES]
        else:
            outs[0][n, :] = part


def partial_sums(right, left, total, apart, rows, name):
    arrays, plan = [], []

    def place(array):
        for i, known in enumerate(arrays):
            if known is array:
                return i
        arrays.append(array)
        return len(arrays) - 1

    for i, (act, sig) in enumerate(right):
        plan.append((0, i, 0, place(act[0]), act[1], act[2]))
        plan.append((0, i, 1, place(sig[0]), sig[1], sig[2]))
    for i, (act, sig, coef) in enumerate(left):
        plan.append((1, i, 0, place(act[0]), act[1], act[2]))
        plan.append((1, i, 1, place(sig[0]), sig[1], sig[2]))
        plan.append((2, i, 0, place(coef[0]), coef[1], coef[2]))
    n_right, n_left = len(right), len(left)
    if apart:
        out_shape = [pltpu.VMEM((OWN, CLASSES), f32)] * n_right
    else:
        out_shape = [pltpu.VMEM((n_right * OWN, LANES), f32)]
    pairs = n_right * n_left * OWN * OWN
    return pl.pallas_call(
        functools.partial(block_kernel, plan, len(arrays), total is not None, apart, rows),
        out_shape=out_shape,
        in_specs=[VMEM] * (len(arrays) + (total is not None)),
        out_specs=[VMEM] * len(out_shape),
        scratch_shapes=[
            pltpu.VMEM((n_right * OWN, 2 * FEAT), bf16),
            pltpu.VMEM((n_left * OWN, 2 * FEAT), bf16),
            pltpu.VMEM((n_left * OWN, 2 * LANES), bf16),
        ],
        cost_estimate=pl.CostEstimate(flops=pairs * 5400, bytes_accessed=8_000_000, transcendentals=0),
        compiler_params=pltpu.CompilerParams(vmem_limit_bytes=24 << 20),
        name=name,
    )(*arrays, *([] if total is None else [total]))


def shards(activations, signals, labels, coefficients):
    coefs = coefficients.T
    groups = ("far", "near")
    a, s, c = {}, {}, {}
    for g in groups:
        a[g, "x"] = send(activations, g, "x")
        s[g, "y"] = send(signals, g, "y")
    c0 = split_coefs(coefs)
    cz = send(c0, "near", "z")
    pairs = arrange(
        [[[(activations, 0), (a[g, "x"], 0)]] for g in groups]
        + [[[(signals, 0), (s[g, "y"], 0)]] for g in groups]
        + [[[(c0, 0), (cz, 0)]]]
        + [[[(activations, 0), (a["near", "x"], 0)], [(signals, 0), (s["near", "y"], 0)], [(c0, 0), (cz, 0)]]],
        "pairs",
    )
    a0x, s0y, c0z, own2 = dict(zip(groups, pairs[:2])), dict(zip(groups, pairs[2:4])), pairs[4], pairs[5]
    ay, sz = {}, {}
    for g in groups:
        ay[g] = send(a0x[g], g, "y")
        sz[g] = send(s0y[g], g, "z")
    cx = send(c0z, "near", "x")
    own2_mate = send(own2, "near", "c")
    ay["far"], ay["near"], sz["far"], sz["near"], cx = lax.optimization_barrier(
        (ay["far"], ay["near"], sz["far"], sz["near"], cx)
    )
    fours = arrange(
        [[[(a0x[g], 0), (ay[g], 0)]] for g in groups]
        + [[[(a0x[g], 1), (ay[g], 1)]] for g in groups]
        + [[[(ay["near"], 0), (ay["near"], 1)], [(sz["near"], 0), (sz["near"], 1)], [(cx, 0), (cx, 1)]]],
        "fours",
    )
    a0y, axxy, next2 = dict(zip(groups, fours[:2])), dict(zip(groups, fours[2:4])), fours[4]
    az, sx = {}, {}
    for g in groups:
        az[g] = send(after(a0y[g], own2_mate), g, "z")
        sx[g] = send(after(s0y[g], next2, own2_mate), g, "x")
    cy = send(after(c0z, next2, own2_mate), "near", "y")
    az["far"], az["near"], sx["far"], sx["near"], cy, next2 = lax.optimization_barrier(
        (az["far"], az["near"], sx["far"], sx["near"], cy, next2)
    )
    mates = [send(v, "near", "c") for v in (next2, az["near"], sx["near"], cy)]
    next2_mate, az_mate, sx_mate, cy_mate = mates
    axz, sxz = {}, {}
    for g in groups:
        axz[g] = send(after(axxy[g], cy), g, "z")
        sxz[g] = send(after(sz[g], cy), g, "x")
    cxy = send(after(cx, *mates), "near", "y")

    def blocks_of(g):
        act = {"": (a0x[g], 0, 0), "x": (a0x[g], 1, 0), "y": (ay[g], 0, 0), "xy": (ay[g], 1, 0)}
        act |= {"z": (az[g], 0, 0), "yz": (az[g], 1, 0), "xz": (axz[g], 0, 0), "xyz": (axz[g], 1, 0)}
        sig = {"": (s0y[g], 0, 0), "y": (s0y[g], 1, 0), "z": (sz[g], 0, 0), "yz": (sz[g], 1, 0)}
        sig |= {"x": (sx[g], 0, 0), "xy": (sx[g], 1, 0), "xz": (sxz[g], 0, 0), "xyz": (sxz[g], 1, 0)}
        return act, sig

    act, sig = blocks_of("far")
    right = {k: (act[k], sig[k]) for k in act}
    act, sig = blocks_of("near")
    coef = {"": (c0z, 0, 0), "z": (c0z, 1, 0), "x": (cx, 0, 0), "xz": (cx, 1, 0)}
    coef |= {"y": (cy, 0, 0), "yz": (cy, 1, 0), "xy": (cxy, 0, 0), "xyz": (cxy, 1, 0)}
    left = {k: (act[k], sig[k], coef[k]) for k in act}
    right_1 = [right[k] for k in ("", "x", "y", "xy", "z", "yz")]
    right_2 = [right[k] for k in ("xz", "xyz")]
    act_mate = {"": (own2_mate, 0, 0), "x": (own2_mate, 1, 0), "y": (next2_mate, 0, 0), "xy": (next2_mate, 1, 0)}
    act_mate |= {"z": (az_mate, 0, 0), "yz": (az_mate, 1, 0)}
    sig_mate = {"": (own2_mate, 0, 1), "y": (own2_mate, 1, 1), "z": (next2_mate, 0, 1), "yz": (next2_mate, 1, 1)}
    sig_mate |= {"x": (sx_mate, 0, 0), "xy": (sx_mate, 1, 0)}
    coef_mate = {"": (own2_mate, 0, 2), "z": (own2_mate, 1, 2), "x": (next2_mate, 0, 2), "xz": (next2_mate, 1, 2)}
    coef_mate |= {"y": (cy_mate, 0, 0), "yz": (cy_mate, 1, 0)}
    first = ("", "x", "y", "z", "yz")
    left_1 = [left[k] for k in first] + [(act_mate[k], sig_mate[k], coef_mate[k]) for k in first]
    (total_1,) = partial_sums(right_1, left_1, None, False, 480, "early")

    axz_mate, sxz_mate, cxy_mate = [send(after(v, total_1), "near", "c") for v in (axz["near"], sxz["near"], cxy)]
    act_mate |= {"xz": (axz_mate, 0, 0), "xyz": (axz_mate, 1, 0)}
    sig_mate |= {"xz": (sxz_mate, 0, 0), "xyz": (sxz_mate, 1, 0)}
    coef_mate |= {"xy": (cxy_mate, 0, 0), "xyz": (cxy_mate, 1, 0)}
    second = ("xy", "xz", "xyz")
    left_2 = [left[k] for k in second] + [(act_mate[k], sig_mate[k], coef_mate[k]) for k in second]
    (total_2,) = partial_sums(right_2, left_1, None, False, 320, "late_right")
    sum_xz, sum_xyz = partial_sums(right_2, left_2, total_2, True, 320, "late_both")
    total_1 = after(total_1, sum_xz)
    own, sum_x, sum_y, sum_xy, sum_z, sum_yz = partial_sums(right_1, left_2, total_1, True, 480, "late_left")

    product = own
    for part, dims in ((sum_xyz, "xyz"), (sum_xz, "xz"), (sum_xy, "xy"), (sum_yz, "yz"), (sum_x, "x"), (sum_y, "y"), (sum_z, "z")):
        product = product + send(part, "far", dims)
    product = product * (1.0 / (FEAT * FEAT))
    classes = jnp.arange(CLASSES, dtype=jnp.int32)
    targets = (labels[:, None] == classes[None, :]).astype(f32) - 1.0 / CLASSES
    return (coefs + damping * (targets - product - ridge * coefs)).T


def solution(mesh):
    in_specs = (P(AXES, None), P(AXES, None), P(AXES), P(None, AXES))
    return jax.shard_map(shards, mesh=mesh, in_specs=in_specs, out_specs=P(None, AXES), check_vma=False)
```

time: 341 us -> 128 us (0.38)
  waiting for transfers between devices: 282 us -> 50.3 us
  starting transfers between devices: 0.19 us -> 50.4 us
  matrix products: 41.4 us -> 0 us
  Pallas kernels: 0 us -> 22.9 us
  between operations: 13.5 us -> 0.15 us
    all_gather x5 -> x0, waiting for transfers between devices: 203 us -> none  [the longest x1 56.3 us: shards(): lax.all_gather(activations, 'row', axis=0, tiled=True)]
    unnamed x7 -> x0, waiting for transfers between devices: 78.9 us -> none
    ppermute x0 -> x35, starting transfers between devices: none -> 50.4 us  [send(): return lax.ppermute(value, AXES, moves(group, dims))]
    ppermute x0 -> x35, waiting for transfers between devices: none -> 50.3 us  [send(): return lax.ppermute(value, AXES, moves(group, dims))]
    dot_general x3 -> x0, matrix products: 41.4 us -> none  [the longest x1 18.6 us: shards(): jnp.dot(far_coefs, kernel, precision=lax.Precision.HIGHEST, preferred_ele...]
    pallas_call x0 -> x7, Pallas kernels: none -> 22.9 us  [the longest x4 22.4 us: partial_sums(): pl.pallas_call(functools.partial(block_kernel, plan, len(arrays), total i...]
  transfers between devices with their start and end apart: 6 -> 35, of which waited for: 6 -> 18; matrix products, arithmetic and copies ran while one was open for 7% -> 0% of each run, Pallas kernels for 0% -> 11%
where the time goes in v2:
time: 128 us
  starting transfers between devices  50.4 us (39%)
  waiting for transfers between devices  50.3 us (39%)
  Pallas kernels  22.9 us (18%)
  local copies, waits for them, and re-layouts  2.84 us (2%)
    ppermute x35, starting transfers between devices, send(): return lax.ppermute(value, AXES, moves(group, dims))  50.4 us
    ppermute x35, waiting for transfers between devices, send(): return lax.ppermute(value, AXES, moves(group, dims))  50.3 us
    pallas_call x4, Pallas kernels, partial_sums(): pl.pallas_call(functools.partial(block_kernel, plan, len(arrays), total i...  22.4 us
    unnamed x10, local copies, waits for them, and re-layouts  2.84 us
  transfers between devices with their start and end apart: 35, of which 18 were waited for; matrix products, arithmetic and copies ran while one was open for 0% of the time, Pallas kernels for 11%

profile of v2, /device:TPU:0, one launch (start us, length us, event | category | flops | bytes accessed | tf_op | source)
XLA Modules:
  0.0 127.5 jit_solution(15668684181105350735)
XLA Ops:
  0.0 0.9 copy-done
  1.0 2.1 %collective-permute-start.4 = (bf16[160,768]{1,0:T(8,128)(2,1)S(1)}, bf16[160,768]{1,0:T(8,128)(2,1)S(1)}, u32[]{:S(2)}, u32[]{:S(2)}) collective-permute-start(bf16[160,768]{1,0:T(8,128)(2,1)S(1)} %split_coefs.1.refs_6_), channel_id=1, source_target_pairs={{0,2},{1,3},{2,0},{3,1},{4,6},{5,7},{6,4},{7,5},{8,10},{9,11},{10,... | collective-permute-start | bytes 737288 | tf_op jit(solution)/shard_map/ppermute | solution.py:48
  3.1 2.8 %collective-permute-start = (bf16[160,768]{1,0:T(8,128)(2,1)}, bf16[160,768]{1,0:T(8,128)(2,1)S(1)}, u32[]{:S(2)}, u32[]{:S(2)}) collective-permute-start(bf16[160,768]{1,0:T(8,128)(2,1)} %refs_0_.1), channel_id=1, source_target_pairs={{0,48},{1,49},{2,50},{3,51},{4,52},{5,53},{6,54},{7,55},{8,56},{9,... | collective-permute-start | bytes 737288 | tf_op jit(solution)/shard_map/ppermute | solution.py:48
  5.8 0.2 collective-permute-start.1
  6.1 3.0 %collective-permute-start.2 = (bf16[160,768]{1,0:T(8,128)(2,1)}, bf16[160,768]{1,0:T(8,128)(2,1)S(1)}, u32[]{:S(2)}, u32[]{:S(2)}) collective-permute-start(bf16[160,768]{1,0:T(8,128)(2,1)} %refs_3_.1), channel_id=1, source_target_pairs={{0,12},{1,13},{2,14},{3,15},{4,8},{5,9},{6,10},{7,11},{8,4},{9,5},... | collective-permute-start | bytes 737288 | tf_op jit(solution)/shard_map/ppermute | solution.py:48
  9.1 0.1 collective-permute-start.3
  9.2 2.7 %collective-permute-done.refs_1_ = bf16[160,768]{1,0:T(8,128)(2,1)S(1)} collective-permute-done((bf16[160,768]{1,0:T(8,128)(2,1)}, bf16[160,768]{1,0:T(8,128)(2,1)S(1)}, u32[]{:S(2)}, u32[]{:S(2)}) %collective-permute-start) | collective-permute-done | bytes 245792 | tf_op jit(solution)/shard_map/ppermute | solution.py:48
  11.9 1.3 collective-permute-done.1.refs_2_
  13.2 1.3 collective-permute-done.2.refs_4_
  14.5 1.5 %collective-permute-done.3.refs_5_ = bf16[160,768]{1,0:T(8,128)(2,1)S(1)} collective-permute-done((bf16[160,768]{1,0:T(8,128)(2,1)}, bf16[160,768]{1,0:T(8,128)(2,1)S(1)}, u32[]{:S(2)}, u32[]{:S(2)}) %collective-permute-start.3) | collective-permute-done | bytes 245792 | tf_op jit(solution)/shard_map/ppermute | solution.py:48
  15.9 0.9 copy-done.2
  16.9 0.9 copy-done.3
  17.8 0.3 pairs.1
  18.1 0.1 collective-permute-start.10
  18.2 1.6 %collective-permute-start.5 = (bf16[320,768]{1,0:T(8,128)(2,1)S(1)}, bf16[320,768]{1,0:T(8,128)(2,1)S(1)}, u32[]{:S(2)}, u32[]{:S(2)}) collective-permute-start(bf16[320,768]{1,0:T(8,128)(2,1)S(1)} %get-tuple-element.49.refs_0_), channel_id=1, source_target_pairs={{0,12},{1,13},{2,14},{3,15},{4,8},{5,9},{6,10},{7,11},{8,4},{9,5},... | collective-permute-start | bytes 1474568 | tf_op jit(solution)/shard_map/ppermute | solution.py:48
  19.7 2.5 %collective-permute-start.7 = (bf16[320,768]{1,0:T(8,128)(2,1)S(1)}, bf16[320,768]{1,0:T(8,128)(2,1)S(1)}, u32[]{:S(2)}, u32[]{:S(2)}) collective-permute-start(bf16[320,768]{1,0:T(8,128)(2,1)S(1)} %get-tuple-element.64.refs_1_), channel_id=1, source_target_pairs={{0,66},{1,67},{2,64},{3,65},{4,70},{5,71},{6,68},{7,69},{8,74},{9,... | collective-permute-start | bytes 1474568 | tf_op jit(solution)/shard_map/ppermute | solution.py:48
  22.3 1.0 collective-permute-start.8
  23.3 9.7 %collective-permute-done.5.refs_1_.refs_3_ = bf16[320,768]{1,0:T(8,128)(2,1)S(1)} collective-permute-done((bf16[320,768]{1,0:T(8,128)(2,1)S(1)}, bf16[320,768]{1,0:T(8,128)(2,1)S(1)}, u32[]{:S(2)}, u32[]{:S(2)}) %collective-permute-start.5) | collective-permute-done | bytes 491552 | tf_op jit(solution)/shard_map/ppermute | solution.py:48
  33.0 1.7 %collective-permute-start.9 = (bf16[320,768]{1,0:T(8,128)(2,1)S(1)}, bf16[320,768]{1,0:T(8,128)(2,1)S(1)}, u32[]{:S(2)}, u32[]{:S(2)}) collective-permute-start(bf16[320,768]{1,0:T(8,128)(2,1)S(1)} %get-tuple-element.66.refs_8_.refs_4_), channel_id=1, source_target_pairs={{0,16},{1,17},{2,18},{3,19},{4,20},{5,21},{6,22},{7,23},{8,24},{9,... | collective-permute-start | bytes 1474568 | tf_op jit(solution)/shard_map/ppermute | solution.py:48
  34.8 0.5 collective-permute-done.8.refs_4_.refs_14_.refs_10_
  35.3 10.5 %collective-permute-done.9.refs_5_.refs_10_.refs_6_.refs_7_.refs_11_ = bf16[320,768]{1,0:T(8,128)(2,1)S(1)} collective-permute-done((bf16[320,768]{1,0:T(8,128)(2,1)S(1)}, bf16[320,768]{1,0:T(8,128)(2,1)S(1)}, u32[]{:S(2)}, u32[]{:S(2)}) %collective-permute-start.9) | collective-permute-done | bytes 491552 | tf_op jit(solution)/shard_map/ppermute | solution.py:48
  45.8 0.2 fours.1
  46.0 0.0 collective-permute-done.10.refs_15_.refs_11_
  46.0 0.1 collective-permute-start.15
  46.1 1.8 %collective-permute-start.14 = (bf16[320,768]{1,0:T(8,128)(2,1)S(1)}, bf16[320,768]{1,0:T(8,128)(2,1)S(1)}, u32[]{:S(2)}, u32[]{:S(2)}) collective-permute-start(bf16[320,768]{1,0:T(8,128)(2,1)S(1)} %get-tuple-element.65.refs_7_.refs_3_), channel_id=1, source_target_pairs={{0,16},{1,17},{2,18},{3,19},{4,20},{5,21},{6,22},{7,23},{8,24},{9,... | collective-permute-start | bytes 1474568 | tf_op jit(solution)/shard_map/ppermute | solution.py:48
  47.9 0.5 collective-permute-start.13
  48.4 0.4 collective-permute-start.12
  48.8 3.8 %collective-permute-start.11 = (bf16[320,768]{1,0:T(8,128)(2,1)S(1)}, bf16[320,768]{1,0:T(8,128)(2,1)S(1)}, u32[]{:S(2)}, u32[]{:S(2)}) collective-permute-start(bf16[320,768]{1,0:T(8,128)(2,1)S(1)} %get-tuple-element.60), channel_id=1, source_target_pairs={{0,66},{1,67},{2,64},{3,65},{4,70},{5,71},{6,68},{7,69},{8,74},{9,... | collective-permute-start | bytes 1474568 | tf_op jit(solution)/shard_map/ppermute | solution.py:48
  52.6 5.4 %collective-permute-done.15.refs_12_.refs_8_ = bf16[320,768]{1,0:T(8,128)(2,1)S(1)} collective-permute-done((bf16[320,768]{1,0:T(8,128)(2,1)S(1)}, bf16[320,768]{1,0:T(8,128)(2,1)S(1)}, u32[]{:S(2)}, u32[]{:S(2)}) %collective-permute-start.15) | collective-permute-done | bytes 491552 | tf_op jit(solution)/shard_map/ppermute | solution.py:48
  58.0 0.1 collective-permute-done.14.refs_9_.refs_5_.refs_3_.refs_7_
  58.1 2.7 %collective-permute-done.13.refs_2_ = bf16[320,768]{1,0:T(8,128)(2,1)S(1)} collective-permute-done((bf16[320,768]{1,0:T(8,128)(2,1)S(1)}, bf16[320,768]{1,0:T(8,128)(2,1)S(1)}, u32[]{:S(2)}, u32[]{:S(2)}) %collective-permute-start.13) | collective-permute-done | bytes 491552 | tf_op jit(solution)/shard_map/ppermute | solution.py:48
  60.7 1.1 collective-permute-done.11.refs_4_
  61.8 0.0 collective-permute-start.16
  61.8 0.5 collective-permute-start.17
  62.3 0.0 collective-permute-start.18
  62.4 0.5 collective-permute-start.19
  62.9 2.8 %collective-permute-start.27 = (bf16[320,768]{1,0:T(8,128)(2,1)S(1)}, bf16[320,768]{1,0:T(8,128)(2,1)S(1)}, u32[]{:S(2)}, u32[]{:S(2)}) collective-permute-start(bf16[320,768]{1,0:T(8,128)(2,1)S(1)} %collective-permute-done.7.refs_5_), channel_id=1, source_target_pairs={{0,48},{1,49},{2,50},{3,51},{4,52},{5,53},{6,54},{7,55},{8,56},{9,... | collective-permute-start | bytes 1474568 | tf_op jit(solution)/shard_map/ppermute | solution.py:48
  65.6 0.2 collective-permute-done.17.refs_19_.refs_15_
  65.8 3.0 %collective-permute-start.26 = (bf16[320,768]{1,0:T(8,128)(2,1)S(1)}, bf16[320,768]{1,0:T(8,128)(2,1)S(1)}, u32[]{:S(2)}, u32[]{:S(2)}) collective-permute-start(bf16[320,768]{1,0:T(8,128)(2,1)S(1)} %get-tuple-element.82), channel_id=1, source_target_pairs={{0,66},{1,67},{2,64},{3,65},{4,70},{5,71},{6,68},{7,69},{8,74},{9,... | collective-permute-start | bytes 1474568 | tf_op jit(solution)/shard_map/ppermute | solution.py:48
  68.8 0.3 collective-permute-start.22
  69.1 0.0 collective-permute-start.21
  69.1 1.9 %collective-permute-start.20 = (bf16[320,768]{1,0:T(8,128)(2,1)S(1)}, bf16[320,768]{1,0:T(8,128)(2,1)S(1)}, u32[]{:S(2)}, u32[]{:S(2)}) collective-permute-start(bf16[320,768]{1,0:T(8,128)(2,1)S(1)} %collective-permute-done.9.refs_5_.refs_10_.refs_6_.refs_7_.refs_11_), channel_id=1, source_target_pairs={{0,4},{1,5},{2,6},{3,7},{4,0},{5,1},{6,2},{7,3},{8,12},{9,13},{10,... | collective-permute-start | bytes 1474568 | tf_op jit(solution)/shard_map/ppermute | solution.py:48
  71.0 10.4 %early.1.refs_17_ = f32[960,384]{1,0:T(8,128)S(1)} custom-call(bf16[320,768]{1,0:T(8,128)(2,1)S(1)} %get-tuple-element.49.refs_0_, bf16[320,768]{1,0:T(8,128)(2,1)S(1)} %get-tuple-element.64.refs_1_, bf16[320,768]{1,0:T(8,128)(2,1)S(1)} %collective-permute-done.13.refs_2_, bf16[320,768]{1,0:T(8,128)(2,1)S(1)} %collective-permute-done.5.refs_1_.refs_3_, ...), custom_call_target="tpu_custom_call" | custom-call | flops 8294400000 | bytes 8000000 | tf_op jit(solution)/shard_map/early/pallas_call | solution.py:171
  81.4 0.4 collective-permute-done.22.refs_6_.refs_10_
  81.8 0.1 collective-permute-done.21.refs_5_.refs_9_
  81.8 0.4 collective-permute-start.24
  82.3 0.3 collective-permute-start.23
  82.6 3.8 %late_right.1.refs_13_ = f32[320,384]{1,0:T(8,128)S(1)} custom-call(bf16[320,768]{1,0:T(8,128)(2,1)S(1)} %collective-permute-done.26.refs_0_, bf16[320,768]{1,0:T(8,128)(2,1)S(1)} %collective-permute-done.27.refs_1_, bf16[320,768]{1,0:T(8,128)(2,1)S(1)} %get-tuple-element.51.refs_2_.refs_6_, bf16[320,768]{1,0:T(8,128)(2,1)S(1)} %get-tuple-element.65.refs_7_.refs_3_, ...), custom_call_target="tpu_custom_call" | custom-call | flops 2764800000 | bytes 8000000 | tf_op jit(solution)/shard_map/late_right/pallas_call | solution.py:171
  86.4 2.3 %late_both.1 = (f32[160,345]{1,0:T(8,128)S(1)}, f32[160,345]{1,0:T(8,128)S(1)}) custom-call(bf16[320,768]{1,0:T(8,128)(2,1)S(1)} %collective-permute-done.26.refs_0_, bf16[320,768]{1,0:T(8,128)(2,1)S(1)} %collective-permute-done.27.refs_1_, bf16[320,768]{1,0:T(8,128)(2,1)S(1)} %collective-permute-done.6.refs_3_.refs_11_.refs_7_.refs_2_.refs_6_, ...), custom_call_target="tpu_custom_call" | custom-call | flops 1658880000 | bytes 8000000 | tf_op jit(solution)/shard_map/late_both/pallas_call | solution.py:171
  88.7 0.0 copy-start.1
  88.7 0.0 copy-start.4
  88.7 6.0 %late_left.1 = (f32[160,345]{1,0:T(8,128)S(1)}, f32[160,345]{1,0:T(8,128)S(1)}, f32[160,345]{1,0:T(8,128)S(1)}, f32[160,345]{1,0:T(8,128)S(1)}, f32[160,345]{1,0:T(8,128)S(1)}, /*index=5*/f32[160,345]{1,0:T(8,128)S(1)}) custom-call(bf16[320,768]{1,0:T(8,128)(2,1)S(1)} %get-tuple-element.49.refs_0_, bf16[320,768]{1,0:T(8,128)(2,1)S(1)} %get-tuple-element.64.refs_1_, ...), custom_call_target="tpu_custom_call" | custom-call | flops 4976640000 | bytes 8000000 | tf_op jit(solution)/shard_map/late_left/pallas_call | solution.py:171
  94.7 3.8 %collective-permute-start.30 = (f32[160,345]{1,0:T(8,128)S(1)}, f32[160,345]{1,0:T(8,128)S(1)}, u32[]{:S(2)}, u32[]{:S(2)}) collective-permute-start(f32[160,345]{1,0:T(8,128)S(1)} %get-tuple-element.88), channel_id=1, source_target_pairs={{0,60},{1,61},{2,62},{3,63},{4,56},{5,57},{6,58},{7,59},{8,52},{9,... | collective-permute-start | bytes 662408 | tf_op jit(solution)/shard_map/ppermute | solution.py:48
  98.4 2.6 %collective-permute-start.31 = (f32[160,345]{1,0:T(8,128)S(1)}, f32[160,345]{1,0:T(8,128)S(1)}, u32[]{:S(2)}, u32[]{:S(2)}) collective-permute-start(f32[160,345]{1,0:T(8,128)S(1)} %get-tuple-element.89), channel_id=1, source_target_pairs={{0,78},{1,79},{2,76},{3,77},{4,74},{5,75},{6,72},{7,73},{8,70},{9,... | collective-permute-start | bytes 662408 | tf_op jit(solution)/shard_map/ppermute | solution.py:48
  101.0 0.5 collective-permute-start.32
  101.5 1.5 %collective-permute-start.33 = (f32[160,345]{1,0:T(8,128)S(1)}, f32[160,345]{1,0:T(8,128)S(1)}, u32[]{:S(2)}, u32[]{:S(2)}) collective-permute-start(f32[160,345]{1,0:T(8,128)S(1)} %get-tuple-element.91), channel_id=1, source_target_pairs={{0,12},{1,13},{2,14},{3,15},{4,8},{5,9},{6,10},{7,11},{8,4},{9,5},... | collective-permute-start | bytes 662408 | tf_op jit(solution)/shard_map/ppermute | solution.py:48
  102.9 1.9 %collective-permute-start.34 = (f32[160,345]{1,0:T(8,128)S(1)}, f32[160,345]{1,0:T(8,128)S(1)}, u32[]{:S(2)}, u32[]{:S(2)}) collective-permute-start(f32[160,345]{1,0:T(8,128)S(1)} %get-tuple-element.92), channel_id=1, source_target_pairs={{0,66},{1,67},{2,64},{3,65},{4,70},{5,71},{6,68},{7,69},{8,74},{9,... | collective-permute-start | bytes 662408 | tf_op jit(solution)/shard_map/ppermute | solution.py:48
  104.8 2.0 %collective-permute-done.30 = f32[160,345]{1,0:T(8,128)S(1)} collective-permute-done((f32[160,345]{1,0:T(8,128)S(1)}, f32[160,345]{1,0:T(8,128)S(1)}, u32[]{:S(2)}, u32[]{:S(2)}) %collective-permute-start.30) | collective-permute-done | bytes 220832 | tf_op jit(solution)/shard_map/ppermute | solution.py:48
  106.8 4.6 %collective-permute-start.28 = (f32[160,345]{1,0:T(8,128)S(1)}, f32[160,345]{1,0:T(8,128)S(1)}, u32[]{:S(2)}, u32[]{:S(2)}) collective-permute-start(f32[160,345]{1,0:T(8,128)S(1)} %get-tuple-element.87), channel_id=1, source_target_pairs={{0,126},{1,127},{2,124},{3,125},{4,122},{5,123},{6,120},{7,121},{8... | collective-permute-start | bytes 662408 | tf_op jit(solution)/shard_map/ppermute | solution.py:48
  111.4 0.7 collective-permute-done.31
  112.1 4.3 %collective-permute-start.29 = (f32[160,345]{1,0:T(8,128)S(1)}, f32[160,345]{1,0:T(8,128)S(1)}, u32[]{:S(2)}, u32[]{:S(2)}) collective-permute-start(f32[160,345]{1,0:T(8,128)S(1)} %get-tuple-element.84), channel_id=1, source_target_pairs={{0,114},{1,115},{2,112},{3,113},{4,118},{5,119},{6,116},{7,117},{8... | collective-permute-start | bytes 662408 | tf_op jit(solution)/shard_map/ppermute | solution.py:48
  116.4 5.5 %collective-permute-done.33 = f32[160,345]{1,0:T(8,128)S(1)} collective-permute-done((f32[160,345]{1,0:T(8,128)S(1)}, f32[160,345]{1,0:T(8,128)S(1)}, u32[]{:S(2)}, u32[]{:S(2)}) %collective-permute-start.33) | collective-permute-done | bytes 220832 | tf_op jit(solution)/shard_map/ppermute | solution.py:48
  122.0 4.7 %collective-permute-done.34 = f32[160,345]{1,0:T(8,128)S(1)} collective-permute-done((f32[160,345]{1,0:T(8,128)S(1)}, f32[160,345]{1,0:T(8,128)S(1)}, u32[]{:S(2)}, u32[]{:S(2)}) %collective-permute-start.34) | collective-permute-done | bytes 220832 | tf_op jit(solution)/shard_map/ppermute | solution.py:48
  126.6 0.9 add_bitcast_fusion
  (24 shorter events, 0.1 us)
Async XLA Ops:
  0.0 0.9 copy-start
  1.0 8.2 %collective-permute-start.4 = (bf16[160,768]{1,0:T(8,128)(2,1)S(1)}, bf16[160,768]{1,0:T(8,128)(2,1)S(1)}, u32[]{:S(2)}, u32[]{:S(2)}) collective-permute-start(bf16[160,768]{1,0:T(8,128)(2,1)S(1)} %split_coefs.1.refs_6_), channel_id=1, source_target_pairs={{0,2},{1,3},{2,0},{3,1},{4,6},{5,7},{6,4},{7,5},{8,10},{9,11},{10,... | collective-permute-start | bytes 737288 | tf_op jit(solution)/shard_map/ppermute | solution.py:48
  3.1 8.8 %collective-permute-start = (bf16[160,768]{1,0:T(8,128)(2,1)}, bf16[160,768]{1,0:T(8,128)(2,1)S(1)}, u32[]{:S(2)}, u32[]{:S(2)}) collective-permute-start(bf16[160,768]{1,0:T(8,128)(2,1)} %refs_0_.1), channel_id=1, source_target_pairs={{0,48},{1,49},{2,50},{3,51},{4,52},{5,53},{6,54},{7,55},{8,56},{9,... | collective-permute-start | bytes 737288 | tf_op jit(solution)/shard_map/ppermute | solution.py:48
  5.8 7.3 %collective-permute-start.1 = (bf16[160,768]{1,0:T(8,128)(2,1)}, bf16[160,768]{1,0:T(8,128)(2,1)S(1)}, u32[]{:S(2)}, u32[]{:S(2)}) collective-permute-start(bf16[160,768]{1,0:T(8,128)(2,1)} %refs_0_.1), channel_id=1, source_target_pairs={{0,16},{1,17},{2,18},{3,19},{4,20},{5,21},{6,22},{7,23},{8,24},{9,... | collective-permute-start | bytes 737288 | tf_op jit(solution)/shard_map/ppermute | solution.py:48
  6.1 8.4 %collective-permute-start.2 = (bf16[160,768]{1,0:T(8,128)(2,1)}, bf16[160,768]{1,0:T(8,128)(2,1)S(1)}, u32[]{:S(2)}, u32[]{:S(2)}) collective-permute-start(bf16[160,768]{1,0:T(8,128)(2,1)} %refs_3_.1), channel_id=1, source_target_pairs={{0,12},{1,13},{2,14},{3,15},{4,8},{5,9},{6,10},{7,11},{8,4},{9,5},... | collective-permute-start | bytes 737288 | tf_op jit(solution)/shard_map/ppermute | solution.py:48
  9.1 6.8 %collective-permute-start.3 = (bf16[160,768]{1,0:T(8,128)(2,1)}, bf16[160,768]{1,0:T(8,128)(2,1)S(1)}, u32[]{:S(2)}, u32[]{:S(2)}) collective-permute-start(bf16[160,768]{1,0:T(8,128)(2,1)} %refs_3_.1), channel_id=1, source_target_pairs={{0,4},{1,5},{2,6},{3,7},{4,0},{5,1},{6,2},{7,3},{8,12},{9,13},{10,... | collective-permute-start | bytes 737288 | tf_op jit(solution)/shard_map/ppermute | solution.py:48
  15.9 0.9 copy-start.2
  16.9 0.9 copy-start.3
  18.1 27.9 %collective-permute-start.10 = (bf16[320,2304]{1,0:T(8,128)(2,1)S(1)}, bf16[320,2304]{1,0:T(8,128)(2,1)S(1)}, u32[]{:S(2)}, u32[]{:S(2)}) collective-permute-start(bf16[320,2304]{1,0:T(8,128)(2,1)S(1)} %get-tuple-element.59), channel_id=1, source_target_pairs={{0,1},{1,0},{2,3},{3,2},{4,5},{5,4},{6,7},{7,6},{8,9},{9,8},{10,11... | collective-permute-start | bytes 4423688 | tf_op jit(solution)/shard_map/ppermute | solution.py:48
  18.2 14.8 %collective-permute-start.5 = (bf16[320,768]{1,0:T(8,128)(2,1)S(1)}, bf16[320,768]{1,0:T(8,128)(2,1)S(1)}, u32[]{:S(2)}, u32[]{:S(2)}) collective-permute-start(bf16[320,768]{1,0:T(8,128)(2,1)S(1)} %get-tuple-element.49.refs_0_), channel_id=1, source_target_pairs={{0,12},{1,13},{2,14},{3,15},{4,8},{5,9},{6,10},{7,11},{8,4},{9,5},... | collective-permute-start | bytes 1474568 | tf_op jit(solution)/shard_map/ppermute | solution.py:48
  19.7 15.0 %collective-permute-start.6 = (bf16[320,768]{1,0:T(8,128)(2,1)S(1)}, bf16[320,768]{1,0:T(8,128)(2,1)S(1)}, u32[]{:S(2)}, u32[]{:S(2)}) collective-permute-start(bf16[320,768]{1,0:T(8,128)(2,1)S(1)} %get-tuple-element.51.refs_2_.refs_6_), channel_id=1, source_target_pairs={{0,4},{1,5},{2,6},{3,7},{4,0},{5,1},{6,2},{7,3},{8,12},{9,13},{10,... | collective-permute-start | bytes 1474568 | tf_op jit(solution)/shard_map/ppermute | solution.py:48
  19.7 15.0 %collective-permute-start.7 = (bf16[320,768]{1,0:T(8,128)(2,1)S(1)}, bf16[320,768]{1,0:T(8,128)(2,1)S(1)}, u32[]{:S(2)}, u32[]{:S(2)}) collective-permute-start(bf16[320,768]{1,0:T(8,128)(2,1)S(1)} %get-tuple-element.64.refs_1_), channel_id=1, source_target_pairs={{0,66},{1,67},{2,64},{3,65},{4,70},{5,71},{6,68},{7,69},{8,74},{9,... | collective-permute-start | bytes 1474568 | tf_op jit(solution)/shard_map/ppermute | solution.py:48
  22.3 13.0 %collective-permute-start.8 = (bf16[320,768]{1,0:T(8,128)(2,1)S(1)}, bf16[320,768]{1,0:T(8,128)(2,1)S(1)}, u32[]{:S(2)}, u32[]{:S(2)}) collective-permute-start(bf16[320,768]{1,0:T(8,128)(2,1)S(1)} %get-tuple-element.65.refs_7_.refs_3_), channel_id=1, source_target_pairs={{0,2},{1,3},{2,0},{3,1},{4,6},{5,7},{6,4},{7,5},{8,10},{9,11},{10,... | collective-permute-start | bytes 1474568 | tf_op jit(solution)/shard_map/ppermute | solution.py:48
  33.0 12.8 %collective-permute-start.9 = (bf16[320,768]{1,0:T(8,128)(2,1)S(1)}, bf16[320,768]{1,0:T(8,128)(2,1)S(1)}, u32[]{:S(2)}, u32[]{:S(2)}) collective-permute-start(bf16[320,768]{1,0:T(8,128)(2,1)S(1)} %get-tuple-element.66.refs_8_.refs_4_), channel_id=1, source_target_pairs={{0,16},{1,17},{2,18},{3,19},{4,20},{5,21},{6,22},{7,23},{8,24},{9,... | collective-permute-start | bytes 1474568 | tf_op jit(solution)/shard_map/ppermute | solution.py:48
  46.0 11.9 %collective-permute-start.15 = (bf16[320,768]{1,0:T(8,128)(2,1)S(1)}, bf16[320,768]{1,0:T(8,128)(2,1)S(1)}, u32[]{:S(2)}, u32[]{:S(2)}) collective-permute-start(bf16[320,768]{1,0:T(8,128)(2,1)S(1)} %get-tuple-element.66.refs_8_.refs_4_), channel_id=1, source_target_pairs={{0,4},{1,5},{2,6},{3,7},{4,0},{5,1},{6,2},{7,3},{8,12},{9,13},{10,... | collective-permute-start | bytes 1474568 | tf_op jit(solution)/shard_map/ppermute | solution.py:48
  46.1 11.9 %collective-permute-start.14 = (bf16[320,768]{1,0:T(8,128)(2,1)S(1)}, bf16[320,768]{1,0:T(8,128)(2,1)S(1)}, u32[]{:S(2)}, u32[]{:S(2)}) collective-permute-start(bf16[320,768]{1,0:T(8,128)(2,1)S(1)} %get-tuple-element.65.refs_7_.refs_3_), channel_id=1, source_target_pairs={{0,16},{1,17},{2,18},{3,19},{4,20},{5,21},{6,22},{7,23},{8,24},{9,... | collective-permute-start | bytes 1474568 | tf_op jit(solution)/shard_map/ppermute | solution.py:48
  47.9 12.8 %collective-permute-start.13 = (bf16[320,768]{1,0:T(8,128)(2,1)S(1)}, bf16[320,768]{1,0:T(8,128)(2,1)S(1)}, u32[]{:S(2)}, u32[]{:S(2)}) collective-permute-start(bf16[320,768]{1,0:T(8,128)(2,1)S(1)} %get-tuple-element.64.refs_1_), channel_id=1, source_target_pairs={{0,48},{1,49},{2,50},{3,51},{4,52},{5,53},{6,54},{7,55},{8,56},{9,... | collective-permute-start | bytes 1474568 | tf_op jit(solution)/shard_map/ppermute | solution.py:48
  48.4 12.3 %collective-permute-start.12 = (bf16[320,768]{1,0:T(8,128)(2,1)S(1)}, bf16[320,768]{1,0:T(8,128)(2,1)S(1)}, u32[]{:S(2)}, u32[]{:S(2)}) collective-permute-start(bf16[320,768]{1,0:T(8,128)(2,1)S(1)} %get-tuple-element.62), channel_id=1, source_target_pairs={{0,2},{1,3},{2,0},{3,1},{4,6},{5,7},{6,4},{7,5},{8,10},{9,11},{10,... | collective-permute-start | bytes 1474568 | tf_op jit(solution)/shard_map/ppermute | solution.py:48
  48.8 13.1 %collective-permute-start.11 = (bf16[320,768]{1,0:T(8,128)(2,1)S(1)}, bf16[320,768]{1,0:T(8,128)(2,1)S(1)}, u32[]{:S(2)}, u32[]{:S(2)}) collective-permute-start(bf16[320,768]{1,0:T(8,128)(2,1)S(1)} %get-tuple-element.60), channel_id=1, source_target_pairs={{0,66},{1,67},{2,64},{3,65},{4,70},{5,71},{6,68},{7,69},{8,74},{9,... | collective-permute-start | bytes 1474568 | tf_op jit(solution)/shard_map/ppermute | solution.py:48
  61.8 7.2 %collective-permute-start.16 = (bf16[320,2304]{1,0:T(8,128)(2,1)S(1)}, bf16[320,2304]{1,0:T(8,128)(2,1)S(1)}, u32[]{:S(2)}, u32[]{:S(2)}) collective-permute-start(bf16[320,2304]{1,0:T(8,128)(2,1)S(1)} %get-tuple-element.71), channel_id=1, source_target_pairs={{0,1},{1,0},{2,3},{3,2},{4,5},{5,4},{6,7},{7,6},{8,9},{9,8},{10,11... | collective-permute-start | bytes 4423688 | tf_op jit(solution)/shard_map/ppermute | solution.py:48
  61.8 4.0 %collective-permute-start.17 = (bf16[320,768]{1,0:T(8,128)(2,1)S(1)}, bf16[320,768]{1,0:T(8,128)(2,1)S(1)}, u32[]{:S(2)}, u32[]{:S(2)}) collective-permute-start(bf16[320,768]{1,0:T(8,128)(2,1)S(1)} %collective-permute-done.12.refs_13_.refs_9_), channel_id=1, source_target_pairs={{0,1},{1,0},{2,3},{3,2},{4,5},{5,4},{6,7},{7,6},{8,9},{9,8},{10,11... | collective-permute-start | bytes 1474568 | tf_op jit(solution)/shard_map/ppermute | solution.py:48
  62.3 6.4 %collective-permute-start.18 = (bf16[320,768]{1,0:T(8,128)(2,1)S(1)}, bf16[320,768]{1,0:T(8,128)(2,1)S(1)}, u32[]{:S(2)}, u32[]{:S(2)}) collective-permute-start(bf16[320,768]{1,0:T(8,128)(2,1)S(1)} %collective-permute-done.14.refs_9_.refs_5_.refs_3_.refs_7_), channel_id=1, source_target_pairs={{0,1},{1,0},{2,3},{3,2},{4,5},{5,4},{6,7},{7,6},{8,9},{9,8},{10,11... | collective-permute-start | bytes 1474568 | tf_op jit(solution)/shard_map/ppermute | solution.py:48
  62.4 6.7 %collective-permute-start.19 = (bf16[320,768]{1,0:T(8,128)(2,1)S(1)}, bf16[320,768]{1,0:T(8,128)(2,1)S(1)}, u32[]{:S(2)}, u32[]{:S(2)}) collective-permute-start(bf16[320,768]{1,0:T(8,128)(2,1)S(1)} %collective-permute-done.15.refs_12_.refs_8_), channel_id=1, source_target_pairs={{0,1},{1,0},{2,3},{3,2},{4,5},{5,4},{6,7},{7,6},{8,9},{9,8},{10,11... | collective-permute-start | bytes 1474568 | tf_op jit(solution)/shard_map/ppermute | solution.py:48
  62.9 19.7 %collective-permute-start.27 = (bf16[320,768]{1,0:T(8,128)(2,1)S(1)}, bf16[320,768]{1,0:T(8,128)(2,1)S(1)}, u32[]{:S(2)}, u32[]{:S(2)}) collective-permute-start(bf16[320,768]{1,0:T(8,128)(2,1)S(1)} %collective-permute-done.7.refs_5_), channel_id=1, source_target_pairs={{0,48},{1,49},{2,50},{3,51},{4,52},{5,53},{6,54},{7,55},{8,56},{9,... | collective-permute-start | bytes 1474568 | tf_op jit(solution)/shard_map/ppermute | solution.py:48
  65.8 16.8 %collective-permute-start.26 = (bf16[320,768]{1,0:T(8,128)(2,1)S(1)}, bf16[320,768]{1,0:T(8,128)(2,1)S(1)}, u32[]{:S(2)}, u32[]{:S(2)}) collective-permute-start(bf16[320,768]{1,0:T(8,128)(2,1)S(1)} %get-tuple-element.82), channel_id=1, source_target_pairs={{0,66},{1,67},{2,64},{3,65},{4,70},{5,71},{6,68},{7,69},{8,74},{9,... | collective-permute-start | bytes 1474568 | tf_op jit(solution)/shard_map/ppermute | solution.py:48
  68.8 13.0 %collective-permute-start.22 = (bf16[320,768]{1,0:T(8,128)(2,1)S(1)}, bf16[320,768]{1,0:T(8,128)(2,1)S(1)}, u32[]{:S(2)}, u32[]{:S(2)}) collective-permute-start(bf16[320,768]{1,0:T(8,128)(2,1)S(1)} %collective-permute-done.8.refs_4_.refs_14_.refs_10_), channel_id=1, source_target_pairs={{0,16},{1,17},{2,18},{3,19},{4,20},{5,21},{6,22},{7,23},{8,24},{9,... | collective-permute-start | bytes 1474568 | tf_op jit(solution)/shard_map/ppermute | solution.py:48
  69.1 12.8 %collective-permute-start.21 = (bf16[320,768]{1,0:T(8,128)(2,1)S(1)}, bf16[320,768]{1,0:T(8,128)(2,1)S(1)}, u32[]{:S(2)}, u32[]{:S(2)}) collective-permute-start(bf16[320,768]{1,0:T(8,128)(2,1)S(1)} %get-tuple-element.76), channel_id=1, source_target_pairs={{0,2},{1,3},{2,0},{3,1},{4,6},{5,7},{6,4},{7,5},{8,10},{9,11},{10,... | collective-permute-start | bytes 1474568 | tf_op jit(solution)/shard_map/ppermute | solution.py:48
  69.1 13.2 %collective-permute-start.20 = (bf16[320,768]{1,0:T(8,128)(2,1)S(1)}, bf16[320,768]{1,0:T(8,128)(2,1)S(1)}, u32[]{:S(2)}, u32[]{:S(2)}) collective-permute-start(bf16[320,768]{1,0:T(8,128)(2,1)S(1)} %collective-permute-done.9.refs_5_.refs_10_.refs_6_.refs_7_.refs_11_), channel_id=1, source_target_pairs={{0,4},{1,5},{2,6},{3,7},{4,0},{5,1},{6,2},{7,3},{8,12},{9,13},{10,... | collective-permute-start | bytes 1474568 | tf_op jit(solution)/shard_map/ppermute | solution.py:48
  81.8 4.6 %collective-permute-start.25 = (bf16[320,768]{1,0:T(8,128)(2,1)S(1)}, bf16[320,768]{1,0:T(8,128)(2,1)S(1)}, u32[]{:S(2)}, u32[]{:S(2)}) collective-permute-start(bf16[320,768]{1,0:T(8,128)(2,1)S(1)} %collective-permute-done.22.refs_6_.refs_10_), channel_id=1, source_target_pairs={{0,1},{1,0},{2,3},{3,2},{4,5},{5,4},{6,7},{7,6},{8,9},{9,8},{10,11... | collective-permute-start | bytes 1474568 | tf_op jit(solution)/shard_map/ppermute | solution.py:48
  81.8 4.5 %collective-permute-start.24 = (bf16[320,768]{1,0:T(8,128)(2,1)S(1)}, bf16[320,768]{1,0:T(8,128)(2,1)S(1)}, u32[]{:S(2)}, u32[]{:S(2)}) collective-permute-start(bf16[320,768]{1,0:T(8,128)(2,1)S(1)} %collective-permute-done.21.refs_5_.refs_9_), channel_id=1, source_target_pairs={{0,1},{1,0},{2,3},{3,2},{4,5},{5,4},{6,7},{7,6},{8,9},{9,8},{10,11... | collective-permute-start | bytes 1474568 | tf_op jit(solution)/shard_map/ppermute | solution.py:48
  82.3 4.1 %collective-permute-start.23 = (bf16[320,768]{1,0:T(8,128)(2,1)S(1)}, bf16[320,768]{1,0:T(8,128)(2,1)S(1)}, u32[]{:S(2)}, u32[]{:S(2)}) collective-permute-start(bf16[320,768]{1,0:T(8,128)(2,1)S(1)} %collective-permute-done.20.refs_4_.refs_8_), channel_id=1, source_target_pairs={{0,1},{1,0},{2,3},{3,2},{4,5},{5,4},{6,7},{7,6},{8,9},{9,8},{10,11... | collective-permute-start | bytes 1474568 | tf_op jit(solution)/shard_map/ppermute | solution.py:48
  88.7 38.0 %copy-start.1 = (f32[345,160]{0,1:T(8,128)S(1)}, f32[345,160]{0,1:T(8,128)}, u32[]{:S(2)}) copy-start(f32[345,160]{0,1:T(8,128)} %param.7) | copy-start | bytes 662404
  88.7 38.0 %copy-start.4 = (s32[160]{0:T(256)S(1)}, s32[160]{0:T(256)}, u32[]{:S(2)}) copy-start(s32[160]{0:T(256)} %param.6) | copy-start | bytes 1924
  94.7 12.2 %collective-permute-start.30 = (f32[160,345]{1,0:T(8,128)S(1)}, f32[160,345]{1,0:T(8,128)S(1)}, u32[]{:S(2)}, u32[]{:S(2)}) collective-permute-start(f32[160,345]{1,0:T(8,128)S(1)} %get-tuple-element.88), channel_id=1, source_target_pairs={{0,60},{1,61},{2,62},{3,63},{4,56},{5,57},{6,58},{7,59},{8,52},{9,... | collective-permute-start | bytes 662408 | tf_op jit(solution)/shard_map/ppermute | solution.py:48
  98.4 13.7 %collective-permute-start.31 = (f32[160,345]{1,0:T(8,128)S(1)}, f32[160,345]{1,0:T(8,128)S(1)}, u32[]{:S(2)}, u32[]{:S(2)}) collective-permute-start(f32[160,345]{1,0:T(8,128)S(1)} %get-tuple-element.89), channel_id=1, source_target_pairs={{0,78},{1,79},{2,76},{3,77},{4,74},{5,75},{6,72},{7,73},{8,70},{9,... | collective-permute-start | bytes 662408 | tf_op jit(solution)/shard_map/ppermute | solution.py:48
  101.0 15.5 %collective-permute-start.32 = (f32[160,345]{1,0:T(8,128)S(1)}, f32[160,345]{1,0:T(8,128)S(1)}, u32[]{:S(2)}, u32[]{:S(2)}) collective-permute-start(f32[160,345]{1,0:T(8,128)S(1)} %get-tuple-element.90), channel_id=1, source_target_pairs={{0,48},{1,49},{2,50},{3,51},{4,52},{5,53},{6,54},{7,55},{8,56},{9,... | collective-permute-start | bytes 662408 | tf_op jit(solution)/shard_map/ppermute | solution.py:48
  101.5 20.5 %collective-permute-start.33 = (f32[160,345]{1,0:T(8,128)S(1)}, f32[160,345]{1,0:T(8,128)S(1)}, u32[]{:S(2)}, u32[]{:S(2)}) collective-permute-start(f32[160,345]{1,0:T(8,128)S(1)} %get-tuple-element.91), channel_id=1, source_target_pairs={{0,12},{1,13},{2,14},{3,15},{4,8},{5,9},{6,10},{7,11},{8,4},{9,5},... | collective-permute-start | bytes 662408 | tf_op jit(solution)/shard_map/ppermute | solution.py:48
  102.9 23.7 %collective-permute-start.34 = (f32[160,345]{1,0:T(8,128)S(1)}, f32[160,345]{1,0:T(8,128)S(1)}, u32[]{:S(2)}, u32[]{:S(2)}) collective-permute-start(f32[160,345]{1,0:T(8,128)S(1)} %get-tuple-element.92), channel_id=1, source_target_pairs={{0,66},{1,67},{2,64},{3,65},{4,70},{5,71},{6,68},{7,69},{8,74},{9,... | collective-permute-start | bytes 662408 | tf_op jit(solution)/shard_map/ppermute | solution.py:48
  106.8 19.8 %collective-permute-start.28 = (f32[160,345]{1,0:T(8,128)S(1)}, f32[160,345]{1,0:T(8,128)S(1)}, u32[]{:S(2)}, u32[]{:S(2)}) collective-permute-start(f32[160,345]{1,0:T(8,128)S(1)} %get-tuple-element.87), channel_id=1, source_target_pairs={{0,126},{1,127},{2,124},{3,125},{4,122},{5,123},{6,120},{7,121},{8... | collective-permute-start | bytes 662408 | tf_op jit(solution)/shard_map/ppermute | solution.py:48
  112.1 14.5 %collective-permute-start.29 = (f32[160,345]{1,0:T(8,128)S(1)}, f32[160,345]{1,0:T(8,128)S(1)}, u32[]{:S(2)}, u32[]{:S(2)}) collective-permute-start(f32[160,345]{1,0:T(8,128)S(1)} %get-tuple-element.84), channel_id=1, source_target_pairs={{0,114},{1,115},{2,112},{3,113},{4,118},{5,119},{6,116},{7,117},{8... | collective-permute-start | bytes 662408 | tf_op jit(solution)/shard_map/ppermute | solution.py:48

commit v3 on v2

--- a/solution.py
+++ b/solution.py
@@ -56,7 +56,9 @@
     return lax.dot_general(a, b, dims, preferred_element_type=f32)
 
 
-def split_kernel(coef, split):
+def stage_kernel(act, sig, coef, act_out, sig_out, split):
+    act_out[...] = act[...]
+    sig_out[...] = sig[...]
     split[...] = jnp.zeros_like(split)
     values = coef[...]
     high = values.astype(bf16)
@@ -64,15 +66,15 @@
     split[:, LANES : LANES + CLASSES] = (values - high.astype(f32)).astype(bf16)
 
 
-def split_coefs(coefs):
+def stage(act, sig, coefs):
     return pl.pallas_call(
-        split_kernel,
-        out_shape=pltpu.VMEM((OWN, 2 * LANES), bf16),
-        in_specs=[VMEM],
-        out_specs=VMEM,
+        stage_kernel,
+        out_shape=[pltpu.VMEM((OWN, FEAT), bf16), pltpu.VMEM((OWN, FEAT), bf16), pltpu.VMEM((OWN, 2 * LANES), bf16)],
+        in_specs=[VMEM] * 3,
+        out_specs=[VMEM] * 3,
         compiler_params=pltpu.CompilerParams(vmem_limit_bytes=4 << 20),
-        name="split_coefs",
-    )(coefs)
+        name="stage",
+    )(act, sig, coefs)
 
 
 def arrange_kernel(plan, n_in, *refs):
@@ -112,19 +114,24 @@
     )(*arrays)
 
 
-def block_kernel(plan, n_in, with_total, apart, rows, *refs):
+def block_kernel(plan, n_in, total_row, apart, keep_left, ready_left, n_right, rows, *refs):
     inputs, refs = refs[:n_in], refs[n_in:]
-    total_in, refs = (refs[0], refs[1:]) if with_total else (None, refs)
-    outs, (right, left, split) = refs[:-3], refs[-3:]
+    if ready_left:
+        (left, split), refs = refs[:2], refs[2:]
+    total_in, refs = (refs[0], refs[1:]) if total_row is not None else (None, refs)
+    outs, refs = (refs[:n_right], refs[n_right:]) if apart else (refs[:1], refs[1:])
+    if not ready_left:
+        (left, split), refs = refs[:2], refs[2:]
+    (right,) = refs
     targets = (right, left, split)
     for target, out_row, out_col, source, row, col in plan:
         targets[target][out_row * OWN : (out_row + 1) * OWN, out_col * FEAT : (out_col + 1) * FEAT] = inputs[source][
             row * OWN : (row + 1) * OWN, col * FEAT : (col + 1) * FEAT
         ]
-    n_right, n_left = right.shape[0], left.shape[0]
-    for start in range(0, n_right, rows):
+    n_left = left.shape[0]
+    for start in range(0, n_right * OWN, rows):
         n = slice(start, start + rows)
-        part = total_in[n, :] if with_total else None
+        part = None if total_in is None else total_in[total_row + start : total_row + start + rows, :]
         at = 0
         while at < n_left:
             size = min(512, n_left - at)
@@ -145,7 +152,7 @@
             outs[0][n, :] = part
 
 
-def partial_sums(right, left, total, apart, rows, name):
+def partial_sums(right, left, total, apart, rows, name, keep_left=False, ready=None):
     arrays, plan = [], []
 
     def place(array):
@@ -162,26 +169,35 @@
         plan.append((1, i, 0, place(act[0]), act[1], act[2]))
         plan.append((1, i, 1, place(sig[0]), sig[1], sig[2]))
         plan.append((2, i, 0, place(coef[0]), coef[1], coef[2]))
-    n_right, n_left = len(right), len(left)
+    n_in, n_right = len(arrays), len(right)
+    left_rows = ready[0].shape[0] if ready else len(left) * OWN
     if apart:
         out_shape = [pltpu.VMEM((OWN, CLASSES), f32)] * n_right
     else:
         out_shape = [pltpu.VMEM((n_right * OWN, LANES), f32)]
-    pairs = n_right * n_left * OWN * OWN
+    left_shape = [pltpu.VMEM((left_rows, 2 * FEAT), bf16), pltpu.VMEM((left_rows, 2 * LANES), bf16)]
+    scratch = [pltpu.VMEM((n_right * OWN, 2 * FEAT), bf16)]
+    if ready:
+        arrays += ready
+    elif keep_left:
+        out_shape = out_shape + left_shape
+    else:
+        scratch = left_shape + scratch
+    if total is not None:
+        arrays.append(total[0])
+    pairs = n_right * OWN * left_rows
     return pl.pallas_call(
-        functools.partial(block_kernel, plan, len(arrays), total is not None, apart, rows),
+        functools.partial(
+            block_kernel, plan, n_in, None if total is None else total[1], apart, keep_left, bool(ready), n_right, rows
+        ),
         out_shape=out_shape,
-        in_specs=[VMEM] * (len(arrays) + (total is not None)),
+        in_specs=[VMEM] * len(arrays),
         out_specs=[VMEM] * len(out_shape),
-        scratch_shapes=[
-            pltpu.VMEM((n_right * OWN, 2 * FEAT), bf16),
-            pltpu.VMEM((n_left * OWN, 2 * FEAT), bf16),
-            pltpu.VMEM((n_left * OWN, 2 * LANES), bf16),
-        ],
+        scratch_shapes=scratch,
         cost_estimate=pl.CostEstimate(flops=pairs * 5400, bytes_accessed=8_000_000, transcendentals=0),
         compiler_params=pltpu.CompilerParams(vmem_limit_bytes=24 << 20),
         name=name,
-    )(*arrays, *([] if total is None else [total]))
+    )(*arrays)
 
 
 def shards(activations, signals, labels, coefficients):
@@ -191,13 +207,13 @@
     for g in groups:
         a[g, "x"] = send(activations, g, "x")
         s[g, "y"] = send(signals, g, "y")
-    c0 = split_coefs(coefs)
+    act_own, sig_own, c0 = stage(activations, signals, coefs)
     cz = send(c0, "near", "z")
     pairs = arrange(
-        [[[(activations, 0), (a[g, "x"], 0)]] for g in groups]
-        + [[[(signals, 0), (s[g, "y"], 0)]] for g in groups]
+        [[[(act_own, 0), (a[g, "x"], 0)]] for g in groups]
+        + [[[(sig_own, 0), (s[g, "y"], 0)]] for g in groups]
         + [[[(c0, 0), (cz, 0)]]]
-        + [[[(activations, 0), (a["near", "x"], 0)], [(signals, 0), (s["near", "y"], 0)], [(c0, 0), (cz, 0)]]],
+        + [[[(act_own, 0), (a["near", "x"], 0)], [(sig_own, 0), (s["near", "y"], 0)], [(c0, 0), (cz, 0)]]],
         "pairs",
     )
     a0x, s0y, c0z, own2 = dict(zip(groups, pairs[:2])), dict(zip(groups, pairs[2:4])), pairs[4], pairs[5]
@@ -206,10 +222,10 @@
         ay[g] = send(a0x[g], g, "y")
         sz[g] = send(s0y[g], g, "z")
     cx = send(c0z, "near", "x")
+    ay["far"], ay["near"], sz["far"], sz["near"], cx, own2 = lax.optimization_barrier(
+        (ay["far"], ay["near"], sz["far"], sz["near"], cx, own2)
+    )
     own2_mate = send(own2, "near", "c")
-    ay["far"], ay["near"], sz["far"], sz["near"], cx = lax.optimization_barrier(
-        (ay["far"], ay["near"], sz["far"], sz["near"], cx)
-    )
     fours = arrange(
         [[[(a0x[g], 0), (ay[g], 0)]] for g in groups]
         + [[[(a0x[g], 1), (ay[g], 1)]] for g in groups]
@@ -219,8 +235,8 @@
     a0y, axxy, next2 = dict(zip(groups, fours[:2])), dict(zip(groups, fours[2:4])), fours[4]
     az, sx = {}, {}
     for g in groups:
-        az[g] = send(after(a0y[g], own2_mate), g, "z")
-        sx[g] = send(after(s0y[g], next2, own2_mate), g, "x")
+        az[g] = send(a0y[g], g, "z")
+        sx[g] = send(after(s0y[g], next2), g, "x")
     cy = send(after(c0z, next2, own2_mate), "near", "y")
     az["far"], az["near"], sx["far"], sx["near"], cy, next2 = lax.optimization_barrier(
         (az["far"], az["near"], sx["far"], sx["near"], cy, next2)
@@ -246,8 +262,8 @@
     coef = {"": (c0z, 0, 0), "z": (c0z, 1, 0), "x": (cx, 0, 0), "xz": (cx, 1, 0)}
     coef |= {"y": (cy, 0, 0), "yz": (cy, 1, 0), "xy": (cxy, 0, 0), "xyz": (cxy, 1, 0)}
     left = {k: (act[k], sig[k], coef[k]) for k in act}
-    right_1 = [right[k] for k in ("", "x", "y", "xy", "z", "yz")]
-    right_2 = [right[k] for k in ("xz", "xyz")]
+    right_1 = [right[k] for k in ("xy", "yz", "x", "y", "z", "")]
+    right_2 = [right[k] for k in ("xyz", "xz")]
     act_mate = {"": (own2_mate, 0, 0), "x": (own2_mate, 1, 0), "y": (next2_mate, 0, 0), "xy": (next2_mate, 1, 0)}
     act_mate |= {"z": (az_mate, 0, 0), "yz": (az_mate, 1, 0)}
     sig_mate = {"": (own2_mate, 0, 1), "y": (own2_mate, 1, 1), "z": (next2_mate, 0, 1), "yz": (next2_mate, 1, 1)}
@@ -265,13 +281,23 @@
     second = ("xy", "xz", "xyz")
     left_2 = [left[k] for k in second] + [(act_mate[k], sig_mate[k], coef_mate[k]) for k in second]
     (total_2,) = partial_sums(right_2, left_1, None, False, 320, "late_right")
-    sum_xz, sum_xyz = partial_sums(right_2, left_2, total_2, True, 320, "late_both")
+    got = {}
+    sum_xyz, sum_xz, *ready = partial_sums(right_2, left_2, (total_2, 0), True, 320, "late_1", keep_left=True)
+    got["xyz"], got["xz"] = send(sum_xyz, "far", "xyz"), send(sum_xz, "far", "xz")
     total_1 = after(total_1, sum_xz)
-    own, sum_x, sum_y, sum_xy, sum_z, sum_yz = partial_sums(right_1, left_2, total_1, True, 480, "late_left")
+    sum_xy, sum_yz = partial_sums(right_1[:2], (), (total_1, 0), True, 320, "late_2", ready=ready)
+    got["xy"], got["yz"] = send(sum_xy, "far", "xy"), send(sum_yz, "far", "yz")
+    total_1 = after(total_1, sum_yz)
+    sum_x, sum_y = partial_sums(right_1[2:4], (), (total_1, 2 * OWN), True, 320, "late_3", ready=ready)
+    got["x"] = send(sum_x, "far", "x")
+    total_1 = after(total_1, sum_y)
+    sum_z, own = partial_sums(right_1[4:], (), (total_1, 4 * OWN), True, 320, "late_4", ready=ready)
+    got["y"] = send(after(sum_y, got["xz"]), "far", "y")
+    got["z"] = send(after(sum_z, got["xyz"]), "far", "z")
 
     product = own
-    for part, dims in ((sum_xyz, "xyz"), (sum_xz, "xz"), (sum_xy, "xy"), (sum_yz, "yz"), (sum_x, "x"), (sum_y, "y"), (sum_z, "z")):
-        product = product + send(part, "far", dims)
+    for part in got.values():
+        product = product + part
     product = product * (1.0 / (FEAT * FEAT))
     classes = jnp.arange(CLASSES, dtype=jnp.int32)
     targets = (labels[:, None] == classes[None, :]).astype(f32) - 1.0 / CLASSES

time: 128 us -> 114 us (0.89)
  waiting for transfers between devices: 50.3 us -> 41.4 us
  starting transfers between devices: 50.4 us -> 44.2 us
    ppermute x35, waiting for transfers between devices: 50.3 us -> 41.4 us  [send(): return lax.ppermute(value, AXES, moves(group, dims))]
    ppermute x35, starting transfers between devices: 50.4 us -> 44.2 us  [send(): return lax.ppermute(value, AXES, moves(group, dims))]
    pallas_call x5 -> x7, Pallas kernels: 22.5 us -> 23.3 us  [the longest x6 23.2 us: partial_sums(): pl.pallas_call(functools.partial(block_kernel, plan, n_in, None if total...]
  transfers between devices with their start and end apart: 35 -> 35, of which waited for: 18 -> 15; matrix products, arithmetic and copies ran while one was open for 0% -> 0% of each run, Pallas kernels for 11% -> 19%
where the time goes in v3:
time: 114 us; the launch traced here: 113 us
  starting transfers between devices  44.2 us (39%)
  waiting for transfers between devices  41.4 us (36%)
  Pallas kernels  23.8 us (21%)
  local copies, waits for them, and re-layouts  2.84 us (2%)
    ppermute x35, starting transfers between devices, send(): return lax.ppermute(value, AXES, moves(group, dims))  44.2 us
    ppermute x35, waiting for transfers between devices, send(): return lax.ppermute(value, AXES, moves(group, dims))  41.4 us
    pallas_call x6, Pallas kernels, partial_sums(): pl.pallas_call(functools.partial(block_kernel, plan, n_in, None if total...  23.2 us
    unnamed x10, local copies, waits for them, and re-layouts  2.84 us
  transfers between devices with their start and end apart: 35, of which 15 were waited for; matrix products, arithmetic and copies ran while one was open for 0% of the time, Pallas kernels for 19%

profile of v3, /device:TPU:0, one launch (start us, length us, event | category | flops | bytes accessed | tf_op | source)
XLA Modules:
  0.0 113.2 jit_solution(18140566113224338836)
XLA Ops:
  0.0 1.6 %collective-permute-start.1 = (bf16[160,768]{1,0:T(8,128)(2,1)}, bf16[160,768]{1,0:T(8,128)(2,1)S(1)}, u32[]{:S(2)}, u32[]{:S(2)}) collective-permute-start(bf16[160,768]{1,0:T(8,128)(2,1)} %act.1), channel_id=1, source_target_pairs={{0,16},{1,17},{2,18},{3,19},{4,20},{5,21},{6,22},{7,23},{8,24},{9,... | collective-permute-start | bytes 737288 | tf_op jit(solution)/shard_map/ppermute | solution.py:48
  1.6 2.1 %collective-permute-start = (bf16[160,768]{1,0:T(8,128)(2,1)}, bf16[160,768]{1,0:T(8,128)(2,1)S(1)}, u32[]{:S(2)}, u32[]{:S(2)}) collective-permute-start(bf16[160,768]{1,0:T(8,128)(2,1)} %act.1), channel_id=1, source_target_pairs={{0,48},{1,49},{2,50},{3,51},{4,52},{5,53},{6,54},{7,55},{8,56},{9,... | collective-permute-start | bytes 737288 | tf_op jit(solution)/shard_map/ppermute | solution.py:48
  3.7 1.6 %collective-permute-start.3 = (bf16[160,768]{1,0:T(8,128)(2,1)}, bf16[160,768]{1,0:T(8,128)(2,1)S(1)}, u32[]{:S(2)}, u32[]{:S(2)}) collective-permute-start(bf16[160,768]{1,0:T(8,128)(2,1)} %sig.1), channel_id=1, source_target_pairs={{0,4},{1,5},{2,6},{3,7},{4,0},{5,1},{6,2},{7,3},{8,12},{9,13},{10,... | collective-permute-start | bytes 737288 | tf_op jit(solution)/shard_map/ppermute | solution.py:48
  5.2 2.2 %collective-permute-start.2 = (bf16[160,768]{1,0:T(8,128)(2,1)}, bf16[160,768]{1,0:T(8,128)(2,1)S(1)}, u32[]{:S(2)}, u32[]{:S(2)}) collective-permute-start(bf16[160,768]{1,0:T(8,128)(2,1)} %sig.1), channel_id=1, source_target_pairs={{0,12},{1,13},{2,14},{3,15},{4,8},{5,9},{6,10},{7,11},{8,4},{9,5},... | collective-permute-start | bytes 737288 | tf_op jit(solution)/shard_map/ppermute | solution.py:48
  7.4 0.9 copy-done
  8.4 0.9 copy-done.2
  9.3 0.9 copy-done.3
  10.3 0.1 stage.1
  10.3 2.0 %collective-permute-start.4 = (bf16[160,768]{1,0:T(8,128)(2,1)S(1)}, bf16[160,768]{1,0:T(8,128)(2,1)S(1)}, u32[]{:S(2)}, u32[]{:S(2)}) collective-permute-start(bf16[160,768]{1,0:T(8,128)(2,1)S(1)} %get-tuple-element.59.refs_6_), channel_id=1, source_target_pairs={{0,2},{1,3},{2,0},{3,1},{4,6},{5,7},{6,4},{7,5},{8,10},{9,11},{10,... | collective-permute-start | bytes 737288 | tf_op jit(solution)/shard_map/ppermute | solution.py:48
  12.3 0.0 collective-permute-done.1.refs_2_
  12.3 0.0 collective-permute-done.refs_1_
  12.4 0.0 collective-permute-done.3.refs_5_
  12.4 1.2 %collective-permute-done.2.refs_4_ = bf16[160,768]{1,0:T(8,128)(2,1)S(1)} collective-permute-done((bf16[160,768]{1,0:T(8,128)(2,1)}, bf16[160,768]{1,0:T(8,128)(2,1)S(1)}, u32[]{:S(2)}, u32[]{:S(2)}) %collective-permute-start.2) | collective-permute-done | bytes 245792 | tf_op jit(solution)/shard_map/ppermute | solution.py:48
  13.5 3.7 %collective-permute-done.4.refs_7_ = bf16[160,768]{1,0:T(8,128)(2,1)S(1)} collective-permute-done((bf16[160,768]{1,0:T(8,128)(2,1)S(1)}, bf16[160,768]{1,0:T(8,128)(2,1)S(1)}, u32[]{:S(2)}, u32[]{:S(2)}) %collective-permute-start.4) | collective-permute-done | bytes 245792 | tf_op jit(solution)/shard_map/ppermute | solution.py:48
  17.2 0.3 pairs.1
  17.4 0.8 collective-permute-start.6
  18.2 1.7 %collective-permute-start.8 = (bf16[320,768]{1,0:T(8,128)(2,1)S(1)}, bf16[320,768]{1,0:T(8,128)(2,1)S(1)}, u32[]{:S(2)}, u32[]{:S(2)}) collective-permute-start(bf16[320,768]{1,0:T(8,128)(2,1)S(1)} %get-tuple-element.74.refs_7_.refs_3_), channel_id=1, source_target_pairs={{0,2},{1,3},{2,0},{3,1},{4,6},{5,7},{6,4},{7,5},{8,10},{9,11},{10,... | collective-permute-start | bytes 1474568 | tf_op jit(solution)/shard_map/ppermute | solution.py:48
  19.9 0.6 collective-permute-start.9
  20.5 0.9 collective-permute-start.5
  21.4 2.5 %collective-permute-start.7 = (bf16[320,768]{1,0:T(8,128)(2,1)S(1)}, bf16[320,768]{1,0:T(8,128)(2,1)S(1)}, u32[]{:S(2)}, u32[]{:S(2)}) collective-permute-start(bf16[320,768]{1,0:T(8,128)(2,1)S(1)} %get-tuple-element.73.refs_5_.refs_3_), channel_id=1, source_target_pairs={{0,66},{1,67},{2,64},{3,65},{4,70},{5,71},{6,68},{7,69},{8,74},{9,... | collective-permute-start | bytes 1474568 | tf_op jit(solution)/shard_map/ppermute | solution.py:48
  23.9 4.7 %collective-permute-done.6.refs_3_.refs_11_.refs_7_.refs_2_ = bf16[320,768]{1,0:T(8,128)(2,1)S(1)} collective-permute-done((bf16[320,768]{1,0:T(8,128)(2,1)S(1)}, bf16[320,768]{1,0:T(8,128)(2,1)S(1)}, u32[]{:S(2)}, u32[]{:S(2)}) %collective-permute-start.6) | collective-permute-done | bytes 491552 | tf_op jit(solution)/shard_map/ppermute | solution.py:48
  28.6 0.4 collective-permute-done.8.refs_4_.refs_14_.refs_10_
  29.0 1.3 %collective-permute-done.9.refs_5_.refs_10_.refs_6_.refs_7_ = bf16[320,768]{1,0:T(8,128)(2,1)S(1)} collective-permute-done((bf16[320,768]{1,0:T(8,128)(2,1)S(1)}, bf16[320,768]{1,0:T(8,128)(2,1)S(1)}, u32[]{:S(2)}, u32[]{:S(2)}) %collective-permute-start.9) | collective-permute-done | bytes 491552 | tf_op jit(solution)/shard_map/ppermute | solution.py:48
  30.3 1.5 %collective-permute-done.5.refs_1_.refs_0_.refs_2_ = bf16[320,768]{1,0:T(8,128)(2,1)S(1)} collective-permute-done((bf16[320,768]{1,0:T(8,128)(2,1)S(1)}, bf16[320,768]{1,0:T(8,128)(2,1)S(1)}, u32[]{:S(2)}, u32[]{:S(2)}) %collective-permute-start.5) | collective-permute-done | bytes 491552 | tf_op jit(solution)/shard_map/ppermute | solution.py:48
  31.8 0.9 collective-permute-done.7.refs_3_.refs_1_
  32.7 0.2 fours.1
  32.9 1.2 %collective-permute-start.12 = (bf16[320,768]{1,0:T(8,128)(2,1)S(1)}, bf16[320,768]{1,0:T(8,128)(2,1)S(1)}, u32[]{:S(2)}, u32[]{:S(2)}) collective-permute-start(bf16[320,768]{1,0:T(8,128)(2,1)S(1)} %get-tuple-element.73.refs_5_.refs_3_), channel_id=1, source_target_pairs={{0,48},{1,49},{2,50},{3,51},{4,52},{5,53},{6,54},{7,55},{8,56},{9,... | collective-permute-start | bytes 1474568 | tf_op jit(solution)/shard_map/ppermute | solution.py:48
  34.2 0.8 collective-permute-start.13
  35.0 2.5 %collective-permute-start.10 = (bf16[320,768]{1,0:T(8,128)(2,1)S(1)}, bf16[320,768]{1,0:T(8,128)(2,1)S(1)}, u32[]{:S(2)}, u32[]{:S(2)}) collective-permute-start(bf16[320,768]{1,0:T(8,128)(2,1)S(1)} %get-tuple-element.70), channel_id=1, source_target_pairs={{0,66},{1,67},{2,64},{3,65},{4,70},{5,71},{6,68},{7,69},{8,74},{9,... | collective-permute-start | bytes 1474568 | tf_op jit(solution)/shard_map/ppermute | solution.py:48
  37.5 0.1 collective-permute-start.11
  37.6 0.5 collective-permute-start.15
  38.1 9.7 %collective-permute-done.12.refs_1_ = bf16[320,768]{1,0:T(8,128)(2,1)S(1)} collective-permute-done((bf16[320,768]{1,0:T(8,128)(2,1)S(1)}, bf16[320,768]{1,0:T(8,128)(2,1)S(1)}, u32[]{:S(2)}, u32[]{:S(2)}) %collective-permute-start.12) | collective-permute-done | bytes 491552 | tf_op jit(solution)/shard_map/ppermute | solution.py:48
  47.9 1.4 %collective-permute-done.10.refs_2_.refs_0_ = bf16[320,768]{1,0:T(8,128)(2,1)S(1)} collective-permute-done((bf16[320,768]{1,0:T(8,128)(2,1)S(1)}, bf16[320,768]{1,0:T(8,128)(2,1)S(1)}, u32[]{:S(2)}, u32[]{:S(2)}) %collective-permute-start.10) | collective-permute-done | bytes 491552 | tf_op jit(solution)/shard_map/ppermute | solution.py:48
  49.3 1.0 collective-permute-done.11.refs_13_.refs_9_
  50.3 0.0 collective-permute-done.15.refs_12_.refs_8_
  50.3 0.5 collective-permute-start.19
  50.8 0.0 collective-permute-start.20
  50.8 0.5 collective-permute-start.21
  51.3 1.5 %collective-permute-start.16 = (bf16[320,768]{1,0:T(8,128)(2,1)S(1)}, bf16[320,768]{1,0:T(8,128)(2,1)S(1)}, u32[]{:S(2)}, u32[]{:S(2)}) collective-permute-start(bf16[320,768]{1,0:T(8,128)(2,1)S(1)} %get-tuple-element.81), channel_id=1, source_target_pairs={{0,66},{1,67},{2,64},{3,65},{4,70},{5,71},{6,68},{7,69},{8,74},{9,... | collective-permute-start | bytes 1474568 | tf_op jit(solution)/shard_map/ppermute | solution.py:48
  52.8 1.5 %collective-permute-done.19.refs_19_.refs_15_ = bf16[320,768]{1,0:T(8,128)(2,1)S(1)} collective-permute-done((bf16[320,768]{1,0:T(8,128)(2,1)S(1)}, bf16[320,768]{1,0:T(8,128)(2,1)S(1)}, u32[]{:S(2)}, u32[]{:S(2)}) %collective-permute-start.19) | collective-permute-done | bytes 491552 | tf_op jit(solution)/shard_map/ppermute | solution.py:48
  54.3 2.1 %collective-permute-start.17 = (bf16[320,768]{1,0:T(8,128)(2,1)S(1)}, bf16[320,768]{1,0:T(8,128)(2,1)S(1)}, u32[]{:S(2)}, u32[]{:S(2)}) collective-permute-start(bf16[320,768]{1,0:T(8,128)(2,1)S(1)} %collective-permute-done.7.refs_3_.refs_1_), channel_id=1, source_target_pairs={{0,48},{1,49},{2,50},{3,51},{4,52},{5,53},{6,54},{7,55},{8,56},{9,... | collective-permute-start | bytes 1474568 | tf_op jit(solution)/shard_map/ppermute | solution.py:48
  56.4 1.7 %collective-permute-start.23 = (bf16[320,768]{1,0:T(8,128)(2,1)S(1)}, bf16[320,768]{1,0:T(8,128)(2,1)S(1)}, u32[]{:S(2)}, u32[]{:S(2)}) collective-permute-start(bf16[320,768]{1,0:T(8,128)(2,1)S(1)} %get-tuple-element.88), channel_id=1, source_target_pairs={{0,2},{1,3},{2,0},{3,1},{4,6},{5,7},{6,4},{7,5},{8,10},{9,11},{10,... | collective-permute-start | bytes 1474568 | tf_op jit(solution)/shard_map/ppermute | solution.py:48
  58.1 0.6 collective-permute-start.24
  58.7 0.6 collective-permute-start.22
  59.4 10.4 %early.1.refs_6_ = f32[960,384]{1,0:T(8,128)S(1)} custom-call(bf16[320,768]{1,0:T(8,128)(2,1)S(1)} %collective-permute-done.5.refs_1_.refs_0_.refs_2_, bf16[320,768]{1,0:T(8,128)(2,1)S(1)} %collective-permute-done.12.refs_1_, bf16[320,768]{1,0:T(8,128)(2,1)S(1)} %collective-permute-done.10.refs_2_.refs_0_, ...), custom_call_target="tpu_custom_call" | custom-call | flops 8294400000 | bytes 8000000 | tf_op jit(solution)/shard_map/early/pallas_call | solution.py:189
  69.8 1.0 collective-permute-done.24.refs_6_
  70.8 0.5 collective-permute-start.27
  71.3 0.0 collective-permute-start.25
  71.4 3.8 %late_right.1.refs_13_ = f32[320,384]{1,0:T(8,128)S(1)} custom-call(bf16[320,768]{1,0:T(8,128)(2,1)S(1)} %collective-permute-done.16.refs_0_, bf16[320,768]{1,0:T(8,128)(2,1)S(1)} %collective-permute-done.17.refs_1_, bf16[320,768]{1,0:T(8,128)(2,1)S(1)} %get-tuple-element.61.refs_2_.refs_6_, bf16[320,768]{1,0:T(8,128)(2,1)S(1)} %get-tuple-element.74.refs_7_.refs_3_, ...), custom_call_target="tpu_custom_call" | custom-call | flops 2764800000 | bytes 8000000 | tf_op jit(solution)/shard_map/late_right/pallas_call | solution.py:189
  75.2 2.3 %late_1.1 = (f32[160,345]{1,0:T(8,128)S(1)}, f32[160,345]{1,0:T(8,128)S(1)}, bf16[960,1536]{1,0:T(8,128)(2,1)S(1)}, bf16[960,768]{1,0:T(8,128)(2,1)S(1)}) custom-call(bf16[320,768]{1,0:T(8,128)(2,1)S(1)} %collective-permute-done.16.refs_0_, bf16[320,768]{1,0:T(8,128)(2,1)S(1)} %collective-permute-done.17.refs_1_, ...), custom_call_target="tpu_custom_call" | custom-call | flops 1658880000 | bytes 8000000 | tf_op jit(solution)/shard_map/late_1/pallas_call | solution.py:189
  77.5 1.6 %collective-permute-start.29 = (f32[160,345]{1,0:T(8,128)S(1)}, f32[160,345]{1,0:T(8,128)S(1)}, u32[]{:S(2)}, u32[]{:S(2)}) collective-permute-start(f32[160,345]{1,0:T(8,128)S(1)} %get-tuple-element.96), channel_id=1, source_target_pairs={{0,114},{1,115},{2,112},{3,113},{4,118},{5,119},{6,116},{7,117},{8... | collective-permute-start | bytes 662408 | tf_op jit(solution)/shard_map/ppermute | solution.py:48
  79.1 2.3 %late_2.1 = (f32[160,345]{1,0:T(8,128)S(1)}, f32[160,345]{1,0:T(8,128)S(1)}) custom-call(bf16[320,768]{1,0:T(8,128)(2,1)S(1)} %collective-permute-done.5.refs_1_.refs_0_.refs_2_, bf16[320,768]{1,0:T(8,128)(2,1)S(1)} %collective-permute-done.12.refs_1_, bf16[320,768]{1,0:T(8,128)(2,1)S(1)} %collective-permute-done.10.refs_2_.refs_0_, ...), custom_call_target="tpu_custom_call" | custom-call | flops 1658880000 | bytes 8000000 | tf_op jit(solution)/shard_map/late_2/pallas_call | solution.py:189
  81.4 4.1 %collective-permute-start.31 = (f32[160,345]{1,0:T(8,128)S(1)}, f32[160,345]{1,0:T(8,128)S(1)}, u32[]{:S(2)}, u32[]{:S(2)}) collective-permute-start(f32[160,345]{1,0:T(8,128)S(1)} %get-tuple-element.98), channel_id=1, source_target_pairs={{0,78},{1,79},{2,76},{3,77},{4,74},{5,75},{6,72},{7,73},{8,70},{9,... | collective-permute-start | bytes 662408 | tf_op jit(solution)/shard_map/ppermute | solution.py:48
  85.5 2.6 %collective-permute-start.28 = (f32[160,345]{1,0:T(8,128)S(1)}, f32[160,345]{1,0:T(8,128)S(1)}, u32[]{:S(2)}, u32[]{:S(2)}) collective-permute-start(f32[160,345]{1,0:T(8,128)S(1)} %get-tuple-element.103), channel_id=1, source_target_pairs={{0,126},{1,127},{2,124},{3,125},{4,122},{5,123},{6,120},{7,121},{8... | collective-permute-start | bytes 662408 | tf_op jit(solution)/shard_map/ppermute | solution.py:48
  88.1 2.3 %late_3.1 = (f32[160,345]{1,0:T(8,128)S(1)}, f32[160,345]{1,0:T(8,128)S(1)}) custom-call(bf16[320,768]{1,0:T(8,128)(2,1)S(1)} %get-tuple-element.60.refs_0_.refs_4_.refs_2_, bf16[320,768]{1,0:T(8,128)(2,1)S(1)} %collective-permute-done.12.refs_1_, bf16[320,768]{1,0:T(8,128)(2,1)S(1)} %collective-permute-done.5.refs_1_.refs_0_.refs_2_, ...), custom_call_target="tpu_custom_call" | custom-call | flops 1658880000 | bytes 8000000 | tf_op jit(solution)/shard_map/late_3/pallas_call | solution.py:189
  90.3 1.5 %collective-permute-start.32 = (f32[160,345]{1,0:T(8,128)S(1)}, f32[160,345]{1,0:T(8,128)S(1)}, u32[]{:S(2)}, u32[]{:S(2)}) collective-permute-start(f32[160,345]{1,0:T(8,128)S(1)} %get-tuple-element.105), channel_id=1, source_target_pairs={{0,48},{1,49},{2,50},{3,51},{4,52},{5,53},{6,54},{7,55},{8,56},{9,... | collective-permute-start | bytes 662408 | tf_op jit(solution)/shard_map/ppermute | solution.py:48
  91.8 3.4 %collective-permute-start.30 = (f32[160,345]{1,0:T(8,128)S(1)}, f32[160,345]{1,0:T(8,128)S(1)}, u32[]{:S(2)}, u32[]{:S(2)}) collective-permute-start(f32[160,345]{1,0:T(8,128)S(1)} %get-tuple-element.104), channel_id=1, source_target_pairs={{0,60},{1,61},{2,62},{3,63},{4,56},{5,57},{6,58},{7,59},{8,52},{9,... | collective-permute-start | bytes 662408 | tf_op jit(solution)/shard_map/ppermute | solution.py:48
  95.2 2.3 %late_4.1 = (f32[160,345]{1,0:T(8,128)S(1)}, f32[160,345]{1,0:T(8,128)S(1)}) custom-call(bf16[320,768]{1,0:T(8,128)(2,1)S(1)} %collective-permute-done.10.refs_2_.refs_0_, bf16[320,768]{1,0:T(8,128)(2,1)S(1)} %collective-permute-done.7.refs_3_.refs_1_, bf16[320,768]{1,0:T(8,128)(2,1)S(1)} %get-tuple-element.60.refs_0_.refs_4_.refs_2_, ...), custom_call_target="tpu_custom_call" | custom-call | flops 1658880000 | bytes 8000000 | tf_op jit(solution)/shard_map/late_4/pallas_call | solution.py:189
  97.4 2.4 %collective-permute-done.28 = f32[160,345]{1,0:T(8,128)S(1)} collective-permute-done((f32[160,345]{1,0:T(8,128)S(1)}, f32[160,345]{1,0:T(8,128)S(1)}, u32[]{:S(2)}, u32[]{:S(2)}) %collective-permute-start.28) | collective-permute-done | bytes 220832 | tf_op jit(solution)/shard_map/ppermute | solution.py:48
  99.8 0.7 collective-permute-start.34
  100.5 1.2 %collective-permute-start.33 = (f32[160,345]{1,0:T(8,128)S(1)}, f32[160,345]{1,0:T(8,128)S(1)}, u32[]{:S(2)}, u32[]{:S(2)}) collective-permute-start(f32[160,345]{1,0:T(8,128)S(1)} %get-tuple-element.106), channel_id=1, source_target_pairs={{0,12},{1,13},{2,14},{3,15},{4,8},{5,9},{6,10},{7,11},{8,4},{9,5},... | collective-permute-start | bytes 662408 | tf_op jit(solution)/shard_map/ppermute | solution.py:48
  101.7 5.8 %collective-permute-done.30 = f32[160,345]{1,0:T(8,128)S(1)} collective-permute-done((f32[160,345]{1,0:T(8,128)S(1)}, f32[160,345]{1,0:T(8,128)S(1)}, u32[]{:S(2)}, u32[]{:S(2)}) %collective-permute-start.30) | collective-permute-done | bytes 220832 | tf_op jit(solution)/shard_map/ppermute | solution.py:48
  107.4 4.9 %collective-permute-done.33 = f32[160,345]{1,0:T(8,128)S(1)} collective-permute-done((f32[160,345]{1,0:T(8,128)S(1)}, f32[160,345]{1,0:T(8,128)S(1)}, u32[]{:S(2)}, u32[]{:S(2)}) %collective-permute-start.33) | collective-permute-done | bytes 220832 | tf_op jit(solution)/shard_map/ppermute | solution.py:48
  112.4 0.9 add_bitcast_fusion
  (26 shorter events, 0.1 us)
Async XLA Ops:
  0.0 12.3 %collective-permute-start.1 = (bf16[160,768]{1,0:T(8,128)(2,1)}, bf16[160,768]{1,0:T(8,128)(2,1)S(1)}, u32[]{:S(2)}, u32[]{:S(2)}) collective-permute-start(bf16[160,768]{1,0:T(8,128)(2,1)} %act.1), channel_id=1, source_target_pairs={{0,16},{1,17},{2,18},{3,19},{4,20},{5,21},{6,22},{7,23},{8,24},{9,... | collective-permute-start | bytes 737288 | tf_op jit(solution)/shard_map/ppermute | solution.py:48
  1.6 10.8 %collective-permute-start = (bf16[160,768]{1,0:T(8,128)(2,1)}, bf16[160,768]{1,0:T(8,128)(2,1)S(1)}, u32[]{:S(2)}, u32[]{:S(2)}) collective-permute-start(bf16[160,768]{1,0:T(8,128)(2,1)} %act.1), channel_id=1, source_target_pairs={{0,48},{1,49},{2,50},{3,51},{4,52},{5,53},{6,54},{7,55},{8,56},{9,... | collective-permute-start | bytes 737288 | tf_op jit(solution)/shard_map/ppermute | solution.py:48
  3.7 8.7 %collective-permute-start.3 = (bf16[160,768]{1,0:T(8,128)(2,1)}, bf16[160,768]{1,0:T(8,128)(2,1)S(1)}, u32[]{:S(2)}, u32[]{:S(2)}) collective-permute-start(bf16[160,768]{1,0:T(8,128)(2,1)} %sig.1), channel_id=1, source_target_pairs={{0,4},{1,5},{2,6},{3,7},{4,0},{5,1},{6,2},{7,3},{8,12},{9,13},{10,... | collective-permute-start | bytes 737288 | tf_op jit(solution)/shard_map/ppermute | solution.py:48
  5.2 8.3 %collective-permute-start.2 = (bf16[160,768]{1,0:T(8,128)(2,1)}, bf16[160,768]{1,0:T(8,128)(2,1)S(1)}, u32[]{:S(2)}, u32[]{:S(2)}) collective-permute-start(bf16[160,768]{1,0:T(8,128)(2,1)} %sig.1), channel_id=1, source_target_pairs={{0,12},{1,13},{2,14},{3,15},{4,8},{5,9},{6,10},{7,11},{8,4},{9,5},... | collective-permute-start | bytes 737288 | tf_op jit(solution)/shard_map/ppermute | solution.py:48
  7.4 0.9 copy-start
  8.4 0.9 copy-start.2
  9.3 0.9 copy-start.3
  10.3 6.8 %collective-permute-start.4 = (bf16[160,768]{1,0:T(8,128)(2,1)S(1)}, bf16[160,768]{1,0:T(8,128)(2,1)S(1)}, u32[]{:S(2)}, u32[]{:S(2)}) collective-permute-start(bf16[160,768]{1,0:T(8,128)(2,1)S(1)} %get-tuple-element.59.refs_6_), channel_id=1, source_target_pairs={{0,2},{1,3},{2,0},{3,1},{4,6},{5,7},{6,4},{7,5},{8,10},{9,11},{10,... | collective-permute-start | bytes 737288 | tf_op jit(solution)/shard_map/ppermute | solution.py:48
  17.4 11.2 %collective-permute-start.6 = (bf16[320,768]{1,0:T(8,128)(2,1)S(1)}, bf16[320,768]{1,0:T(8,128)(2,1)S(1)}, u32[]{:S(2)}, u32[]{:S(2)}) collective-permute-start(bf16[320,768]{1,0:T(8,128)(2,1)S(1)} %get-tuple-element.61.refs_2_.refs_6_), channel_id=1, source_target_pairs={{0,4},{1,5},{2,6},{3,7},{4,0},{5,1},{6,2},{7,3},{8,12},{9,13},{10,... | collective-permute-start | bytes 1474568 | tf_op jit(solution)/shard_map/ppermute | solution.py:48
  18.2 10.8 %collective-permute-start.8 = (bf16[320,768]{1,0:T(8,128)(2,1)S(1)}, bf16[320,768]{1,0:T(8,128)(2,1)S(1)}, u32[]{:S(2)}, u32[]{:S(2)}) collective-permute-start(bf16[320,768]{1,0:T(8,128)(2,1)S(1)} %get-tuple-element.74.refs_7_.refs_3_), channel_id=1, source_target_pairs={{0,2},{1,3},{2,0},{3,1},{4,6},{5,7},{6,4},{7,5},{8,10},{9,11},{10,... | collective-permute-start | bytes 1474568 | tf_op jit(solution)/shard_map/ppermute | solution.py:48
  19.9 10.4 %collective-permute-start.9 = (bf16[320,768]{1,0:T(8,128)(2,1)S(1)}, bf16[320,768]{1,0:T(8,128)(2,1)S(1)}, u32[]{:S(2)}, u32[]{:S(2)}) collective-permute-start(bf16[320,768]{1,0:T(8,128)(2,1)S(1)} %get-tuple-element.76.refs_8_.refs_4_), channel_id=1, source_target_pairs={{0,16},{1,17},{2,18},{3,19},{4,20},{5,21},{6,22},{7,23},{8,24},{9,... | collective-permute-start | bytes 1474568 | tf_op jit(solution)/shard_map/ppermute | solution.py:48
  20.5 11.3 %collective-permute-start.5 = (bf16[320,768]{1,0:T(8,128)(2,1)S(1)}, bf16[320,768]{1,0:T(8,128)(2,1)S(1)}, u32[]{:S(2)}, u32[]{:S(2)}) collective-permute-start(bf16[320,768]{1,0:T(8,128)(2,1)S(1)} %get-tuple-element.60.refs_0_.refs_4_.refs_2_), channel_id=1, source_target_pairs={{0,12},{1,13},{2,14},{3,15},{4,8},{5,9},{6,10},{7,11},{8,4},{9,5},... | collective-permute-start | bytes 1474568 | tf_op jit(solution)/shard_map/ppermute | solution.py:48
  21.4 11.3 %collective-permute-start.7 = (bf16[320,768]{1,0:T(8,128)(2,1)S(1)}, bf16[320,768]{1,0:T(8,128)(2,1)S(1)}, u32[]{:S(2)}, u32[]{:S(2)}) collective-permute-start(bf16[320,768]{1,0:T(8,128)(2,1)S(1)} %get-tuple-element.73.refs_5_.refs_3_), channel_id=1, source_target_pairs={{0,66},{1,67},{2,64},{3,65},{4,70},{5,71},{6,68},{7,69},{8,74},{9,... | collective-permute-start | bytes 1474568 | tf_op jit(solution)/shard_map/ppermute | solution.py:48
  32.7 4.9 %collective-permute-start.14 = (bf16[320,2304]{1,0:T(8,128)(2,1)S(1)}, bf16[320,2304]{1,0:T(8,128)(2,1)S(1)}, u32[]{:S(2)}, u32[]{:S(2)}) collective-permute-start(bf16[320,2304]{1,0:T(8,128)(2,1)S(1)} %get-tuple-element.75), channel_id=1, source_target_pairs={{0,1},{1,0},{2,3},{3,2},{4,5},{5,4},{6,7},{7,6},{8,9},{9,8},{10,11... | collective-permute-start | bytes 4423688 | tf_op jit(solution)/shard_map/ppermute | solution.py:48
  32.9 14.9 %collective-permute-start.12 = (bf16[320,768]{1,0:T(8,128)(2,1)S(1)}, bf16[320,768]{1,0:T(8,128)(2,1)S(1)}, u32[]{:S(2)}, u32[]{:S(2)}) collective-permute-start(bf16[320,768]{1,0:T(8,128)(2,1)S(1)} %get-tuple-element.73.refs_5_.refs_3_), channel_id=1, source_target_pairs={{0,48},{1,49},{2,50},{3,51},{4,52},{5,53},{6,54},{7,55},{8,56},{9,... | collective-permute-start | bytes 1474568 | tf_op jit(solution)/shard_map/ppermute | solution.py:48
  34.2 13.7 %collective-permute-start.13 = (bf16[320,768]{1,0:T(8,128)(2,1)S(1)}, bf16[320,768]{1,0:T(8,128)(2,1)S(1)}, u32[]{:S(2)}, u32[]{:S(2)}) collective-permute-start(bf16[320,768]{1,0:T(8,128)(2,1)S(1)} %get-tuple-element.74.refs_7_.refs_3_), channel_id=1, source_target_pairs={{0,16},{1,17},{2,18},{3,19},{4,20},{5,21},{6,22},{7,23},{8,24},{9,... | collective-permute-start | bytes 1474568 | tf_op jit(solution)/shard_map/ppermute | solution.py:48
  35.0 14.3 %collective-permute-start.10 = (bf16[320,768]{1,0:T(8,128)(2,1)S(1)}, bf16[320,768]{1,0:T(8,128)(2,1)S(1)}, u32[]{:S(2)}, u32[]{:S(2)}) collective-permute-start(bf16[320,768]{1,0:T(8,128)(2,1)S(1)} %get-tuple-element.70), channel_id=1, source_target_pairs={{0,66},{1,67},{2,64},{3,65},{4,70},{5,71},{6,68},{7,69},{8,74},{9,... | collective-permute-start | bytes 1474568 | tf_op jit(solution)/shard_map/ppermute | solution.py:48
  37.5 12.8 %collective-permute-start.11 = (bf16[320,768]{1,0:T(8,128)(2,1)S(1)}, bf16[320,768]{1,0:T(8,128)(2,1)S(1)}, u32[]{:S(2)}, u32[]{:S(2)}) collective-permute-start(bf16[320,768]{1,0:T(8,128)(2,1)S(1)} %get-tuple-element.71), channel_id=1, source_target_pairs={{0,2},{1,3},{2,0},{3,1},{4,6},{5,7},{6,4},{7,5},{8,10},{9,11},{10,... | collective-permute-start | bytes 1474568 | tf_op jit(solution)/shard_map/ppermute | solution.py:48
  37.6 12.7 %collective-permute-start.15 = (bf16[320,768]{1,0:T(8,128)(2,1)S(1)}, bf16[320,768]{1,0:T(8,128)(2,1)S(1)}, u32[]{:S(2)}, u32[]{:S(2)}) collective-permute-start(bf16[320,768]{1,0:T(8,128)(2,1)S(1)} %get-tuple-element.76.refs_8_.refs_4_), channel_id=1, source_target_pairs={{0,4},{1,5},{2,6},{3,7},{4,0},{5,1},{6,2},{7,3},{8,12},{9,13},{10,... | collective-permute-start | bytes 1474568 | tf_op jit(solution)/shard_map/ppermute | solution.py:48
  50.3 8.4 %collective-permute-start.18 = (bf16[320,2304]{1,0:T(8,128)(2,1)S(1)}, bf16[320,2304]{1,0:T(8,128)(2,1)S(1)}, u32[]{:S(2)}, u32[]{:S(2)}) collective-permute-start(bf16[320,2304]{1,0:T(8,128)(2,1)S(1)} %get-tuple-element.84), channel_id=1, source_target_pairs={{0,1},{1,0},{2,3},{3,2},{4,5},{5,4},{6,7},{7,6},{8,9},{9,8},{10,11... | collective-permute-start | bytes 4423688 | tf_op jit(solution)/shard_map/ppermute | solution.py:48
  50.3 4.0 %collective-permute-start.19 = (bf16[320,768]{1,0:T(8,128)(2,1)S(1)}, bf16[320,768]{1,0:T(8,128)(2,1)S(1)}, u32[]{:S(2)}, u32[]{:S(2)}) collective-permute-start(bf16[320,768]{1,0:T(8,128)(2,1)S(1)} %collective-permute-done.11.refs_13_.refs_9_), channel_id=1, source_target_pairs={{0,1},{1,0},{2,3},{3,2},{4,5},{5,4},{6,7},{7,6},{8,9},{9,8},{10,11... | collective-permute-start | bytes 1474568 | tf_op jit(solution)/shard_map/ppermute | solution.py:48
  50.8 5.6 %collective-permute-start.20 = (bf16[320,768]{1,0:T(8,128)(2,1)S(1)}, bf16[320,768]{1,0:T(8,128)(2,1)S(1)}, u32[]{:S(2)}, u32[]{:S(2)}) collective-permute-start(bf16[320,768]{1,0:T(8,128)(2,1)S(1)} %collective-permute-done.13.refs_9_.refs_5_.refs_3_), channel_id=1, source_target_pairs={{0,1},{1,0},{2,3},{3,2},{4,5},{5,4},{6,7},{7,6},{8,9},{9,8},{10,11... | collective-permute-start | bytes 1474568 | tf_op jit(solution)/shard_map/ppermute | solution.py:48
  50.8 7.3 %collective-permute-start.21 = (bf16[320,768]{1,0:T(8,128)(2,1)S(1)}, bf16[320,768]{1,0:T(8,128)(2,1)S(1)}, u32[]{:S(2)}, u32[]{:S(2)}) collective-permute-start(bf16[320,768]{1,0:T(8,128)(2,1)S(1)} %collective-permute-done.15.refs_12_.refs_8_), channel_id=1, source_target_pairs={{0,1},{1,0},{2,3},{3,2},{4,5},{5,4},{6,7},{7,6},{8,9},{9,8},{10,11... | collective-permute-start | bytes 1474568 | tf_op jit(solution)/shard_map/ppermute | solution.py:48
  51.3 20.0 %collective-permute-start.16 = (bf16[320,768]{1,0:T(8,128)(2,1)S(1)}, bf16[320,768]{1,0:T(8,128)(2,1)S(1)}, u32[]{:S(2)}, u32[]{:S(2)}) collective-permute-start(bf16[320,768]{1,0:T(8,128)(2,1)S(1)} %get-tuple-element.81), channel_id=1, source_target_pairs={{0,66},{1,67},{2,64},{3,65},{4,70},{5,71},{6,68},{7,69},{8,74},{9,... | collective-permute-start | bytes 1474568 | tf_op jit(solution)/shard_map/ppermute | solution.py:48
  54.3 17.1 %collective-permute-start.17 = (bf16[320,768]{1,0:T(8,128)(2,1)S(1)}, bf16[320,768]{1,0:T(8,128)(2,1)S(1)}, u32[]{:S(2)}, u32[]{:S(2)}) collective-permute-start(bf16[320,768]{1,0:T(8,128)(2,1)S(1)} %collective-permute-done.7.refs_3_.refs_1_), channel_id=1, source_target_pairs={{0,48},{1,49},{2,50},{3,51},{4,52},{5,53},{6,54},{7,55},{8,56},{9,... | collective-permute-start | bytes 1474568 | tf_op jit(solution)/shard_map/ppermute | solution.py:48
  56.4 14.5 %collective-permute-start.23 = (bf16[320,768]{1,0:T(8,128)(2,1)S(1)}, bf16[320,768]{1,0:T(8,128)(2,1)S(1)}, u32[]{:S(2)}, u32[]{:S(2)}) collective-permute-start(bf16[320,768]{1,0:T(8,128)(2,1)S(1)} %get-tuple-element.88), channel_id=1, source_target_pairs={{0,2},{1,3},{2,0},{3,1},{4,6},{5,7},{6,4},{7,5},{8,10},{9,11},{10,... | collective-permute-start | bytes 1474568 | tf_op jit(solution)/shard_map/ppermute | solution.py:48
  58.1 12.7 %collective-permute-start.24 = (bf16[320,768]{1,0:T(8,128)(2,1)S(1)}, bf16[320,768]{1,0:T(8,128)(2,1)S(1)}, u32[]{:S(2)}, u32[]{:S(2)}) collective-permute-start(bf16[320,768]{1,0:T(8,128)(2,1)S(1)} %collective-permute-done.8.refs_4_.refs_14_.refs_10_), channel_id=1, source_target_pairs={{0,16},{1,17},{2,18},{3,19},{4,20},{5,21},{6,22},{7,23},{8,24},{9,... | collective-permute-start | bytes 1474568 | tf_op jit(solution)/shard_map/ppermute | solution.py:48
  58.7 12.6 %collective-permute-start.22 = (bf16[320,768]{1,0:T(8,128)(2,1)S(1)}, bf16[320,768]{1,0:T(8,128)(2,1)S(1)}, u32[]{:S(2)}, u32[]{:S(2)}) collective-permute-start(bf16[320,768]{1,0:T(8,128)(2,1)S(1)} %collective-permute-done.9.refs_5_.refs_10_.refs_6_.refs_7_), channel_id=1, source_target_pairs={{0,4},{1,5},{2,6},{3,7},{4,0},{5,1},{6,2},{7,3},{8,12},{9,13},{10,... | collective-permute-start | bytes 1474568 | tf_op jit(solution)/shard_map/ppermute | solution.py:48
  70.8 4.3 %collective-permute-start.26 = (bf16[320,768]{1,0:T(8,128)(2,1)S(1)}, bf16[320,768]{1,0:T(8,128)(2,1)S(1)}, u32[]{:S(2)}, u32[]{:S(2)}) collective-permute-start(bf16[320,768]{1,0:T(8,128)(2,1)S(1)} %collective-permute-done.23.refs_5_), channel_id=1, source_target_pairs={{0,1},{1,0},{2,3},{3,2},{4,5},{5,4},{6,7},{7,6},{8,9},{9,8},{10,11... | collective-permute-start | bytes 1474568 | tf_op jit(solution)/shard_map/ppermute | solution.py:48
  70.8 4.3 %collective-permute-start.27 = (bf16[320,768]{1,0:T(8,128)(2,1)S(1)}, bf16[320,768]{1,0:T(8,128)(2,1)S(1)}, u32[]{:S(2)}, u32[]{:S(2)}) collective-permute-start(bf16[320,768]{1,0:T(8,128)(2,1)S(1)} %collective-permute-done.24.refs_6_), channel_id=1, source_target_pairs={{0,1},{1,0},{2,3},{3,2},{4,5},{5,4},{6,7},{7,6},{8,9},{9,8},{10,11... | collective-permute-start | bytes 1474568 | tf_op jit(solution)/shard_map/ppermute | solution.py:48
  71.3 3.8 %collective-permute-start.25 = (bf16[320,768]{1,0:T(8,128)(2,1)S(1)}, bf16[320,768]{1,0:T(8,128)(2,1)S(1)}, u32[]{:S(2)}, u32[]{:S(2)}) collective-permute-start(bf16[320,768]{1,0:T(8,128)(2,1)S(1)} %collective-permute-done.22.refs_4_), channel_id=1, source_target_pairs={{0,1},{1,0},{2,3},{3,2},{4,5},{5,4},{6,7},{7,6},{8,9},{9,8},{10,11... | collective-permute-start | bytes 1474568 | tf_op jit(solution)/shard_map/ppermute | solution.py:48
  77.5 19.9 %collective-permute-start.29 = (f32[160,345]{1,0:T(8,128)S(1)}, f32[160,345]{1,0:T(8,128)S(1)}, u32[]{:S(2)}, u32[]{:S(2)}) collective-permute-start(f32[160,345]{1,0:T(8,128)S(1)} %get-tuple-element.96), channel_id=1, source_target_pairs={{0,114},{1,115},{2,112},{3,113},{4,118},{5,119},{6,116},{7,117},{8... | collective-permute-start | bytes 662408 | tf_op jit(solution)/shard_map/ppermute | solution.py:48
  81.4 26.1 %collective-permute-start.31 = (f32[160,345]{1,0:T(8,128)S(1)}, f32[160,345]{1,0:T(8,128)S(1)}, u32[]{:S(2)}, u32[]{:S(2)}) collective-permute-start(f32[160,345]{1,0:T(8,128)S(1)} %get-tuple-element.98), channel_id=1, source_target_pairs={{0,78},{1,79},{2,76},{3,77},{4,74},{5,75},{6,72},{7,73},{8,70},{9,... | collective-permute-start | bytes 662408 | tf_op jit(solution)/shard_map/ppermute | solution.py:48
  85.5 14.3 %collective-permute-start.28 = (f32[160,345]{1,0:T(8,128)S(1)}, f32[160,345]{1,0:T(8,128)S(1)}, u32[]{:S(2)}, u32[]{:S(2)}) collective-permute-start(f32[160,345]{1,0:T(8,128)S(1)} %get-tuple-element.103), channel_id=1, source_target_pairs={{0,126},{1,127},{2,124},{3,125},{4,122},{5,123},{6,120},{7,121},{8... | collective-permute-start | bytes 662408 | tf_op jit(solution)/shard_map/ppermute | solution.py:48
  90.3 11.3 %collective-permute-start.32 = (f32[160,345]{1,0:T(8,128)S(1)}, f32[160,345]{1,0:T(8,128)S(1)}, u32[]{:S(2)}, u32[]{:S(2)}) collective-permute-start(f32[160,345]{1,0:T(8,128)S(1)} %get-tuple-element.105), channel_id=1, source_target_pairs={{0,48},{1,49},{2,50},{3,51},{4,52},{5,53},{6,54},{7,55},{8,56},{9,... | collective-permute-start | bytes 662408 | tf_op jit(solution)/shard_map/ppermute | solution.py:48
  91.8 20.6 %copy-start.1 = (f32[345,160]{0,1:T(8,128)S(1)}, f32[345,160]{0,1:T(8,128)}, u32[]{:S(2)}) copy-start(f32[345,160]{0,1:T(8,128)} %param.7) | copy-start | bytes 662404
  91.8 20.6 %copy-start.4 = (s32[160]{0:T(256)S(1)}, s32[160]{0:T(256)}, u32[]{:S(2)}) copy-start(s32[160]{0:T(256)} %param.6) | copy-start | bytes 1924
  91.8 15.6 %collective-permute-start.30 = (f32[160,345]{1,0:T(8,128)S(1)}, f32[160,345]{1,0:T(8,128)S(1)}, u32[]{:S(2)}, u32[]{:S(2)}) collective-permute-start(f32[160,345]{1,0:T(8,128)S(1)} %get-tuple-element.104), channel_id=1, source_target_pairs={{0,60},{1,61},{2,62},{3,63},{4,56},{5,57},{6,58},{7,59},{8,52},{9,... | collective-permute-start | bytes 662408 | tf_op jit(solution)/shard_map/ppermute | solution.py:48
  99.8 7.7 %collective-permute-start.34 = (f32[160,345]{1,0:T(8,128)S(1)}, f32[160,345]{1,0:T(8,128)S(1)}, u32[]{:S(2)}, u32[]{:S(2)}) collective-permute-start(f32[160,345]{1,0:T(8,128)S(1)} %get-tuple-element.108), channel_id=1, source_target_pairs={{0,66},{1,67},{2,64},{3,65},{4,70},{5,71},{6,68},{7,69},{8,74},{9,... | collective-permute-start | bytes 662408 | tf_op jit(solution)/shard_map/ppermute | solution.py:48
  100.5 11.9 %collective-permute-start.33 = (f32[160,345]{1,0:T(8,128)S(1)}, f32[160,345]{1,0:T(8,128)S(1)}, u32[]{:S(2)}, u32[]{:S(2)}) collective-permute-start(f32[160,345]{1,0:T(8,128)S(1)} %get-tuple-element.106), channel_id=1, source_target_pairs={{0,12},{1,13},{2,14},{3,15},{4,8},{5,9},{6,10},{7,11},{8,4},{9,5},... | collective-permute-start | bytes 662408 | tf_op jit(solution)/shard_map/ppermute | solution.py:48

commit v4 on v3

--- a/solution.py
+++ b/solution.py
@@ -56,9 +56,7 @@
     return lax.dot_general(a, b, dims, preferred_element_type=f32)
 
 
-def stage_kernel(act, sig, coef, act_out, sig_out, split):
-    act_out[...] = act[...]
-    sig_out[...] = sig[...]
+def split_kernel(coef, split):
     split[...] = jnp.zeros_like(split)
     values = coef[...]
     high = values.astype(bf16)
@@ -66,15 +64,15 @@
     split[:, LANES : LANES + CLASSES] = (values - high.astype(f32)).astype(bf16)
 
 
-def stage(act, sig, coefs):
+def split_coefs(coefs):
     return pl.pallas_call(
-        stage_kernel,
-        out_shape=[pltpu.VMEM((OWN, FEAT), bf16), pltpu.VMEM((OWN, FEAT), bf16), pltpu.VMEM((OWN, 2 * LANES), bf16)],
-        in_specs=[VMEM] * 3,
-        out_specs=[VMEM] * 3,
+        split_kernel,
+        out_shape=pltpu.VMEM((OWN, 2 * LANES), bf16),
+        in_specs=[VMEM],
+        out_specs=VMEM,
         compiler_params=pltpu.CompilerParams(vmem_limit_bytes=4 << 20),
-        name="stage",
-    )(act, sig, coefs)
+        name="split_coefs",
+    )(coefs)
 
 
 def arrange_kernel(plan, n_in, *refs):
@@ -207,8 +205,17 @@
     for g in groups:
         a[g, "x"] = send(activations, g, "x")
         s[g, "y"] = send(signals, g, "y")
-    act_own, sig_own, c0 = stage(activations, signals, coefs)
+    c0 = split_coefs(coefs)
     cz = send(c0, "near", "z")
+    act_own, sig_own = arrange([[[(after(v, c0), 0)]] for v in (activations, signals)], "own_rows")
+
+    def together(*values):
+        return lax.optimization_barrier(values)
+
+    a["far", "x"], a["near", "x"], s["far", "y"], s["near", "y"], cz = together(
+        a["far", "x"], a["near", "x"], s["far", "y"], s["near", "y"], cz
+    )
+
     pairs = arrange(
         [[[(act_own, 0), (a[g, "x"], 0)]] for g in groups]
         + [[[(sig_own, 0), (s[g, "y"], 0)]] for g in groups]
@@ -217,37 +224,36 @@
         "pairs",
     )
     a0x, s0y, c0z, own2 = dict(zip(groups, pairs[:2])), dict(zip(groups, pairs[2:4])), pairs[4], pairs[5]
+    own2_mate = send(own2, "near", "c")
     ay, sz = {}, {}
     for g in groups:
         ay[g] = send(a0x[g], g, "y")
         sz[g] = send(s0y[g], g, "z")
-    cx = send(c0z, "near", "x")
-    ay["far"], ay["near"], sz["far"], sz["near"], cx, own2 = lax.optimization_barrier(
-        (ay["far"], ay["near"], sz["far"], sz["near"], cx, own2)
+    cx = send(after(c0z, own2_mate), "near", "x")
+    ay["far"], ay["near"], sz["far"], sz["near"], cx = together(ay["far"], ay["near"], sz["far"], sz["near"], cx)
+    n = "near"
+    turned = arrange(
+        [[[(a0x[g], k), (ay[g], k)]] for k in (0, 1) for g in groups]
+        + [[[(ay[n], 0), (ay[n], 1)], [(sz[n], 0), (sz[n], 1)], [(cx, 0), (cx, 1)]]],
+        "turn",
     )
-    own2_mate = send(own2, "near", "c")
-    fours = arrange(
-        [[[(a0x[g], 0), (ay[g], 0)]] for g in groups]
-        + [[[(a0x[g], 1), (ay[g], 1)]] for g in groups]
-        + [[[(ay["near"], 0), (ay["near"], 1)], [(sz["near"], 0), (sz["near"], 1)], [(cx, 0), (cx, 1)]]],
-        "fours",
-    )
-    a0y, axxy, next2 = dict(zip(groups, fours[:2])), dict(zip(groups, fours[2:4])), fours[4]
+    a0y, axxy, next2 = dict(zip(groups, turned[:2])), dict(zip(groups, turned[2:4])), turned[4]
+    next2_mate = send(next2, n, "c")
     az, sx = {}, {}
     for g in groups:
+        sx[g] = send(after(s0y[g], sz[g]), g, "x")
         az[g] = send(a0y[g], g, "z")
-        sx[g] = send(after(s0y[g], next2), g, "x")
-    cy = send(after(c0z, next2, own2_mate), "near", "y")
-    az["far"], az["near"], sx["far"], sx["near"], cy, next2 = lax.optimization_barrier(
-        (az["far"], az["near"], sx["far"], sx["near"], cy, next2)
+    cy = send(after(c0z, cx, next2_mate), n, "y")
+    az["far"], az[n], sx["far"], sx[n], cy, axxy["far"], axxy[n], sz["far"], sz[n], cx = together(
+        az["far"], az[n], sx["far"], sx[n], cy, axxy["far"], axxy[n], sz["far"], sz[n], cx
     )
-    mates = [send(v, "near", "c") for v in (next2, az["near"], sx["near"], cy)]
-    next2_mate, az_mate, sx_mate, cy_mate = mates
+    az_mate, sx_mate, cy_mate = small = [send(v, n, "c") for v in (az[n], sx[n], cy)]
     axz, sxz = {}, {}
-    for g in groups:
-        axz[g] = send(after(axxy[g], cy), g, "z")
-        sxz[g] = send(after(sz[g], cy), g, "x")
-    cxy = send(after(cx, *mates), "near", "y")
+    axz[n] = send(axxy[n], n, "z")
+    sxz[n] = send(sz[n], n, "x")
+    cxy = send(after(cx, *small), n, "y")
+    axz["far"] = send(after(axxy["far"], *small), "far", "z")
+    sxz["far"] = send(after(sz["far"], *small), "far", "x")
 
     def blocks_of(g):
         act = {"": (a0x[g], 0, 0), "x": (a0x[g], 1, 0), "y": (ay[g], 0, 0), "xy": (ay[g], 1, 0)}
@@ -281,23 +287,20 @@
     second = ("xy", "xz", "xyz")
     left_2 = [left[k] for k in second] + [(act_mate[k], sig_mate[k], coef_mate[k]) for k in second]
     (total_2,) = partial_sums(right_2, left_1, None, False, 320, "late_right")
-    got = {}
     sum_xyz, sum_xz, *ready = partial_sums(right_2, left_2, (total_2, 0), True, 320, "late_1", keep_left=True)
-    got["xyz"], got["xz"] = send(sum_xyz, "far", "xyz"), send(sum_xz, "far", "xz")
+    got_xyz, part_x = send(sum_xyz, "far", "xyz"), send(sum_xz, "far", "z")
     total_1 = after(total_1, sum_xz)
     sum_xy, sum_yz = partial_sums(right_1[:2], (), (total_1, 0), True, 320, "late_2", ready=ready)
-    got["xy"], got["yz"] = send(sum_xy, "far", "xy"), send(sum_yz, "far", "yz")
+    part_y, part_z = send(sum_xy, "far", "x"), send(sum_yz, "far", "y")
     total_1 = after(total_1, sum_yz)
     sum_x, sum_y = partial_sums(right_1[2:4], (), (total_1, 2 * OWN), True, 320, "late_3", ready=ready)
-    got["x"] = send(sum_x, "far", "x")
-    total_1 = after(total_1, sum_y)
+    total_1 = after(total_1, sum_y, got_xyz)
     sum_z, own = partial_sums(right_1[4:], (), (total_1, 4 * OWN), True, 320, "late_4", ready=ready)
-    got["y"] = send(after(sum_y, got["xz"]), "far", "y")
-    got["z"] = send(after(sum_z, got["xyz"]), "far", "z")
-
-    product = own
-    for part in got.values():
-        product = product + part
+    got_x = send(after(sum_x + part_x, own), "far", "x")
+    got_y = send(after(sum_y + part_y, own), "far", "y")
+    got_z = send(after(sum_z + part_z, own), "far", "z")
+
+    product = own + got_xyz + got_x + got_y + got_z
     product = product * (1.0 / (FEAT * FEAT))
     classes = jnp.arange(CLASSES, dtype=jnp.int32)
     targets = (labels[:, None] == classes[None, :]).astype(f32) - 1.0 / CLASSES

time: 114 us -> 108 us (0.947)
  starting transfers between devices: 44.2 us -> 41.1 us
  waiting for transfers between devices: 41.4 us -> 38.5 us
    ppermute x35, starting transfers between devices: 44.2 us -> 41.1 us  [send(): return lax.ppermute(value, AXES, moves(group, dims))]
    ppermute x35, waiting for transfers between devices: 41.4 us -> 38.5 us  [send(): return lax.ppermute(value, AXES, moves(group, dims))]
  transfers between devices with their start and end apart: 35 -> 35, of which waited for: 15 -> 18; matrix products, arithmetic and copies ran while one was open for 0% -> 0% of each run, Pallas kernels for 19% -> 20%
where the time goes in v4:
time: 108 us; the launch traced here: 107 us
  starting transfers between devices  41.1 us (38%)
  waiting for transfers between devices  38.5 us (36%)
  Pallas kernels  23.8 us (22%)
  local copies, waits for them, and re-layouts  2.84 us (3%)
    ppermute x35, starting transfers between devices, send(): return lax.ppermute(value, AXES, moves(group, dims))  41.1 us
    ppermute x35, waiting for transfers between devices, send(): return lax.ppermute(value, AXES, moves(group, dims))  38.5 us
    pallas_call x6, Pallas kernels, partial_sums(): pl.pallas_call(functools.partial(block_kernel, plan, n_in, None if total...  23.3 us
    unnamed x10, local copies, waits for them, and re-layouts  2.84 us
  transfers between devices with their start and end apart: 35, of which 18 were waited for; matrix products, arithmetic and copies ran while one was open for 0% of the time, Pallas kernels for 20%

profile of v4, /device:TPU:0, one launch (start us, length us, event | category | flops | bytes accessed | tf_op | source)
XLA Modules:
  0.0 107.5 jit_solution(14375962039252060814)
XLA Ops:
  0.0 0.9 copy-done
  1.0 2.1 %collective-permute-start.4 = (bf16[160,768]{1,0:T(8,128)(2,1)S(1)}, bf16[160,768]{1,0:T(8,128)(2,1)S(1)}, u32[]{:S(2)}, u32[]{:S(2)}) collective-permute-start(bf16[160,768]{1,0:T(8,128)(2,1)S(1)} %split_coefs.1.refs_6_), channel_id=1, source_target_pairs={{0,2},{1,3},{2,0},{3,1},{4,6},{5,7},{6,4},{7,5},{8,10},{9,11},{10,... | collective-permute-start | bytes 737288 | tf_op jit(solution)/shard_map/ppermute | solution.py:48
  3.1 1.5 %collective-permute-start.1 = (bf16[160,768]{1,0:T(8,128)(2,1)}, bf16[160,768]{1,0:T(8,128)(2,1)S(1)}, u32[]{:S(2)}, u32[]{:S(2)}) collective-permute-start(bf16[160,768]{1,0:T(8,128)(2,1)} %refs_0_), channel_id=1, source_target_pairs={{0,16},{1,17},{2,18},{3,19},{4,20},{5,21},{6,22},{7,23},{8,24},{9,... | collective-permute-start | bytes 737288 | tf_op jit(solution)/shard_map/ppermute | solution.py:48
  4.6 2.1 %collective-permute-start = (bf16[160,768]{1,0:T(8,128)(2,1)}, bf16[160,768]{1,0:T(8,128)(2,1)S(1)}, u32[]{:S(2)}, u32[]{:S(2)}) collective-permute-start(bf16[160,768]{1,0:T(8,128)(2,1)} %refs_0_), channel_id=1, source_target_pairs={{0,48},{1,49},{2,50},{3,51},{4,52},{5,53},{6,54},{7,55},{8,56},{9,... | collective-permute-start | bytes 737288 | tf_op jit(solution)/shard_map/ppermute | solution.py:48
  6.7 1.6 %collective-permute-start.3 = (bf16[160,768]{1,0:T(8,128)(2,1)}, bf16[160,768]{1,0:T(8,128)(2,1)S(1)}, u32[]{:S(2)}, u32[]{:S(2)}) collective-permute-start(bf16[160,768]{1,0:T(8,128)(2,1)} %refs_1_), channel_id=1, source_target_pairs={{0,4},{1,5},{2,6},{3,7},{4,0},{5,1},{6,2},{7,3},{8,12},{9,13},{10,... | collective-permute-start | bytes 737288 | tf_op jit(solution)/shard_map/ppermute | solution.py:48
  8.2 2.2 %collective-permute-start.2 = (bf16[160,768]{1,0:T(8,128)(2,1)}, bf16[160,768]{1,0:T(8,128)(2,1)S(1)}, u32[]{:S(2)}, u32[]{:S(2)}) collective-permute-start(bf16[160,768]{1,0:T(8,128)(2,1)} %refs_1_), channel_id=1, source_target_pairs={{0,12},{1,13},{2,14},{3,15},{4,8},{5,9},{6,10},{7,11},{8,4},{9,5},... | collective-permute-start | bytes 737288 | tf_op jit(solution)/shard_map/ppermute | solution.py:48
  10.4 0.9 copy-done.2
  11.4 0.9 copy-done.3
  12.4 0.8 collective-permute-done.refs_1_
  13.1 0.6 collective-permute-done.3.refs_5_
  13.7 2.5 %collective-permute-done.2.refs_4_ = bf16[160,768]{1,0:T(8,128)(2,1)S(1)} collective-permute-done((bf16[160,768]{1,0:T(8,128)(2,1)}, bf16[160,768]{1,0:T(8,128)(2,1)S(1)}, u32[]{:S(2)}, u32[]{:S(2)}) %collective-permute-start.2) | collective-permute-done | bytes 245792 | tf_op jit(solution)/shard_map/ppermute | solution.py:48
  16.2 0.3 pairs.1
  16.5 0.1 collective-permute-start.9
  16.6 0.1 collective-permute-start.6
  16.7 0.5 collective-permute-start.8
  17.1 2.2 %collective-permute-start.5 = (bf16[320,768]{1,0:T(8,128)(2,1)S(1)}, bf16[320,768]{1,0:T(8,128)(2,1)S(1)}, u32[]{:S(2)}, u32[]{:S(2)}) collective-permute-start(bf16[320,768]{1,0:T(8,128)(2,1)S(1)} %get-tuple-element.75.refs_0_.refs_4_.refs_2_), channel_id=1, source_target_pairs={{0,12},{1,13},{2,14},{3,15},{4,8},{5,9},{6,10},{7,11},{8,4},{9,5},... | collective-permute-start | bytes 1474568 | tf_op jit(solution)/shard_map/ppermute | solution.py:48
  19.3 3.8 %collective-permute-start.7 = (bf16[320,768]{1,0:T(8,128)(2,1)S(1)}, bf16[320,768]{1,0:T(8,128)(2,1)S(1)}, u32[]{:S(2)}, u32[]{:S(2)}) collective-permute-start(bf16[320,768]{1,0:T(8,128)(2,1)S(1)} %get-tuple-element.89.refs_5_.refs_3_), channel_id=1, source_target_pairs={{0,66},{1,67},{2,64},{3,65},{4,70},{5,71},{6,68},{7,69},{8,74},{9,... | collective-permute-start | bytes 1474568 | tf_op jit(solution)/shard_map/ppermute | solution.py:48
  23.1 0.6 collective-permute-start.10
  23.7 6.5 %collective-permute-done.6.refs_3_.refs_11_.refs_7_.refs_2_ = bf16[320,768]{1,0:T(8,128)(2,1)S(1)} collective-permute-done((bf16[320,768]{1,0:T(8,128)(2,1)S(1)}, bf16[320,768]{1,0:T(8,128)(2,1)S(1)}, u32[]{:S(2)}, u32[]{:S(2)}) %collective-permute-start.6) | collective-permute-done | bytes 491552 | tf_op jit(solution)/shard_map/ppermute | solution.py:48
  30.2 1.3 %collective-permute-done.5.refs_1_.refs_0_.refs_2_ = bf16[320,768]{1,0:T(8,128)(2,1)S(1)} collective-permute-done((bf16[320,768]{1,0:T(8,128)(2,1)S(1)}, bf16[320,768]{1,0:T(8,128)(2,1)S(1)}, u32[]{:S(2)}, u32[]{:S(2)}) %collective-permute-start.5) | collective-permute-done | bytes 491552 | tf_op jit(solution)/shard_map/ppermute | solution.py:48
  31.5 2.7 %collective-permute-done.7.refs_3_.refs_1_ = bf16[320,768]{1,0:T(8,128)(2,1)S(1)} collective-permute-done((bf16[320,768]{1,0:T(8,128)(2,1)S(1)}, bf16[320,768]{1,0:T(8,128)(2,1)S(1)}, u32[]{:S(2)}, u32[]{:S(2)}) %collective-permute-start.7) | collective-permute-done | bytes 491552 | tf_op jit(solution)/shard_map/ppermute | solution.py:48
  34.2 1.5 %collective-permute-done.10.refs_5_.refs_10_.refs_6_.refs_7_ = bf16[320,768]{1,0:T(8,128)(2,1)S(1)} collective-permute-done((bf16[320,768]{1,0:T(8,128)(2,1)S(1)}, bf16[320,768]{1,0:T(8,128)(2,1)S(1)}, u32[]{:S(2)}, u32[]{:S(2)}) %collective-permute-start.10) | collective-permute-done | bytes 491552 | tf_op jit(solution)/shard_map/ppermute | solution.py:48
  35.7 0.2 turn.1
  35.9 0.1 collective-permute-start.15
  36.0 0.7 collective-permute-start.14
  36.7 0.9 collective-permute-start.13
  37.6 1.5 %collective-permute-start.11 = (bf16[320,768]{1,0:T(8,128)(2,1)S(1)}, bf16[320,768]{1,0:T(8,128)(2,1)S(1)}, u32[]{:S(2)}, u32[]{:S(2)}) collective-permute-start(bf16[320,768]{1,0:T(8,128)(2,1)S(1)} %get-tuple-element.86), channel_id=1, source_target_pairs={{0,66},{1,67},{2,64},{3,65},{4,70},{5,71},{6,68},{7,69},{8,74},{9,... | collective-permute-start | bytes 1474568 | tf_op jit(solution)/shard_map/ppermute | solution.py:48
  39.1 0.2 collective-permute-done.15.refs_17_.refs_13_.refs_8_
  39.3 1.2 %collective-permute-start.16 = (bf16[320,768]{1,0:T(8,128)(2,1)S(1)}, bf16[320,768]{1,0:T(8,128)(2,1)S(1)}, u32[]{:S(2)}, u32[]{:S(2)}) collective-permute-start(bf16[320,768]{1,0:T(8,128)(2,1)S(1)} %get-tuple-element.92.refs_8_.refs_4_), channel_id=1, source_target_pairs={{0,4},{1,5},{2,6},{3,7},{4,0},{5,1},{6,2},{7,3},{8,12},{9,13},{10,... | collective-permute-start | bytes 1474568 | tf_op jit(solution)/shard_map/ppermute | solution.py:48
  40.4 9.2 %collective-permute-done.14.refs_9_.refs_5_.refs_3_ = bf16[320,768]{1,0:T(8,128)(2,1)S(1)} collective-permute-done((bf16[320,768]{1,0:T(8,128)(2,1)S(1)}, bf16[320,768]{1,0:T(8,128)(2,1)S(1)}, u32[]{:S(2)}, u32[]{:S(2)}) %collective-permute-start.14) | collective-permute-done | bytes 491552 | tf_op jit(solution)/shard_map/ppermute | solution.py:48
  49.7 1.5 %collective-permute-done.13.refs_1_ = bf16[320,768]{1,0:T(8,128)(2,1)S(1)} collective-permute-done((bf16[320,768]{1,0:T(8,128)(2,1)S(1)}, bf16[320,768]{1,0:T(8,128)(2,1)S(1)}, u32[]{:S(2)}, u32[]{:S(2)}) %collective-permute-start.13) | collective-permute-done | bytes 491552 | tf_op jit(solution)/shard_map/ppermute | solution.py:48
  51.2 0.6 collective-permute-done.11.refs_2_.refs_0_
  51.8 0.7 collective-permute-done.16.refs_12_.refs_8_
  52.6 0.5 collective-permute-start.19
  53.1 0.0 collective-permute-start.18
  53.1 1.0 collective-permute-start.23
  54.1 1.1 %collective-permute-start.24 = (bf16[320,768]{1,0:T(8,128)(2,1)S(1)}, bf16[320,768]{1,0:T(8,128)(2,1)S(1)}, u32[]{:S(2)}, u32[]{:S(2)}) collective-permute-start(bf16[320,768]{1,0:T(8,128)(2,1)S(1)} %collective-permute-done.8.refs_4_.refs_14_.refs_10_), channel_id=1, source_target_pairs={{0,16},{1,17},{2,18},{3,19},{4,20},{5,21},{6,22},{7,23},{8,24},{9,... | collective-permute-start | bytes 1474568 | tf_op jit(solution)/shard_map/ppermute | solution.py:48
  55.2 0.7 collective-permute-done.18.refs_16_.refs_12_.refs_9_
  55.8 1.5 %collective-permute-start.20 = (bf16[320,768]{1,0:T(8,128)(2,1)S(1)}, bf16[320,768]{1,0:T(8,128)(2,1)S(1)}, u32[]{:S(2)}, u32[]{:S(2)}) collective-permute-start(bf16[320,768]{1,0:T(8,128)(2,1)S(1)} %get-tuple-element.101), channel_id=1, source_target_pairs={{0,66},{1,67},{2,64},{3,65},{4,70},{5,71},{6,68},{7,69},{8,74},{9,... | collective-permute-start | bytes 1474568 | tf_op jit(solution)/shard_map/ppermute | solution.py:48
  57.3 1.9 %collective-permute-start.21 = (bf16[320,768]{1,0:T(8,128)(2,1)S(1)}, bf16[320,768]{1,0:T(8,128)(2,1)S(1)}, u32[]{:S(2)}, u32[]{:S(2)}) collective-permute-start(bf16[320,768]{1,0:T(8,128)(2,1)S(1)} %collective-permute-done.7.refs_3_.refs_1_), channel_id=1, source_target_pairs={{0,48},{1,49},{2,50},{3,51},{4,52},{5,53},{6,54},{7,55},{8,56},{9,... | collective-permute-start | bytes 1474568 | tf_op jit(solution)/shard_map/ppermute | solution.py:48
  59.2 1.2 %collective-permute-start.22 = (bf16[320,768]{1,0:T(8,128)(2,1)S(1)}, bf16[320,768]{1,0:T(8,128)(2,1)S(1)}, u32[]{:S(2)}, u32[]{:S(2)}) collective-permute-start(bf16[320,768]{1,0:T(8,128)(2,1)S(1)} %collective-permute-done.10.refs_5_.refs_10_.refs_6_.refs_7_), channel_id=1, source_target_pairs={{0,4},{1,5},{2,6},{3,7},{4,0},{5,1},{6,2},{7,3},{8,12},{9,13},{10,... | collective-permute-start | bytes 1474568 | tf_op jit(solution)/shard_map/ppermute | solution.py:48
  60.3 10.4 %early.1.refs_6_ = f32[960,384]{1,0:T(8,128)S(1)} custom-call(bf16[320,768]{1,0:T(8,128)(2,1)S(1)} %collective-permute-done.5.refs_1_.refs_0_.refs_2_, bf16[320,768]{1,0:T(8,128)(2,1)S(1)} %collective-permute-done.13.refs_1_, bf16[320,768]{1,0:T(8,128)(2,1)S(1)} %collective-permute-done.11.refs_2_.refs_0_, ...), custom_call_target="tpu_custom_call" | custom-call | flops 8294400000 | bytes 8000000 | tf_op jit(solution)/shard_map/early/pallas_call | solution.py:187
  70.8 0.1 collective-permute-start.26
  70.9 0.5 collective-permute-start.27
  71.4 0.5 collective-permute-done.22.refs_4_
  71.9 3.8 %late_right.1.refs_13_ = f32[320,384]{1,0:T(8,128)S(1)} custom-call(bf16[320,768]{1,0:T(8,128)(2,1)S(1)} %collective-permute-done.20.refs_0_, bf16[320,768]{1,0:T(8,128)(2,1)S(1)} %collective-permute-done.21.refs_1_, bf16[320,768]{1,0:T(8,128)(2,1)S(1)} %get-tuple-element.76.refs_2_.refs_6_, bf16[320,768]{1,0:T(8,128)(2,1)S(1)} %get-tuple-element.90.refs_7_.refs_3_, ...), custom_call_target="tpu_custom_call" | custom-call | flops 2764800000 | bytes 8000000 | tf_op jit(solution)/shard_map/late_right/pallas_call | solution.py:187
  75.7 2.3 %late_1.1 = (f32[160,345]{1,0:T(8,128)S(1)}, f32[160,345]{1,0:T(8,128)S(1)}, bf16[960,1536]{1,0:T(8,128)(2,1)S(1)}, bf16[960,768]{1,0:T(8,128)(2,1)S(1)}) custom-call(bf16[320,768]{1,0:T(8,128)(2,1)S(1)} %collective-permute-done.20.refs_0_, bf16[320,768]{1,0:T(8,128)(2,1)S(1)} %collective-permute-done.21.refs_1_, ...), custom_call_target="tpu_custom_call" | custom-call | flops 1658880000 | bytes 8000000 | tf_op jit(solution)/shard_map/late_1/pallas_call | solution.py:187
  78.0 1.6 %collective-permute-start.29 = (f32[160,345]{1,0:T(8,128)S(1)}, f32[160,345]{1,0:T(8,128)S(1)}, u32[]{:S(2)}, u32[]{:S(2)}) collective-permute-start(f32[160,345]{1,0:T(8,128)S(1)} %get-tuple-element.113), channel_id=1, source_target_pairs={{0,66},{1,67},{2,64},{3,65},{4,70},{5,71},{6,68},{7,69},{8,74},{9,... | collective-permute-start | bytes 662408 | tf_op jit(solution)/shard_map/ppermute | solution.py:48
  79.6 3.1 %collective-permute-start.28 = (f32[160,345]{1,0:T(8,128)S(1)}, f32[160,345]{1,0:T(8,128)S(1)}, u32[]{:S(2)}, u32[]{:S(2)}) collective-permute-start(f32[160,345]{1,0:T(8,128)S(1)} %get-tuple-element.118), channel_id=1, source_target_pairs={{0,126},{1,127},{2,124},{3,125},{4,122},{5,123},{6,120},{7,121},{8... | collective-permute-start | bytes 662408 | tf_op jit(solution)/shard_map/ppermute | solution.py:48
  82.7 2.3 %late_2.1 = (f32[160,345]{1,0:T(8,128)S(1)}, f32[160,345]{1,0:T(8,128)S(1)}) custom-call(bf16[320,768]{1,0:T(8,128)(2,1)S(1)} %collective-permute-done.5.refs_1_.refs_0_.refs_2_, bf16[320,768]{1,0:T(8,128)(2,1)S(1)} %collective-permute-done.13.refs_1_, bf16[320,768]{1,0:T(8,128)(2,1)S(1)} %collective-permute-done.11.refs_2_.refs_0_, ...), custom_call_target="tpu_custom_call" | custom-call | flops 1658880000 | bytes 8000000 | tf_op jit(solution)/shard_map/late_2/pallas_call | solution.py:187
  85.0 2.3 %collective-permute-start.33 = (f32[160,345]{1,0:T(8,128)S(1)}, f32[160,345]{1,0:T(8,128)S(1)}, u32[]{:S(2)}, u32[]{:S(2)}) collective-permute-start(f32[160,345]{1,0:T(8,128)S(1)} %get-tuple-element.115), channel_id=1, source_target_pairs={{0,12},{1,13},{2,14},{3,15},{4,8},{5,9},{6,10},{7,11},{8,4},{9,5},... | collective-permute-start | bytes 662408 | tf_op jit(solution)/shard_map/ppermute | solution.py:48
  87.2 1.8 %collective-permute-start.31 = (f32[160,345]{1,0:T(8,128)S(1)}, f32[160,345]{1,0:T(8,128)S(1)}, u32[]{:S(2)}, u32[]{:S(2)}) collective-permute-start(f32[160,345]{1,0:T(8,128)S(1)} %get-tuple-element.123), channel_id=1, source_target_pairs={{0,48},{1,49},{2,50},{3,51},{4,52},{5,53},{6,54},{7,55},{8,56},{9,... | collective-permute-start | bytes 662408 | tf_op jit(solution)/shard_map/ppermute | solution.py:48
  89.0 2.3 %late_3.1 = (f32[160,345]{1,0:T(8,128)S(1)}, f32[160,345]{1,0:T(8,128)S(1)}) custom-call(bf16[320,768]{1,0:T(8,128)(2,1)S(1)} %get-tuple-element.75.refs_0_.refs_4_.refs_2_, bf16[320,768]{1,0:T(8,128)(2,1)S(1)} %collective-permute-done.13.refs_1_, bf16[320,768]{1,0:T(8,128)(2,1)S(1)} %collective-permute-done.5.refs_1_.refs_0_.refs_2_, ...), custom_call_target="tpu_custom_call" | custom-call | flops 1658880000 | bytes 8000000 | tf_op jit(solution)/shard_map/late_3/pallas_call | solution.py:187
  91.3 2.5 %collective-permute-done.28 = f32[160,345]{1,0:T(8,128)S(1)} collective-permute-done((f32[160,345]{1,0:T(8,128)S(1)}, f32[160,345]{1,0:T(8,128)S(1)}, u32[]{:S(2)}, u32[]{:S(2)}) %collective-permute-start.28) | collective-permute-done | bytes 220832 | tf_op jit(solution)/shard_map/ppermute | solution.py:48
  93.8 2.3 %late_4.1 = (f32[160,345]{1,0:T(8,128)S(1)}, f32[160,345]{1,0:T(8,128)S(1)}) custom-call(bf16[320,768]{1,0:T(8,128)(2,1)S(1)} %collective-permute-done.11.refs_2_.refs_0_, bf16[320,768]{1,0:T(8,128)(2,1)S(1)} %collective-permute-done.7.refs_3_.refs_1_, bf16[320,768]{1,0:T(8,128)(2,1)S(1)} %get-tuple-element.75.refs_0_.refs_4_.refs_2_, ...), custom_call_target="tpu_custom_call" | custom-call | flops 1658880000 | bytes 8000000 | tf_op jit(solution)/shard_map/late_4/pallas_call | solution.py:187
  96.1 0.0 copy-start.1
  96.1 0.0 copy-start.4
  96.1 1.5 %collective-permute-start.30 = (f32[160,345]{1,0:T(8,128)S(1)}, f32[160,345]{1,0:T(8,128)S(1)}, u32[]{:S(2)}, u32[]{:S(2)}) collective-permute-start(f32[160,345]{1,0:T(8,128)S(1)} %add.26), channel_id=1, source_target_pairs={{0,48},{1,49},{2,50},{3,51},{4,52},{5,53},{6,54},{7,55},{8,56},{9,... | collective-permute-start | bytes 662408 | tf_op jit(solution)/shard_map/ppermute | solution.py:48
  97.6 0.8 collective-permute-start.32
  98.4 1.6 %collective-permute-start.34 = (f32[160,345]{1,0:T(8,128)S(1)}, f32[160,345]{1,0:T(8,128)S(1)}, u32[]{:S(2)}, u32[]{:S(2)}) collective-permute-start(f32[160,345]{1,0:T(8,128)S(1)} %add.30), channel_id=1, source_target_pairs={{0,66},{1,67},{2,64},{3,65},{4,70},{5,71},{6,68},{7,69},{8,74},{9,... | collective-permute-start | bytes 662408 | tf_op jit(solution)/shard_map/ppermute | solution.py:48
  100.0 3.9 %collective-permute-done.30 = f32[160,345]{1,0:T(8,128)S(1)} collective-permute-done((f32[160,345]{1,0:T(8,128)S(1)}, f32[160,345]{1,0:T(8,128)S(1)}, u32[]{:S(2)}, u32[]{:S(2)}) %collective-permute-start.30) | collective-permute-done | bytes 220832 | tf_op jit(solution)/shard_map/ppermute | solution.py:48
  104.0 1.5 %collective-permute-done.32 = f32[160,345]{1,0:T(8,128)S(1)} collective-permute-done((f32[160,345]{1,0:T(8,128)S(1)}, f32[160,345]{1,0:T(8,128)S(1)}, u32[]{:S(2)}, u32[]{:S(2)}) %collective-permute-start.32) | collective-permute-done | bytes 220832 | tf_op jit(solution)/shard_map/ppermute | solution.py:48
  105.4 1.2 %collective-permute-done.34 = f32[160,345]{1,0:T(8,128)S(1)} collective-permute-done((f32[160,345]{1,0:T(8,128)S(1)}, f32[160,345]{1,0:T(8,128)S(1)}, u32[]{:S(2)}, u32[]{:S(2)}) %collective-permute-start.34) | collective-permute-done | bytes 220832 | tf_op jit(solution)/shard_map/ppermute | solution.py:48
  106.6 0.8 add_bitcast_fusion
  (30 shorter events, 0.2 us)
Async XLA Ops:
  0.0 0.9 copy-start
  1.0 11.4 %collective-permute-start.4 = (bf16[160,768]{1,0:T(8,128)(2,1)S(1)}, bf16[160,768]{1,0:T(8,128)(2,1)S(1)}, u32[]{:S(2)}, u32[]{:S(2)}) collective-permute-start(bf16[160,768]{1,0:T(8,128)(2,1)S(1)} %split_coefs.1.refs_6_), channel_id=1, source_target_pairs={{0,2},{1,3},{2,0},{3,1},{4,6},{5,7},{6,4},{7,5},{8,10},{9,11},{10,... | collective-permute-start | bytes 737288 | tf_op jit(solution)/shard_map/ppermute | solution.py:48
  3.1 9.3 %collective-permute-start.1 = (bf16[160,768]{1,0:T(8,128)(2,1)}, bf16[160,768]{1,0:T(8,128)(2,1)S(1)}, u32[]{:S(2)}, u32[]{:S(2)}) collective-permute-start(bf16[160,768]{1,0:T(8,128)(2,1)} %refs_0_), channel_id=1, source_target_pairs={{0,16},{1,17},{2,18},{3,19},{4,20},{5,21},{6,22},{7,23},{8,24},{9,... | collective-permute-start | bytes 737288 | tf_op jit(solution)/shard_map/ppermute | solution.py:48
  4.6 8.6 %collective-permute-start = (bf16[160,768]{1,0:T(8,128)(2,1)}, bf16[160,768]{1,0:T(8,128)(2,1)S(1)}, u32[]{:S(2)}, u32[]{:S(2)}) collective-permute-start(bf16[160,768]{1,0:T(8,128)(2,1)} %refs_0_), channel_id=1, source_target_pairs={{0,48},{1,49},{2,50},{3,51},{4,52},{5,53},{6,54},{7,55},{8,56},{9,... | collective-permute-start | bytes 737288 | tf_op jit(solution)/shard_map/ppermute | solution.py:48
  6.7 7.1 %collective-permute-start.3 = (bf16[160,768]{1,0:T(8,128)(2,1)}, bf16[160,768]{1,0:T(8,128)(2,1)S(1)}, u32[]{:S(2)}, u32[]{:S(2)}) collective-permute-start(bf16[160,768]{1,0:T(8,128)(2,1)} %refs_1_), channel_id=1, source_target_pairs={{0,4},{1,5},{2,6},{3,7},{4,0},{5,1},{6,2},{7,3},{8,12},{9,13},{10,... | collective-permute-start | bytes 737288 | tf_op jit(solution)/shard_map/ppermute | solution.py:48
  8.2 8.0 %collective-permute-start.2 = (bf16[160,768]{1,0:T(8,128)(2,1)}, bf16[160,768]{1,0:T(8,128)(2,1)S(1)}, u32[]{:S(2)}, u32[]{:S(2)}) collective-permute-start(bf16[160,768]{1,0:T(8,128)(2,1)} %refs_1_), channel_id=1, source_target_pairs={{0,12},{1,13},{2,14},{3,15},{4,8},{5,9},{6,10},{7,11},{8,4},{9,5},... | collective-permute-start | bytes 737288 | tf_op jit(solution)/shard_map/ppermute | solution.py:48
  10.4 0.9 copy-start.2
  11.4 0.9 copy-start.3
  16.5 6.6 %collective-permute-start.9 = (bf16[320,2304]{1,0:T(8,128)(2,1)S(1)}, bf16[320,2304]{1,0:T(8,128)(2,1)S(1)}, u32[]{:S(2)}, u32[]{:S(2)}) collective-permute-start(bf16[320,2304]{1,0:T(8,128)(2,1)S(1)} %get-tuple-element.80), channel_id=1, source_target_pairs={{0,1},{1,0},{2,3},{3,2},{4,5},{5,4},{6,7},{7,6},{8,9},{9,8},{10,11... | collective-permute-start | bytes 4423688 | tf_op jit(solution)/shard_map/ppermute | solution.py:48
  16.6 13.6 %collective-permute-start.6 = (bf16[320,768]{1,0:T(8,128)(2,1)S(1)}, bf16[320,768]{1,0:T(8,128)(2,1)S(1)}, u32[]{:S(2)}, u32[]{:S(2)}) collective-permute-start(bf16[320,768]{1,0:T(8,128)(2,1)S(1)} %get-tuple-element.76.refs_2_.refs_6_), channel_id=1, source_target_pairs={{0,4},{1,5},{2,6},{3,7},{4,0},{5,1},{6,2},{7,3},{8,12},{9,13},{10,... | collective-permute-start | bytes 1474568 | tf_op jit(solution)/shard_map/ppermute | solution.py:48
  16.7 13.5 %collective-permute-start.8 = (bf16[320,768]{1,0:T(8,128)(2,1)S(1)}, bf16[320,768]{1,0:T(8,128)(2,1)S(1)}, u32[]{:S(2)}, u32[]{:S(2)}) collective-permute-start(bf16[320,768]{1,0:T(8,128)(2,1)S(1)} %get-tuple-element.90.refs_7_.refs_3_), channel_id=1, source_target_pairs={{0,2},{1,3},{2,0},{3,1},{4,6},{5,7},{6,4},{7,5},{8,10},{9,11},{10,... | collective-permute-start | bytes 1474568 | tf_op jit(solution)/shard_map/ppermute | solution.py:48
  17.1 14.4 %collective-permute-start.5 = (bf16[320,768]{1,0:T(8,128)(2,1)S(1)}, bf16[320,768]{1,0:T(8,128)(2,1)S(1)}, u32[]{:S(2)}, u32[]{:S(2)}) collective-permute-start(bf16[320,768]{1,0:T(8,128)(2,1)S(1)} %get-tuple-element.75.refs_0_.refs_4_.refs_2_), channel_id=1, source_target_pairs={{0,12},{1,13},{2,14},{3,15},{4,8},{5,9},{6,10},{7,11},{8,4},{9,5},... | collective-permute-start | bytes 1474568 | tf_op jit(solution)/shard_map/ppermute | solution.py:48
  19.3 14.9 %collective-permute-start.7 = (bf16[320,768]{1,0:T(8,128)(2,1)S(1)}, bf16[320,768]{1,0:T(8,128)(2,1)S(1)}, u32[]{:S(2)}, u32[]{:S(2)}) collective-permute-start(bf16[320,768]{1,0:T(8,128)(2,1)S(1)} %get-tuple-element.89.refs_5_.refs_3_), channel_id=1, source_target_pairs={{0,66},{1,67},{2,64},{3,65},{4,70},{5,71},{6,68},{7,69},{8,74},{9,... | collective-permute-start | bytes 1474568 | tf_op jit(solution)/shard_map/ppermute | solution.py:48
  23.1 12.6 %collective-permute-start.10 = (bf16[320,768]{1,0:T(8,128)(2,1)S(1)}, bf16[320,768]{1,0:T(8,128)(2,1)S(1)}, u32[]{:S(2)}, u32[]{:S(2)}) collective-permute-start(bf16[320,768]{1,0:T(8,128)(2,1)S(1)} %get-tuple-element.92.refs_8_.refs_4_), channel_id=1, source_target_pairs={{0,16},{1,17},{2,18},{3,19},{4,20},{5,21},{6,22},{7,23},{8,24},{9,... | collective-permute-start | bytes 1474568 | tf_op jit(solution)/shard_map/ppermute | solution.py:48
  35.9 3.3 %collective-permute-start.15 = (bf16[320,2304]{1,0:T(8,128)(2,1)S(1)}, bf16[320,2304]{1,0:T(8,128)(2,1)S(1)}, u32[]{:S(2)}, u32[]{:S(2)}) collective-permute-start(bf16[320,2304]{1,0:T(8,128)(2,1)S(1)} %get-tuple-element.91), channel_id=1, source_target_pairs={{0,1},{1,0},{2,3},{3,2},{4,5},{5,4},{6,7},{7,6},{8,9},{9,8},{10,11... | collective-permute-start | bytes 4423688 | tf_op jit(solution)/shard_map/ppermute | solution.py:48
  36.0 13.6 %collective-permute-start.14 = (bf16[320,768]{1,0:T(8,128)(2,1)S(1)}, bf16[320,768]{1,0:T(8,128)(2,1)S(1)}, u32[]{:S(2)}, u32[]{:S(2)}) collective-permute-start(bf16[320,768]{1,0:T(8,128)(2,1)S(1)} %get-tuple-element.90.refs_7_.refs_3_), channel_id=1, source_target_pairs={{0,16},{1,17},{2,18},{3,19},{4,20},{5,21},{6,22},{7,23},{8,24},{9,... | collective-permute-start | bytes 1474568 | tf_op jit(solution)/shard_map/ppermute | solution.py:48
  36.7 14.5 %collective-permute-start.13 = (bf16[320,768]{1,0:T(8,128)(2,1)S(1)}, bf16[320,768]{1,0:T(8,128)(2,1)S(1)}, u32[]{:S(2)}, u32[]{:S(2)}) collective-permute-start(bf16[320,768]{1,0:T(8,128)(2,1)S(1)} %get-tuple-element.89.refs_5_.refs_3_), channel_id=1, source_target_pairs={{0,48},{1,49},{2,50},{3,51},{4,52},{5,53},{6,54},{7,55},{8,56},{9,... | collective-permute-start | bytes 1474568 | tf_op jit(solution)/shard_map/ppermute | solution.py:48
  37.6 14.2 %collective-permute-start.11 = (bf16[320,768]{1,0:T(8,128)(2,1)S(1)}, bf16[320,768]{1,0:T(8,128)(2,1)S(1)}, u32[]{:S(2)}, u32[]{:S(2)}) collective-permute-start(bf16[320,768]{1,0:T(8,128)(2,1)S(1)} %get-tuple-element.86), channel_id=1, source_target_pairs={{0,66},{1,67},{2,64},{3,65},{4,70},{5,71},{6,68},{7,69},{8,74},{9,... | collective-permute-start | bytes 1474568 | tf_op jit(solution)/shard_map/ppermute | solution.py:48
  39.1 12.7 %collective-permute-start.12 = (bf16[320,768]{1,0:T(8,128)(2,1)S(1)}, bf16[320,768]{1,0:T(8,128)(2,1)S(1)}, u32[]{:S(2)}, u32[]{:S(2)}) collective-permute-start(bf16[320,768]{1,0:T(8,128)(2,1)S(1)} %get-tuple-element.87), channel_id=1, source_target_pairs={{0,2},{1,3},{2,0},{3,1},{4,6},{5,7},{6,4},{7,5},{8,10},{9,11},{10,... | collective-permute-start | bytes 1474568 | tf_op jit(solution)/shard_map/ppermute | solution.py:48
  39.3 13.3 %collective-permute-start.16 = (bf16[320,768]{1,0:T(8,128)(2,1)S(1)}, bf16[320,768]{1,0:T(8,128)(2,1)S(1)}, u32[]{:S(2)}, u32[]{:S(2)}) collective-permute-start(bf16[320,768]{1,0:T(8,128)(2,1)S(1)} %get-tuple-element.92.refs_8_.refs_4_), channel_id=1, source_target_pairs={{0,4},{1,5},{2,6},{3,7},{4,0},{5,1},{6,2},{7,3},{8,12},{9,13},{10,... | collective-permute-start | bytes 1474568 | tf_op jit(solution)/shard_map/ppermute | solution.py:48
  52.5 2.6 %collective-permute-start.17 = (bf16[320,768]{1,0:T(8,128)(2,1)S(1)}, bf16[320,768]{1,0:T(8,128)(2,1)S(1)}, u32[]{:S(2)}, u32[]{:S(2)}) collective-permute-start(bf16[320,768]{1,0:T(8,128)(2,1)S(1)} %collective-permute-done.12.refs_13_.refs_9_), channel_id=1, source_target_pairs={{0,1},{1,0},{2,3},{3,2},{4,5},{5,4},{6,7},{7,6},{8,9},{9,8},{10,11... | collective-permute-start | bytes 1474568 | tf_op jit(solution)/shard_map/ppermute | solution.py:48
  52.6 2.6 %collective-permute-start.19 = (bf16[320,768]{1,0:T(8,128)(2,1)S(1)}, bf16[320,768]{1,0:T(8,128)(2,1)S(1)}, u32[]{:S(2)}, u32[]{:S(2)}) collective-permute-start(bf16[320,768]{1,0:T(8,128)(2,1)S(1)} %collective-permute-done.16.refs_12_.refs_8_), channel_id=1, source_target_pairs={{0,1},{1,0},{2,3},{3,2},{4,5},{5,4},{6,7},{7,6},{8,9},{9,8},{10,11... | collective-permute-start | bytes 1474568 | tf_op jit(solution)/shard_map/ppermute | solution.py:48
  53.1 2.8 %collective-permute-start.18 = (bf16[320,768]{1,0:T(8,128)(2,1)S(1)}, bf16[320,768]{1,0:T(8,128)(2,1)S(1)}, u32[]{:S(2)}, u32[]{:S(2)}) collective-permute-start(bf16[320,768]{1,0:T(8,128)(2,1)S(1)} %collective-permute-done.14.refs_9_.refs_5_.refs_3_), channel_id=1, source_target_pairs={{0,1},{1,0},{2,3},{3,2},{4,5},{5,4},{6,7},{7,6},{8,9},{9,8},{10,11... | collective-permute-start | bytes 1474568 | tf_op jit(solution)/shard_map/ppermute | solution.py:48
  53.1 17.7 %collective-permute-start.23 = (bf16[320,768]{1,0:T(8,128)(2,1)S(1)}, bf16[320,768]{1,0:T(8,128)(2,1)S(1)}, u32[]{:S(2)}, u32[]{:S(2)}) collective-permute-start(bf16[320,768]{1,0:T(8,128)(2,1)S(1)} %get-tuple-element.105), channel_id=1, source_target_pairs={{0,2},{1,3},{2,0},{3,1},{4,6},{5,7},{6,4},{7,5},{8,10},{9,11},{10,... | collective-permute-start | bytes 1474568 | tf_op jit(solution)/shard_map/ppermute | solution.py:48
  54.1 16.7 %collective-permute-start.24 = (bf16[320,768]{1,0:T(8,128)(2,1)S(1)}, bf16[320,768]{1,0:T(8,128)(2,1)S(1)}, u32[]{:S(2)}, u32[]{:S(2)}) collective-permute-start(bf16[320,768]{1,0:T(8,128)(2,1)S(1)} %collective-permute-done.8.refs_4_.refs_14_.refs_10_), channel_id=1, source_target_pairs={{0,16},{1,17},{2,18},{3,19},{4,20},{5,21},{6,22},{7,23},{8,24},{9,... | collective-permute-start | bytes 1474568 | tf_op jit(solution)/shard_map/ppermute | solution.py:48
  55.8 16.1 %collective-permute-start.20 = (bf16[320,768]{1,0:T(8,128)(2,1)S(1)}, bf16[320,768]{1,0:T(8,128)(2,1)S(1)}, u32[]{:S(2)}, u32[]{:S(2)}) collective-permute-start(bf16[320,768]{1,0:T(8,128)(2,1)S(1)} %get-tuple-element.101), channel_id=1, source_target_pairs={{0,66},{1,67},{2,64},{3,65},{4,70},{5,71},{6,68},{7,69},{8,74},{9,... | collective-permute-start | bytes 1474568 | tf_op jit(solution)/shard_map/ppermute | solution.py:48
  57.3 14.6 %collective-permute-start.21 = (bf16[320,768]{1,0:T(8,128)(2,1)S(1)}, bf16[320,768]{1,0:T(8,128)(2,1)S(1)}, u32[]{:S(2)}, u32[]{:S(2)}) collective-permute-start(bf16[320,768]{1,0:T(8,128)(2,1)S(1)} %collective-permute-done.7.refs_3_.refs_1_), channel_id=1, source_target_pairs={{0,48},{1,49},{2,50},{3,51},{4,52},{5,53},{6,54},{7,55},{8,56},{9,... | collective-permute-start | bytes 1474568 | tf_op jit(solution)/shard_map/ppermute | solution.py:48
  59.2 12.7 %collective-permute-start.22 = (bf16[320,768]{1,0:T(8,128)(2,1)S(1)}, bf16[320,768]{1,0:T(8,128)(2,1)S(1)}, u32[]{:S(2)}, u32[]{:S(2)}) collective-permute-start(bf16[320,768]{1,0:T(8,128)(2,1)S(1)} %collective-permute-done.10.refs_5_.refs_10_.refs_6_.refs_7_), channel_id=1, source_target_pairs={{0,4},{1,5},{2,6},{3,7},{4,0},{5,1},{6,2},{7,3},{8,12},{9,13},{10,... | collective-permute-start | bytes 1474568 | tf_op jit(solution)/shard_map/ppermute | solution.py:48
  70.8 4.9 %collective-permute-start.26 = (bf16[320,768]{1,0:T(8,128)(2,1)S(1)}, bf16[320,768]{1,0:T(8,128)(2,1)S(1)}, u32[]{:S(2)}, u32[]{:S(2)}) collective-permute-start(bf16[320,768]{1,0:T(8,128)(2,1)S(1)} %collective-permute-done.23.refs_5_), channel_id=1, source_target_pairs={{0,1},{1,0},{2,3},{3,2},{4,5},{5,4},{6,7},{7,6},{8,9},{9,8},{10,11... | collective-permute-start | bytes 1474568 | tf_op jit(solution)/shard_map/ppermute | solution.py:48
  70.9 4.8 %collective-permute-start.27 = (bf16[320,768]{1,0:T(8,128)(2,1)S(1)}, bf16[320,768]{1,0:T(8,128)(2,1)S(1)}, u32[]{:S(2)}, u32[]{:S(2)}) collective-permute-start(bf16[320,768]{1,0:T(8,128)(2,1)S(1)} %collective-permute-done.24.refs_6_), channel_id=1, source_target_pairs={{0,1},{1,0},{2,3},{3,2},{4,5},{5,4},{6,7},{7,6},{8,9},{9,8},{10,11... | collective-permute-start | bytes 1474568 | tf_op jit(solution)/shard_map/ppermute | solution.py:48
  71.9 3.8 %collective-permute-start.25 = (bf16[320,768]{1,0:T(8,128)(2,1)S(1)}, bf16[320,768]{1,0:T(8,128)(2,1)S(1)}, u32[]{:S(2)}, u32[]{:S(2)}) collective-permute-start(bf16[320,768]{1,0:T(8,128)(2,1)S(1)} %collective-permute-done.22.refs_4_), channel_id=1, source_target_pairs={{0,1},{1,0},{2,3},{3,2},{4,5},{5,4},{6,7},{7,6},{8,9},{9,8},{10,11... | collective-permute-start | bytes 1474568 | tf_op jit(solution)/shard_map/ppermute | solution.py:48
  78.0 15.8 %collective-permute-start.29 = (f32[160,345]{1,0:T(8,128)S(1)}, f32[160,345]{1,0:T(8,128)S(1)}, u32[]{:S(2)}, u32[]{:S(2)}) collective-permute-start(f32[160,345]{1,0:T(8,128)S(1)} %get-tuple-element.113), channel_id=1, source_target_pairs={{0,66},{1,67},{2,64},{3,65},{4,70},{5,71},{6,68},{7,69},{8,74},{9,... | collective-permute-start | bytes 662408 | tf_op jit(solution)/shard_map/ppermute | solution.py:48
  79.6 14.2 %collective-permute-start.28 = (f32[160,345]{1,0:T(8,128)S(1)}, f32[160,345]{1,0:T(8,128)S(1)}, u32[]{:S(2)}, u32[]{:S(2)}) collective-permute-start(f32[160,345]{1,0:T(8,128)S(1)} %get-tuple-element.118), channel_id=1, source_target_pairs={{0,126},{1,127},{2,124},{3,125},{4,122},{5,123},{6,120},{7,121},{8... | collective-permute-start | bytes 662408 | tf_op jit(solution)/shard_map/ppermute | solution.py:48
  85.0 13.4 %collective-permute-start.33 = (f32[160,345]{1,0:T(8,128)S(1)}, f32[160,345]{1,0:T(8,128)S(1)}, u32[]{:S(2)}, u32[]{:S(2)}) collective-permute-start(f32[160,345]{1,0:T(8,128)S(1)} %get-tuple-element.115), channel_id=1, source_target_pairs={{0,12},{1,13},{2,14},{3,15},{4,8},{5,9},{6,10},{7,11},{8,4},{9,5},... | collective-permute-start | bytes 662408 | tf_op jit(solution)/shard_map/ppermute | solution.py:48
  87.2 10.3 %collective-permute-start.31 = (f32[160,345]{1,0:T(8,128)S(1)}, f32[160,345]{1,0:T(8,128)S(1)}, u32[]{:S(2)}, u32[]{:S(2)}) collective-permute-start(f32[160,345]{1,0:T(8,128)S(1)} %get-tuple-element.123), channel_id=1, source_target_pairs={{0,48},{1,49},{2,50},{3,51},{4,52},{5,53},{6,54},{7,55},{8,56},{9,... | collective-permute-start | bytes 662408 | tf_op jit(solution)/shard_map/ppermute | solution.py:48
  96.1 10.5 %copy-start.1 = (f32[345,160]{0,1:T(8,128)S(1)}, f32[345,160]{0,1:T(8,128)}, u32[]{:S(2)}) copy-start(f32[345,160]{0,1:T(8,128)} %param.7) | copy-start | bytes 662404
  96.1 10.5 %copy-start.4 = (s32[160]{0:T(256)S(1)}, s32[160]{0:T(256)}, u32[]{:S(2)}) copy-start(s32[160]{0:T(256)} %param.6) | copy-start | bytes 1924
  96.1 7.8 %collective-permute-start.30 = (f32[160,345]{1,0:T(8,128)S(1)}, f32[160,345]{1,0:T(8,128)S(1)}, u32[]{:S(2)}, u32[]{:S(2)}) collective-permute-start(f32[160,345]{1,0:T(8,128)S(1)} %add.26), channel_id=1, source_target_pairs={{0,48},{1,49},{2,50},{3,51},{4,52},{5,53},{6,54},{7,55},{8,56},{9,... | collective-permute-start | bytes 662408 | tf_op jit(solution)/shard_map/ppermute | solution.py:48
  97.6 7.8 %collective-permute-start.32 = (f32[160,345]{1,0:T(8,128)S(1)}, f32[160,345]{1,0:T(8,128)S(1)}, u32[]{:S(2)}, u32[]{:S(2)}) collective-permute-start(f32[160,345]{1,0:T(8,128)S(1)} %add.28), channel_id=1, source_target_pairs={{0,12},{1,13},{2,14},{3,15},{4,8},{5,9},{6,10},{7,11},{8,4},{9,5},... | collective-permute-start | bytes 662408 | tf_op jit(solution)/shard_map/ppermute | solution.py:48
  98.4 8.2 %collective-permute-start.34 = (f32[160,345]{1,0:T(8,128)S(1)}, f32[160,345]{1,0:T(8,128)S(1)}, u32[]{:S(2)}, u32[]{:S(2)}) collective-permute-start(f32[160,345]{1,0:T(8,128)S(1)} %add.30), channel_id=1, source_target_pairs={{0,66},{1,67},{2,64},{3,65},{4,70},{5,71},{6,68},{7,69},{8,74},{9,... | collective-permute-start | bytes 662408 | tf_op jit(solution)/shard_map/ppermute | solution.py:48

commit v5 on v4

v5 whole, which is shorter than its diff:
```python
import functools

import jax
import jax.numpy as jnp
from jax import lax
from jax.experimental import pallas as pl
from jax.experimental.pallas import tpu as pltpu
from jax.sharding import PartitionSpec as P

FEAT = 768
CLASSES = 345
LANES = 384
OWN = 160
AXES = ("row", "col")

damping = 0.8
ridge = 0.1

f32, bf16 = jnp.float32, jnp.bfloat16
NT = (((1,), (1,)), ((), ()))
NN = (((1,), (0,)), ((), ()))
VMEM = pl.BlockSpec(memory_space=pltpu.VMEM)


def encode(x, y, z, core):
    return ((((z >> 1) * 4 + x) * 4 + y) * 2 + (z & 1)) * 2 + core


def decode(index):
    return (index >> 4) & 3, (index >> 2) & 3, (index >> 6) * 2 + ((index >> 1) & 1), index & 1


def moves(group, dims):
    pairs = []
    for index in range(128):
        x, y, z, core = decode(index)
        place = {"x": x, "y": y, "z": z}
        for dim in dims:
            if dim == "c":
                core ^= 1
            else:
                place[dim] = 3 - place[dim] if group == "far" else place[dim] ^ 1
        pairs.append((index, encode(place["x"], place["y"], place["z"], core)))
    return pairs


def send(value, group, dims):
    return lax.ppermute(value, AXES, moves(group, dims))


def after(value, *others):
    return lax.optimization_barrier((value, *others))[0]


def dot(a, b, dims):
    return lax.dot_general(a, b, dims, preferred_element_type=f32)


def split_kernel(coef, split):
    split[...] = jnp.zeros_like(split)
    values = coef[...]
    high = values.astype(bf16)
    split[:, :CLASSES] = high
    split[:, LANES : LANES + CLASSES] = (values - high.astype(f32)).astype(bf16)


def split_coefs(coefs):
    return pl.pallas_call(
        split_kernel,
        out_shape=pltpu.VMEM((OWN, 2 * LANES), bf16),
        in_specs=[VMEM],
        out_specs=VMEM,
        compiler_params=pltpu.CompilerParams(vmem_limit_bytes=4 << 20),
        name="split_coefs",
    )(coefs)


def arrange_kernel(plan, n_in, *refs):
    for out, pieces in zip(refs[n_in:], plan):
        for source, row, out_row, out_col in pieces:
            out[out_row * OWN : (out_row + 1) * OWN, out_col * FEAT : (out_col + 1) * FEAT] = refs[source][
                row * OWN : (row + 1) * OWN, :
            ]


def arrange(outputs, name):
    arrays, plan, shapes = [], [], []

    def place(array):
        for i, known in enumerate(arrays):
            if known is array:
                return i
        arrays.append(array)
        return len(arrays) - 1

    for columns in outputs:
        plan.append(
            [
                (place(array), block, out_row, out_col)
                for out_col, column in enumerate(columns)
                for out_row, (array, block) in enumerate(column)
            ]
        )
        shapes.append(pltpu.VMEM((len(columns[0]) * OWN, len(columns) * FEAT), bf16))
    return pl.pallas_call(
        functools.partial(arrange_kernel, plan, len(arrays)),
        out_shape=shapes,
        in_specs=[VMEM] * len(arrays),
        out_specs=[VMEM] * len(shapes),
        compiler_params=pltpu.CompilerParams(vmem_limit_bytes=8 << 20),
        name=name,
    )(*arrays)


def block_kernel(plan, n_in, parts, left_ready, apart, *refs):
    inputs, refs = refs[:n_in], refs[n_in:]
    if left_ready:
        (left, split), refs = refs[:2], refs[2:]
    rights, totals = [None] * len(parts), [None] * len(parts)
    for i, (ready, _, _, total_row) in enumerate(parts):
        if ready:
            rights[i], refs = refs[0], refs[1:]
        if total_row is not None:
            totals[i], refs = refs[0], refs[1:]
    n_outs = sum(part[2] for part in parts) // OWN if apart else len(parts)
    outs, refs = refs[:n_outs], refs[n_outs:]
    if not left_ready:
        (left, split), refs = refs[:2], refs[2:]
    for i, (ready, _, _, _) in enumerate(parts):
        if not ready:
            rights[i], refs = refs[0], refs[1:]
    targets = (left, split, *rights)
    for target, out_row, out_col, source, row, col in plan:
        targets[target][out_row * OWN : (out_row + 1) * OWN, out_col * FEAT : (out_col + 1) * FEAT] = inputs[source][
            row * OWN : (row + 1) * OWN, col * FEAT : (col + 1) * FEAT
        ]
    done = 0
    for i, (_, first, count, total_row) in enumerate(parts):
        right = rights[i]
        rows = 480 if count % 480 == 0 else 320
        for start in range(0, count, rows):
            n = slice(first + start, first + start + rows)
            part = None
            if total_row is not None:
                part = totals[i][total_row + start : total_row + start + rows, :]
            for at in range(0, left.shape[0], 512):
                m = slice(at, min(at + 512, left.shape[0]))
                gram_a = dot(right[n, :FEAT], left[m, :FEAT], NT)
                gram_s = dot(right[n, FEAT:], left[m, FEAT:], NT)
                kernel = gram_a * gram_s
                high = kernel.astype(bf16)
                low = (kernel - high.astype(f32)).astype(bf16)
                both = dot(high, split[m, :], NN)
                new = both[:, :LANES] + both[:, LANES:] + dot(low, split[m, :LANES], NN)
                part = new if part is None else part + new
            if apart:
                for k in range(rows // OWN):
                    outs[done + k][...] = part[k * OWN : (k + 1) * OWN, :CLASSES]
                done += rows // OWN
            else:
                outs[i][start : start + rows, :] = part


def partial_sums(rights, left, apart, name):
    arrays, plan = [], []

    def place(array):
        for i, known in enumerate(arrays):
            if known is array:
                return i
        arrays.append(array)
        return len(arrays) - 1

    left_ready = isinstance(left, tuple)
    if not left_ready:
        for i, (act, sig, coef) in enumerate(left):
            plan.append((0, i, 0, place(act[0]), act[1], act[2]))
            plan.append((0, i, 1, place(sig[0]), sig[1], sig[2]))
            plan.append((1, i, 0, place(coef[0]), coef[1], coef[2]))
    for target, (blocks, *_) in enumerate(rights):
        if isinstance(blocks, list):
            for i, (act, sig) in enumerate(blocks):
                plan.append((2 + target, i, 0, place(act[0]), act[1], act[2]))
                plan.append((2 + target, i, 1, place(sig[0]), sig[1], sig[2]))
    n_in = len(arrays)
    left_rows = left[0].shape[0] if left_ready else len(left) * OWN
    if left_ready:
        arrays += left
    parts, laid = [], []
    for blocks, first, count, total, total_row in rights:
        ready = not isinstance(blocks, list)
        parts.append((ready, first, count, None if total is None else total_row))
        if ready:
            arrays.append(blocks)
        else:
            laid.append(pltpu.VMEM((len(blocks) * OWN, 2 * FEAT), bf16))
        if total is not None:
            arrays.append(total)
    if not left_ready:
        laid = [pltpu.VMEM((left_rows, 2 * FEAT), bf16), pltpu.VMEM((left_rows, 2 * LANES), bf16)] + laid
    if apart:
        sums = [pltpu.VMEM((OWN, CLASSES), f32)] * (sum(part[2] for part in parts) // OWN)
    else:
        sums = [pltpu.VMEM((part[2], LANES), f32) for part in parts]
    outs = pl.pallas_call(
        functools.partial(block_kernel, plan, n_in, parts, left_ready, apart),
        out_shape=sums + laid,
        in_specs=[VMEM] * len(arrays),
        out_specs=[VMEM] * (len(sums) + len(laid)),
        cost_estimate=pl.CostEstimate(
            flops=sum(part[2] for part in parts) * left_rows * 5400, bytes_accessed=1_000_000, transcendentals=0
        ),
        compiler_params=pltpu.CompilerParams(vmem_limit_bytes=16 << 20),
        name=name,
    )(*arrays)
    return outs[: len(sums)], outs[len(sums) :]


def shards(activations, signals, labels, coefficients):
    coefs = coefficients.T
    groups = ("far", "near")
    a, s, c = {}, {}, {}
    for g in groups:
        a[g, "x"] = send(activations, g, "x")
        s[g, "y"] = send(signals, g, "y")
    c0 = split_coefs(coefs)
    cz = send(c0, "near", "z")
    act_own, sig_own = arrange([[[(after(v, c0), 0)]] for v in (activations, signals)], "own_rows")

    def together(*values):
        return lax.optimization_barrier(values)

    a["far", "x"], a["near", "x"], s["far", "y"], s["near", "y"], cz = together(
        a["far", "x"], a["near", "x"], s["far", "y"], s["near", "y"], cz
    )

    pairs = arrange(
        [[[(act_own, 0), (a[g, "x"], 0)]] for g in groups]
        + [[[(sig_own, 0), (s[g, "y"], 0)]] for g in groups]
        + [[[(c0, 0), (cz, 0)]]],
        "pairs",
    )
    a0x, s0y, c0z = dict(zip(groups, pairs[:2])), dict(zip(groups, pairs[2:4])), pairs[4]
    ay, sz = {}, {}
    for g in groups:
        ay[g] = send(a0x[g], g, "y")
        sz[g] = send(s0y[g], g, "z")
    cx = send(c0z, "near", "x")
    ay["far"], ay["near"], sz["far"], sz["near"], cx = together(ay["far"], ay["near"], sz["far"], sz["near"], cx)
    turned = arrange(
        [[[(a0x[g], k), (ay[g], k)]] for k in (0, 1) for g in groups],
        "turn",
    )
    a0y, axxy = dict(zip(groups, turned[:2])), dict(zip(groups, turned[2:]))
    az, sx = {}, {}
    for g in groups:
        sx[g] = send(after(s0y[g], sz[g]), g, "x")
    cy = send(after(c0z, cx), "near", "y")
    for g in groups:
        az[g] = send(a0y[g], g, "z")
    n = "near"
    (four,) = arrange(
        [
            [
                [(a0x[n], 0), (a0x[n], 1), (ay[n], 0), (ay[n], 1)],
                [(s0y[n], 0), (s0y[n], 1), (sz[n], 0), (sz[n], 1)],
                [(c0z, 0), (c0z, 1), (cx, 0), (cx, 1)],
            ]
        ],
        "four",
    )
    az["far"], az[n], sx["far"], sx[n], cy, four, axxy[n], sz[n], axxy["far"], sz["far"] = together(
        az["far"], az[n], sx["far"], sx[n], cy, four, axxy[n], sz[n], axxy["far"], sz["far"]
    )
    az_mate, sx_mate, cy_mate = small = [send(v, n, "c") for v in (az[n], sx[n], cy)]
    axz, sxz = {}, {}
    axz[n] = send(axxy[n], n, "z")
    sxz[n] = send(sz[n], n, "x")
    axz["far"] = send(after(axxy["far"], *small), "far", "z")
    sxz["far"] = send(after(sz["far"], *small), "far", "x")
    four_mate = send(after(four, *small), n, "c")
    cxy = send(after(cx, cy, four_mate), n, "y")

    def blocks_of(g):
        act = {"": (a0x[g], 0, 0), "x": (a0x[g], 1, 0), "y": (ay[g], 0, 0), "xy": (ay[g], 1, 0)}
        act |= {"z": (az[g], 0, 0), "yz": (az[g], 1, 0), "xz": (axz[g], 0, 0), "xyz": (axz[g], 1, 0)}
        sig = {"": (s0y[g], 0, 0), "y": (s0y[g], 1, 0), "z": (sz[g], 0, 0), "yz": (sz[g], 1, 0)}
        sig |= {"x": (sx[g], 0, 0), "xy": (sx[g], 1, 0), "xz": (sxz[g], 0, 0), "xyz": (sxz[g], 1, 0)}
        return act, sig

    act, sig = blocks_of("far")
    right = {k: (act[k], sig[k]) for k in act}
    act, sig = blocks_of("near")
    coef = {"": (c0z, 0, 0), "z": (c0z, 1, 0), "x": (cx, 0, 0), "xz": (cx, 1, 0)}
    coef |= {"y": (cy, 0, 0), "yz": (cy, 1, 0), "xy": (cxy, 0, 0), "xyz": (cxy, 1, 0)}
    left = {k: (act[k], sig[k], coef[k]) for k in act}
    right_1 = [right[k] for k in ("xy", "yz", "x", "y", "z", "")]
    right_2 = [right[k] for k in ("xz", "xyz")]
    first, second = ("", "x", "y", "z", "yz"), ("xy", "xz", "xyz")

    coef[""] = (after(c0z, *small), 0, 0)
    act_mate = {"": (four_mate, 0, 0), "x": (four_mate, 1, 0), "y": (four_mate, 2, 0), "xy": (four_mate, 3, 0)}
    act_mate |= {"z": (az_mate, 0, 0), "yz": (az_mate, 1, 0)}
    sig_mate = {"": (four_mate, 0, 1), "y": (four_mate, 1, 1), "z": (four_mate, 2, 1), "yz": (four_mate, 3, 1)}
    sig_mate |= {"x": (sx_mate, 0, 0), "xy": (sx_mate, 1, 0)}
    coef_mate = {"": (four_mate, 0, 2), "z": (four_mate, 1, 2), "x": (four_mate, 2, 2), "xz": (four_mate, 3, 2)}
    coef_mate |= {"y": (cy_mate, 0, 0), "yz": (cy_mate, 1, 0)}
    left_1 = [(left[k][0], left[k][1], coef[k]) for k in first]
    left_1 += [(act_mate[k], sig_mate[k], coef_mate[k]) for k in first]
    (total_1,), (rows_1, coefs_1, wide_1) = partial_sums([(right_1, 0, 960, None, 0)], left_1, False, "early")
    axz_mate, sxz_mate = [send(after(v, total_1), n, "c") for v in (axz[n], sxz[n])]
    cxy_mate = send(cxy, n, "c")
    (total_2,), (wide_2,) = partial_sums(
        [(right_2, 0, 320, None, 0)], (after(rows_1, total_1), coefs_1), False, "early_right"
    )
    left["xy"] = (left["xy"][0], left["xy"][1], (after(cxy, total_2), 0, 0))
    (total_1, total_2), _ = partial_sums(
        [(wide_1, 0, 960, total_1, 0), (wide_2, 0, 320, total_2, 0)], [left[k] for k in second], False, "second_own"
    )
    act_mate |= {"xz": (axz_mate, 0, 0), "xyz": (axz_mate, 1, 0)}
    sig_mate |= {"xz": (sxz_mate, 0, 0), "xyz": (sxz_mate, 1, 0)}
    coef_mate |= {"xy": (cxy_mate, 0, 0), "xyz": (cxy_mate, 1, 0)}
    left_mate = {k: (act_mate[k], sig_mate[k], coef_mate[k]) for k in second}

    (sum_xz, sum_xyz, sum_xy, sum_yz), (rows_2, coefs_2) = partial_sums(
        [(wide_2, 0, 320, total_2, 0), (wide_1, 0, 320, total_1, 0)], [left_mate[k] for k in second], True, "second_mate_far"
    )
    part_x, part_y, part_z = send(sum_xz, "far", "z"), send(sum_xy, "far", "x"), send(sum_yz, "far", "y")
    got_xyz = send(sum_xyz, "far", "xyz")
    (sum_x, sum_y, sum_z, own), _ = partial_sums(
        [(wide_1, 320, 640, total_1, 320)], (after(rows_2, sum_xz), coefs_2), True, "second_mate_near"
    )
    got_x = send(after(sum_x + part_x, own), "far", "x")
    got_y = send(after(sum_y + part_y, own), "far", "y")
    got_z = send(after(sum_z + part_z, own), "far", "z")

    product = own + got_xyz + got_x + got_y + got_z
    product = product * (1.0 / (FEAT * FEAT))
    classes = jnp.arange(CLASSES, dtype=jnp.int32)
    targets = (labels[:, None] == classes[None, :]).astype(f32) - 1.0 / CLASSES
    return (coefs + damping * (targets - product - ridge * coefs)).T


def solution(mesh):
    in_specs = (P(AXES, None), P(AXES, None), P(AXES), P(None, AXES))
    return jax.shard_map(shards, mesh=mesh, in_specs=in_specs, out_specs=P(None, AXES), check_vma=False)
```

time: 108 us -> 105 us (0.972)
  waiting for transfers between devices: 38.5 us -> 33.5 us
  starting transfers between devices: 41.1 us -> 44 us
    ppermute x35 -> x34, waiting for transfers between devices: 38.5 us -> 33.5 us  [send(): return lax.ppermute(value, AXES, moves(group, dims))]
    ppermute x35 -> x34, starting transfers between devices: 41.1 us -> 44 us  [send(): return lax.ppermute(value, AXES, moves(group, dims))]
    pallas_call x6 -> x5, Pallas kernels: 23.3 us -> 22.6 us  [partial_sums(): pl.pallas_call(functools.partial(block_kernel, plan, n_in, parts, left_re...]
  transfers between devices with their start and end apart: 35 -> 34, of which waited for: 18 -> 23; matrix products, arithmetic and copies ran while one was open for 0% -> 0% of each run, Pallas kernels for 20% -> 20%
where the time goes in v5:
time: 105 us
  starting transfers between devices  44 us (42%)
  waiting for transfers between devices  33.5 us (32%)
  Pallas kernels  23.2 us (22%)
  local copies, waits for them, and re-layouts  2.84 us (3%)
    ppermute x34, starting transfers between devices, send(): return lax.ppermute(value, AXES, moves(group, dims))  44 us
    ppermute x34, waiting for transfers between devices, send(): return lax.ppermute(value, AXES, moves(group, dims))  33.5 us
    pallas_call x5, Pallas kernels, partial_sums(): pl.pallas_call(functools.partial(block_kernel, plan, n_in, parts, left_re...  22.6 us
    unnamed x10, local copies, waits for them, and re-layouts  2.84 us
  transfers between devices with their start and end apart: 34, of which 23 were waited for; matrix products, arithmetic and copies ran while one was open for 0% of the time, Pallas kernels for 20%

profile of v5, /device:TPU:0, one launch (start us, length us, event | category | flops | bytes accessed | tf_op | source)
XLA Modules:
  0.0 104.5 jit_solution(15339653379000410961)
XLA Ops:
  0.0 0.9 copy-done
  1.0 2.1 %collective-permute-start.4 = (bf16[160,768]{1,0:T(8,128)(2,1)S(1)}, bf16[160,768]{1,0:T(8,128)(2,1)S(1)}, u32[]{:S(2)}, u32[]{:S(2)}) collective-permute-start(bf16[160,768]{1,0:T(8,128)(2,1)S(1)} %split_coefs.1.refs_6_), channel_id=1, source_target_pairs={{0,2},{1,3},{2,0},{3,1},{4,6},{5,7},{6,4},{7,5},{8,10},{9,11},{10,... | collective-permute-start | bytes 737288 | tf_op jit(solution)/shard_map/ppermute | solution.py:48
  3.1 2.8 %collective-permute-start = (bf16[160,768]{1,0:T(8,128)(2,1)}, bf16[160,768]{1,0:T(8,128)(2,1)S(1)}, u32[]{:S(2)}, u32[]{:S(2)}) collective-permute-start(bf16[160,768]{1,0:T(8,128)(2,1)} %refs_0_), channel_id=1, source_target_pairs={{0,48},{1,49},{2,50},{3,51},{4,52},{5,53},{6,54},{7,55},{8,56},{9,... | collective-permute-start | bytes 737288 | tf_op jit(solution)/shard_map/ppermute | solution.py:48
  5.8 0.2 collective-permute-start.1
  6.1 3.0 %collective-permute-start.2 = (bf16[160,768]{1,0:T(8,128)(2,1)}, bf16[160,768]{1,0:T(8,128)(2,1)S(1)}, u32[]{:S(2)}, u32[]{:S(2)}) collective-permute-start(bf16[160,768]{1,0:T(8,128)(2,1)} %refs_1_), channel_id=1, source_target_pairs={{0,12},{1,13},{2,14},{3,15},{4,8},{5,9},{6,10},{7,11},{8,4},{9,5},... | collective-permute-start | bytes 737288 | tf_op jit(solution)/shard_map/ppermute | solution.py:48
  9.1 0.1 collective-permute-start.3
  9.2 0.9 copy-done.2
  10.2 0.9 copy-done.3
  11.2 0.8 collective-permute-done.refs_1_
  11.9 1.3 %collective-permute-done.1.refs_2_ = bf16[160,768]{1,0:T(8,128)(2,1)S(1)} collective-permute-done((bf16[160,768]{1,0:T(8,128)(2,1)}, bf16[160,768]{1,0:T(8,128)(2,1)S(1)}, u32[]{:S(2)}, u32[]{:S(2)}) %collective-permute-start.1) | collective-permute-done | bytes 245792 | tf_op jit(solution)/shard_map/ppermute | solution.py:48
  13.2 1.3 %collective-permute-done.2.refs_4_ = bf16[160,768]{1,0:T(8,128)(2,1)S(1)} collective-permute-done((bf16[160,768]{1,0:T(8,128)(2,1)}, bf16[160,768]{1,0:T(8,128)(2,1)S(1)}, u32[]{:S(2)}, u32[]{:S(2)}) %collective-permute-start.2) | collective-permute-done | bytes 245792 | tf_op jit(solution)/shard_map/ppermute | solution.py:48
  14.5 1.5 %collective-permute-done.3.refs_5_ = bf16[160,768]{1,0:T(8,128)(2,1)S(1)} collective-permute-done((bf16[160,768]{1,0:T(8,128)(2,1)}, bf16[160,768]{1,0:T(8,128)(2,1)S(1)}, u32[]{:S(2)}, u32[]{:S(2)}) %collective-permute-start.3) | collective-permute-done | bytes 245792 | tf_op jit(solution)/shard_map/ppermute | solution.py:48
  15.9 0.2 pairs.1
  16.1 1.8 %collective-permute-start.9 = (bf16[320,768]{1,0:T(8,128)(2,1)S(1)}, bf16[320,768]{1,0:T(8,128)(2,1)S(1)}, u32[]{:S(2)}, u32[]{:S(2)}) collective-permute-start(bf16[320,768]{1,0:T(8,128)(2,1)S(1)} %get-tuple-element.105.refs_4_.refs_2_.refs_9_), channel_id=1, source_target_pairs={{0,16},{1,17},{2,18},{3,19},{4,20},{5,21},{6,22},{7,23},{8,24},{9,... | collective-permute-start | bytes 1474568 | tf_op jit(solution)/shard_map/ppermute | solution.py:48
  17.9 0.3 collective-permute-start.6
  18.2 0.4 collective-permute-start.8
  18.6 1.2 %collective-permute-start.5 = (bf16[320,768]{1,0:T(8,128)(2,1)S(1)}, bf16[320,768]{1,0:T(8,128)(2,1)S(1)}, u32[]{:S(2)}, u32[]{:S(2)}) collective-permute-start(bf16[320,768]{1,0:T(8,128)(2,1)S(1)} %get-tuple-element.81.refs_0_.refs_18_), channel_id=1, source_target_pairs={{0,12},{1,13},{2,14},{3,15},{4,8},{5,9},{6,10},{7,11},{8,4},{9,5},... | collective-permute-start | bytes 1474568 | tf_op jit(solution)/shard_map/ppermute | solution.py:48
  19.8 3.8 %collective-permute-start.7 = (bf16[320,768]{1,0:T(8,128)(2,1)S(1)}, bf16[320,768]{1,0:T(8,128)(2,1)S(1)}, u32[]{:S(2)}, u32[]{:S(2)}) collective-permute-start(bf16[320,768]{1,0:T(8,128)(2,1)S(1)} %get-tuple-element.91.refs_19_), channel_id=1, source_target_pairs={{0,66},{1,67},{2,64},{3,65},{4,70},{5,71},{6,68},{7,69},{8,74},{9,... | collective-permute-start | bytes 1474568 | tf_op jit(solution)/shard_map/ppermute | solution.py:48
  23.6 3.6 %collective-permute-done.9.refs_5_.refs_4_ = bf16[320,768]{1,0:T(8,128)(2,1)S(1)} collective-permute-done((bf16[320,768]{1,0:T(8,128)(2,1)S(1)}, bf16[320,768]{1,0:T(8,128)(2,1)S(1)}, u32[]{:S(2)}, u32[]{:S(2)}) %collective-permute-start.9) | collective-permute-done | bytes 491552 | tf_op jit(solution)/shard_map/ppermute | solution.py:48
  27.1 1.4 %collective-permute-done.6.refs_3_.refs_1_.refs_5_.refs_0_ = bf16[320,768]{1,0:T(8,128)(2,1)S(1)} collective-permute-done((bf16[320,768]{1,0:T(8,128)(2,1)S(1)}, bf16[320,768]{1,0:T(8,128)(2,1)S(1)}, u32[]{:S(2)}, u32[]{:S(2)}) %collective-permute-start.6) | collective-permute-done | bytes 491552 | tf_op jit(solution)/shard_map/ppermute | solution.py:48
  28.5 0.2 collective-permute-done.8.refs_3_.refs_8_
  28.8 1.6 %collective-permute-done.5.refs_1_.refs_14_ = bf16[320,768]{1,0:T(8,128)(2,1)S(1)} collective-permute-done((bf16[320,768]{1,0:T(8,128)(2,1)S(1)}, bf16[320,768]{1,0:T(8,128)(2,1)S(1)}, u32[]{:S(2)}, u32[]{:S(2)}) %collective-permute-start.5) | collective-permute-done | bytes 491552 | tf_op jit(solution)/shard_map/ppermute | solution.py:48
  30.3 1.8 %collective-permute-done.7.refs_17_ = bf16[320,768]{1,0:T(8,128)(2,1)S(1)} collective-permute-done((bf16[320,768]{1,0:T(8,128)(2,1)S(1)}, bf16[320,768]{1,0:T(8,128)(2,1)S(1)}, u32[]{:S(2)}, u32[]{:S(2)}) %collective-permute-start.7) | collective-permute-done | bytes 491552 | tf_op jit(solution)/shard_map/ppermute | solution.py:48
  32.2 1.1 %collective-permute-start.14 = (bf16[320,768]{1,0:T(8,128)(2,1)S(1)}, bf16[320,768]{1,0:T(8,128)(2,1)S(1)}, u32[]{:S(2)}, u32[]{:S(2)}) collective-permute-start(bf16[320,768]{1,0:T(8,128)(2,1)S(1)} %get-tuple-element.105.refs_4_.refs_2_.refs_9_), channel_id=1, source_target_pairs={{0,4},{1,5},{2,6},{3,7},{4,0},{5,1},{6,2},{7,3},{8,12},{9,13},{10,... | collective-permute-start | bytes 1474568 | tf_op jit(solution)/shard_map/ppermute | solution.py:48
  33.3 0.4 collective-permute-start.13
  33.7 1.0 collective-permute-start.12
  34.7 0.1 turn.1
  34.8 3.0 %collective-permute-start.10 = (bf16[320,768]{1,0:T(8,128)(2,1)S(1)}, bf16[320,768]{1,0:T(8,128)(2,1)S(1)}, u32[]{:S(2)}, u32[]{:S(2)}) collective-permute-start(bf16[320,768]{1,0:T(8,128)(2,1)S(1)} %get-tuple-element.88), channel_id=1, source_target_pairs={{0,66},{1,67},{2,64},{3,65},{4,70},{5,71},{6,68},{7,69},{8,74},{9,... | collective-permute-start | bytes 1474568 | tf_op jit(solution)/shard_map/ppermute | solution.py:48
  37.8 0.2 four.1
  38.0 3.8 %collective-permute-done.14.refs_6_ = bf16[320,768]{1,0:T(8,128)(2,1)S(1)} collective-permute-done((bf16[320,768]{1,0:T(8,128)(2,1)S(1)}, bf16[320,768]{1,0:T(8,128)(2,1)S(1)}, u32[]{:S(2)}, u32[]{:S(2)}) %collective-permute-start.14) | collective-permute-done | bytes 491552 | tf_op jit(solution)/shard_map/ppermute | solution.py:48
  41.9 0.6 collective-permute-done.13.refs_3_.refs_1_
  42.5 1.4 %collective-permute-done.12.refs_15_ = bf16[320,768]{1,0:T(8,128)(2,1)S(1)} collective-permute-done((bf16[320,768]{1,0:T(8,128)(2,1)S(1)}, bf16[320,768]{1,0:T(8,128)(2,1)S(1)}, u32[]{:S(2)}, u32[]{:S(2)}) %collective-permute-start.12) | collective-permute-done | bytes 491552 | tf_op jit(solution)/shard_map/ppermute | solution.py:48
  43.8 1.1 %collective-permute-done.10.refs_16_ = bf16[320,768]{1,0:T(8,128)(2,1)S(1)} collective-permute-done((bf16[320,768]{1,0:T(8,128)(2,1)S(1)}, bf16[320,768]{1,0:T(8,128)(2,1)S(1)}, u32[]{:S(2)}, u32[]{:S(2)}) %collective-permute-start.10) | collective-permute-done | bytes 491552 | tf_op jit(solution)/shard_map/ppermute | solution.py:48
  44.9 1.7 %collective-permute-done.11.refs_7_ = bf16[320,768]{1,0:T(8,128)(2,1)S(1)} collective-permute-done((bf16[320,768]{1,0:T(8,128)(2,1)S(1)}, bf16[320,768]{1,0:T(8,128)(2,1)S(1)}, u32[]{:S(2)}, u32[]{:S(2)}) %collective-permute-start.11) | collective-permute-done | bytes 491552 | tf_op jit(solution)/shard_map/ppermute | solution.py:48
  46.7 0.5 collective-permute-start.16
  47.2 1.3 %collective-permute-done.15.refs_13_ = bf16[320,768]{1,0:T(8,128)(2,1)S(1)} collective-permute-done((bf16[320,768]{1,0:T(8,128)(2,1)S(1)}, bf16[320,768]{1,0:T(8,128)(2,1)S(1)}, u32[]{:S(2)}, u32[]{:S(2)}) %collective-permute-start.15) | collective-permute-done | bytes 491552 | tf_op jit(solution)/shard_map/ppermute | solution.py:48
  48.5 0.7 collective-permute-done.16.refs_11_.refs_1_
  49.2 0.7 collective-permute-done.17.refs_12_
  49.9 0.1 collective-permute-start.18
  50.1 0.7 collective-permute-start.23
  50.8 2.6 %collective-permute-start.26 = (bf16[320,768]{1,0:T(8,128)(2,1)S(1)}, bf16[320,768]{1,0:T(8,128)(2,1)S(1)}, u32[]{:S(2)}, u32[]{:S(2)}) collective-permute-start(bf16[320,768]{1,0:T(8,128)(2,1)S(1)} %collective-permute-done.7.refs_17_), channel_id=1, source_target_pairs={{0,48},{1,49},{2,50},{3,51},{4,52},{5,53},{6,54},{7,55},{8,56},{9,... | collective-permute-start | bytes 1474568 | tf_op jit(solution)/shard_map/ppermute | solution.py:48
  53.4 1.2 %collective-permute-start.25 = (bf16[320,768]{1,0:T(8,128)(2,1)S(1)}, bf16[320,768]{1,0:T(8,128)(2,1)S(1)}, u32[]{:S(2)}, u32[]{:S(2)}) collective-permute-start(bf16[320,768]{1,0:T(8,128)(2,1)S(1)} %get-tuple-element.114), channel_id=1, source_target_pairs={{0,66},{1,67},{2,64},{3,65},{4,70},{5,71},{6,68},{7,69},{8,74},{9,... | collective-permute-start | bytes 1474568 | tf_op jit(solution)/shard_map/ppermute | solution.py:48
  54.6 0.7 collective-permute-done.18.refs_10_.refs_0_
  55.3 1.1 %collective-permute-start.19 = (bf16[320,768]{1,0:T(8,128)(2,1)S(1)}, bf16[320,768]{1,0:T(8,128)(2,1)S(1)}, u32[]{:S(2)}, u32[]{:S(2)}) collective-permute-start(bf16[320,768]{1,0:T(8,128)(2,1)S(1)} %collective-permute-done.9.refs_5_.refs_4_), channel_id=1, source_target_pairs={{0,4},{1,5},{2,6},{3,7},{4,0},{5,1},{6,2},{7,3},{8,12},{9,13},{10,... | collective-permute-start | bytes 1474568 | tf_op jit(solution)/shard_map/ppermute | solution.py:48
  56.4 10.4 %early.1 = (f32[960,384]{1,0:T(8,128)S(1)}, bf16[1600,1536]{1,0:T(8,128)(2,1)S(1)}, bf16[1600,768]{1,0:T(8,128)(2,1)S(1)}, bf16[960,1536]{1,0:T(8,128)(2,1)S(1)}) custom-call(bf16[320,768]{1,0:T(8,128)(2,1)S(1)} %get-tuple-element.82.refs_2_.refs_0_, bf16[320,768]{1,0:T(8,128)(2,1)S(1)} %get-tuple-element.93.refs_2_.refs_1_, ...), custom_call_target="tpu_custom_call" | custom-call | flops 8294400000 | bytes 1000000 | tf_op jit(solution)/shard_map/early/pallas_call | solution.py:205
  66.9 0.1 collective-permute-start.24
  67.0 0.5 collective-permute-start.22
  67.5 1.1 %collective-permute-done.19.refs_2_.refs_6_ = bf16[320,768]{1,0:T(8,128)(2,1)S(1)} collective-permute-done((bf16[320,768]{1,0:T(8,128)(2,1)S(1)}, bf16[320,768]{1,0:T(8,128)(2,1)S(1)}, u32[]{:S(2)}, u32[]{:S(2)}) %collective-permute-start.19) | collective-permute-done | bytes 491552 | tf_op jit(solution)/shard_map/ppermute | solution.py:48
  68.6 3.8 %early_right.1 = (f32[320,384]{1,0:T(8,128)S(1)}, bf16[320,1536]{1,0:T(8,128)(2,1)S(1)}) custom-call(bf16[320,768]{1,0:T(8,128)(2,1)S(1)} %collective-permute-done.25.refs_0_, bf16[320,768]{1,0:T(8,128)(2,1)S(1)} %collective-permute-done.26.refs_1_, bf16[1600,1536]{1,0:T(8,128)(2,1)S(1)} %get-tuple-element.117.refs_2_, ...), custom_call_target="tpu_custom_call" | custom-call | flops 2764800000 | bytes 1000000 | tf_op jit(solution)/shard_map/early_right/pallas_call | solution.py:205
  72.4 4.0 %second_own.1 = (f32[960,384]{1,0:T(8,128)S(1)}, f32[320,384]{1,0:T(8,128)S(1)}, bf16[480,1536]{1,0:T(8,128)(2,1)}, bf16[480,768]{1,0:T(8,128)(2,1)}) custom-call(bf16[320,768]{1,0:T(8,128)(2,1)S(1)} %collective-permute-done.6.refs_3_.refs_1_.refs_5_.refs_0_, bf16[320,768]{1,0:T(8,128)(2,1)S(1)} %collective-permute-done.13.refs_3_.refs_1_, ...), custom_call_target="tpu_custom_call" | custom-call | flops 3317760000 | bytes 1000000 | tf_op jit(solution)/shard_map/second_own/pallas_call | solution.py:205
  76.4 2.2 %second_mate_far.1 = (f32[160,345]{1,0:T(8,128)S(1)}, f32[160,345]{1,0:T(8,128)S(1)}, f32[160,345]{1,0:T(8,128)S(1)}, f32[160,345]{1,0:T(8,128)S(1)}, bf16[480,1...) custom-call(bf16[640,2304]{1,0:T(8,128)(2,1)S(1)} %collective-permute-done.18.refs_10_.refs_0_, ...), custom_call_target="tpu_custom_call" | custom-call | flops 1658880000 | bytes 1000000 | tf_op jit(solution)/shard_map/second_mate_far/pallas_call | solution.py:205
  78.7 1.3 %collective-permute-start.28 = (f32[160,345]{1,0:T(8,128)S(1)}, f32[160,345]{1,0:T(8,128)S(1)}, u32[]{:S(2)}, u32[]{:S(2)}) collective-permute-start(f32[160,345]{1,0:T(8,128)S(1)} %get-tuple-element.126), channel_id=1, source_target_pairs={{0,66},{1,67},{2,64},{3,65},{4,70},{5,71},{6,68},{7,69},{8,74},{9,... | collective-permute-start | bytes 662408 | tf_op jit(solution)/shard_map/ppermute | solution.py:48
  79.9 2.2 %collective-permute-start.30 = (f32[160,345]{1,0:T(8,128)S(1)}, f32[160,345]{1,0:T(8,128)S(1)}, u32[]{:S(2)}, u32[]{:S(2)}) collective-permute-start(f32[160,345]{1,0:T(8,128)S(1)} %get-tuple-element.134), channel_id=1, source_target_pairs={{0,48},{1,49},{2,50},{3,51},{4,52},{5,53},{6,54},{7,55},{8,56},{9,... | collective-permute-start | bytes 662408 | tf_op jit(solution)/shard_map/ppermute | solution.py:48
  82.2 1.5 %collective-permute-start.32 = (f32[160,345]{1,0:T(8,128)S(1)}, f32[160,345]{1,0:T(8,128)S(1)}, u32[]{:S(2)}, u32[]{:S(2)}) collective-permute-start(f32[160,345]{1,0:T(8,128)S(1)} %get-tuple-element.137), channel_id=1, source_target_pairs={{0,12},{1,13},{2,14},{3,15},{4,8},{5,9},{6,10},{7,11},{8,4},{9,5},... | collective-permute-start | bytes 662408 | tf_op jit(solution)/shard_map/ppermute | solution.py:48
  83.7 3.7 %collective-permute-start.27 = (f32[160,345]{1,0:T(8,128)S(1)}, f32[160,345]{1,0:T(8,128)S(1)}, u32[]{:S(2)}, u32[]{:S(2)}) collective-permute-start(f32[160,345]{1,0:T(8,128)S(1)} %get-tuple-element.130), channel_id=1, source_target_pairs={{0,126},{1,127},{2,124},{3,125},{4,122},{5,123},{6,120},{7,121},{8... | collective-permute-start | bytes 662408 | tf_op jit(solution)/shard_map/ppermute | solution.py:48
  87.3 2.2 %second_mate_near.1 = (f32[160,345]{1,0:T(8,128)S(1)}, f32[160,345]{1,0:T(8,128)S(1)}, f32[160,345]{1,0:T(8,128)S(1)}, f32[160,345]{1,0:T(8,128)S(1)}) custom-call(bf16[480,1536]{1,0:T(8,128)(2,1)S(1)} %get-tuple-element.127.refs_0_, bf16[480,768]{1,0:T(8,128)(2,1)S(1)} %get-tuple-element.128.refs_1_, ...), custom_call_target="tpu_custom_call" | custom-call | flops 1658880000 | bytes 1000000 | tf_op jit(solution)/shard_map/second_mate_near/pallas_call | solution.py:205
  89.6 2.3 %collective-permute-start.29 = (f32[160,345]{1,0:T(8,128)S(1)}, f32[160,345]{1,0:T(8,128)S(1)}, u32[]{:S(2)}, u32[]{:S(2)}) collective-permute-start(f32[160,345]{1,0:T(8,128)S(1)} %add.26), channel_id=1, source_target_pairs={{0,48},{1,49},{2,50},{3,51},{4,52},{5,53},{6,54},{7,55},{8,56},{9,... | collective-permute-start | bytes 662408 | tf_op jit(solution)/shard_map/ppermute | solution.py:48
  91.9 1.5 %collective-permute-start.31 = (f32[160,345]{1,0:T(8,128)S(1)}, f32[160,345]{1,0:T(8,128)S(1)}, u32[]{:S(2)}, u32[]{:S(2)}) collective-permute-start(f32[160,345]{1,0:T(8,128)S(1)} %add.28), channel_id=1, source_target_pairs={{0,12},{1,13},{2,14},{3,15},{4,8},{5,9},{6,10},{7,11},{8,4},{9,5},... | collective-permute-start | bytes 662408 | tf_op jit(solution)/shard_map/ppermute | solution.py:48
  93.5 2.7 %collective-permute-done.32 = f32[160,345]{1,0:T(8,128)S(1)} collective-permute-done((f32[160,345]{1,0:T(8,128)S(1)}, f32[160,345]{1,0:T(8,128)S(1)}, u32[]{:S(2)}, u32[]{:S(2)}) %collective-permute-start.32) | collective-permute-done | bytes 220832 | tf_op jit(solution)/shard_map/ppermute | solution.py:48
  96.2 3.3 %collective-permute-start.33 = (f32[160,345]{1,0:T(8,128)S(1)}, f32[160,345]{1,0:T(8,128)S(1)}, u32[]{:S(2)}, u32[]{:S(2)}) collective-permute-start(f32[160,345]{1,0:T(8,128)S(1)} %add.30), channel_id=1, source_target_pairs={{0,66},{1,67},{2,64},{3,65},{4,70},{5,71},{6,68},{7,69},{8,74},{9,... | collective-permute-start | bytes 662408 | tf_op jit(solution)/shard_map/ppermute | solution.py:48
  99.5 0.9 collective-permute-done.29
  100.4 1.4 %collective-permute-done.31 = f32[160,345]{1,0:T(8,128)S(1)} collective-permute-done((f32[160,345]{1,0:T(8,128)S(1)}, f32[160,345]{1,0:T(8,128)S(1)}, u32[]{:S(2)}, u32[]{:S(2)}) %collective-permute-start.31) | collective-permute-done | bytes 220832 | tf_op jit(solution)/shard_map/ppermute | solution.py:48
  101.7 1.9 %collective-permute-done.33 = f32[160,345]{1,0:T(8,128)S(1)} collective-permute-done((f32[160,345]{1,0:T(8,128)S(1)}, f32[160,345]{1,0:T(8,128)S(1)}, u32[]{:S(2)}, u32[]{:S(2)}) %collective-permute-start.33) | collective-permute-done | bytes 220832 | tf_op jit(solution)/shard_map/ppermute | solution.py:48
  103.7 0.8 add_bitcast_fusion
  (28 shorter events, 0.2 us)
Async XLA Ops:
  0.0 0.9 copy-start
  1.0 10.1 %collective-permute-start.4 = (bf16[160,768]{1,0:T(8,128)(2,1)S(1)}, bf16[160,768]{1,0:T(8,128)(2,1)S(1)}, u32[]{:S(2)}, u32[]{:S(2)}) collective-permute-start(bf16[160,768]{1,0:T(8,128)(2,1)S(1)} %split_coefs.1.refs_6_), channel_id=1, source_target_pairs={{0,2},{1,3},{2,0},{3,1},{4,6},{5,7},{6,4},{7,5},{8,10},{9,11},{10,... | collective-permute-start | bytes 737288 | tf_op jit(solution)/shard_map/ppermute | solution.py:48
  3.1 8.8 %collective-permute-start = (bf16[160,768]{1,0:T(8,128)(2,1)}, bf16[160,768]{1,0:T(8,128)(2,1)S(1)}, u32[]{:S(2)}, u32[]{:S(2)}) collective-permute-start(bf16[160,768]{1,0:T(8,128)(2,1)} %refs_0_), channel_id=1, source_target_pairs={{0,48},{1,49},{2,50},{3,51},{4,52},{5,53},{6,54},{7,55},{8,56},{9,... | collective-permute-start | bytes 737288 | tf_op jit(solution)/shard_map/ppermute | solution.py:48
  5.8 7.3 %collective-permute-start.1 = (bf16[160,768]{1,0:T(8,128)(2,1)}, bf16[160,768]{1,0:T(8,128)(2,1)S(1)}, u32[]{:S(2)}, u32[]{:S(2)}) collective-permute-start(bf16[160,768]{1,0:T(8,128)(2,1)} %refs_0_), channel_id=1, source_target_pairs={{0,16},{1,17},{2,18},{3,19},{4,20},{5,21},{6,22},{7,23},{8,24},{9,... | collective-permute-start | bytes 737288 | tf_op jit(solution)/shard_map/ppermute | solution.py:48
  6.1 8.4 %collective-permute-start.2 = (bf16[160,768]{1,0:T(8,128)(2,1)}, bf16[160,768]{1,0:T(8,128)(2,1)S(1)}, u32[]{:S(2)}, u32[]{:S(2)}) collective-permute-start(bf16[160,768]{1,0:T(8,128)(2,1)} %refs_1_), channel_id=1, source_target_pairs={{0,12},{1,13},{2,14},{3,15},{4,8},{5,9},{6,10},{7,11},{8,4},{9,5},... | collective-permute-start | bytes 737288 | tf_op jit(solution)/shard_map/ppermute | solution.py:48
  9.1 6.8 %collective-permute-start.3 = (bf16[160,768]{1,0:T(8,128)(2,1)}, bf16[160,768]{1,0:T(8,128)(2,1)S(1)}, u32[]{:S(2)}, u32[]{:S(2)}) collective-permute-start(bf16[160,768]{1,0:T(8,128)(2,1)} %refs_1_), channel_id=1, source_target_pairs={{0,4},{1,5},{2,6},{3,7},{4,0},{5,1},{6,2},{7,3},{8,12},{9,13},{10,... | collective-permute-start | bytes 737288 | tf_op jit(solution)/shard_map/ppermute | solution.py:48
  9.2 0.9 copy-start.2
  10.2 0.9 copy-start.3
  16.1 11.1 %collective-permute-start.9 = (bf16[320,768]{1,0:T(8,128)(2,1)S(1)}, bf16[320,768]{1,0:T(8,128)(2,1)S(1)}, u32[]{:S(2)}, u32[]{:S(2)}) collective-permute-start(bf16[320,768]{1,0:T(8,128)(2,1)S(1)} %get-tuple-element.105.refs_4_.refs_2_.refs_9_), channel_id=1, source_target_pairs={{0,16},{1,17},{2,18},{3,19},{4,20},{5,21},{6,22},{7,23},{8,24},{9,... | collective-permute-start | bytes 1474568 | tf_op jit(solution)/shard_map/ppermute | solution.py:48
  17.9 10.6 %collective-permute-start.6 = (bf16[320,768]{1,0:T(8,128)(2,1)S(1)}, bf16[320,768]{1,0:T(8,128)(2,1)S(1)}, u32[]{:S(2)}, u32[]{:S(2)}) collective-permute-start(bf16[320,768]{1,0:T(8,128)(2,1)S(1)} %get-tuple-element.82.refs_2_.refs_0_), channel_id=1, source_target_pairs={{0,4},{1,5},{2,6},{3,7},{4,0},{5,1},{6,2},{7,3},{8,12},{9,13},{10,... | collective-permute-start | bytes 1474568 | tf_op jit(solution)/shard_map/ppermute | solution.py:48
  18.2 10.5 %collective-permute-start.8 = (bf16[320,768]{1,0:T(8,128)(2,1)S(1)}, bf16[320,768]{1,0:T(8,128)(2,1)S(1)}, u32[]{:S(2)}, u32[]{:S(2)}) collective-permute-start(bf16[320,768]{1,0:T(8,128)(2,1)S(1)} %get-tuple-element.93.refs_2_.refs_1_), channel_id=1, source_target_pairs={{0,2},{1,3},{2,0},{3,1},{4,6},{5,7},{6,4},{7,5},{8,10},{9,11},{10,... | collective-permute-start | bytes 1474568 | tf_op jit(solution)/shard_map/ppermute | solution.py:48
  18.6 11.7 %collective-permute-start.5 = (bf16[320,768]{1,0:T(8,128)(2,1)S(1)}, bf16[320,768]{1,0:T(8,128)(2,1)S(1)}, u32[]{:S(2)}, u32[]{:S(2)}) collective-permute-start(bf16[320,768]{1,0:T(8,128)(2,1)S(1)} %get-tuple-element.81.refs_0_.refs_18_), channel_id=1, source_target_pairs={{0,12},{1,13},{2,14},{3,15},{4,8},{5,9},{6,10},{7,11},{8,4},{9,5},... | collective-permute-start | bytes 1474568 | tf_op jit(solution)/shard_map/ppermute | solution.py:48
  19.8 12.4 %collective-permute-start.7 = (bf16[320,768]{1,0:T(8,128)(2,1)S(1)}, bf16[320,768]{1,0:T(8,128)(2,1)S(1)}, u32[]{:S(2)}, u32[]{:S(2)}) collective-permute-start(bf16[320,768]{1,0:T(8,128)(2,1)S(1)} %get-tuple-element.91.refs_19_), channel_id=1, source_target_pairs={{0,66},{1,67},{2,64},{3,65},{4,70},{5,71},{6,68},{7,69},{8,74},{9,... | collective-permute-start | bytes 1474568 | tf_op jit(solution)/shard_map/ppermute | solution.py:48
  32.2 9.7 %collective-permute-start.14 = (bf16[320,768]{1,0:T(8,128)(2,1)S(1)}, bf16[320,768]{1,0:T(8,128)(2,1)S(1)}, u32[]{:S(2)}, u32[]{:S(2)}) collective-permute-start(bf16[320,768]{1,0:T(8,128)(2,1)S(1)} %get-tuple-element.105.refs_4_.refs_2_.refs_9_), channel_id=1, source_target_pairs={{0,4},{1,5},{2,6},{3,7},{4,0},{5,1},{6,2},{7,3},{8,12},{9,13},{10,... | collective-permute-start | bytes 1474568 | tf_op jit(solution)/shard_map/ppermute | solution.py:48
  33.3 9.2 %collective-permute-start.13 = (bf16[320,768]{1,0:T(8,128)(2,1)S(1)}, bf16[320,768]{1,0:T(8,128)(2,1)S(1)}, u32[]{:S(2)}, u32[]{:S(2)}) collective-permute-start(bf16[320,768]{1,0:T(8,128)(2,1)S(1)} %get-tuple-element.93.refs_2_.refs_1_), channel_id=1, source_target_pairs={{0,16},{1,17},{2,18},{3,19},{4,20},{5,21},{6,22},{7,23},{8,24},{9,... | collective-permute-start | bytes 1474568 | tf_op jit(solution)/shard_map/ppermute | solution.py:48
  33.7 10.2 %collective-permute-start.12 = (bf16[320,768]{1,0:T(8,128)(2,1)S(1)}, bf16[320,768]{1,0:T(8,128)(2,1)S(1)}, u32[]{:S(2)}, u32[]{:S(2)}) collective-permute-start(bf16[320,768]{1,0:T(8,128)(2,1)S(1)} %get-tuple-element.91.refs_19_), channel_id=1, source_target_pairs={{0,48},{1,49},{2,50},{3,51},{4,52},{5,53},{6,54},{7,55},{8,56},{9,... | collective-permute-start | bytes 1474568 | tf_op jit(solution)/shard_map/ppermute | solution.py:48
  34.8 10.1 %collective-permute-start.10 = (bf16[320,768]{1,0:T(8,128)(2,1)S(1)}, bf16[320,768]{1,0:T(8,128)(2,1)S(1)}, u32[]{:S(2)}, u32[]{:S(2)}) collective-permute-start(bf16[320,768]{1,0:T(8,128)(2,1)S(1)} %get-tuple-element.88), channel_id=1, source_target_pairs={{0,66},{1,67},{2,64},{3,65},{4,70},{5,71},{6,68},{7,69},{8,74},{9,... | collective-permute-start | bytes 1474568 | tf_op jit(solution)/shard_map/ppermute | solution.py:48
  37.8 8.8 %collective-permute-start.11 = (bf16[320,768]{1,0:T(8,128)(2,1)S(1)}, bf16[320,768]{1,0:T(8,128)(2,1)S(1)}, u32[]{:S(2)}, u32[]{:S(2)}) collective-permute-start(bf16[320,768]{1,0:T(8,128)(2,1)S(1)} %get-tuple-element.89), channel_id=1, source_target_pairs={{0,2},{1,3},{2,0},{3,1},{4,6},{5,7},{6,4},{7,5},{8,10},{9,11},{10,... | collective-permute-start | bytes 1474568 | tf_op jit(solution)/shard_map/ppermute | solution.py:48
  46.7 1.9 %collective-permute-start.15 = (bf16[320,768]{1,0:T(8,128)(2,1)S(1)}, bf16[320,768]{1,0:T(8,128)(2,1)S(1)}, u32[]{:S(2)}, u32[]{:S(2)}) collective-permute-start(bf16[320,768]{1,0:T(8,128)(2,1)S(1)} %collective-permute-done.11.refs_7_), channel_id=1, source_target_pairs={{0,1},{1,0},{2,3},{3,2},{4,5},{5,4},{6,7},{7,6},{8,9},{9,8},{10,11... | collective-permute-start | bytes 1474568 | tf_op jit(solution)/shard_map/ppermute | solution.py:48
  46.7 2.6 %collective-permute-start.16 = (bf16[320,768]{1,0:T(8,128)(2,1)S(1)}, bf16[320,768]{1,0:T(8,128)(2,1)S(1)}, u32[]{:S(2)}, u32[]{:S(2)}) collective-permute-start(bf16[320,768]{1,0:T(8,128)(2,1)S(1)} %collective-permute-done.13.refs_3_.refs_1_), channel_id=1, source_target_pairs={{0,1},{1,0},{2,3},{3,2},{4,5},{5,4},{6,7},{7,6},{8,9},{9,8},{10,11... | collective-permute-start | bytes 1474568 | tf_op jit(solution)/shard_map/ppermute | solution.py:48
  47.2 2.8 %collective-permute-start.17 = (bf16[320,768]{1,0:T(8,128)(2,1)S(1)}, bf16[320,768]{1,0:T(8,128)(2,1)S(1)}, u32[]{:S(2)}, u32[]{:S(2)}) collective-permute-start(bf16[320,768]{1,0:T(8,128)(2,1)S(1)} %collective-permute-done.14.refs_6_), channel_id=1, source_target_pairs={{0,1},{1,0},{2,3},{3,2},{4,5},{5,4},{6,7},{7,6},{8,9},{9,8},{10,11... | collective-permute-start | bytes 1474568 | tf_op jit(solution)/shard_map/ppermute | solution.py:48
  49.9 5.4 %collective-permute-start.18 = (bf16[640,2304]{1,0:T(8,128)(2,1)S(1)}, bf16[640,2304]{1,0:T(8,128)(2,1)S(1)}, u32[]{:S(2)}, u32[]{:S(2)}) collective-permute-start(bf16[640,2304]{1,0:T(8,128)(2,1)S(1)} %four.1), channel_id=1, source_target_pairs={{0,1},{1,0},{2,3},{3,2},{4,5},{5,4},{6,7},{7,6},{8,9},{9,8},{10,11... | collective-permute-start | bytes 8847368 | tf_op jit(solution)/shard_map/ppermute | solution.py:48
  50.1 16.9 %collective-permute-start.21 = (bf16[320,768]{1,0:T(8,128)(2,1)S(1)}, bf16[320,768]{1,0:T(8,128)(2,1)S(1)}, u32[]{:S(2)}, u32[]{:S(2)}) collective-permute-start(bf16[320,768]{1,0:T(8,128)(2,1)S(1)} %get-tuple-element.104), channel_id=1, source_target_pairs={{0,2},{1,3},{2,0},{3,1},{4,6},{5,7},{6,4},{7,5},{8,10},{9,11},{10,... | collective-permute-start | bytes 1474568 | tf_op jit(solution)/shard_map/ppermute | solution.py:48
  50.1 16.8 %collective-permute-start.23 = (bf16[320,768]{1,0:T(8,128)(2,1)S(1)}, bf16[320,768]{1,0:T(8,128)(2,1)S(1)}, u32[]{:S(2)}, u32[]{:S(2)}) collective-permute-start(bf16[320,768]{1,0:T(8,128)(2,1)S(1)} %collective-permute-done.8.refs_3_.refs_8_), channel_id=1, source_target_pairs={{0,16},{1,17},{2,18},{3,19},{4,20},{5,21},{6,22},{7,23},{8,24},{9,... | collective-permute-start | bytes 1474568 | tf_op jit(solution)/shard_map/ppermute | solution.py:48
  50.8 17.8 %collective-permute-start.26 = (bf16[320,768]{1,0:T(8,128)(2,1)S(1)}, bf16[320,768]{1,0:T(8,128)(2,1)S(1)}, u32[]{:S(2)}, u32[]{:S(2)}) collective-permute-start(bf16[320,768]{1,0:T(8,128)(2,1)S(1)} %collective-permute-done.7.refs_17_), channel_id=1, source_target_pairs={{0,48},{1,49},{2,50},{3,51},{4,52},{5,53},{6,54},{7,55},{8,56},{9,... | collective-permute-start | bytes 1474568 | tf_op jit(solution)/shard_map/ppermute | solution.py:48
  53.4 15.2 %collective-permute-start.25 = (bf16[320,768]{1,0:T(8,128)(2,1)S(1)}, bf16[320,768]{1,0:T(8,128)(2,1)S(1)}, u32[]{:S(2)}, u32[]{:S(2)}) collective-permute-start(bf16[320,768]{1,0:T(8,128)(2,1)S(1)} %get-tuple-element.114), channel_id=1, source_target_pairs={{0,66},{1,67},{2,64},{3,65},{4,70},{5,71},{6,68},{7,69},{8,74},{9,... | collective-permute-start | bytes 1474568 | tf_op jit(solution)/shard_map/ppermute | solution.py:48
  55.3 13.3 %collective-permute-start.19 = (bf16[320,768]{1,0:T(8,128)(2,1)S(1)}, bf16[320,768]{1,0:T(8,128)(2,1)S(1)}, u32[]{:S(2)}, u32[]{:S(2)}) collective-permute-start(bf16[320,768]{1,0:T(8,128)(2,1)S(1)} %collective-permute-done.9.refs_5_.refs_4_), channel_id=1, source_target_pairs={{0,4},{1,5},{2,6},{3,7},{4,0},{5,1},{6,2},{7,3},{8,12},{9,13},{10,... | collective-permute-start | bytes 1474568 | tf_op jit(solution)/shard_map/ppermute | solution.py:48
  66.9 9.5 %collective-permute-start.24 = (bf16[320,768]{1,0:T(8,128)(2,1)S(1)}, bf16[320,768]{1,0:T(8,128)(2,1)S(1)}, u32[]{:S(2)}, u32[]{:S(2)}) collective-permute-start(bf16[320,768]{1,0:T(8,128)(2,1)S(1)} %collective-permute-done.23.refs_4_), channel_id=1, source_target_pairs={{0,1},{1,0},{2,3},{3,2},{4,5},{5,4},{6,7},{7,6},{8,9},{9,8},{10,11... | collective-permute-start | bytes 1474568 | tf_op jit(solution)/shard_map/ppermute | solution.py:48
  67.0 9.4 %collective-permute-start.22 = (bf16[320,768]{1,0:T(8,128)(2,1)S(1)}, bf16[320,768]{1,0:T(8,128)(2,1)S(1)}, u32[]{:S(2)}, u32[]{:S(2)}) collective-permute-start(bf16[320,768]{1,0:T(8,128)(2,1)S(1)} %collective-permute-done.21.refs_3_), channel_id=1, source_target_pairs={{0,1},{1,0},{2,3},{3,2},{4,5},{5,4},{6,7},{7,6},{8,9},{9,8},{10,11... | collective-permute-start | bytes 1474568 | tf_op jit(solution)/shard_map/ppermute | solution.py:48
  68.6 7.8 %collective-permute-start.20 = (bf16[320,768]{1,0:T(8,128)(2,1)S(1)}, bf16[320,768]{1,0:T(8,128)(2,1)S(1)}, u32[]{:S(2)}, u32[]{:S(2)}) collective-permute-start(bf16[320,768]{1,0:T(8,128)(2,1)S(1)} %collective-permute-done.19.refs_2_.refs_6_), channel_id=1, source_target_pairs={{0,1},{1,0},{2,3},{3,2},{4,5},{5,4},{6,7},{7,6},{8,9},{9,8},{10,11... | collective-permute-start | bytes 1474568 | tf_op jit(solution)/shard_map/ppermute | solution.py:48
  78.7 10.9 %collective-permute-start.28 = (f32[160,345]{1,0:T(8,128)S(1)}, f32[160,345]{1,0:T(8,128)S(1)}, u32[]{:S(2)}, u32[]{:S(2)}) collective-permute-start(f32[160,345]{1,0:T(8,128)S(1)} %get-tuple-element.126), channel_id=1, source_target_pairs={{0,66},{1,67},{2,64},{3,65},{4,70},{5,71},{6,68},{7,69},{8,74},{9,... | collective-permute-start | bytes 662408 | tf_op jit(solution)/shard_map/ppermute | solution.py:48
  79.9 11.9 %collective-permute-start.30 = (f32[160,345]{1,0:T(8,128)S(1)}, f32[160,345]{1,0:T(8,128)S(1)}, u32[]{:S(2)}, u32[]{:S(2)}) collective-permute-start(f32[160,345]{1,0:T(8,128)S(1)} %get-tuple-element.134), channel_id=1, source_target_pairs={{0,48},{1,49},{2,50},{3,51},{4,52},{5,53},{6,54},{7,55},{8,56},{9,... | collective-permute-start | bytes 662408 | tf_op jit(solution)/shard_map/ppermute | solution.py:48
  82.2 14.0 %collective-permute-start.32 = (f32[160,345]{1,0:T(8,128)S(1)}, f32[160,345]{1,0:T(8,128)S(1)}, u32[]{:S(2)}, u32[]{:S(2)}) collective-permute-start(f32[160,345]{1,0:T(8,128)S(1)} %get-tuple-element.137), channel_id=1, source_target_pairs={{0,12},{1,13},{2,14},{3,15},{4,8},{5,9},{6,10},{7,11},{8,4},{9,5},... | collective-permute-start | bytes 662408 | tf_op jit(solution)/shard_map/ppermute | solution.py:48
  83.7 15.9 %collective-permute-start.27 = (f32[160,345]{1,0:T(8,128)S(1)}, f32[160,345]{1,0:T(8,128)S(1)}, u32[]{:S(2)}, u32[]{:S(2)}) collective-permute-start(f32[160,345]{1,0:T(8,128)S(1)} %get-tuple-element.130), channel_id=1, source_target_pairs={{0,126},{1,127},{2,124},{3,125},{4,122},{5,123},{6,120},{7,121},{8... | collective-permute-start | bytes 662408 | tf_op jit(solution)/shard_map/ppermute | solution.py:48
  87.3 16.4 %copy-start.1 = (f32[345,160]{0,1:T(8,128)S(1)}, f32[345,160]{0,1:T(8,128)}, u32[]{:S(2)}) copy-start(f32[345,160]{0,1:T(8,128)} %param.7) | copy-start | bytes 662404
  87.3 16.4 %copy-start.4 = (s32[160]{0:T(256)S(1)}, s32[160]{0:T(256)}, u32[]{:S(2)}) copy-start(s32[160]{0:T(256)} %param.6) | copy-start | bytes 1924
  89.6 10.8 %collective-permute-start.29 = (f32[160,345]{1,0:T(8,128)S(1)}, f32[160,345]{1,0:T(8,128)S(1)}, u32[]{:S(2)}, u32[]{:S(2)}) collective-permute-start(f32[160,345]{1,0:T(8,128)S(1)} %add.26), channel_id=1, source_target_pairs={{0,48},{1,49},{2,50},{3,51},{4,52},{5,53},{6,54},{7,55},{8,56},{9,... | collective-permute-start | bytes 662408 | tf_op jit(solution)/shard_map/ppermute | solution.py:48
  91.9 9.8 %collective-permute-start.31 = (f32[160,345]{1,0:T(8,128)S(1)}, f32[160,345]{1,0:T(8,128)S(1)}, u32[]{:S(2)}, u32[]{:S(2)}) collective-permute-start(f32[160,345]{1,0:T(8,128)S(1)} %add.28), channel_id=1, source_target_pairs={{0,12},{1,13},{2,14},{3,15},{4,8},{5,9},{6,10},{7,11},{8,4},{9,5},... | collective-permute-start | bytes 662408 | tf_op jit(solution)/shard_map/ppermute | solution.py:48
  96.2 7.5 %collective-permute-start.33 = (f32[160,345]{1,0:T(8,128)S(1)}, f32[160,345]{1,0:T(8,128)S(1)}, u32[]{:S(2)}, u32[]{:S(2)}) collective-permute-start(f32[160,345]{1,0:T(8,128)S(1)} %add.30), channel_id=1, source_target_pairs={{0,66},{1,67},{2,64},{3,65},{4,70},{5,71},{6,68},{7,69},{8,74},{9,... | collective-permute-start | bytes 662408 | tf_op jit(solution)/shard_map/ppermute | solution.py:48

commit v6 on v5

--- a/solution.py
+++ b/solution.py
@@ -313,22 +313,19 @@
     (total_2,), (wide_2,) = partial_sums(
         [(right_2, 0, 320, None, 0)], (after(rows_1, total_1), coefs_1), False, "early_right"
     )
-    left["xy"] = (left["xy"][0], left["xy"][1], (after(cxy, total_2), 0, 0))
-    (total_1, total_2), _ = partial_sums(
-        [(wide_1, 0, 960, total_1, 0), (wide_2, 0, 320, total_2, 0)], [left[k] for k in second], False, "second_own"
-    )
     act_mate |= {"xz": (axz_mate, 0, 0), "xyz": (axz_mate, 1, 0)}
     sig_mate |= {"xz": (sxz_mate, 0, 0), "xyz": (sxz_mate, 1, 0)}
     coef_mate |= {"xy": (cxy_mate, 0, 0), "xyz": (cxy_mate, 1, 0)}
-    left_mate = {k: (act_mate[k], sig_mate[k], coef_mate[k]) for k in second}
+    left_2 = [left[k] for k in second]
+    left_2 += [(act_mate[k], sig_mate[k], coef_mate[k]) for k in second]
 
     (sum_xz, sum_xyz, sum_xy, sum_yz), (rows_2, coefs_2) = partial_sums(
-        [(wide_2, 0, 320, total_2, 0), (wide_1, 0, 320, total_1, 0)], [left_mate[k] for k in second], True, "second_mate_far"
+        [(wide_2, 0, 320, total_2, 0), (wide_1, 0, 320, total_1, 0)], left_2, True, "second_far"
     )
     part_x, part_y, part_z = send(sum_xz, "far", "z"), send(sum_xy, "far", "x"), send(sum_yz, "far", "y")
     got_xyz = send(sum_xyz, "far", "xyz")
     (sum_x, sum_y, sum_z, own), _ = partial_sums(
-        [(wide_1, 320, 640, total_1, 320)], (after(rows_2, sum_xz), coefs_2), True, "second_mate_near"
+        [(wide_1, 320, 640, total_1, 320)], (after(rows_2, sum_xz), coefs_2), True, "second_near"
     )
     got_x = send(after(sum_x + part_x, own), "far", "x")
     got_y = send(after(sum_y + part_y, own), "far", "y")

time: 105 us -> 103 us (0.981)
    pallas_call x5 -> x4, Pallas kernels: 22.6 us -> 22.7 us  [partial_sums(): pl.pallas_call(functools.partial(block_kernel, plan, n_in, parts, left_re...]
  transfers between devices with their start and end apart: 34 -> 34, of which waited for: 23 -> 23; matrix products, arithmetic and copies ran while one was open for 0% -> 0% of each run, Pallas kernels for 20% -> 18%
where the time goes in v6:
time: 103 us
  starting transfers between devices  43 us (42%)
  waiting for transfers between devices  32.7 us (32%)
  Pallas kernels  23.2 us (23%)
  local copies, waits for them, and re-layouts  2.84 us (3%)
    ppermute x34, starting transfers between devices, send(): return lax.ppermute(value, AXES, moves(group, dims))  43 us
    ppermute x34, waiting for transfers between devices, send(): return lax.ppermute(value, AXES, moves(group, dims))  32.7 us
    pallas_call x4, Pallas kernels, partial_sums(): pl.pallas_call(functools.partial(block_kernel, plan, n_in, parts, left_re...  22.7 us
    unnamed x10, local copies, waits for them, and re-layouts  2.84 us
  transfers between devices with their start and end apart: 34, of which 23 were waited for; matrix products, arithmetic and copies ran while one was open for 0% of the time, Pallas kernels for 18%

profile of v6, /device:TPU:0, one launch (start us, length us, event | category | flops | bytes accessed | tf_op | source)
XLA Modules:
  0.0 102.8 jit_solution(12473490602095602359)
XLA Ops:
  0.0 0.9 copy-done
  1.0 2.1 %collective-permute-start.4 = (bf16[160,768]{1,0:T(8,128)(2,1)S(1)}, bf16[160,768]{1,0:T(8,128)(2,1)S(1)}, u32[]{:S(2)}, u32[]{:S(2)}) collective-permute-start(bf16[160,768]{1,0:T(8,128)(2,1)S(1)} %split_coefs.1.refs_6_), channel_id=1, source_target_pairs={{0,2},{1,3},{2,0},{3,1},{4,6},{5,7},{6,4},{7,5},{8,10},{9,11},{10,... | collective-permute-start | bytes 737288 | tf_op jit(solution)/shard_map/ppermute | solution.py:48
  3.1 2.8 %collective-permute-start = (bf16[160,768]{1,0:T(8,128)(2,1)}, bf16[160,768]{1,0:T(8,128)(2,1)S(1)}, u32[]{:S(2)}, u32[]{:S(2)}) collective-permute-start(bf16[160,768]{1,0:T(8,128)(2,1)} %refs_0_), channel_id=1, source_target_pairs={{0,48},{1,49},{2,50},{3,51},{4,52},{5,53},{6,54},{7,55},{8,56},{9,... | collective-permute-start | bytes 737288 | tf_op jit(solution)/shard_map/ppermute | solution.py:48
  5.8 0.2 collective-permute-start.1
  6.1 3.0 %collective-permute-start.2 = (bf16[160,768]{1,0:T(8,128)(2,1)}, bf16[160,768]{1,0:T(8,128)(2,1)S(1)}, u32[]{:S(2)}, u32[]{:S(2)}) collective-permute-start(bf16[160,768]{1,0:T(8,128)(2,1)} %refs_1_), channel_id=1, source_target_pairs={{0,12},{1,13},{2,14},{3,15},{4,8},{5,9},{6,10},{7,11},{8,4},{9,5},... | collective-permute-start | bytes 737288 | tf_op jit(solution)/shard_map/ppermute | solution.py:48
  9.1 0.1 collective-permute-start.3
  9.2 0.9 copy-done.2
  10.2 0.9 copy-done.3
  11.2 0.8 collective-permute-done.refs_1_
  11.9 1.3 %collective-permute-done.1.refs_2_ = bf16[160,768]{1,0:T(8,128)(2,1)S(1)} collective-permute-done((bf16[160,768]{1,0:T(8,128)(2,1)}, bf16[160,768]{1,0:T(8,128)(2,1)S(1)}, u32[]{:S(2)}, u32[]{:S(2)}) %collective-permute-start.1) | collective-permute-done | bytes 245792 | tf_op jit(solution)/shard_map/ppermute | solution.py:48
  13.2 1.3 %collective-permute-done.2.refs_4_ = bf16[160,768]{1,0:T(8,128)(2,1)S(1)} collective-permute-done((bf16[160,768]{1,0:T(8,128)(2,1)}, bf16[160,768]{1,0:T(8,128)(2,1)S(1)}, u32[]{:S(2)}, u32[]{:S(2)}) %collective-permute-start.2) | collective-permute-done | bytes 245792 | tf_op jit(solution)/shard_map/ppermute | solution.py:48
  14.5 1.5 %collective-permute-done.3.refs_5_ = bf16[160,768]{1,0:T(8,128)(2,1)S(1)} collective-permute-done((bf16[160,768]{1,0:T(8,128)(2,1)}, bf16[160,768]{1,0:T(8,128)(2,1)S(1)}, u32[]{:S(2)}, u32[]{:S(2)}) %collective-permute-start.3) | collective-permute-done | bytes 245792 | tf_op jit(solution)/shard_map/ppermute | solution.py:48
  15.9 0.2 pairs.1
  16.1 1.8 %collective-permute-start.9 = (bf16[320,768]{1,0:T(8,128)(2,1)S(1)}, bf16[320,768]{1,0:T(8,128)(2,1)S(1)}, u32[]{:S(2)}, u32[]{:S(2)}) collective-permute-start(bf16[320,768]{1,0:T(8,128)(2,1)S(1)} %get-tuple-element.103.refs_4_.refs_2_.refs_9_), channel_id=1, source_target_pairs={{0,16},{1,17},{2,18},{3,19},{4,20},{5,21},{6,22},{7,23},{8,24},{9,... | collective-permute-start | bytes 1474568 | tf_op jit(solution)/shard_map/ppermute | solution.py:48
  17.9 0.3 collective-permute-start.6
  18.2 0.4 collective-permute-start.8
  18.6 1.2 %collective-permute-start.5 = (bf16[320,768]{1,0:T(8,128)(2,1)S(1)}, bf16[320,768]{1,0:T(8,128)(2,1)S(1)}, u32[]{:S(2)}, u32[]{:S(2)}) collective-permute-start(bf16[320,768]{1,0:T(8,128)(2,1)S(1)} %get-tuple-element.78.refs_0_.refs_18_), channel_id=1, source_target_pairs={{0,12},{1,13},{2,14},{3,15},{4,8},{5,9},{6,10},{7,11},{8,4},{9,5},... | collective-permute-start | bytes 1474568 | tf_op jit(solution)/shard_map/ppermute | solution.py:48
  19.8 3.8 %collective-permute-start.7 = (bf16[320,768]{1,0:T(8,128)(2,1)S(1)}, bf16[320,768]{1,0:T(8,128)(2,1)S(1)}, u32[]{:S(2)}, u32[]{:S(2)}) collective-permute-start(bf16[320,768]{1,0:T(8,128)(2,1)S(1)} %get-tuple-element.88.refs_19_), channel_id=1, source_target_pairs={{0,66},{1,67},{2,64},{3,65},{4,70},{5,71},{6,68},{7,69},{8,74},{9,... | collective-permute-start | bytes 1474568 | tf_op jit(solution)/shard_map/ppermute | solution.py:48
  23.6 3.6 %collective-permute-done.9.refs_5_.refs_4_ = bf16[320,768]{1,0:T(8,128)(2,1)S(1)} collective-permute-done((bf16[320,768]{1,0:T(8,128)(2,1)S(1)}, bf16[320,768]{1,0:T(8,128)(2,1)S(1)}, u32[]{:S(2)}, u32[]{:S(2)}) %collective-permute-start.9) | collective-permute-done | bytes 491552 | tf_op jit(solution)/shard_map/ppermute | solution.py:48
  27.1 1.4 %collective-permute-done.6.refs_3_.refs_1_.refs_5_.refs_0_ = bf16[320,768]{1,0:T(8,128)(2,1)S(1)} collective-permute-done((bf16[320,768]{1,0:T(8,128)(2,1)S(1)}, bf16[320,768]{1,0:T(8,128)(2,1)S(1)}, u32[]{:S(2)}, u32[]{:S(2)}) %collective-permute-start.6) | collective-permute-done | bytes 491552 | tf_op jit(solution)/shard_map/ppermute | solution.py:48
  28.5 0.2 collective-permute-done.8.refs_3_.refs_8_
  28.8 1.6 %collective-permute-done.5.refs_1_.refs_14_ = bf16[320,768]{1,0:T(8,128)(2,1)S(1)} collective-permute-done((bf16[320,768]{1,0:T(8,128)(2,1)S(1)}, bf16[320,768]{1,0:T(8,128)(2,1)S(1)}, u32[]{:S(2)}, u32[]{:S(2)}) %collective-permute-start.5) | collective-permute-done | bytes 491552 | tf_op jit(solution)/shard_map/ppermute | solution.py:48
  30.3 1.8 %collective-permute-done.7.refs_17_ = bf16[320,768]{1,0:T(8,128)(2,1)S(1)} collective-permute-done((bf16[320,768]{1,0:T(8,128)(2,1)S(1)}, bf16[320,768]{1,0:T(8,128)(2,1)S(1)}, u32[]{:S(2)}, u32[]{:S(2)}) %collective-permute-start.7) | collective-permute-done | bytes 491552 | tf_op jit(solution)/shard_map/ppermute | solution.py:48
  32.2 1.1 %collective-permute-start.14 = (bf16[320,768]{1,0:T(8,128)(2,1)S(1)}, bf16[320,768]{1,0:T(8,128)(2,1)S(1)}, u32[]{:S(2)}, u32[]{:S(2)}) collective-permute-start(bf16[320,768]{1,0:T(8,128)(2,1)S(1)} %get-tuple-element.103.refs_4_.refs_2_.refs_9_), channel_id=1, source_target_pairs={{0,4},{1,5},{2,6},{3,7},{4,0},{5,1},{6,2},{7,3},{8,12},{9,13},{10,... | collective-permute-start | bytes 1474568 | tf_op jit(solution)/shard_map/ppermute | solution.py:48
  33.3 0.4 collective-permute-start.13
  33.7 1.0 collective-permute-start.12
  34.7 0.1 turn.1
  34.8 3.0 %collective-permute-start.10 = (bf16[320,768]{1,0:T(8,128)(2,1)S(1)}, bf16[320,768]{1,0:T(8,128)(2,1)S(1)}, u32[]{:S(2)}, u32[]{:S(2)}) collective-permute-start(bf16[320,768]{1,0:T(8,128)(2,1)S(1)} %get-tuple-element.85), channel_id=1, source_target_pairs={{0,66},{1,67},{2,64},{3,65},{4,70},{5,71},{6,68},{7,69},{8,74},{9,... | collective-permute-start | bytes 1474568 | tf_op jit(solution)/shard_map/ppermute | solution.py:48
  37.8 0.2 four.1
  38.0 3.8 %collective-permute-done.14.refs_6_ = bf16[320,768]{1,0:T(8,128)(2,1)S(1)} collective-permute-done((bf16[320,768]{1,0:T(8,128)(2,1)S(1)}, bf16[320,768]{1,0:T(8,128)(2,1)S(1)}, u32[]{:S(2)}, u32[]{:S(2)}) %collective-permute-start.14) | collective-permute-done | bytes 491552 | tf_op jit(solution)/shard_map/ppermute | solution.py:48
  41.9 0.6 collective-permute-done.13.refs_3_.refs_1_
  42.5 1.4 %collective-permute-done.12.refs_15_ = bf16[320,768]{1,0:T(8,128)(2,1)S(1)} collective-permute-done((bf16[320,768]{1,0:T(8,128)(2,1)S(1)}, bf16[320,768]{1,0:T(8,128)(2,1)S(1)}, u32[]{:S(2)}, u32[]{:S(2)}) %collective-permute-start.12) | collective-permute-done | bytes 491552 | tf_op jit(solution)/shard_map/ppermute | solution.py:48
  43.8 1.1 %collective-permute-done.10.refs_16_ = bf16[320,768]{1,0:T(8,128)(2,1)S(1)} collective-permute-done((bf16[320,768]{1,0:T(8,128)(2,1)S(1)}, bf16[320,768]{1,0:T(8,128)(2,1)S(1)}, u32[]{:S(2)}, u32[]{:S(2)}) %collective-permute-start.10) | collective-permute-done | bytes 491552 | tf_op jit(solution)/shard_map/ppermute | solution.py:48
  44.9 1.7 %collective-permute-done.11.refs_7_ = bf16[320,768]{1,0:T(8,128)(2,1)S(1)} collective-permute-done((bf16[320,768]{1,0:T(8,128)(2,1)S(1)}, bf16[320,768]{1,0:T(8,128)(2,1)S(1)}, u32[]{:S(2)}, u32[]{:S(2)}) %collective-permute-start.11) | collective-permute-done | bytes 491552 | tf_op jit(solution)/shard_map/ppermute | solution.py:48
  46.7 0.5 collective-permute-start.16
  47.2 0.0 collective-permute-start.17
  47.2 1.3 %collective-permute-done.15.refs_13_ = bf16[320,768]{1,0:T(8,128)(2,1)S(1)} collective-permute-done((bf16[320,768]{1,0:T(8,128)(2,1)S(1)}, bf16[320,768]{1,0:T(8,128)(2,1)S(1)}, u32[]{:S(2)}, u32[]{:S(2)}) %collective-permute-start.15) | collective-permute-done | bytes 491552 | tf_op jit(solution)/shard_map/ppermute | solution.py:48
  48.5 0.7 collective-permute-done.16.refs_11_.refs_7_
  49.2 0.7 collective-permute-done.17.refs_12_
  49.9 0.1 collective-permute-start.18
  50.1 0.7 collective-permute-start.21
  50.8 2.6 %collective-permute-start.26 = (bf16[320,768]{1,0:T(8,128)(2,1)S(1)}, bf16[320,768]{1,0:T(8,128)(2,1)S(1)}, u32[]{:S(2)}, u32[]{:S(2)}) collective-permute-start(bf16[320,768]{1,0:T(8,128)(2,1)S(1)} %collective-permute-done.7.refs_17_), channel_id=1, source_target_pairs={{0,48},{1,49},{2,50},{3,51},{4,52},{5,53},{6,54},{7,55},{8,56},{9,... | collective-permute-start | bytes 1474568 | tf_op jit(solution)/shard_map/ppermute | solution.py:48
  53.4 1.2 %collective-permute-start.25 = (bf16[320,768]{1,0:T(8,128)(2,1)S(1)}, bf16[320,768]{1,0:T(8,128)(2,1)S(1)}, u32[]{:S(2)}, u32[]{:S(2)}) collective-permute-start(bf16[320,768]{1,0:T(8,128)(2,1)S(1)} %get-tuple-element.111), channel_id=1, source_target_pairs={{0,66},{1,67},{2,64},{3,65},{4,70},{5,71},{6,68},{7,69},{8,74},{9,... | collective-permute-start | bytes 1474568 | tf_op jit(solution)/shard_map/ppermute | solution.py:48
  54.6 0.7 collective-permute-done.18.refs_10_.refs_6_
  55.3 1.1 %collective-permute-start.19 = (bf16[320,768]{1,0:T(8,128)(2,1)S(1)}, bf16[320,768]{1,0:T(8,128)(2,1)S(1)}, u32[]{:S(2)}, u32[]{:S(2)}) collective-permute-start(bf16[320,768]{1,0:T(8,128)(2,1)S(1)} %collective-permute-done.9.refs_5_.refs_4_), channel_id=1, source_target_pairs={{0,4},{1,5},{2,6},{3,7},{4,0},{5,1},{6,2},{7,3},{8,12},{9,13},{10,... | collective-permute-start | bytes 1474568 | tf_op jit(solution)/shard_map/ppermute | solution.py:48
  56.4 10.4 %early.1 = (f32[960,384]{1,0:T(8,128)S(1)}, bf16[1600,1536]{1,0:T(8,128)(2,1)S(1)}, bf16[1600,768]{1,0:T(8,128)(2,1)S(1)}, bf16[960,1536]{1,0:T(8,128)(2,1)S(1)}) custom-call(bf16[320,768]{1,0:T(8,128)(2,1)S(1)} %get-tuple-element.79.refs_2_.refs_0_, bf16[320,768]{1,0:T(8,128)(2,1)S(1)} %get-tuple-element.90.refs_2_.refs_1_, ...), custom_call_target="tpu_custom_call" | custom-call | flops 8294400000 | bytes 1000000 | tf_op jit(solution)/shard_map/early/pallas_call | solution.py:205
  66.9 0.1 collective-permute-start.24
  67.0 0.5 collective-permute-start.23
  67.5 1.1 %collective-permute-done.19.refs_2_ = bf16[320,768]{1,0:T(8,128)(2,1)S(1)} collective-permute-done((bf16[320,768]{1,0:T(8,128)(2,1)S(1)}, bf16[320,768]{1,0:T(8,128)(2,1)S(1)}, u32[]{:S(2)}, u32[]{:S(2)}) %collective-permute-start.19) | collective-permute-done | bytes 491552 | tf_op jit(solution)/shard_map/ppermute | solution.py:48
  68.6 3.8 %early_right.1 = (f32[320,384]{1,0:T(8,128)S(1)}, bf16[320,1536]{1,0:T(8,128)(2,1)S(1)}) custom-call(bf16[320,768]{1,0:T(8,128)(2,1)S(1)} %collective-permute-done.25.refs_0_, bf16[320,768]{1,0:T(8,128)(2,1)S(1)} %collective-permute-done.26.refs_1_, bf16[1600,1536]{1,0:T(8,128)(2,1)S(1)} %get-tuple-element.114.refs_2_, ...), custom_call_target="tpu_custom_call" | custom-call | flops 2764800000 | bytes 1000000 | tf_op jit(solution)/shard_map/early_right/pallas_call | solution.py:205
  72.4 4.2 %second_far.1 = (f32[160,345]{1,0:T(8,128)S(1)}, f32[160,345]{1,0:T(8,128)S(1)}, f32[160,345]{1,0:T(8,128)S(1)}, f32[160,345]{1,0:T(8,128)S(1)}, bf16[960,1536]{...) custom-call(bf16[320,768]{1,0:T(8,128)(2,1)S(1)} %collective-permute-done.6.refs_3_.refs_1_.refs_5_.refs_0_, ...), custom_call_target="tpu_custom_call" | custom-call | flops 3317760000 | bytes 1000000 | tf_op jit(solution)/shard_map/second_far/pallas_call | solution.py:205
  76.7 1.3 %collective-permute-start.28 = (f32[160,345]{1,0:T(8,128)S(1)}, f32[160,345]{1,0:T(8,128)S(1)}, u32[]{:S(2)}, u32[]{:S(2)}) collective-permute-start(f32[160,345]{1,0:T(8,128)S(1)} %get-tuple-element.120), channel_id=1, source_target_pairs={{0,66},{1,67},{2,64},{3,65},{4,70},{5,71},{6,68},{7,69},{8,74},{9,... | collective-permute-start | bytes 662408 | tf_op jit(solution)/shard_map/ppermute | solution.py:48
  78.0 2.2 %collective-permute-start.30 = (f32[160,345]{1,0:T(8,128)S(1)}, f32[160,345]{1,0:T(8,128)S(1)}, u32[]{:S(2)}, u32[]{:S(2)}) collective-permute-start(f32[160,345]{1,0:T(8,128)S(1)} %get-tuple-element.128), channel_id=1, source_target_pairs={{0,48},{1,49},{2,50},{3,51},{4,52},{5,53},{6,54},{7,55},{8,56},{9,... | collective-permute-start | bytes 662408 | tf_op jit(solution)/shard_map/ppermute | solution.py:48
  80.2 1.4 %collective-permute-start.32 = (f32[160,345]{1,0:T(8,128)S(1)}, f32[160,345]{1,0:T(8,128)S(1)}, u32[]{:S(2)}, u32[]{:S(2)}) collective-permute-start(f32[160,345]{1,0:T(8,128)S(1)} %get-tuple-element.131), channel_id=1, source_target_pairs={{0,12},{1,13},{2,14},{3,15},{4,8},{5,9},{6,10},{7,11},{8,4},{9,5},... | collective-permute-start | bytes 662408 | tf_op jit(solution)/shard_map/ppermute | solution.py:48
  81.6 3.7 %collective-permute-start.27 = (f32[160,345]{1,0:T(8,128)S(1)}, f32[160,345]{1,0:T(8,128)S(1)}, u32[]{:S(2)}, u32[]{:S(2)}) collective-permute-start(f32[160,345]{1,0:T(8,128)S(1)} %get-tuple-element.124), channel_id=1, source_target_pairs={{0,126},{1,127},{2,124},{3,125},{4,122},{5,123},{6,120},{7,121},{8... | collective-permute-start | bytes 662408 | tf_op jit(solution)/shard_map/ppermute | solution.py:48
  85.3 4.2 %second_near.1 = (f32[160,345]{1,0:T(8,128)S(1)}, f32[160,345]{1,0:T(8,128)S(1)}, f32[160,345]{1,0:T(8,128)S(1)}, f32[160,345]{1,0:T(8,128)S(1)}) custom-call(bf16[960,1536]{1,0:T(8,128)(2,1)S(1)} %get-tuple-element.121.refs_0_, bf16[960,768]{1,0:T(8,128)(2,1)S(1)} %get-tuple-element.122.refs_1_, bf16[960,1536]{1,0:T(8,128)(2,1)S(1)} %get-tuple-element.118.refs_13_.refs_2_, ...), custom_call_target="tpu_custom_call" | custom-call | flops 3317760000 | bytes 1000000 | tf_op jit(solution)/shard_map/second_near/pallas_call | solution.py:205
  89.6 2.3 %collective-permute-start.29 = (f32[160,345]{1,0:T(8,128)S(1)}, f32[160,345]{1,0:T(8,128)S(1)}, u32[]{:S(2)}, u32[]{:S(2)}) collective-permute-start(f32[160,345]{1,0:T(8,128)S(1)} %add.26), channel_id=1, source_target_pairs={{0,48},{1,49},{2,50},{3,51},{4,52},{5,53},{6,54},{7,55},{8,56},{9,... | collective-permute-start | bytes 662408 | tf_op jit(solution)/shard_map/ppermute | solution.py:48
  92.0 1.5 %collective-permute-start.31 = (f32[160,345]{1,0:T(8,128)S(1)}, f32[160,345]{1,0:T(8,128)S(1)}, u32[]{:S(2)}, u32[]{:S(2)}) collective-permute-start(f32[160,345]{1,0:T(8,128)S(1)} %add.28), channel_id=1, source_target_pairs={{0,12},{1,13},{2,14},{3,15},{4,8},{5,9},{6,10},{7,11},{8,4},{9,5},... | collective-permute-start | bytes 662408 | tf_op jit(solution)/shard_map/ppermute | solution.py:48
  93.5 1.0 collective-permute-done.32
  94.5 2.4 %collective-permute-start.33 = (f32[160,345]{1,0:T(8,128)S(1)}, f32[160,345]{1,0:T(8,128)S(1)}, u32[]{:S(2)}, u32[]{:S(2)}) collective-permute-start(f32[160,345]{1,0:T(8,128)S(1)} %add.30), channel_id=1, source_target_pairs={{0,66},{1,67},{2,64},{3,65},{4,70},{5,71},{6,68},{7,69},{8,74},{9,... | collective-permute-start | bytes 662408 | tf_op jit(solution)/shard_map/ppermute | solution.py:48
  96.9 1.5 %collective-permute-done.29 = f32[160,345]{1,0:T(8,128)S(1)} collective-permute-done((f32[160,345]{1,0:T(8,128)S(1)}, f32[160,345]{1,0:T(8,128)S(1)}, u32[]{:S(2)}, u32[]{:S(2)}) %collective-permute-start.29) | collective-permute-done | bytes 220832 | tf_op jit(solution)/shard_map/ppermute | solution.py:48
  98.4 1.8 %collective-permute-done.31 = f32[160,345]{1,0:T(8,128)S(1)} collective-permute-done((f32[160,345]{1,0:T(8,128)S(1)}, f32[160,345]{1,0:T(8,128)S(1)}, u32[]{:S(2)}, u32[]{:S(2)}) %collective-permute-start.31) | collective-permute-done | bytes 220832 | tf_op jit(solution)/shard_map/ppermute | solution.py:48
  100.2 1.8 %collective-permute-done.33 = f32[160,345]{1,0:T(8,128)S(1)} collective-permute-done((f32[160,345]{1,0:T(8,128)S(1)}, f32[160,345]{1,0:T(8,128)S(1)}, u32[]{:S(2)}, u32[]{:S(2)}) %collective-permute-start.33) | collective-permute-done | bytes 220832 | tf_op jit(solution)/shard_map/ppermute | solution.py:48
  102.0 0.8 add_bitcast_fusion
  (27 shorter events, 0.2 us)
Async XLA Ops:
  0.0 0.9 copy-start
  1.0 10.1 %collective-permute-start.4 = (bf16[160,768]{1,0:T(8,128)(2,1)S(1)}, bf16[160,768]{1,0:T(8,128)(2,1)S(1)}, u32[]{:S(2)}, u32[]{:S(2)}) collective-permute-start(bf16[160,768]{1,0:T(8,128)(2,1)S(1)} %split_coefs.1.refs_6_), channel_id=1, source_target_pairs={{0,2},{1,3},{2,0},{3,1},{4,6},{5,7},{6,4},{7,5},{8,10},{9,11},{10,... | collective-permute-start | bytes 737288 | tf_op jit(solution)/shard_map/ppermute | solution.py:48
  3.1 8.8 %collective-permute-start = (bf16[160,768]{1,0:T(8,128)(2,1)}, bf16[160,768]{1,0:T(8,128)(2,1)S(1)}, u32[]{:S(2)}, u32[]{:S(2)}) collective-permute-start(bf16[160,768]{1,0:T(8,128)(2,1)} %refs_0_), channel_id=1, source_target_pairs={{0,48},{1,49},{2,50},{3,51},{4,52},{5,53},{6,54},{7,55},{8,56},{9,... | collective-permute-start | bytes 737288 | tf_op jit(solution)/shard_map/ppermute | solution.py:48
  5.8 7.3 %collective-permute-start.1 = (bf16[160,768]{1,0:T(8,128)(2,1)}, bf16[160,768]{1,0:T(8,128)(2,1)S(1)}, u32[]{:S(2)}, u32[]{:S(2)}) collective-permute-start(bf16[160,768]{1,0:T(8,128)(2,1)} %refs_0_), channel_id=1, source_target_pairs={{0,16},{1,17},{2,18},{3,19},{4,20},{5,21},{6,22},{7,23},{8,24},{9,... | collective-permute-start | bytes 737288 | tf_op jit(solution)/shard_map/ppermute | solution.py:48
  6.1 8.4 %collective-permute-start.2 = (bf16[160,768]{1,0:T(8,128)(2,1)}, bf16[160,768]{1,0:T(8,128)(2,1)S(1)}, u32[]{:S(2)}, u32[]{:S(2)}) collective-permute-start(bf16[160,768]{1,0:T(8,128)(2,1)} %refs_1_), channel_id=1, source_target_pairs={{0,12},{1,13},{2,14},{3,15},{4,8},{5,9},{6,10},{7,11},{8,4},{9,5},... | collective-permute-start | bytes 737288 | tf_op jit(solution)/shard_map/ppermute | solution.py:48
  9.1 6.8 %collective-permute-start.3 = (bf16[160,768]{1,0:T(8,128)(2,1)}, bf16[160,768]{1,0:T(8,128)(2,1)S(1)}, u32[]{:S(2)}, u32[]{:S(2)}) collective-permute-start(bf16[160,768]{1,0:T(8,128)(2,1)} %refs_1_), channel_id=1, source_target_pairs={{0,4},{1,5},{2,6},{3,7},{4,0},{5,1},{6,2},{7,3},{8,12},{9,13},{10,... | collective-permute-start | bytes 737288 | tf_op jit(solution)/shard_map/ppermute | solution.py:48
  9.2 0.9 copy-start.2
  10.2 0.9 copy-start.3
  16.1 11.1 %collective-permute-start.9 = (bf16[320,768]{1,0:T(8,128)(2,1)S(1)}, bf16[320,768]{1,0:T(8,128)(2,1)S(1)}, u32[]{:S(2)}, u32[]{:S(2)}) collective-permute-start(bf16[320,768]{1,0:T(8,128)(2,1)S(1)} %get-tuple-element.103.refs_4_.refs_2_.refs_9_), channel_id=1, source_target_pairs={{0,16},{1,17},{2,18},{3,19},{4,20},{5,21},{6,22},{7,23},{8,24},{9,... | collective-permute-start | bytes 1474568 | tf_op jit(solution)/shard_map/ppermute | solution.py:48
  17.9 10.6 %collective-permute-start.6 = (bf16[320,768]{1,0:T(8,128)(2,1)S(1)}, bf16[320,768]{1,0:T(8,128)(2,1)S(1)}, u32[]{:S(2)}, u32[]{:S(2)}) collective-permute-start(bf16[320,768]{1,0:T(8,128)(2,1)S(1)} %get-tuple-element.79.refs_2_.refs_0_), channel_id=1, source_target_pairs={{0,4},{1,5},{2,6},{3,7},{4,0},{5,1},{6,2},{7,3},{8,12},{9,13},{10,... | collective-permute-start | bytes 1474568 | tf_op jit(solution)/shard_map/ppermute | solution.py:48
  18.2 10.5 %collective-permute-start.8 = (bf16[320,768]{1,0:T(8,128)(2,1)S(1)}, bf16[320,768]{1,0:T(8,128)(2,1)S(1)}, u32[]{:S(2)}, u32[]{:S(2)}) collective-permute-start(bf16[320,768]{1,0:T(8,128)(2,1)S(1)} %get-tuple-element.90.refs_2_.refs_1_), channel_id=1, source_target_pairs={{0,2},{1,3},{2,0},{3,1},{4,6},{5,7},{6,4},{7,5},{8,10},{9,11},{10,... | collective-permute-start | bytes 1474568 | tf_op jit(solution)/shard_map/ppermute | solution.py:48
  18.6 11.7 %collective-permute-start.5 = (bf16[320,768]{1,0:T(8,128)(2,1)S(1)}, bf16[320,768]{1,0:T(8,128)(2,1)S(1)}, u32[]{:S(2)}, u32[]{:S(2)}) collective-permute-start(bf16[320,768]{1,0:T(8,128)(2,1)S(1)} %get-tuple-element.78.refs_0_.refs_18_), channel_id=1, source_target_pairs={{0,12},{1,13},{2,14},{3,15},{4,8},{5,9},{6,10},{7,11},{8,4},{9,5},... | collective-permute-start | bytes 1474568 | tf_op jit(solution)/shard_map/ppermute | solution.py:48
  19.8 12.4 %collective-permute-start.7 = (bf16[320,768]{1,0:T(8,128)(2,1)S(1)}, bf16[320,768]{1,0:T(8,128)(2,1)S(1)}, u32[]{:S(2)}, u32[]{:S(2)}) collective-permute-start(bf16[320,768]{1,0:T(8,128)(2,1)S(1)} %get-tuple-element.88.refs_19_), channel_id=1, source_target_pairs={{0,66},{1,67},{2,64},{3,65},{4,70},{5,71},{6,68},{7,69},{8,74},{9,... | collective-permute-start | bytes 1474568 | tf_op jit(solution)/shard_map/ppermute | solution.py:48
  32.2 9.7 %collective-permute-start.14 = (bf16[320,768]{1,0:T(8,128)(2,1)S(1)}, bf16[320,768]{1,0:T(8,128)(2,1)S(1)}, u32[]{:S(2)}, u32[]{:S(2)}) collective-permute-start(bf16[320,768]{1,0:T(8,128)(2,1)S(1)} %get-tuple-element.103.refs_4_.refs_2_.refs_9_), channel_id=1, source_target_pairs={{0,4},{1,5},{2,6},{3,7},{4,0},{5,1},{6,2},{7,3},{8,12},{9,13},{10,... | collective-permute-start | bytes 1474568 | tf_op jit(solution)/shard_map/ppermute | solution.py:48
  33.3 9.2 %collective-permute-start.13 = (bf16[320,768]{1,0:T(8,128)(2,1)S(1)}, bf16[320,768]{1,0:T(8,128)(2,1)S(1)}, u32[]{:S(2)}, u32[]{:S(2)}) collective-permute-start(bf16[320,768]{1,0:T(8,128)(2,1)S(1)} %get-tuple-element.90.refs_2_.refs_1_), channel_id=1, source_target_pairs={{0,16},{1,17},{2,18},{3,19},{4,20},{5,21},{6,22},{7,23},{8,24},{9,... | collective-permute-start | bytes 1474568 | tf_op jit(solution)/shard_map/ppermute | solution.py:48
  33.7 10.2 %collective-permute-start.12 = (bf16[320,768]{1,0:T(8,128)(2,1)S(1)}, bf16[320,768]{1,0:T(8,128)(2,1)S(1)}, u32[]{:S(2)}, u32[]{:S(2)}) collective-permute-start(bf16[320,768]{1,0:T(8,128)(2,1)S(1)} %get-tuple-element.88.refs_19_), channel_id=1, source_target_pairs={{0,48},{1,49},{2,50},{3,51},{4,52},{5,53},{6,54},{7,55},{8,56},{9,... | collective-permute-start | bytes 1474568 | tf_op jit(solution)/shard_map/ppermute | solution.py:48
  34.8 10.1 %collective-permute-start.10 = (bf16[320,768]{1,0:T(8,128)(2,1)S(1)}, bf16[320,768]{1,0:T(8,128)(2,1)S(1)}, u32[]{:S(2)}, u32[]{:S(2)}) collective-permute-start(bf16[320,768]{1,0:T(8,128)(2,1)S(1)} %get-tuple-element.85), channel_id=1, source_target_pairs={{0,66},{1,67},{2,64},{3,65},{4,70},{5,71},{6,68},{7,69},{8,74},{9,... | collective-permute-start | bytes 1474568 | tf_op jit(solution)/shard_map/ppermute | solution.py:48
  37.8 8.8 %collective-permute-start.11 = (bf16[320,768]{1,0:T(8,128)(2,1)S(1)}, bf16[320,768]{1,0:T(8,128)(2,1)S(1)}, u32[]{:S(2)}, u32[]{:S(2)}) collective-permute-start(bf16[320,768]{1,0:T(8,128)(2,1)S(1)} %get-tuple-element.86), channel_id=1, source_target_pairs={{0,2},{1,3},{2,0},{3,1},{4,6},{5,7},{6,4},{7,5},{8,10},{9,11},{10,... | collective-permute-start | bytes 1474568 | tf_op jit(solution)/shard_map/ppermute | solution.py:48
  46.7 1.9 %collective-permute-start.15 = (bf16[320,768]{1,0:T(8,128)(2,1)S(1)}, bf16[320,768]{1,0:T(8,128)(2,1)S(1)}, u32[]{:S(2)}, u32[]{:S(2)}) collective-permute-start(bf16[320,768]{1,0:T(8,128)(2,1)S(1)} %collective-permute-done.11.refs_7_), channel_id=1, source_target_pairs={{0,1},{1,0},{2,3},{3,2},{4,5},{5,4},{6,7},{7,6},{8,9},{9,8},{10,11... | collective-permute-start | bytes 1474568 | tf_op jit(solution)/shard_map/ppermute | solution.py:48
  46.7 2.6 %collective-permute-start.16 = (bf16[320,768]{1,0:T(8,128)(2,1)S(1)}, bf16[320,768]{1,0:T(8,128)(2,1)S(1)}, u32[]{:S(2)}, u32[]{:S(2)}) collective-permute-start(bf16[320,768]{1,0:T(8,128)(2,1)S(1)} %collective-permute-done.13.refs_3_.refs_1_), channel_id=1, source_target_pairs={{0,1},{1,0},{2,3},{3,2},{4,5},{5,4},{6,7},{7,6},{8,9},{9,8},{10,11... | collective-permute-start | bytes 1474568 | tf_op jit(solution)/shard_map/ppermute | solution.py:48
  47.2 2.8 %collective-permute-start.17 = (bf16[320,768]{1,0:T(8,128)(2,1)S(1)}, bf16[320,768]{1,0:T(8,128)(2,1)S(1)}, u32[]{:S(2)}, u32[]{:S(2)}) collective-permute-start(bf16[320,768]{1,0:T(8,128)(2,1)S(1)} %collective-permute-done.14.refs_6_), channel_id=1, source_target_pairs={{0,1},{1,0},{2,3},{3,2},{4,5},{5,4},{6,7},{7,6},{8,9},{9,8},{10,11... | collective-permute-start | bytes 1474568 | tf_op jit(solution)/shard_map/ppermute | solution.py:48
  49.9 5.4 %collective-permute-start.18 = (bf16[640,2304]{1,0:T(8,128)(2,1)S(1)}, bf16[640,2304]{1,0:T(8,128)(2,1)S(1)}, u32[]{:S(2)}, u32[]{:S(2)}) collective-permute-start(bf16[640,2304]{1,0:T(8,128)(2,1)S(1)} %four.1), channel_id=1, source_target_pairs={{0,1},{1,0},{2,3},{3,2},{4,5},{5,4},{6,7},{7,6},{8,9},{9,8},{10,11... | collective-permute-start | bytes 8847368 | tf_op jit(solution)/shard_map/ppermute | solution.py:48
  50.1 16.8 %collective-permute-start.21 = (bf16[320,768]{1,0:T(8,128)(2,1)S(1)}, bf16[320,768]{1,0:T(8,128)(2,1)S(1)}, u32[]{:S(2)}, u32[]{:S(2)}) collective-permute-start(bf16[320,768]{1,0:T(8,128)(2,1)S(1)} %collective-permute-done.8.refs_3_.refs_8_), channel_id=1, source_target_pairs={{0,16},{1,17},{2,18},{3,19},{4,20},{5,21},{6,22},{7,23},{8,24},{9,... | collective-permute-start | bytes 1474568 | tf_op jit(solution)/shard_map/ppermute | solution.py:48
  50.7 16.2 %collective-permute-start.20 = (bf16[320,768]{1,0:T(8,128)(2,1)S(1)}, bf16[320,768]{1,0:T(8,128)(2,1)S(1)}, u32[]{:S(2)}, u32[]{:S(2)}) collective-permute-start(bf16[320,768]{1,0:T(8,128)(2,1)S(1)} %get-tuple-element.101), channel_id=1, source_target_pairs={{0,2},{1,3},{2,0},{3,1},{4,6},{5,7},{6,4},{7,5},{8,10},{9,11},{10,... | collective-permute-start | bytes 1474568 | tf_op jit(solution)/shard_map/ppermute | solution.py:48
  50.8 17.8 %collective-permute-start.26 = (bf16[320,768]{1,0:T(8,128)(2,1)S(1)}, bf16[320,768]{1,0:T(8,128)(2,1)S(1)}, u32[]{:S(2)}, u32[]{:S(2)}) collective-permute-start(bf16[320,768]{1,0:T(8,128)(2,1)S(1)} %collective-permute-done.7.refs_17_), channel_id=1, source_target_pairs={{0,48},{1,49},{2,50},{3,51},{4,52},{5,53},{6,54},{7,55},{8,56},{9,... | collective-permute-start | bytes 1474568 | tf_op jit(solution)/shard_map/ppermute | solution.py:48
  53.4 15.2 %collective-permute-start.25 = (bf16[320,768]{1,0:T(8,128)(2,1)S(1)}, bf16[320,768]{1,0:T(8,128)(2,1)S(1)}, u32[]{:S(2)}, u32[]{:S(2)}) collective-permute-start(bf16[320,768]{1,0:T(8,128)(2,1)S(1)} %get-tuple-element.111), channel_id=1, source_target_pairs={{0,66},{1,67},{2,64},{3,65},{4,70},{5,71},{6,68},{7,69},{8,74},{9,... | collective-permute-start | bytes 1474568 | tf_op jit(solution)/shard_map/ppermute | solution.py:48
  55.3 13.3 %collective-permute-start.19 = (bf16[320,768]{1,0:T(8,128)(2,1)S(1)}, bf16[320,768]{1,0:T(8,128)(2,1)S(1)}, u32[]{:S(2)}, u32[]{:S(2)}) collective-permute-start(bf16[320,768]{1,0:T(8,128)(2,1)S(1)} %collective-permute-done.9.refs_5_.refs_4_), channel_id=1, source_target_pairs={{0,4},{1,5},{2,6},{3,7},{4,0},{5,1},{6,2},{7,3},{8,12},{9,13},{10,... | collective-permute-start | bytes 1474568 | tf_op jit(solution)/shard_map/ppermute | solution.py:48
  66.9 5.5 %collective-permute-start.24 = (bf16[320,768]{1,0:T(8,128)(2,1)S(1)}, bf16[320,768]{1,0:T(8,128)(2,1)S(1)}, u32[]{:S(2)}, u32[]{:S(2)}) collective-permute-start(bf16[320,768]{1,0:T(8,128)(2,1)S(1)} %collective-permute-done.21.refs_4_), channel_id=1, source_target_pairs={{0,1},{1,0},{2,3},{3,2},{4,5},{5,4},{6,7},{7,6},{8,9},{9,8},{10,11... | collective-permute-start | bytes 1474568 | tf_op jit(solution)/shard_map/ppermute | solution.py:48
  67.0 5.4 %collective-permute-start.23 = (bf16[320,768]{1,0:T(8,128)(2,1)S(1)}, bf16[320,768]{1,0:T(8,128)(2,1)S(1)}, u32[]{:S(2)}, u32[]{:S(2)}) collective-permute-start(bf16[320,768]{1,0:T(8,128)(2,1)S(1)} %collective-permute-done.20.refs_3_), channel_id=1, source_target_pairs={{0,1},{1,0},{2,3},{3,2},{4,5},{5,4},{6,7},{7,6},{8,9},{9,8},{10,11... | collective-permute-start | bytes 1474568 | tf_op jit(solution)/shard_map/ppermute | solution.py:48
  68.6 3.8 %collective-permute-start.22 = (bf16[320,768]{1,0:T(8,128)(2,1)S(1)}, bf16[320,768]{1,0:T(8,128)(2,1)S(1)}, u32[]{:S(2)}, u32[]{:S(2)}) collective-permute-start(bf16[320,768]{1,0:T(8,128)(2,1)S(1)} %collective-permute-done.19.refs_2_), channel_id=1, source_target_pairs={{0,1},{1,0},{2,3},{3,2},{4,5},{5,4},{6,7},{7,6},{8,9},{9,8},{10,11... | collective-permute-start | bytes 1474568 | tf_op jit(solution)/shard_map/ppermute | solution.py:48
  76.7 12.9 %collective-permute-start.28 = (f32[160,345]{1,0:T(8,128)S(1)}, f32[160,345]{1,0:T(8,128)S(1)}, u32[]{:S(2)}, u32[]{:S(2)}) collective-permute-start(f32[160,345]{1,0:T(8,128)S(1)} %get-tuple-element.120), channel_id=1, source_target_pairs={{0,66},{1,67},{2,64},{3,65},{4,70},{5,71},{6,68},{7,69},{8,74},{9,... | collective-permute-start | bytes 662408 | tf_op jit(solution)/shard_map/ppermute | solution.py:48
  78.0 14.0 %collective-permute-start.30 = (f32[160,345]{1,0:T(8,128)S(1)}, f32[160,345]{1,0:T(8,128)S(1)}, u32[]{:S(2)}, u32[]{:S(2)}) collective-permute-start(f32[160,345]{1,0:T(8,128)S(1)} %get-tuple-element.128), channel_id=1, source_target_pairs={{0,48},{1,49},{2,50},{3,51},{4,52},{5,53},{6,54},{7,55},{8,56},{9,... | collective-permute-start | bytes 662408 | tf_op jit(solution)/shard_map/ppermute | solution.py:48
  80.2 14.3 %collective-permute-start.32 = (f32[160,345]{1,0:T(8,128)S(1)}, f32[160,345]{1,0:T(8,128)S(1)}, u32[]{:S(2)}, u32[]{:S(2)}) collective-permute-start(f32[160,345]{1,0:T(8,128)S(1)} %get-tuple-element.131), channel_id=1, source_target_pairs={{0,12},{1,13},{2,14},{3,15},{4,8},{5,9},{6,10},{7,11},{8,4},{9,5},... | collective-permute-start | bytes 662408 | tf_op jit(solution)/shard_map/ppermute | solution.py:48
  81.6 15.2 %collective-permute-start.27 = (f32[160,345]{1,0:T(8,128)S(1)}, f32[160,345]{1,0:T(8,128)S(1)}, u32[]{:S(2)}, u32[]{:S(2)}) collective-permute-start(f32[160,345]{1,0:T(8,128)S(1)} %get-tuple-element.124), channel_id=1, source_target_pairs={{0,126},{1,127},{2,124},{3,125},{4,122},{5,123},{6,120},{7,121},{8... | collective-permute-start | bytes 662408 | tf_op jit(solution)/shard_map/ppermute | solution.py:48
  85.3 16.7 %copy-start.1 = (f32[345,160]{0,1:T(8,128)S(1)}, f32[345,160]{0,1:T(8,128)}, u32[]{:S(2)}) copy-start(f32[345,160]{0,1:T(8,128)} %param.7) | copy-start | bytes 662404
  85.3 16.7 %copy-start.4 = (s32[160]{0:T(256)S(1)}, s32[160]{0:T(256)}, u32[]{:S(2)}) copy-start(s32[160]{0:T(256)} %param.6) | copy-start | bytes 1924
  89.6 8.8 %collective-permute-start.29 = (f32[160,345]{1,0:T(8,128)S(1)}, f32[160,345]{1,0:T(8,128)S(1)}, u32[]{:S(2)}, u32[]{:S(2)}) collective-permute-start(f32[160,345]{1,0:T(8,128)S(1)} %add.26), channel_id=1, source_target_pairs={{0,48},{1,49},{2,50},{3,51},{4,52},{5,53},{6,54},{7,55},{8,56},{9,... | collective-permute-start | bytes 662408 | tf_op jit(solution)/shard_map/ppermute | solution.py:48
  92.0 8.2 %collective-permute-start.31 = (f32[160,345]{1,0:T(8,128)S(1)}, f32[160,345]{1,0:T(8,128)S(1)}, u32[]{:S(2)}, u32[]{:S(2)}) collective-permute-start(f32[160,345]{1,0:T(8,128)S(1)} %add.28), channel_id=1, source_target_pairs={{0,12},{1,13},{2,14},{3,15},{4,8},{5,9},{6,10},{7,11},{8,4},{9,5},... | collective-permute-start | bytes 662408 | tf_op jit(solution)/shard_map/ppermute | solution.py:48
  94.5 7.5 %collective-permute-start.33 = (f32[160,345]{1,0:T(8,128)S(1)}, f32[160,345]{1,0:T(8,128)S(1)}, u32[]{:S(2)}, u32[]{:S(2)}) collective-permute-start(f32[160,345]{1,0:T(8,128)S(1)} %add.30), channel_id=1, source_target_pairs={{0,66},{1,67},{2,64},{3,65},{4,70},{5,71},{6,68},{7,69},{8,74},{9,... | collective-permute-start | bytes 662408 | tf_op jit(solution)/shard_map/ppermute | solution.py:48

commit v7 on v6

--- a/solution.py
+++ b/solution.py
@@ -112,7 +112,12 @@
     )(*arrays)
 
 
+def block_rows(count):
+    return 480 if count % 480 == 0 else count
+
+
 def block_kernel(plan, n_in, parts, left_ready, apart, *refs):
+    refs, (high, low) = refs[:-2], refs[-2:]
     inputs, refs = refs[:n_in], refs[n_in:]
     if left_ready:
         (left, split), refs = refs[:2], refs[2:]
@@ -137,22 +142,21 @@
     done = 0
     for i, (_, first, count, total_row) in enumerate(parts):
         right = rights[i]
-        rows = 480 if count % 480 == 0 else 320
+        rows = block_rows(count)
         for start in range(0, count, rows):
             n = slice(first + start, first + start + rows)
-            part = None
-            if total_row is not None:
-                part = totals[i][total_row + start : total_row + start + rows, :]
             for at in range(0, left.shape[0], 512):
                 m = slice(at, min(at + 512, left.shape[0]))
                 gram_a = dot(right[n, :FEAT], left[m, :FEAT], NT)
                 gram_s = dot(right[n, FEAT:], left[m, FEAT:], NT)
                 kernel = gram_a * gram_s
-                high = kernel.astype(bf16)
-                low = (kernel - high.astype(f32)).astype(bf16)
-                both = dot(high, split[m, :], NN)
-                new = both[:, :LANES] + both[:, LANES:] + dot(low, split[m, :LANES], NN)
-                part = new if part is None else part + new
+                rounded = kernel.astype(bf16)
+                high[:rows, m] = rounded
+                low[:rows, m] = (kernel - rounded.astype(f32)).astype(bf16)
+            both = dot(high[:rows, :], split[...], NN)
+            part = both[:, :LANES] + both[:, LANES:] + dot(low[:rows, :], split[:, :LANES], NN)
+            if total_row is not None:
+                part = part + totals[i][total_row + start : total_row + start + rows, :]
             if apart:
                 for k in range(rows // OWN):
                     outs[done + k][...] = part[k * OWN : (k + 1) * OWN, :CLASSES]
@@ -207,6 +211,7 @@
         out_shape=sums + laid,
         in_specs=[VMEM] * len(arrays),
         out_specs=[VMEM] * (len(sums) + len(laid)),
+        scratch_shapes=[pltpu.VMEM((max(block_rows(part[2]) for part in parts), left_rows), bf16)] * 2,
         cost_estimate=pl.CostEstimate(
             flops=sum(part[2] for part in parts) * left_rows * 5400, bytes_accessed=1_000_000, transcendentals=0
         ),
@@ -276,10 +281,11 @@
     axz, sxz = {}, {}
     axz[n] = send(axxy[n], n, "z")
     sxz[n] = send(sz[n], n, "x")
-    axz["far"] = send(after(axxy["far"], *small), "far", "z")
+
     sxz["far"] = send(after(sz["far"], *small), "far", "x")
     four_mate = send(after(four, *small), n, "c")
-    cxy = send(after(cx, cy, four_mate), n, "y")
+    cxy = send(after(cx, *small), n, "y")
+    axz["far"] = send(after(axxy["far"], four_mate), "far", "z")
 
     def blocks_of(g):
         act = {"": (a0x[g], 0, 0), "x": (a0x[g], 1, 0), "y": (ay[g], 0, 0), "xy": (ay[g], 1, 0)}
@@ -309,7 +315,7 @@
     left_1 += [(act_mate[k], sig_mate[k], coef_mate[k]) for k in first]
     (total_1,), (rows_1, coefs_1, wide_1) = partial_sums([(right_1, 0, 960, None, 0)], left_1, False, "early")
     axz_mate, sxz_mate = [send(after(v, total_1), n, "c") for v in (axz[n], sxz[n])]
-    cxy_mate = send(cxy, n, "c")
+    cxy_mate = send(after(cxy, total_1), n, "c")
     (total_2,), (wide_2,) = partial_sums(
         [(right_2, 0, 320, None, 0)], (after(rows_1, total_1), coefs_1), False, "early_right"
     )

time: 103 us -> 102 us (level)
  Pallas kernels: 23.2 us -> 21.9 us
    pallas_call x4, Pallas kernels: 22.7 us -> 21.4 us  [partial_sums(): pl.pallas_call(functools.partial(block_kernel, plan, n_in, parts, left_re...]
  transfers between devices with their start and end apart: 34 -> 34, of which waited for: 23 -> 23; matrix products, arithmetic and copies ran while one was open for 0% -> 0% of each run, Pallas kernels for 18% -> 17%
where the time goes in v7:
time: 102 us
  starting transfers between devices  43.2 us (42%)
  waiting for transfers between devices  33.2 us (33%)
  Pallas kernels  21.9 us (21%)
  local copies, waits for them, and re-layouts  2.84 us (3%)
    ppermute x34, starting transfers between devices, send(): return lax.ppermute(value, AXES, moves(group, dims))  43.2 us
    ppermute x34, waiting for transfers between devices, send(): return lax.ppermute(value, AXES, moves(group, dims))  33.2 us
    pallas_call x4, Pallas kernels, partial_sums(): pl.pallas_call(functools.partial(block_kernel, plan, n_in, parts, left_re...  21.4 us
    unnamed x10, local copies, waits for them, and re-layouts  2.84 us
  transfers between devices with their start and end apart: 34, of which 23 were waited for; matrix products, arithmetic and copies ran while one was open for 0% of the time, Pallas kernels for 17%

profile of v7, /device:TPU:0, one launch (start us, length us, event | category | flops | bytes accessed | tf_op | source)
XLA Modules:
  0.0 102.3 jit_solution(10200404514106070079)
XLA Ops:
  0.0 0.9 copy-done
  1.0 2.1 %collective-permute-start.4 = (bf16[160,768]{1,0:T(8,128)(2,1)S(1)}, bf16[160,768]{1,0:T(8,128)(2,1)S(1)}, u32[]{:S(2)}, u32[]{:S(2)}) collective-permute-start(bf16[160,768]{1,0:T(8,128)(2,1)S(1)} %split_coefs.1.refs_6_), channel_id=1, source_target_pairs={{0,2},{1,3},{2,0},{3,1},{4,6},{5,7},{6,4},{7,5},{8,10},{9,11},{10,... | collective-permute-start | bytes 737288 | tf_op jit(solution)/shard_map/ppermute | solution.py:48
  3.1 2.8 %collective-permute-start = (bf16[160,768]{1,0:T(8,128)(2,1)}, bf16[160,768]{1,0:T(8,128)(2,1)S(1)}, u32[]{:S(2)}, u32[]{:S(2)}) collective-permute-start(bf16[160,768]{1,0:T(8,128)(2,1)} %refs_0_), channel_id=1, source_target_pairs={{0,48},{1,49},{2,50},{3,51},{4,52},{5,53},{6,54},{7,55},{8,56},{9,... | collective-permute-start | bytes 737288 | tf_op jit(solution)/shard_map/ppermute | solution.py:48
  5.8 0.2 collective-permute-start.1
  6.1 3.0 %collective-permute-start.2 = (bf16[160,768]{1,0:T(8,128)(2,1)}, bf16[160,768]{1,0:T(8,128)(2,1)S(1)}, u32[]{:S(2)}, u32[]{:S(2)}) collective-permute-start(bf16[160,768]{1,0:T(8,128)(2,1)} %refs_1_), channel_id=1, source_target_pairs={{0,12},{1,13},{2,14},{3,15},{4,8},{5,9},{6,10},{7,11},{8,4},{9,5},... | collective-permute-start | bytes 737288 | tf_op jit(solution)/shard_map/ppermute | solution.py:48
  9.1 0.1 collective-permute-start.3
  9.2 0.9 copy-done.2
  10.2 0.9 copy-done.3
  11.2 0.8 collective-permute-done.refs_1_
  11.9 1.3 %collective-permute-done.1.refs_2_ = bf16[160,768]{1,0:T(8,128)(2,1)S(1)} collective-permute-done((bf16[160,768]{1,0:T(8,128)(2,1)}, bf16[160,768]{1,0:T(8,128)(2,1)S(1)}, u32[]{:S(2)}, u32[]{:S(2)}) %collective-permute-start.1) | collective-permute-done | bytes 245792 | tf_op jit(solution)/shard_map/ppermute | solution.py:48
  13.2 1.3 %collective-permute-done.2.refs_4_ = bf16[160,768]{1,0:T(8,128)(2,1)S(1)} collective-permute-done((bf16[160,768]{1,0:T(8,128)(2,1)}, bf16[160,768]{1,0:T(8,128)(2,1)S(1)}, u32[]{:S(2)}, u32[]{:S(2)}) %collective-permute-start.2) | collective-permute-done | bytes 245792 | tf_op jit(solution)/shard_map/ppermute | solution.py:48
  14.5 1.5 %collective-permute-done.3.refs_5_ = bf16[160,768]{1,0:T(8,128)(2,1)S(1)} collective-permute-done((bf16[160,768]{1,0:T(8,128)(2,1)}, bf16[160,768]{1,0:T(8,128)(2,1)S(1)}, u32[]{:S(2)}, u32[]{:S(2)}) %collective-permute-start.3) | collective-permute-done | bytes 245792 | tf_op jit(solution)/shard_map/ppermute | solution.py:48
  15.9 0.2 pairs.1
  16.1 1.8 %collective-permute-start.9 = (bf16[320,768]{1,0:T(8,128)(2,1)S(1)}, bf16[320,768]{1,0:T(8,128)(2,1)S(1)}, u32[]{:S(2)}, u32[]{:S(2)}) collective-permute-start(bf16[320,768]{1,0:T(8,128)(2,1)S(1)} %get-tuple-element.104.refs_4_.refs_2_.refs_9_), channel_id=1, source_target_pairs={{0,16},{1,17},{2,18},{3,19},{4,20},{5,21},{6,22},{7,23},{8,24},{9,... | collective-permute-start | bytes 1474568 | tf_op jit(solution)/shard_map/ppermute | solution.py:48
  17.9 0.3 collective-permute-start.6
  18.2 0.4 collective-permute-start.8
  18.6 1.2 %collective-permute-start.5 = (bf16[320,768]{1,0:T(8,128)(2,1)S(1)}, bf16[320,768]{1,0:T(8,128)(2,1)S(1)}, u32[]{:S(2)}, u32[]{:S(2)}) collective-permute-start(bf16[320,768]{1,0:T(8,128)(2,1)S(1)} %get-tuple-element.79.refs_0_.refs_18_), channel_id=1, source_target_pairs={{0,12},{1,13},{2,14},{3,15},{4,8},{5,9},{6,10},{7,11},{8,4},{9,5},... | collective-permute-start | bytes 1474568 | tf_op jit(solution)/shard_map/ppermute | solution.py:48
  19.8 3.8 %collective-permute-start.7 = (bf16[320,768]{1,0:T(8,128)(2,1)S(1)}, bf16[320,768]{1,0:T(8,128)(2,1)S(1)}, u32[]{:S(2)}, u32[]{:S(2)}) collective-permute-start(bf16[320,768]{1,0:T(8,128)(2,1)S(1)} %get-tuple-element.89.refs_19_), channel_id=1, source_target_pairs={{0,66},{1,67},{2,64},{3,65},{4,70},{5,71},{6,68},{7,69},{8,74},{9,... | collective-permute-start | bytes 1474568 | tf_op jit(solution)/shard_map/ppermute | solution.py:48
  23.6 3.6 %collective-permute-done.9.refs_5_.refs_4_ = bf16[320,768]{1,0:T(8,128)(2,1)S(1)} collective-permute-done((bf16[320,768]{1,0:T(8,128)(2,1)S(1)}, bf16[320,768]{1,0:T(8,128)(2,1)S(1)}, u32[]{:S(2)}, u32[]{:S(2)}) %collective-permute-start.9) | collective-permute-done | bytes 491552 | tf_op jit(solution)/shard_map/ppermute | solution.py:48
  27.1 1.4 %collective-permute-done.6.refs_3_.refs_1_.refs_5_.refs_0_ = bf16[320,768]{1,0:T(8,128)(2,1)S(1)} collective-permute-done((bf16[320,768]{1,0:T(8,128)(2,1)S(1)}, bf16[320,768]{1,0:T(8,128)(2,1)S(1)}, u32[]{:S(2)}, u32[]{:S(2)}) %collective-permute-start.6) | collective-permute-done | bytes 491552 | tf_op jit(solution)/shard_map/ppermute | solution.py:48
  28.5 0.2 collective-permute-done.8.refs_3_.refs_8_
  28.8 1.6 %collective-permute-done.5.refs_1_.refs_14_ = bf16[320,768]{1,0:T(8,128)(2,1)S(1)} collective-permute-done((bf16[320,768]{1,0:T(8,128)(2,1)S(1)}, bf16[320,768]{1,0:T(8,128)(2,1)S(1)}, u32[]{:S(2)}, u32[]{:S(2)}) %collective-permute-start.5) | collective-permute-done | bytes 491552 | tf_op jit(solution)/shard_map/ppermute | solution.py:48
  30.3 1.8 %collective-permute-done.7.refs_17_ = bf16[320,768]{1,0:T(8,128)(2,1)S(1)} collective-permute-done((bf16[320,768]{1,0:T(8,128)(2,1)S(1)}, bf16[320,768]{1,0:T(8,128)(2,1)S(1)}, u32[]{:S(2)}, u32[]{:S(2)}) %collective-permute-start.7) | collective-permute-done | bytes 491552 | tf_op jit(solution)/shard_map/ppermute | solution.py:48
  32.2 1.1 %collective-permute-start.14 = (bf16[320,768]{1,0:T(8,128)(2,1)S(1)}, bf16[320,768]{1,0:T(8,128)(2,1)S(1)}, u32[]{:S(2)}, u32[]{:S(2)}) collective-permute-start(bf16[320,768]{1,0:T(8,128)(2,1)S(1)} %get-tuple-element.104.refs_4_.refs_2_.refs_9_), channel_id=1, source_target_pairs={{0,4},{1,5},{2,6},{3,7},{4,0},{5,1},{6,2},{7,3},{8,12},{9,13},{10,... | collective-permute-start | bytes 1474568 | tf_op jit(solution)/shard_map/ppermute | solution.py:48
  33.3 0.4 collective-permute-start.13
  33.7 1.0 collective-permute-start.12
  34.7 0.1 turn.1
  34.8 3.0 %collective-permute-start.10 = (bf16[320,768]{1,0:T(8,128)(2,1)S(1)}, bf16[320,768]{1,0:T(8,128)(2,1)S(1)}, u32[]{:S(2)}, u32[]{:S(2)}) collective-permute-start(bf16[320,768]{1,0:T(8,128)(2,1)S(1)} %get-tuple-element.86), channel_id=1, source_target_pairs={{0,66},{1,67},{2,64},{3,65},{4,70},{5,71},{6,68},{7,69},{8,74},{9,... | collective-permute-start | bytes 1474568 | tf_op jit(solution)/shard_map/ppermute | solution.py:48
  37.8 0.2 four.1
  38.0 3.8 %collective-permute-done.14.refs_6_ = bf16[320,768]{1,0:T(8,128)(2,1)S(1)} collective-permute-done((bf16[320,768]{1,0:T(8,128)(2,1)S(1)}, bf16[320,768]{1,0:T(8,128)(2,1)S(1)}, u32[]{:S(2)}, u32[]{:S(2)}) %collective-permute-start.14) | collective-permute-done | bytes 491552 | tf_op jit(solution)/shard_map/ppermute | solution.py:48
  41.9 0.6 collective-permute-done.13.refs_3_.refs_1_
  42.5 1.4 %collective-permute-done.12.refs_15_ = bf16[320,768]{1,0:T(8,128)(2,1)S(1)} collective-permute-done((bf16[320,768]{1,0:T(8,128)(2,1)S(1)}, bf16[320,768]{1,0:T(8,128)(2,1)S(1)}, u32[]{:S(2)}, u32[]{:S(2)}) %collective-permute-start.12) | collective-permute-done | bytes 491552 | tf_op jit(solution)/shard_map/ppermute | solution.py:48
  43.8 1.1 %collective-permute-done.10.refs_16_ = bf16[320,768]{1,0:T(8,128)(2,1)S(1)} collective-permute-done((bf16[320,768]{1,0:T(8,128)(2,1)S(1)}, bf16[320,768]{1,0:T(8,128)(2,1)S(1)}, u32[]{:S(2)}, u32[]{:S(2)}) %collective-permute-start.10) | collective-permute-done | bytes 491552 | tf_op jit(solution)/shard_map/ppermute | solution.py:48
  44.9 1.7 %collective-permute-done.11.refs_7_ = bf16[320,768]{1,0:T(8,128)(2,1)S(1)} collective-permute-done((bf16[320,768]{1,0:T(8,128)(2,1)S(1)}, bf16[320,768]{1,0:T(8,128)(2,1)S(1)}, u32[]{:S(2)}, u32[]{:S(2)}) %collective-permute-start.11) | collective-permute-done | bytes 491552 | tf_op jit(solution)/shard_map/ppermute | solution.py:48
  46.7 0.5 collective-permute-start.16
  47.2 1.3 %collective-permute-done.15.refs_13_ = bf16[320,768]{1,0:T(8,128)(2,1)S(1)} collective-permute-done((bf16[320,768]{1,0:T(8,128)(2,1)S(1)}, bf16[320,768]{1,0:T(8,128)(2,1)S(1)}, u32[]{:S(2)}, u32[]{:S(2)}) %collective-permute-start.15) | collective-permute-done | bytes 491552 | tf_op jit(solution)/shard_map/ppermute | solution.py:48
  48.5 0.7 collective-permute-done.16.refs_11_.refs_7_
  49.2 0.7 collective-permute-done.17.refs_12_
  49.9 0.1 collective-permute-start.21
  50.1 0.7 collective-permute-start.20
  50.8 2.6 %collective-permute-start.26 = (bf16[320,768]{1,0:T(8,128)(2,1)S(1)}, bf16[320,768]{1,0:T(8,128)(2,1)S(1)}, u32[]{:S(2)}, u32[]{:S(2)}) collective-permute-start(bf16[320,768]{1,0:T(8,128)(2,1)S(1)} %collective-permute-done.7.refs_17_), channel_id=1, source_target_pairs={{0,48},{1,49},{2,50},{3,51},{4,52},{5,53},{6,54},{7,55},{8,56},{9,... | collective-permute-start | bytes 1474568 | tf_op jit(solution)/shard_map/ppermute | solution.py:48
  53.4 0.9 collective-permute-start.18
  54.3 1.0 %collective-permute-done.21.refs_10_.refs_6_ = bf16[640,2304]{1,0:T(8,128)(2,1)S(1)} collective-permute-done((bf16[640,2304]{1,0:T(8,128)(2,1)S(1)}, bf16[640,2304]{1,0:T(8,128)(2,1)S(1)}, u32[]{:S(2)}, u32[]{:S(2)}) %collective-permute-start.21) | collective-permute-done | bytes 2949152 | tf_op jit(solution)/shard_map/ppermute | solution.py:48
  55.3 1.2 %collective-permute-start.25 = (bf16[320,768]{1,0:T(8,128)(2,1)S(1)}, bf16[320,768]{1,0:T(8,128)(2,1)S(1)}, u32[]{:S(2)}, u32[]{:S(2)}) collective-permute-start(bf16[320,768]{1,0:T(8,128)(2,1)S(1)} %get-tuple-element.113), channel_id=1, source_target_pairs={{0,66},{1,67},{2,64},{3,65},{4,70},{5,71},{6,68},{7,69},{8,74},{9,... | collective-permute-start | bytes 1474568 | tf_op jit(solution)/shard_map/ppermute | solution.py:48
  56.5 10.0 %early.1 = (f32[960,384]{1,0:T(8,128)S(1)}, bf16[1600,1536]{1,0:T(8,128)(2,1)S(1)}, bf16[1600,768]{1,0:T(8,128)(2,1)S(1)}, bf16[960,1536]{1,0:T(8,128)(2,1)S(1)}) custom-call(bf16[320,768]{1,0:T(8,128)(2,1)S(1)} %get-tuple-element.80.refs_2_.refs_0_, bf16[320,768]{1,0:T(8,128)(2,1)S(1)} %get-tuple-element.91.refs_2_.refs_1_, ...), custom_call_target="tpu_custom_call" | custom-call | flops 8294400000 | bytes 1000000 | tf_op jit(solution)/shard_map/early/pallas_call | solution.py:209
  66.5 0.1 collective-permute-start.24
  66.6 0.5 collective-permute-start.23
  67.1 0.3 collective-permute-start.22
  67.4 2.4 %collective-permute-done.25.refs_0_ = bf16[320,768]{1,0:T(8,128)(2,1)S(1)} collective-permute-done((bf16[320,768]{1,0:T(8,128)(2,1)S(1)}, bf16[320,768]{1,0:T(8,128)(2,1)S(1)}, u32[]{:S(2)}, u32[]{:S(2)}) %collective-permute-start.25) | collective-permute-done | bytes 491552 | tf_op jit(solution)/shard_map/ppermute | solution.py:48
  69.8 3.5 %early_right.1 = (f32[320,384]{1,0:T(8,128)S(1)}, bf16[320,1536]{1,0:T(8,128)(2,1)S(1)}) custom-call(bf16[320,768]{1,0:T(8,128)(2,1)S(1)} %collective-permute-done.25.refs_0_, bf16[320,768]{1,0:T(8,128)(2,1)S(1)} %collective-permute-done.26.refs_1_, bf16[1600,1536]{1,0:T(8,128)(2,1)S(1)} %get-tuple-element.116.refs_2_, ...), custom_call_target="tpu_custom_call" | custom-call | flops 2764800000 | bytes 1000000 | tf_op jit(solution)/shard_map/early_right/pallas_call | solution.py:209
  73.3 4.0 %second_far.1 = (f32[160,345]{1,0:T(8,128)S(1)}, f32[160,345]{1,0:T(8,128)S(1)}, f32[160,345]{1,0:T(8,128)S(1)}, f32[160,345]{1,0:T(8,128)S(1)}, bf16[960,1536]{...) custom-call(bf16[320,768]{1,0:T(8,128)(2,1)S(1)} %collective-permute-done.6.refs_3_.refs_1_.refs_5_.refs_0_, ...), custom_call_target="tpu_custom_call" | custom-call | flops 3317760000 | bytes 1000000 | tf_op jit(solution)/shard_map/second_far/pallas_call | solution.py:209
  77.3 1.3 %collective-permute-start.28 = (f32[160,345]{1,0:T(8,128)S(1)}, f32[160,345]{1,0:T(8,128)S(1)}, u32[]{:S(2)}, u32[]{:S(2)}) collective-permute-start(f32[160,345]{1,0:T(8,128)S(1)} %get-tuple-element.122), channel_id=1, source_target_pairs={{0,66},{1,67},{2,64},{3,65},{4,70},{5,71},{6,68},{7,69},{8,74},{9,... | collective-permute-start | bytes 662408 | tf_op jit(solution)/shard_map/ppermute | solution.py:48
  78.6 2.2 %collective-permute-start.30 = (f32[160,345]{1,0:T(8,128)S(1)}, f32[160,345]{1,0:T(8,128)S(1)}, u32[]{:S(2)}, u32[]{:S(2)}) collective-permute-start(f32[160,345]{1,0:T(8,128)S(1)} %get-tuple-element.130), channel_id=1, source_target_pairs={{0,48},{1,49},{2,50},{3,51},{4,52},{5,53},{6,54},{7,55},{8,56},{9,... | collective-permute-start | bytes 662408 | tf_op jit(solution)/shard_map/ppermute | solution.py:48
  80.8 1.5 %collective-permute-start.32 = (f32[160,345]{1,0:T(8,128)S(1)}, f32[160,345]{1,0:T(8,128)S(1)}, u32[]{:S(2)}, u32[]{:S(2)}) collective-permute-start(f32[160,345]{1,0:T(8,128)S(1)} %get-tuple-element.133), channel_id=1, source_target_pairs={{0,12},{1,13},{2,14},{3,15},{4,8},{5,9},{6,10},{7,11},{8,4},{9,5},... | collective-permute-start | bytes 662408 | tf_op jit(solution)/shard_map/ppermute | solution.py:48
  82.3 3.7 %collective-permute-start.27 = (f32[160,345]{1,0:T(8,128)S(1)}, f32[160,345]{1,0:T(8,128)S(1)}, u32[]{:S(2)}, u32[]{:S(2)}) collective-permute-start(f32[160,345]{1,0:T(8,128)S(1)} %get-tuple-element.126), channel_id=1, source_target_pairs={{0,126},{1,127},{2,124},{3,125},{4,122},{5,123},{6,120},{7,121},{8... | collective-permute-start | bytes 662408 | tf_op jit(solution)/shard_map/ppermute | solution.py:48
  86.0 3.9 %second_near.1 = (f32[160,345]{1,0:T(8,128)S(1)}, f32[160,345]{1,0:T(8,128)S(1)}, f32[160,345]{1,0:T(8,128)S(1)}, f32[160,345]{1,0:T(8,128)S(1)}) custom-call(bf16[960,1536]{1,0:T(8,128)(2,1)S(1)} %get-tuple-element.123.refs_0_, bf16[960,768]{1,0:T(8,128)(2,1)S(1)} %get-tuple-element.124.refs_1_, bf16[960,1536]{1,0:T(8,128)(2,1)S(1)} %get-tuple-element.120.refs_13_.refs_2_, ...), custom_call_target="tpu_custom_call" | custom-call | flops 3317760000 | bytes 1000000 | tf_op jit(solution)/shard_map/second_near/pallas_call | solution.py:209
  90.0 2.3 %collective-permute-start.29 = (f32[160,345]{1,0:T(8,128)S(1)}, f32[160,345]{1,0:T(8,128)S(1)}, u32[]{:S(2)}, u32[]{:S(2)}) collective-permute-start(f32[160,345]{1,0:T(8,128)S(1)} %add.26), channel_id=1, source_target_pairs={{0,48},{1,49},{2,50},{3,51},{4,52},{5,53},{6,54},{7,55},{8,56},{9,... | collective-permute-start | bytes 662408 | tf_op jit(solution)/shard_map/ppermute | solution.py:48
  92.3 1.5 %collective-permute-start.31 = (f32[160,345]{1,0:T(8,128)S(1)}, f32[160,345]{1,0:T(8,128)S(1)}, u32[]{:S(2)}, u32[]{:S(2)}) collective-permute-start(f32[160,345]{1,0:T(8,128)S(1)} %add.28), channel_id=1, source_target_pairs={{0,12},{1,13},{2,14},{3,15},{4,8},{5,9},{6,10},{7,11},{8,4},{9,5},... | collective-permute-start | bytes 662408 | tf_op jit(solution)/shard_map/ppermute | solution.py:48
  93.9 0.1 collective-permute-done.32
  94.0 2.5 %collective-permute-start.33 = (f32[160,345]{1,0:T(8,128)S(1)}, f32[160,345]{1,0:T(8,128)S(1)}, u32[]{:S(2)}, u32[]{:S(2)}) collective-permute-start(f32[160,345]{1,0:T(8,128)S(1)} %add.30), channel_id=1, source_target_pairs={{0,66},{1,67},{2,64},{3,65},{4,70},{5,71},{6,68},{7,69},{8,74},{9,... | collective-permute-start | bytes 662408 | tf_op jit(solution)/shard_map/ppermute | solution.py:48
  96.5 1.4 %collective-permute-done.29 = f32[160,345]{1,0:T(8,128)S(1)} collective-permute-done((f32[160,345]{1,0:T(8,128)S(1)}, f32[160,345]{1,0:T(8,128)S(1)}, u32[]{:S(2)}, u32[]{:S(2)}) %collective-permute-start.29) | collective-permute-done | bytes 220832 | tf_op jit(solution)/shard_map/ppermute | solution.py:48
  97.8 2.0 %collective-permute-done.31 = f32[160,345]{1,0:T(8,128)S(1)} collective-permute-done((f32[160,345]{1,0:T(8,128)S(1)}, f32[160,345]{1,0:T(8,128)S(1)}, u32[]{:S(2)}, u32[]{:S(2)}) %collective-permute-start.31) | collective-permute-done | bytes 220832 | tf_op jit(solution)/shard_map/ppermute | solution.py:48
  99.8 1.6 %collective-permute-done.33 = f32[160,345]{1,0:T(8,128)S(1)} collective-permute-done((f32[160,345]{1,0:T(8,128)S(1)}, f32[160,345]{1,0:T(8,128)S(1)}, u32[]{:S(2)}, u32[]{:S(2)}) %collective-permute-start.33) | collective-permute-done | bytes 220832 | tf_op jit(solution)/shard_map/ppermute | solution.py:48
  101.4 0.8 add_bitcast_fusion
  (27 shorter events, 0.2 us)
Async XLA Ops:
  0.0 0.9 copy-start
  1.0 10.1 %collective-permute-start.4 = (bf16[160,768]{1,0:T(8,128)(2,1)S(1)}, bf16[160,768]{1,0:T(8,128)(2,1)S(1)}, u32[]{:S(2)}, u32[]{:S(2)}) collective-permute-start(bf16[160,768]{1,0:T(8,128)(2,1)S(1)} %split_coefs.1.refs_6_), channel_id=1, source_target_pairs={{0,2},{1,3},{2,0},{3,1},{4,6},{5,7},{6,4},{7,5},{8,10},{9,11},{10,... | collective-permute-start | bytes 737288 | tf_op jit(solution)/shard_map/ppermute | solution.py:48
  3.1 8.8 %collective-permute-start = (bf16[160,768]{1,0:T(8,128)(2,1)}, bf16[160,768]{1,0:T(8,128)(2,1)S(1)}, u32[]{:S(2)}, u32[]{:S(2)}) collective-permute-start(bf16[160,768]{1,0:T(8,128)(2,1)} %refs_0_), channel_id=1, source_target_pairs={{0,48},{1,49},{2,50},{3,51},{4,52},{5,53},{6,54},{7,55},{8,56},{9,... | collective-permute-start | bytes 737288 | tf_op jit(solution)/shard_map/ppermute | solution.py:48
  5.8 7.3 %collective-permute-start.1 = (bf16[160,768]{1,0:T(8,128)(2,1)}, bf16[160,768]{1,0:T(8,128)(2,1)S(1)}, u32[]{:S(2)}, u32[]{:S(2)}) collective-permute-start(bf16[160,768]{1,0:T(8,128)(2,1)} %refs_0_), channel_id=1, source_target_pairs={{0,16},{1,17},{2,18},{3,19},{4,20},{5,21},{6,22},{7,23},{8,24},{9,... | collective-permute-start | bytes 737288 | tf_op jit(solution)/shard_map/ppermute | solution.py:48
  6.1 8.4 %collective-permute-start.2 = (bf16[160,768]{1,0:T(8,128)(2,1)}, bf16[160,768]{1,0:T(8,128)(2,1)S(1)}, u32[]{:S(2)}, u32[]{:S(2)}) collective-permute-start(bf16[160,768]{1,0:T(8,128)(2,1)} %refs_1_), channel_id=1, source_target_pairs={{0,12},{1,13},{2,14},{3,15},{4,8},{5,9},{6,10},{7,11},{8,4},{9,5},... | collective-permute-start | bytes 737288 | tf_op jit(solution)/shard_map/ppermute | solution.py:48
  9.1 6.8 %collective-permute-start.3 = (bf16[160,768]{1,0:T(8,128)(2,1)}, bf16[160,768]{1,0:T(8,128)(2,1)S(1)}, u32[]{:S(2)}, u32[]{:S(2)}) collective-permute-start(bf16[160,768]{1,0:T(8,128)(2,1)} %refs_1_), channel_id=1, source_target_pairs={{0,4},{1,5},{2,6},{3,7},{4,0},{5,1},{6,2},{7,3},{8,12},{9,13},{10,... | collective-permute-start | bytes 737288 | tf_op jit(solution)/shard_map/ppermute | solution.py:48
  9.2 0.9 copy-start.2
  10.2 0.9 copy-start.3
  16.1 11.1 %collective-permute-start.9 = (bf16[320,768]{1,0:T(8,128)(2,1)S(1)}, bf16[320,768]{1,0:T(8,128)(2,1)S(1)}, u32[]{:S(2)}, u32[]{:S(2)}) collective-permute-start(bf16[320,768]{1,0:T(8,128)(2,1)S(1)} %get-tuple-element.104.refs_4_.refs_2_.refs_9_), channel_id=1, source_target_pairs={{0,16},{1,17},{2,18},{3,19},{4,20},{5,21},{6,22},{7,23},{8,24},{9,... | collective-permute-start | bytes 1474568 | tf_op jit(solution)/shard_map/ppermute | solution.py:48
  17.9 10.6 %collective-permute-start.6 = (bf16[320,768]{1,0:T(8,128)(2,1)S(1)}, bf16[320,768]{1,0:T(8,128)(2,1)S(1)}, u32[]{:S(2)}, u32[]{:S(2)}) collective-permute-start(bf16[320,768]{1,0:T(8,128)(2,1)S(1)} %get-tuple-element.80.refs_2_.refs_0_), channel_id=1, source_target_pairs={{0,4},{1,5},{2,6},{3,7},{4,0},{5,1},{6,2},{7,3},{8,12},{9,13},{10,... | collective-permute-start | bytes 1474568 | tf_op jit(solution)/shard_map/ppermute | solution.py:48
  18.2 10.5 %collective-permute-start.8 = (bf16[320,768]{1,0:T(8,128)(2,1)S(1)}, bf16[320,768]{1,0:T(8,128)(2,1)S(1)}, u32[]{:S(2)}, u32[]{:S(2)}) collective-permute-start(bf16[320,768]{1,0:T(8,128)(2,1)S(1)} %get-tuple-element.91.refs_2_.refs_1_), channel_id=1, source_target_pairs={{0,2},{1,3},{2,0},{3,1},{4,6},{5,7},{6,4},{7,5},{8,10},{9,11},{10,... | collective-permute-start | bytes 1474568 | tf_op jit(solution)/shard_map/ppermute | solution.py:48
  18.6 11.7 %collective-permute-start.5 = (bf16[320,768]{1,0:T(8,128)(2,1)S(1)}, bf16[320,768]{1,0:T(8,128)(2,1)S(1)}, u32[]{:S(2)}, u32[]{:S(2)}) collective-permute-start(bf16[320,768]{1,0:T(8,128)(2,1)S(1)} %get-tuple-element.79.refs_0_.refs_18_), channel_id=1, source_target_pairs={{0,12},{1,13},{2,14},{3,15},{4,8},{5,9},{6,10},{7,11},{8,4},{9,5},... | collective-permute-start | bytes 1474568 | tf_op jit(solution)/shard_map/ppermute | solution.py:48
  19.8 12.4 %collective-permute-start.7 = (bf16[320,768]{1,0:T(8,128)(2,1)S(1)}, bf16[320,768]{1,0:T(8,128)(2,1)S(1)}, u32[]{:S(2)}, u32[]{:S(2)}) collective-permute-start(bf16[320,768]{1,0:T(8,128)(2,1)S(1)} %get-tuple-element.89.refs_19_), channel_id=1, source_target_pairs={{0,66},{1,67},{2,64},{3,65},{4,70},{5,71},{6,68},{7,69},{8,74},{9,... | collective-permute-start | bytes 1474568 | tf_op jit(solution)/shard_map/ppermute | solution.py:48
  32.2 9.7 %collective-permute-start.14 = (bf16[320,768]{1,0:T(8,128)(2,1)S(1)}, bf16[320,768]{1,0:T(8,128)(2,1)S(1)}, u32[]{:S(2)}, u32[]{:S(2)}) collective-permute-start(bf16[320,768]{1,0:T(8,128)(2,1)S(1)} %get-tuple-element.104.refs_4_.refs_2_.refs_9_), channel_id=1, source_target_pairs={{0,4},{1,5},{2,6},{3,7},{4,0},{5,1},{6,2},{7,3},{8,12},{9,13},{10,... | collective-permute-start | bytes 1474568 | tf_op jit(solution)/shard_map/ppermute | solution.py:48
  33.3 9.2 %collective-permute-start.13 = (bf16[320,768]{1,0:T(8,128)(2,1)S(1)}, bf16[320,768]{1,0:T(8,128)(2,1)S(1)}, u32[]{:S(2)}, u32[]{:S(2)}) collective-permute-start(bf16[320,768]{1,0:T(8,128)(2,1)S(1)} %get-tuple-element.91.refs_2_.refs_1_), channel_id=1, source_target_pairs={{0,16},{1,17},{2,18},{3,19},{4,20},{5,21},{6,22},{7,23},{8,24},{9,... | collective-permute-start | bytes 1474568 | tf_op jit(solution)/shard_map/ppermute | solution.py:48
  33.7 10.2 %collective-permute-start.12 = (bf16[320,768]{1,0:T(8,128)(2,1)S(1)}, bf16[320,768]{1,0:T(8,128)(2,1)S(1)}, u32[]{:S(2)}, u32[]{:S(2)}) collective-permute-start(bf16[320,768]{1,0:T(8,128)(2,1)S(1)} %get-tuple-element.89.refs_19_), channel_id=1, source_target_pairs={{0,48},{1,49},{2,50},{3,51},{4,52},{5,53},{6,54},{7,55},{8,56},{9,... | collective-permute-start | bytes 1474568 | tf_op jit(solution)/shard_map/ppermute | solution.py:48
  34.8 10.1 %collective-permute-start.10 = (bf16[320,768]{1,0:T(8,128)(2,1)S(1)}, bf16[320,768]{1,0:T(8,128)(2,1)S(1)}, u32[]{:S(2)}, u32[]{:S(2)}) collective-permute-start(bf16[320,768]{1,0:T(8,128)(2,1)S(1)} %get-tuple-element.86), channel_id=1, source_target_pairs={{0,66},{1,67},{2,64},{3,65},{4,70},{5,71},{6,68},{7,69},{8,74},{9,... | collective-permute-start | bytes 1474568 | tf_op jit(solution)/shard_map/ppermute | solution.py:48
  37.8 8.8 %collective-permute-start.11 = (bf16[320,768]{1,0:T(8,128)(2,1)S(1)}, bf16[320,768]{1,0:T(8,128)(2,1)S(1)}, u32[]{:S(2)}, u32[]{:S(2)}) collective-permute-start(bf16[320,768]{1,0:T(8,128)(2,1)S(1)} %get-tuple-element.87), channel_id=1, source_target_pairs={{0,2},{1,3},{2,0},{3,1},{4,6},{5,7},{6,4},{7,5},{8,10},{9,11},{10,... | collective-permute-start | bytes 1474568 | tf_op jit(solution)/shard_map/ppermute | solution.py:48
  46.7 1.9 %collective-permute-start.15 = (bf16[320,768]{1,0:T(8,128)(2,1)S(1)}, bf16[320,768]{1,0:T(8,128)(2,1)S(1)}, u32[]{:S(2)}, u32[]{:S(2)}) collective-permute-start(bf16[320,768]{1,0:T(8,128)(2,1)S(1)} %collective-permute-done.11.refs_7_), channel_id=1, source_target_pairs={{0,1},{1,0},{2,3},{3,2},{4,5},{5,4},{6,7},{7,6},{8,9},{9,8},{10,11... | collective-permute-start | bytes 1474568 | tf_op jit(solution)/shard_map/ppermute | solution.py:48
  46.7 2.6 %collective-permute-start.16 = (bf16[320,768]{1,0:T(8,128)(2,1)S(1)}, bf16[320,768]{1,0:T(8,128)(2,1)S(1)}, u32[]{:S(2)}, u32[]{:S(2)}) collective-permute-start(bf16[320,768]{1,0:T(8,128)(2,1)S(1)} %collective-permute-done.13.refs_3_.refs_1_), channel_id=1, source_target_pairs={{0,1},{1,0},{2,3},{3,2},{4,5},{5,4},{6,7},{7,6},{8,9},{9,8},{10,11... | collective-permute-start | bytes 1474568 | tf_op jit(solution)/shard_map/ppermute | solution.py:48
  47.2 2.8 %collective-permute-start.17 = (bf16[320,768]{1,0:T(8,128)(2,1)S(1)}, bf16[320,768]{1,0:T(8,128)(2,1)S(1)}, u32[]{:S(2)}, u32[]{:S(2)}) collective-permute-start(bf16[320,768]{1,0:T(8,128)(2,1)S(1)} %collective-permute-done.14.refs_6_), channel_id=1, source_target_pairs={{0,1},{1,0},{2,3},{3,2},{4,5},{5,4},{6,7},{7,6},{8,9},{9,8},{10,11... | collective-permute-start | bytes 1474568 | tf_op jit(solution)/shard_map/ppermute | solution.py:48
  49.9 5.4 %collective-permute-start.21 = (bf16[640,2304]{1,0:T(8,128)(2,1)S(1)}, bf16[640,2304]{1,0:T(8,128)(2,1)S(1)}, u32[]{:S(2)}, u32[]{:S(2)}) collective-permute-start(bf16[640,2304]{1,0:T(8,128)(2,1)S(1)} %four.1), channel_id=1, source_target_pairs={{0,1},{1,0},{2,3},{3,2},{4,5},{5,4},{6,7},{7,6},{8,9},{9,8},{10,11... | collective-permute-start | bytes 8847368 | tf_op jit(solution)/shard_map/ppermute | solution.py:48
  50.1 16.4 %collective-permute-start.20 = (bf16[320,768]{1,0:T(8,128)(2,1)S(1)}, bf16[320,768]{1,0:T(8,128)(2,1)S(1)}, u32[]{:S(2)}, u32[]{:S(2)}) collective-permute-start(bf16[320,768]{1,0:T(8,128)(2,1)S(1)} %collective-permute-done.8.refs_3_.refs_8_), channel_id=1, source_target_pairs={{0,16},{1,17},{2,18},{3,19},{4,20},{5,21},{6,22},{7,23},{8,24},{9,... | collective-permute-start | bytes 1474568 | tf_op jit(solution)/shard_map/ppermute | solution.py:48
  50.7 15.9 %collective-permute-start.19 = (bf16[320,768]{1,0:T(8,128)(2,1)S(1)}, bf16[320,768]{1,0:T(8,128)(2,1)S(1)}, u32[]{:S(2)}, u32[]{:S(2)}) collective-permute-start(bf16[320,768]{1,0:T(8,128)(2,1)S(1)} %get-tuple-element.100), channel_id=1, source_target_pairs={{0,2},{1,3},{2,0},{3,1},{4,6},{5,7},{6,4},{7,5},{8,10},{9,11},{10,... | collective-permute-start | bytes 1474568 | tf_op jit(solution)/shard_map/ppermute | solution.py:48
  50.8 16.7 %collective-permute-start.26 = (bf16[320,768]{1,0:T(8,128)(2,1)S(1)}, bf16[320,768]{1,0:T(8,128)(2,1)S(1)}, u32[]{:S(2)}, u32[]{:S(2)}) collective-permute-start(bf16[320,768]{1,0:T(8,128)(2,1)S(1)} %collective-permute-done.7.refs_17_), channel_id=1, source_target_pairs={{0,48},{1,49},{2,50},{3,51},{4,52},{5,53},{6,54},{7,55},{8,56},{9,... | collective-permute-start | bytes 1474568 | tf_op jit(solution)/shard_map/ppermute | solution.py:48
  53.4 13.7 %collective-permute-start.18 = (bf16[320,768]{1,0:T(8,128)(2,1)S(1)}, bf16[320,768]{1,0:T(8,128)(2,1)S(1)}, u32[]{:S(2)}, u32[]{:S(2)}) collective-permute-start(bf16[320,768]{1,0:T(8,128)(2,1)S(1)} %collective-permute-done.9.refs_5_.refs_4_), channel_id=1, source_target_pairs={{0,4},{1,5},{2,6},{3,7},{4,0},{5,1},{6,2},{7,3},{8,12},{9,13},{10,... | collective-permute-start | bytes 1474568 | tf_op jit(solution)/shard_map/ppermute | solution.py:48
  55.3 14.5 %collective-permute-start.25 = (bf16[320,768]{1,0:T(8,128)(2,1)S(1)}, bf16[320,768]{1,0:T(8,128)(2,1)S(1)}, u32[]{:S(2)}, u32[]{:S(2)}) collective-permute-start(bf16[320,768]{1,0:T(8,128)(2,1)S(1)} %get-tuple-element.113), channel_id=1, source_target_pairs={{0,66},{1,67},{2,64},{3,65},{4,70},{5,71},{6,68},{7,69},{8,74},{9,... | collective-permute-start | bytes 1474568 | tf_op jit(solution)/shard_map/ppermute | solution.py:48
  66.5 6.8 %collective-permute-start.24 = (bf16[320,768]{1,0:T(8,128)(2,1)S(1)}, bf16[320,768]{1,0:T(8,128)(2,1)S(1)}, u32[]{:S(2)}, u32[]{:S(2)}) collective-permute-start(bf16[320,768]{1,0:T(8,128)(2,1)S(1)} %collective-permute-done.20.refs_4_), channel_id=1, source_target_pairs={{0,1},{1,0},{2,3},{3,2},{4,5},{5,4},{6,7},{7,6},{8,9},{9,8},{10,11... | collective-permute-start | bytes 1474568 | tf_op jit(solution)/shard_map/ppermute | solution.py:48
  66.6 6.7 %collective-permute-start.23 = (bf16[320,768]{1,0:T(8,128)(2,1)S(1)}, bf16[320,768]{1,0:T(8,128)(2,1)S(1)}, u32[]{:S(2)}, u32[]{:S(2)}) collective-permute-start(bf16[320,768]{1,0:T(8,128)(2,1)S(1)} %collective-permute-done.19.refs_3_), channel_id=1, source_target_pairs={{0,1},{1,0},{2,3},{3,2},{4,5},{5,4},{6,7},{7,6},{8,9},{9,8},{10,11... | collective-permute-start | bytes 1474568 | tf_op jit(solution)/shard_map/ppermute | solution.py:48
  67.1 6.2 %collective-permute-start.22 = (bf16[320,768]{1,0:T(8,128)(2,1)S(1)}, bf16[320,768]{1,0:T(8,128)(2,1)S(1)}, u32[]{:S(2)}, u32[]{:S(2)}) collective-permute-start(bf16[320,768]{1,0:T(8,128)(2,1)S(1)} %collective-permute-done.18.refs_2_), channel_id=1, source_target_pairs={{0,1},{1,0},{2,3},{3,2},{4,5},{5,4},{6,7},{7,6},{8,9},{9,8},{10,11... | collective-permute-start | bytes 1474568 | tf_op jit(solution)/shard_map/ppermute | solution.py:48
  77.3 12.6 %collective-permute-start.28 = (f32[160,345]{1,0:T(8,128)S(1)}, f32[160,345]{1,0:T(8,128)S(1)}, u32[]{:S(2)}, u32[]{:S(2)}) collective-permute-start(f32[160,345]{1,0:T(8,128)S(1)} %get-tuple-element.122), channel_id=1, source_target_pairs={{0,66},{1,67},{2,64},{3,65},{4,70},{5,71},{6,68},{7,69},{8,74},{9,... | collective-permute-start | bytes 662408 | tf_op jit(solution)/shard_map/ppermute | solution.py:48
  78.6 13.7 %collective-permute-start.30 = (f32[160,345]{1,0:T(8,128)S(1)}, f32[160,345]{1,0:T(8,128)S(1)}, u32[]{:S(2)}, u32[]{:S(2)}) collective-permute-start(f32[160,345]{1,0:T(8,128)S(1)} %get-tuple-element.130), channel_id=1, source_target_pairs={{0,48},{1,49},{2,50},{3,51},{4,52},{5,53},{6,54},{7,55},{8,56},{9,... | collective-permute-start | bytes 662408 | tf_op jit(solution)/shard_map/ppermute | solution.py:48
  80.8 13.1 %collective-permute-start.32 = (f32[160,345]{1,0:T(8,128)S(1)}, f32[160,345]{1,0:T(8,128)S(1)}, u32[]{:S(2)}, u32[]{:S(2)}) collective-permute-start(f32[160,345]{1,0:T(8,128)S(1)} %get-tuple-element.133), channel_id=1, source_target_pairs={{0,12},{1,13},{2,14},{3,15},{4,8},{5,9},{6,10},{7,11},{8,4},{9,5},... | collective-permute-start | bytes 662408 | tf_op jit(solution)/shard_map/ppermute | solution.py:48
  82.3 14.2 %collective-permute-start.27 = (f32[160,345]{1,0:T(8,128)S(1)}, f32[160,345]{1,0:T(8,128)S(1)}, u32[]{:S(2)}, u32[]{:S(2)}) collective-permute-start(f32[160,345]{1,0:T(8,128)S(1)} %get-tuple-element.126), channel_id=1, source_target_pairs={{0,126},{1,127},{2,124},{3,125},{4,122},{5,123},{6,120},{7,121},{8... | collective-permute-start | bytes 662408 | tf_op jit(solution)/shard_map/ppermute | solution.py:48
  86.0 15.5 %copy-start.1 = (f32[345,160]{0,1:T(8,128)S(1)}, f32[345,160]{0,1:T(8,128)}, u32[]{:S(2)}) copy-start(f32[345,160]{0,1:T(8,128)} %param.7) | copy-start | bytes 662404
  86.0 15.5 %copy-start.4 = (s32[160]{0:T(256)S(1)}, s32[160]{0:T(256)}, u32[]{:S(2)}) copy-start(s32[160]{0:T(256)} %param.6) | copy-start | bytes 1924
  90.0 7.9 %collective-permute-start.29 = (f32[160,345]{1,0:T(8,128)S(1)}, f32[160,345]{1,0:T(8,128)S(1)}, u32[]{:S(2)}, u32[]{:S(2)}) collective-permute-start(f32[160,345]{1,0:T(8,128)S(1)} %add.26), channel_id=1, source_target_pairs={{0,48},{1,49},{2,50},{3,51},{4,52},{5,53},{6,54},{7,55},{8,56},{9,... | collective-permute-start | bytes 662408 | tf_op jit(solution)/shard_map/ppermute | solution.py:48
  92.3 7.5 %collective-permute-start.31 = (f32[160,345]{1,0:T(8,128)S(1)}, f32[160,345]{1,0:T(8,128)S(1)}, u32[]{:S(2)}, u32[]{:S(2)}) collective-permute-start(f32[160,345]{1,0:T(8,128)S(1)} %add.28), channel_id=1, source_target_pairs={{0,12},{1,13},{2,14},{3,15},{4,8},{5,9},{6,10},{7,11},{8,4},{9,5},... | collective-permute-start | bytes 662408 | tf_op jit(solution)/shard_map/ppermute | solution.py:48
  94.0 7.5 %collective-permute-start.33 = (f32[160,345]{1,0:T(8,128)S(1)}, f32[160,345]{1,0:T(8,128)S(1)}, u32[]{:S(2)}, u32[]{:S(2)}) collective-permute-start(f32[160,345]{1,0:T(8,128)S(1)} %add.30), channel_id=1, source_target_pairs={{0,66},{1,67},{2,64},{3,65},{4,70},{5,71},{6,68},{7,69},{8,74},{9,... | collective-permute-start | bytes 662408 | tf_op jit(solution)/shard_map/ppermute | solution.py:48

commit v8 on v7

--- a/solution.py
+++ b/solution.py
@@ -330,12 +330,14 @@
     )
     part_x, part_y, part_z = send(sum_xz, "far", "z"), send(sum_xy, "far", "x"), send(sum_yz, "far", "y")
     got_xyz = send(sum_xyz, "far", "xyz")
-    (sum_x, sum_y, sum_z, own), _ = partial_sums(
-        [(wide_1, 320, 640, total_1, 320)], (after(rows_2, sum_xz), coefs_2), True, "second_near"
-    )
-    got_x = send(after(sum_x + part_x, own), "far", "x")
-    got_y = send(after(sum_y + part_y, own), "far", "y")
-    got_z = send(after(sum_z + part_z, own), "far", "z")
+    (sum_x, sum_y, sum_z), _ = partial_sums(
+        [(wide_1, 320, 480, total_1, 320)], (after(rows_2, sum_xz), coefs_2), True, "second_near"
+    )
+    got_x = send(after(sum_x + part_x, sum_z), "far", "x")
+    got_y = send(after(sum_y + part_y, sum_z), "far", "y")
+    last = sum_z + part_z
+    got_z = send(last, "far", "z")
+    (own,), _ = partial_sums([(wide_1, 800, 160, total_1, 800)], (after(rows_2, last), coefs_2), True, "second_here")
 
     product = own + got_xyz + got_x + got_y + got_z
     product = product * (1.0 / (FEAT * FEAT))

time: 102 us -> 102 us (level)
  starting transfers between devices: 43.2 us -> 42 us
    ppermute x34, starting transfers between devices: 43.2 us -> 42 us  [send(): return lax.ppermute(value, AXES, moves(group, dims))]
    pallas_call x4 -> x5, Pallas kernels: 21.4 us -> 21.9 us  [partial_sums(): pl.pallas_call(functools.partial(block_kernel, plan, n_in, parts, left_re...]
  transfers between devices with their start and end apart: 34 -> 34, of which waited for: 23 -> 23; matrix products, arithmetic and copies ran while one was open for 0% -> 0% of each run, Pallas kernels for 17% -> 18%
where the time goes in v8:
time: 102 us
  starting transfers between devices  42 us (41%)
  waiting for transfers between devices  33.7 us (33%)
  Pallas kernels  22.5 us (22%)
  local copies, waits for them, and re-layouts  2.84 us (3%)
    ppermute x34, starting transfers between devices, send(): return lax.ppermute(value, AXES, moves(group, dims))  42 us
    ppermute x34, waiting for transfers between devices, send(): return lax.ppermute(value, AXES, moves(group, dims))  33.7 us
    pallas_call x5, Pallas kernels, partial_sums(): pl.pallas_call(functools.partial(block_kernel, plan, n_in, parts, left_re...  21.9 us
    unnamed x10, local copies, waits for them, and re-layouts  2.84 us
  transfers between devices with their start and end apart: 34, of which 23 were waited for; matrix products, arithmetic and copies ran while one was open for 0% of the time, Pallas kernels for 18%

profile of v8, /device:TPU:0, one launch (start us, length us, event | category | flops | bytes accessed | tf_op | source)
XLA Modules:
  0.0 102.1 jit_solution(16638100326775509088)
XLA Ops:
  0.0 0.9 copy-done
  1.0 2.1 %collective-permute-start.4 = (bf16[160,768]{1,0:T(8,128)(2,1)S(1)}, bf16[160,768]{1,0:T(8,128)(2,1)S(1)}, u32[]{:S(2)}, u32[]{:S(2)}) collective-permute-start(bf16[160,768]{1,0:T(8,128)(2,1)S(1)} %split_coefs.1.refs_6_), channel_id=1, source_target_pairs={{0,2},{1,3},{2,0},{3,1},{4,6},{5,7},{6,4},{7,5},{8,10},{9,11},{10,... | collective-permute-start | bytes 737288 | tf_op jit(solution)/shard_map/ppermute | solution.py:48
  3.1 2.8 %collective-permute-start = (bf16[160,768]{1,0:T(8,128)(2,1)}, bf16[160,768]{1,0:T(8,128)(2,1)S(1)}, u32[]{:S(2)}, u32[]{:S(2)}) collective-permute-start(bf16[160,768]{1,0:T(8,128)(2,1)} %refs_0_), channel_id=1, source_target_pairs={{0,48},{1,49},{2,50},{3,51},{4,52},{5,53},{6,54},{7,55},{8,56},{9,... | collective-permute-start | bytes 737288 | tf_op jit(solution)/shard_map/ppermute | solution.py:48
  5.8 0.2 collective-permute-start.1
  6.1 3.0 %collective-permute-start.2 = (bf16[160,768]{1,0:T(8,128)(2,1)}, bf16[160,768]{1,0:T(8,128)(2,1)S(1)}, u32[]{:S(2)}, u32[]{:S(2)}) collective-permute-start(bf16[160,768]{1,0:T(8,128)(2,1)} %refs_1_), channel_id=1, source_target_pairs={{0,12},{1,13},{2,14},{3,15},{4,8},{5,9},{6,10},{7,11},{8,4},{9,5},... | collective-permute-start | bytes 737288 | tf_op jit(solution)/shard_map/ppermute | solution.py:48
  9.1 0.1 collective-permute-start.3
  9.2 0.9 copy-done.2
  10.2 0.9 copy-done.3
  11.2 0.8 collective-permute-done.refs_1_
  11.9 1.3 %collective-permute-done.1.refs_2_ = bf16[160,768]{1,0:T(8,128)(2,1)S(1)} collective-permute-done((bf16[160,768]{1,0:T(8,128)(2,1)}, bf16[160,768]{1,0:T(8,128)(2,1)S(1)}, u32[]{:S(2)}, u32[]{:S(2)}) %collective-permute-start.1) | collective-permute-done | bytes 245792 | tf_op jit(solution)/shard_map/ppermute | solution.py:48
  13.2 1.3 %collective-permute-done.2.refs_4_ = bf16[160,768]{1,0:T(8,128)(2,1)S(1)} collective-permute-done((bf16[160,768]{1,0:T(8,128)(2,1)}, bf16[160,768]{1,0:T(8,128)(2,1)S(1)}, u32[]{:S(2)}, u32[]{:S(2)}) %collective-permute-start.2) | collective-permute-done | bytes 245792 | tf_op jit(solution)/shard_map/ppermute | solution.py:48
  14.5 1.5 %collective-permute-done.3.refs_5_ = bf16[160,768]{1,0:T(8,128)(2,1)S(1)} collective-permute-done((bf16[160,768]{1,0:T(8,128)(2,1)}, bf16[160,768]{1,0:T(8,128)(2,1)S(1)}, u32[]{:S(2)}, u32[]{:S(2)}) %collective-permute-start.3) | collective-permute-done | bytes 245792 | tf_op jit(solution)/shard_map/ppermute | solution.py:48
  15.9 0.2 pairs.1
  16.1 1.8 %collective-permute-start.9 = (bf16[320,768]{1,0:T(8,128)(2,1)S(1)}, bf16[320,768]{1,0:T(8,128)(2,1)S(1)}, u32[]{:S(2)}, u32[]{:S(2)}) collective-permute-start(bf16[320,768]{1,0:T(8,128)(2,1)S(1)} %get-tuple-element.103.refs_4_.refs_2_.refs_9_), channel_id=1, source_target_pairs={{0,16},{1,17},{2,18},{3,19},{4,20},{5,21},{6,22},{7,23},{8,24},{9,... | collective-permute-start | bytes 1474568 | tf_op jit(solution)/shard_map/ppermute | solution.py:48
  17.9 0.3 collective-permute-start.6
  18.2 0.4 collective-permute-start.8
  18.6 1.2 %collective-permute-start.5 = (bf16[320,768]{1,0:T(8,128)(2,1)S(1)}, bf16[320,768]{1,0:T(8,128)(2,1)S(1)}, u32[]{:S(2)}, u32[]{:S(2)}) collective-permute-start(bf16[320,768]{1,0:T(8,128)(2,1)S(1)} %get-tuple-element.78.refs_0_.refs_18_), channel_id=1, source_target_pairs={{0,12},{1,13},{2,14},{3,15},{4,8},{5,9},{6,10},{7,11},{8,4},{9,5},... | collective-permute-start | bytes 1474568 | tf_op jit(solution)/shard_map/ppermute | solution.py:48
  19.8 3.8 %collective-permute-start.7 = (bf16[320,768]{1,0:T(8,128)(2,1)S(1)}, bf16[320,768]{1,0:T(8,128)(2,1)S(1)}, u32[]{:S(2)}, u32[]{:S(2)}) collective-permute-start(bf16[320,768]{1,0:T(8,128)(2,1)S(1)} %get-tuple-element.88.refs_19_), channel_id=1, source_target_pairs={{0,66},{1,67},{2,64},{3,65},{4,70},{5,71},{6,68},{7,69},{8,74},{9,... | collective-permute-start | bytes 1474568 | tf_op jit(solution)/shard_map/ppermute | solution.py:48
  23.6 3.6 %collective-permute-done.9.refs_5_.refs_4_ = bf16[320,768]{1,0:T(8,128)(2,1)S(1)} collective-permute-done((bf16[320,768]{1,0:T(8,128)(2,1)S(1)}, bf16[320,768]{1,0:T(8,128)(2,1)S(1)}, u32[]{:S(2)}, u32[]{:S(2)}) %collective-permute-start.9) | collective-permute-done | bytes 491552 | tf_op jit(solution)/shard_map/ppermute | solution.py:48
  27.1 1.4 %collective-permute-done.6.refs_3_.refs_1_.refs_5_.refs_0_ = bf16[320,768]{1,0:T(8,128)(2,1)S(1)} collective-permute-done((bf16[320,768]{1,0:T(8,128)(2,1)S(1)}, bf16[320,768]{1,0:T(8,128)(2,1)S(1)}, u32[]{:S(2)}, u32[]{:S(2)}) %collective-permute-start.6) | collective-permute-done | bytes 491552 | tf_op jit(solution)/shard_map/ppermute | solution.py:48
  28.5 0.2 collective-permute-done.8.refs_3_.refs_8_
  28.8 1.6 %collective-permute-done.5.refs_1_.refs_14_ = bf16[320,768]{1,0:T(8,128)(2,1)S(1)} collective-permute-done((bf16[320,768]{1,0:T(8,128)(2,1)S(1)}, bf16[320,768]{1,0:T(8,128)(2,1)S(1)}, u32[]{:S(2)}, u32[]{:S(2)}) %collective-permute-start.5) | collective-permute-done | bytes 491552 | tf_op jit(solution)/shard_map/ppermute | solution.py:48
  30.3 1.8 %collective-permute-done.7.refs_17_ = bf16[320,768]{1,0:T(8,128)(2,1)S(1)} collective-permute-done((bf16[320,768]{1,0:T(8,128)(2,1)S(1)}, bf16[320,768]{1,0:T(8,128)(2,1)S(1)}, u32[]{:S(2)}, u32[]{:S(2)}) %collective-permute-start.7) | collective-permute-done | bytes 491552 | tf_op jit(solution)/shard_map/ppermute | solution.py:48
  32.2 1.1 %collective-permute-start.14 = (bf16[320,768]{1,0:T(8,128)(2,1)S(1)}, bf16[320,768]{1,0:T(8,128)(2,1)S(1)}, u32[]{:S(2)}, u32[]{:S(2)}) collective-permute-start(bf16[320,768]{1,0:T(8,128)(2,1)S(1)} %get-tuple-element.103.refs_4_.refs_2_.refs_9_), channel_id=1, source_target_pairs={{0,4},{1,5},{2,6},{3,7},{4,0},{5,1},{6,2},{7,3},{8,12},{9,13},{10,... | collective-permute-start | bytes 1474568 | tf_op jit(solution)/shard_map/ppermute | solution.py:48
  33.3 0.4 collective-permute-start.13
  33.7 1.0 collective-permute-start.12
  34.7 0.1 turn.1
  34.8 3.0 %collective-permute-start.10 = (bf16[320,768]{1,0:T(8,128)(2,1)S(1)}, bf16[320,768]{1,0:T(8,128)(2,1)S(1)}, u32[]{:S(2)}, u32[]{:S(2)}) collective-permute-start(bf16[320,768]{1,0:T(8,128)(2,1)S(1)} %get-tuple-element.85), channel_id=1, source_target_pairs={{0,66},{1,67},{2,64},{3,65},{4,70},{5,71},{6,68},{7,69},{8,74},{9,... | collective-permute-start | bytes 1474568 | tf_op jit(solution)/shard_map/ppermute | solution.py:48
  37.8 0.2 four.1
  38.0 3.8 %collective-permute-done.14.refs_6_ = bf16[320,768]{1,0:T(8,128)(2,1)S(1)} collective-permute-done((bf16[320,768]{1,0:T(8,128)(2,1)S(1)}, bf16[320,768]{1,0:T(8,128)(2,1)S(1)}, u32[]{:S(2)}, u32[]{:S(2)}) %collective-permute-start.14) | collective-permute-done | bytes 491552 | tf_op jit(solution)/shard_map/ppermute | solution.py:48
  41.9 0.6 collective-permute-done.13.refs_3_.refs_1_
  42.5 1.4 %collective-permute-done.12.refs_15_ = bf16[320,768]{1,0:T(8,128)(2,1)S(1)} collective-permute-done((bf16[320,768]{1,0:T(8,128)(2,1)S(1)}, bf16[320,768]{1,0:T(8,128)(2,1)S(1)}, u32[]{:S(2)}, u32[]{:S(2)}) %collective-permute-start.12) | collective-permute-done | bytes 491552 | tf_op jit(solution)/shard_map/ppermute | solution.py:48
  43.8 1.1 %collective-permute-done.10.refs_16_ = bf16[320,768]{1,0:T(8,128)(2,1)S(1)} collective-permute-done((bf16[320,768]{1,0:T(8,128)(2,1)S(1)}, bf16[320,768]{1,0:T(8,128)(2,1)S(1)}, u32[]{:S(2)}, u32[]{:S(2)}) %collective-permute-start.10) | collective-permute-done | bytes 491552 | tf_op jit(solution)/shard_map/ppermute | solution.py:48
  44.9 1.7 %collective-permute-done.11.refs_7_ = bf16[320,768]{1,0:T(8,128)(2,1)S(1)} collective-permute-done((bf16[320,768]{1,0:T(8,128)(2,1)S(1)}, bf16[320,768]{1,0:T(8,128)(2,1)S(1)}, u32[]{:S(2)}, u32[]{:S(2)}) %collective-permute-start.11) | collective-permute-done | bytes 491552 | tf_op jit(solution)/shard_map/ppermute | solution.py:48
  46.7 0.5 collective-permute-start.16
  47.2 1.3 %collective-permute-done.15.refs_13_ = bf16[320,768]{1,0:T(8,128)(2,1)S(1)} collective-permute-done((bf16[320,768]{1,0:T(8,128)(2,1)S(1)}, bf16[320,768]{1,0:T(8,128)(2,1)S(1)}, u32[]{:S(2)}, u32[]{:S(2)}) %collective-permute-start.15) | collective-permute-done | bytes 491552 | tf_op jit(solution)/shard_map/ppermute | solution.py:48
  48.5 0.7 collective-permute-done.16.refs_11_.refs_7_
  49.2 0.7 collective-permute-done.17.refs_12_
  49.9 0.1 collective-permute-start.21
  50.1 0.7 collective-permute-start.20
  50.8 2.6 %collective-permute-start.26 = (bf16[320,768]{1,0:T(8,128)(2,1)S(1)}, bf16[320,768]{1,0:T(8,128)(2,1)S(1)}, u32[]{:S(2)}, u32[]{:S(2)}) collective-permute-start(bf16[320,768]{1,0:T(8,128)(2,1)S(1)} %collective-permute-done.7.refs_17_), channel_id=1, source_target_pairs={{0,48},{1,49},{2,50},{3,51},{4,52},{5,53},{6,54},{7,55},{8,56},{9,... | collective-permute-start | bytes 1474568 | tf_op jit(solution)/shard_map/ppermute | solution.py:48
  53.4 0.9 collective-permute-start.18
  54.3 1.0 %collective-permute-done.21.refs_10_.refs_6_ = bf16[640,2304]{1,0:T(8,128)(2,1)S(1)} collective-permute-done((bf16[640,2304]{1,0:T(8,128)(2,1)S(1)}, bf16[640,2304]{1,0:T(8,128)(2,1)S(1)}, u32[]{:S(2)}, u32[]{:S(2)}) %collective-permute-start.21) | collective-permute-done | bytes 2949152 | tf_op jit(solution)/shard_map/ppermute | solution.py:48
  55.3 1.2 %collective-permute-start.25 = (bf16[320,768]{1,0:T(8,128)(2,1)S(1)}, bf16[320,768]{1,0:T(8,128)(2,1)S(1)}, u32[]{:S(2)}, u32[]{:S(2)}) collective-permute-start(bf16[320,768]{1,0:T(8,128)(2,1)S(1)} %get-tuple-element.112), channel_id=1, source_target_pairs={{0,66},{1,67},{2,64},{3,65},{4,70},{5,71},{6,68},{7,69},{8,74},{9,... | collective-permute-start | bytes 1474568 | tf_op jit(solution)/shard_map/ppermute | solution.py:48
  56.5 10.0 %early.1 = (f32[960,384]{1,0:T(8,128)S(1)}, bf16[1600,1536]{1,0:T(8,128)(2,1)S(1)}, bf16[1600,768]{1,0:T(8,128)(2,1)S(1)}, bf16[960,1536]{1,0:T(8,128)(2,1)S(1)}) custom-call(bf16[320,768]{1,0:T(8,128)(2,1)S(1)} %get-tuple-element.79.refs_2_.refs_0_, bf16[320,768]{1,0:T(8,128)(2,1)S(1)} %get-tuple-element.90.refs_2_.refs_1_, ...), custom_call_target="tpu_custom_call" | custom-call | flops 8294400000 | bytes 1000000 | tf_op jit(solution)/shard_map/early/pallas_call | solution.py:209
  66.6 0.5 collective-permute-start.23
  67.1 0.3 collective-permute-start.22
  67.4 2.4 %collective-permute-done.25.refs_0_ = bf16[320,768]{1,0:T(8,128)(2,1)S(1)} collective-permute-done((bf16[320,768]{1,0:T(8,128)(2,1)S(1)}, bf16[320,768]{1,0:T(8,128)(2,1)S(1)}, u32[]{:S(2)}, u32[]{:S(2)}) %collective-permute-start.25) | collective-permute-done | bytes 491552 | tf_op jit(solution)/shard_map/ppermute | solution.py:48
  69.8 3.5 %early_right.1 = (f32[320,384]{1,0:T(8,128)S(1)}, bf16[320,1536]{1,0:T(8,128)(2,1)S(1)}) custom-call(bf16[320,768]{1,0:T(8,128)(2,1)S(1)} %collective-permute-done.25.refs_0_, bf16[320,768]{1,0:T(8,128)(2,1)S(1)} %collective-permute-done.26.refs_1_, bf16[1600,1536]{1,0:T(8,128)(2,1)S(1)} %get-tuple-element.115.refs_2_, ...), custom_call_target="tpu_custom_call" | custom-call | flops 2764800000 | bytes 1000000 | tf_op jit(solution)/shard_map/early_right/pallas_call | solution.py:209
  73.3 4.0 %second_far.1 = (f32[160,345]{1,0:T(8,128)S(1)}, f32[160,345]{1,0:T(8,128)S(1)}, f32[160,345]{1,0:T(8,128)S(1)}, f32[160,345]{1,0:T(8,128)S(1)}, bf16[960,1536]{...) custom-call(bf16[320,768]{1,0:T(8,128)(2,1)S(1)} %collective-permute-done.6.refs_3_.refs_1_.refs_5_.refs_0_, ...), custom_call_target="tpu_custom_call" | custom-call | flops 3317760000 | bytes 1000000 | tf_op jit(solution)/shard_map/second_far/pallas_call | solution.py:209
  77.3 1.3 %collective-permute-start.29 = (f32[160,345]{1,0:T(8,128)S(1)}, f32[160,345]{1,0:T(8,128)S(1)}, u32[]{:S(2)}, u32[]{:S(2)}) collective-permute-start(f32[160,345]{1,0:T(8,128)S(1)} %get-tuple-element.121), channel_id=1, source_target_pairs={{0,66},{1,67},{2,64},{3,65},{4,70},{5,71},{6,68},{7,69},{8,74},{9,... | collective-permute-start | bytes 662408 | tf_op jit(solution)/shard_map/ppermute | solution.py:48
  78.6 1.5 %collective-permute-start.27 = (f32[160,345]{1,0:T(8,128)S(1)}, f32[160,345]{1,0:T(8,128)S(1)}, u32[]{:S(2)}, u32[]{:S(2)}) collective-permute-start(f32[160,345]{1,0:T(8,128)S(1)} %get-tuple-element.125), channel_id=1, source_target_pairs={{0,12},{1,13},{2,14},{3,15},{4,8},{5,9},{6,10},{7,11},{8,4},{9,5},... | collective-permute-start | bytes 662408 | tf_op jit(solution)/shard_map/ppermute | solution.py:48
  80.1 2.2 %collective-permute-start.31 = (f32[160,345]{1,0:T(8,128)S(1)}, f32[160,345]{1,0:T(8,128)S(1)}, u32[]{:S(2)}, u32[]{:S(2)}) collective-permute-start(f32[160,345]{1,0:T(8,128)S(1)} %get-tuple-element.131), channel_id=1, source_target_pairs={{0,48},{1,49},{2,50},{3,51},{4,52},{5,53},{6,54},{7,55},{8,56},{9,... | collective-permute-start | bytes 662408 | tf_op jit(solution)/shard_map/ppermute | solution.py:48
  82.3 3.7 %collective-permute-start.28 = (f32[160,345]{1,0:T(8,128)S(1)}, f32[160,345]{1,0:T(8,128)S(1)}, u32[]{:S(2)}, u32[]{:S(2)}) collective-permute-start(f32[160,345]{1,0:T(8,128)S(1)} %get-tuple-element.127), channel_id=1, source_target_pairs={{0,126},{1,127},{2,124},{3,125},{4,122},{5,123},{6,120},{7,121},{8... | collective-permute-start | bytes 662408 | tf_op jit(solution)/shard_map/ppermute | solution.py:48
  86.0 3.0 %second_near.1 = (f32[160,345]{1,0:T(8,128)S(1)}, f32[160,345]{1,0:T(8,128)S(1)}, f32[160,345]{1,0:T(8,128)S(1)}) custom-call(bf16[960,1536]{1,0:T(8,128)(2,1)S(1)} %get-tuple-element.126.refs_0_, bf16[960,768]{1,0:T(8,128)(2,1)S(1)} %get-tuple-element.123.refs_1_, bf16[960,1536]{1,0:T(8,128)(2,1)S(1)} %get-tuple-element.119.refs_13_.refs_2_, ...), custom_call_target="tpu_custom_call" | custom-call | flops 2488320000 | bytes 1000000 | tf_op jit(solution)/shard_map/second_near/pallas_call | solution.py:209
  89.0 2.3 %collective-permute-start.30 = (f32[160,345]{1,0:T(8,128)S(1)}, f32[160,345]{1,0:T(8,128)S(1)}, u32[]{:S(2)}, u32[]{:S(2)}) collective-permute-start(f32[160,345]{1,0:T(8,128)S(1)} %add.27), channel_id=1, source_target_pairs={{0,48},{1,49},{2,50},{3,51},{4,52},{5,53},{6,54},{7,55},{8,56},{9,... | collective-permute-start | bytes 662408 | tf_op jit(solution)/shard_map/ppermute | solution.py:48
  91.4 1.5 %collective-permute-start.32 = (f32[160,345]{1,0:T(8,128)S(1)}, f32[160,345]{1,0:T(8,128)S(1)}, u32[]{:S(2)}, u32[]{:S(2)}) collective-permute-start(f32[160,345]{1,0:T(8,128)S(1)} %add.29), channel_id=1, source_target_pairs={{0,12},{1,13},{2,14},{3,15},{4,8},{5,9},{6,10},{7,11},{8,4},{9,5},... | collective-permute-start | bytes 662408 | tf_op jit(solution)/shard_map/ppermute | solution.py:48
  93.0 1.3 %collective-permute-start.33 = (f32[160,345]{1,0:T(8,128)S(1)}, f32[160,345]{1,0:T(8,128)S(1)}, u32[]{:S(2)}, u32[]{:S(2)}) collective-permute-start(f32[160,345]{1,0:T(8,128)S(1)} %add.25), channel_id=1, source_target_pairs={{0,66},{1,67},{2,64},{3,65},{4,70},{5,71},{6,68},{7,69},{8,74},{9,... | collective-permute-start | bytes 662408 | tf_op jit(solution)/shard_map/ppermute | solution.py:48
  94.3 1.5 %second_here.1 = f32[160,345]{1,0:T(8,128)S(1)} custom-call(bf16[960,1536]{1,0:T(8,128)(2,1)S(1)} %get-tuple-element.126.refs_0_, bf16[960,768]{1,0:T(8,128)(2,1)S(1)} %get-tuple-element.123.refs_1_, bf16[960,1536]{1,0:T(8,128)(2,1)S(1)} %get-tuple-element.119.refs_13_.refs_2_, f32[960,384]{1,0:T(8,128)S(1)} %get-tuple-element.107.refs_14_.refs_3_), custom_call_target="tpu_custom_call" | custom-call | flops 829440000 | bytes 1000000 | tf_op jit(solution)/shard_map/second_here/pallas_call | solution.py:209
  95.8 1.8 %collective-permute-done.28 = f32[160,345]{1,0:T(8,128)S(1)} collective-permute-done((f32[160,345]{1,0:T(8,128)S(1)}, f32[160,345]{1,0:T(8,128)S(1)}, u32[]{:S(2)}, u32[]{:S(2)}) %collective-permute-start.28) | collective-permute-done | bytes 220832 | tf_op jit(solution)/shard_map/ppermute | solution.py:48
  97.5 0.9 collective-permute-done.30
  98.4 1.4 %collective-permute-done.32 = f32[160,345]{1,0:T(8,128)S(1)} collective-permute-done((f32[160,345]{1,0:T(8,128)S(1)}, f32[160,345]{1,0:T(8,128)S(1)}, u32[]{:S(2)}, u32[]{:S(2)}) %collective-permute-start.32) | collective-permute-done | bytes 220832 | tf_op jit(solution)/shard_map/ppermute | solution.py:48
  99.8 1.4 %collective-permute-done.33 = f32[160,345]{1,0:T(8,128)S(1)} collective-permute-done((f32[160,345]{1,0:T(8,128)S(1)}, f32[160,345]{1,0:T(8,128)S(1)}, u32[]{:S(2)}, u32[]{:S(2)}) %collective-permute-start.33) | collective-permute-done | bytes 220832 | tf_op jit(solution)/shard_map/ppermute | solution.py:48
  101.3 0.8 add_bitcast_fusion
  (28 shorter events, 0.3 us)
Async XLA Ops:
  0.0 0.9 copy-start
  1.0 10.1 %collective-permute-start.4 = (bf16[160,768]{1,0:T(8,128)(2,1)S(1)}, bf16[160,768]{1,0:T(8,128)(2,1)S(1)}, u32[]{:S(2)}, u32[]{:S(2)}) collective-permute-start(bf16[160,768]{1,0:T(8,128)(2,1)S(1)} %split_coefs.1.refs_6_), channel_id=1, source_target_pairs={{0,2},{1,3},{2,0},{3,1},{4,6},{5,7},{6,4},{7,5},{8,10},{9,11},{10,... | collective-permute-start | bytes 737288 | tf_op jit(solution)/shard_map/ppermute | solution.py:48
  3.1 8.8 %collective-permute-start = (bf16[160,768]{1,0:T(8,128)(2,1)}, bf16[160,768]{1,0:T(8,128)(2,1)S(1)}, u32[]{:S(2)}, u32[]{:S(2)}) collective-permute-start(bf16[160,768]{1,0:T(8,128)(2,1)} %refs_0_), channel_id=1, source_target_pairs={{0,48},{1,49},{2,50},{3,51},{4,52},{5,53},{6,54},{7,55},{8,56},{9,... | collective-permute-start | bytes 737288 | tf_op jit(solution)/shard_map/ppermute | solution.py:48
  5.8 7.3 %collective-permute-start.1 = (bf16[160,768]{1,0:T(8,128)(2,1)}, bf16[160,768]{1,0:T(8,128)(2,1)S(1)}, u32[]{:S(2)}, u32[]{:S(2)}) collective-permute-start(bf16[160,768]{1,0:T(8,128)(2,1)} %refs_0_), channel_id=1, source_target_pairs={{0,16},{1,17},{2,18},{3,19},{4,20},{5,21},{6,22},{7,23},{8,24},{9,... | collective-permute-start | bytes 737288 | tf_op jit(solution)/shard_map/ppermute | solution.py:48
  6.1 8.4 %collective-permute-start.2 = (bf16[160,768]{1,0:T(8,128)(2,1)}, bf16[160,768]{1,0:T(8,128)(2,1)S(1)}, u32[]{:S(2)}, u32[]{:S(2)}) collective-permute-start(bf16[160,768]{1,0:T(8,128)(2,1)} %refs_1_), channel_id=1, source_target_pairs={{0,12},{1,13},{2,14},{3,15},{4,8},{5,9},{6,10},{7,11},{8,4},{9,5},... | collective-permute-start | bytes 737288 | tf_op jit(solution)/shard_map/ppermute | solution.py:48
  9.1 6.8 %collective-permute-start.3 = (bf16[160,768]{1,0:T(8,128)(2,1)}, bf16[160,768]{1,0:T(8,128)(2,1)S(1)}, u32[]{:S(2)}, u32[]{:S(2)}) collective-permute-start(bf16[160,768]{1,0:T(8,128)(2,1)} %refs_1_), channel_id=1, source_target_pairs={{0,4},{1,5},{2,6},{3,7},{4,0},{5,1},{6,2},{7,3},{8,12},{9,13},{10,... | collective-permute-start | bytes 737288 | tf_op jit(solution)/shard_map/ppermute | solution.py:48
  9.2 0.9 copy-start.2
  10.2 0.9 copy-start.3
  16.1 11.1 %collective-permute-start.9 = (bf16[320,768]{1,0:T(8,128)(2,1)S(1)}, bf16[320,768]{1,0:T(8,128)(2,1)S(1)}, u32[]{:S(2)}, u32[]{:S(2)}) collective-permute-start(bf16[320,768]{1,0:T(8,128)(2,1)S(1)} %get-tuple-element.103.refs_4_.refs_2_.refs_9_), channel_id=1, source_target_pairs={{0,16},{1,17},{2,18},{3,19},{4,20},{5,21},{6,22},{7,23},{8,24},{9,... | collective-permute-start | bytes 1474568 | tf_op jit(solution)/shard_map/ppermute | solution.py:48
  17.9 10.6 %collective-permute-start.6 = (bf16[320,768]{1,0:T(8,128)(2,1)S(1)}, bf16[320,768]{1,0:T(8,128)(2,1)S(1)}, u32[]{:S(2)}, u32[]{:S(2)}) collective-permute-start(bf16[320,768]{1,0:T(8,128)(2,1)S(1)} %get-tuple-element.79.refs_2_.refs_0_), channel_id=1, source_target_pairs={{0,4},{1,5},{2,6},{3,7},{4,0},{5,1},{6,2},{7,3},{8,12},{9,13},{10,... | collective-permute-start | bytes 1474568 | tf_op jit(solution)/shard_map/ppermute | solution.py:48
  18.2 10.5 %collective-permute-start.8 = (bf16[320,768]{1,0:T(8,128)(2,1)S(1)}, bf16[320,768]{1,0:T(8,128)(2,1)S(1)}, u32[]{:S(2)}, u32[]{:S(2)}) collective-permute-start(bf16[320,768]{1,0:T(8,128)(2,1)S(1)} %get-tuple-element.90.refs_2_.refs_1_), channel_id=1, source_target_pairs={{0,2},{1,3},{2,0},{3,1},{4,6},{5,7},{6,4},{7,5},{8,10},{9,11},{10,... | collective-permute-start | bytes 1474568 | tf_op jit(solution)/shard_map/ppermute | solution.py:48
  18.6 11.7 %collective-permute-start.5 = (bf16[320,768]{1,0:T(8,128)(2,1)S(1)}, bf16[320,768]{1,0:T(8,128)(2,1)S(1)}, u32[]{:S(2)}, u32[]{:S(2)}) collective-permute-start(bf16[320,768]{1,0:T(8,128)(2,1)S(1)} %get-tuple-element.78.refs_0_.refs_18_), channel_id=1, source_target_pairs={{0,12},{1,13},{2,14},{3,15},{4,8},{5,9},{6,10},{7,11},{8,4},{9,5},... | collective-permute-start | bytes 1474568 | tf_op jit(solution)/shard_map/ppermute | solution.py:48
  19.8 12.4 %collective-permute-start.7 = (bf16[320,768]{1,0:T(8,128)(2,1)S(1)}, bf16[320,768]{1,0:T(8,128)(2,1)S(1)}, u32[]{:S(2)}, u32[]{:S(2)}) collective-permute-start(bf16[320,768]{1,0:T(8,128)(2,1)S(1)} %get-tuple-element.88.refs_19_), channel_id=1, source_target_pairs={{0,66},{1,67},{2,64},{3,65},{4,70},{5,71},{6,68},{7,69},{8,74},{9,... | collective-permute-start | bytes 1474568 | tf_op jit(solution)/shard_map/ppermute | solution.py:48
  32.2 9.7 %collective-permute-start.14 = (bf16[320,768]{1,0:T(8,128)(2,1)S(1)}, bf16[320,768]{1,0:T(8,128)(2,1)S(1)}, u32[]{:S(2)}, u32[]{:S(2)}) collective-permute-start(bf16[320,768]{1,0:T(8,128)(2,1)S(1)} %get-tuple-element.103.refs_4_.refs_2_.refs_9_), channel_id=1, source_target_pairs={{0,4},{1,5},{2,6},{3,7},{4,0},{5,1},{6,2},{7,3},{8,12},{9,13},{10,... | collective-permute-start | bytes 1474568 | tf_op jit(solution)/shard_map/ppermute | solution.py:48
  33.3 9.2 %collective-permute-start.13 = (bf16[320,768]{1,0:T(8,128)(2,1)S(1)}, bf16[320,768]{1,0:T(8,128)(2,1)S(1)}, u32[]{:S(2)}, u32[]{:S(2)}) collective-permute-start(bf16[320,768]{1,0:T(8,128)(2,1)S(1)} %get-tuple-element.90.refs_2_.refs_1_), channel_id=1, source_target_pairs={{0,16},{1,17},{2,18},{3,19},{4,20},{5,21},{6,22},{7,23},{8,24},{9,... | collective-permute-start | bytes 1474568 | tf_op jit(solution)/shard_map/ppermute | solution.py:48
  33.7 10.2 %collective-permute-start.12 = (bf16[320,768]{1,0:T(8,128)(2,1)S(1)}, bf16[320,768]{1,0:T(8,128)(2,1)S(1)}, u32[]{:S(2)}, u32[]{:S(2)}) collective-permute-start(bf16[320,768]{1,0:T(8,128)(2,1)S(1)} %get-tuple-element.88.refs_19_), channel_id=1, source_target_pairs={{0,48},{1,49},{2,50},{3,51},{4,52},{5,53},{6,54},{7,55},{8,56},{9,... | collective-permute-start | bytes 1474568 | tf_op jit(solution)/shard_map/ppermute | solution.py:48
  34.8 10.1 %collective-permute-start.10 = (bf16[320,768]{1,0:T(8,128)(2,1)S(1)}, bf16[320,768]{1,0:T(8,128)(2,1)S(1)}, u32[]{:S(2)}, u32[]{:S(2)}) collective-permute-start(bf16[320,768]{1,0:T(8,128)(2,1)S(1)} %get-tuple-element.85), channel_id=1, source_target_pairs={{0,66},{1,67},{2,64},{3,65},{4,70},{5,71},{6,68},{7,69},{8,74},{9,... | collective-permute-start | bytes 1474568 | tf_op jit(solution)/shard_map/ppermute | solution.py:48
  37.8 8.8 %collective-permute-start.11 = (bf16[320,768]{1,0:T(8,128)(2,1)S(1)}, bf16[320,768]{1,0:T(8,128)(2,1)S(1)}, u32[]{:S(2)}, u32[]{:S(2)}) collective-permute-start(bf16[320,768]{1,0:T(8,128)(2,1)S(1)} %get-tuple-element.86), channel_id=1, source_target_pairs={{0,2},{1,3},{2,0},{3,1},{4,6},{5,7},{6,4},{7,5},{8,10},{9,11},{10,... | collective-permute-start | bytes 1474568 | tf_op jit(solution)/shard_map/ppermute | solution.py:48
  46.7 1.9 %collective-permute-start.15 = (bf16[320,768]{1,0:T(8,128)(2,1)S(1)}, bf16[320,768]{1,0:T(8,128)(2,1)S(1)}, u32[]{:S(2)}, u32[]{:S(2)}) collective-permute-start(bf16[320,768]{1,0:T(8,128)(2,1)S(1)} %collective-permute-done.11.refs_7_), channel_id=1, source_target_pairs={{0,1},{1,0},{2,3},{3,2},{4,5},{5,4},{6,7},{7,6},{8,9},{9,8},{10,11... | collective-permute-start | bytes 1474568 | tf_op jit(solution)/shard_map/ppermute | solution.py:48
  46.7 2.6 %collective-permute-start.16 = (bf16[320,768]{1,0:T(8,128)(2,1)S(1)}, bf16[320,768]{1,0:T(8,128)(2,1)S(1)}, u32[]{:S(2)}, u32[]{:S(2)}) collective-permute-start(bf16[320,768]{1,0:T(8,128)(2,1)S(1)} %collective-permute-done.13.refs_3_.refs_1_), channel_id=1, source_target_pairs={{0,1},{1,0},{2,3},{3,2},{4,5},{5,4},{6,7},{7,6},{8,9},{9,8},{10,11... | collective-permute-start | bytes 1474568 | tf_op jit(solution)/shard_map/ppermute | solution.py:48
  47.2 2.8 %collective-permute-start.17 = (bf16[320,768]{1,0:T(8,128)(2,1)S(1)}, bf16[320,768]{1,0:T(8,128)(2,1)S(1)}, u32[]{:S(2)}, u32[]{:S(2)}) collective-permute-start(bf16[320,768]{1,0:T(8,128)(2,1)S(1)} %collective-permute-done.14.refs_6_), channel_id=1, source_target_pairs={{0,1},{1,0},{2,3},{3,2},{4,5},{5,4},{6,7},{7,6},{8,9},{9,8},{10,11... | collective-permute-start | bytes 1474568 | tf_op jit(solution)/shard_map/ppermute | solution.py:48
  49.9 5.4 %collective-permute-start.21 = (bf16[640,2304]{1,0:T(8,128)(2,1)S(1)}, bf16[640,2304]{1,0:T(8,128)(2,1)S(1)}, u32[]{:S(2)}, u32[]{:S(2)}) collective-permute-start(bf16[640,2304]{1,0:T(8,128)(2,1)S(1)} %four.1), channel_id=1, source_target_pairs={{0,1},{1,0},{2,3},{3,2},{4,5},{5,4},{6,7},{7,6},{8,9},{9,8},{10,11... | collective-permute-start | bytes 8847368 | tf_op jit(solution)/shard_map/ppermute | solution.py:48
  50.1 16.4 %collective-permute-start.20 = (bf16[320,768]{1,0:T(8,128)(2,1)S(1)}, bf16[320,768]{1,0:T(8,128)(2,1)S(1)}, u32[]{:S(2)}, u32[]{:S(2)}) collective-permute-start(bf16[320,768]{1,0:T(8,128)(2,1)S(1)} %collective-permute-done.8.refs_3_.refs_8_), channel_id=1, source_target_pairs={{0,16},{1,17},{2,18},{3,19},{4,20},{5,21},{6,22},{7,23},{8,24},{9,... | collective-permute-start | bytes 1474568 | tf_op jit(solution)/shard_map/ppermute | solution.py:48
  50.7 15.9 %collective-permute-start.19 = (bf16[320,768]{1,0:T(8,128)(2,1)S(1)}, bf16[320,768]{1,0:T(8,128)(2,1)S(1)}, u32[]{:S(2)}, u32[]{:S(2)}) collective-permute-start(bf16[320,768]{1,0:T(8,128)(2,1)S(1)} %get-tuple-element.99), channel_id=1, source_target_pairs={{0,2},{1,3},{2,0},{3,1},{4,6},{5,7},{6,4},{7,5},{8,10},{9,11},{10,... | collective-permute-start | bytes 1474568 | tf_op jit(solution)/shard_map/ppermute | solution.py:48
  50.8 16.7 %collective-permute-start.26 = (bf16[320,768]{1,0:T(8,128)(2,1)S(1)}, bf16[320,768]{1,0:T(8,128)(2,1)S(1)}, u32[]{:S(2)}, u32[]{:S(2)}) collective-permute-start(bf16[320,768]{1,0:T(8,128)(2,1)S(1)} %collective-permute-done.7.refs_17_), channel_id=1, source_target_pairs={{0,48},{1,49},{2,50},{3,51},{4,52},{5,53},{6,54},{7,55},{8,56},{9,... | collective-permute-start | bytes 1474568 | tf_op jit(solution)/shard_map/ppermute | solution.py:48
  53.4 13.7 %collective-permute-start.18 = (bf16[320,768]{1,0:T(8,128)(2,1)S(1)}, bf16[320,768]{1,0:T(8,128)(2,1)S(1)}, u32[]{:S(2)}, u32[]{:S(2)}) collective-permute-start(bf16[320,768]{1,0:T(8,128)(2,1)S(1)} %collective-permute-done.9.refs_5_.refs_4_), channel_id=1, source_target_pairs={{0,4},{1,5},{2,6},{3,7},{4,0},{5,1},{6,2},{7,3},{8,12},{9,13},{10,... | collective-permute-start | bytes 1474568 | tf_op jit(solution)/shard_map/ppermute | solution.py:48
  55.3 14.5 %collective-permute-start.25 = (bf16[320,768]{1,0:T(8,128)(2,1)S(1)}, bf16[320,768]{1,0:T(8,128)(2,1)S(1)}, u32[]{:S(2)}, u32[]{:S(2)}) collective-permute-start(bf16[320,768]{1,0:T(8,128)(2,1)S(1)} %get-tuple-element.112), channel_id=1, source_target_pairs={{0,66},{1,67},{2,64},{3,65},{4,70},{5,71},{6,68},{7,69},{8,74},{9,... | collective-permute-start | bytes 1474568 | tf_op jit(solution)/shard_map/ppermute | solution.py:48
  66.5 6.8 %collective-permute-start.24 = (bf16[320,768]{1,0:T(8,128)(2,1)S(1)}, bf16[320,768]{1,0:T(8,128)(2,1)S(1)}, u32[]{:S(2)}, u32[]{:S(2)}) collective-permute-start(bf16[320,768]{1,0:T(8,128)(2,1)S(1)} %collective-permute-done.20.refs_4_), channel_id=1, source_target_pairs={{0,1},{1,0},{2,3},{3,2},{4,5},{5,4},{6,7},{7,6},{8,9},{9,8},{10,11... | collective-permute-start | bytes 1474568 | tf_op jit(solution)/shard_map/ppermute | solution.py:48
  66.6 6.7 %collective-permute-start.23 = (bf16[320,768]{1,0:T(8,128)(2,1)S(1)}, bf16[320,768]{1,0:T(8,128)(2,1)S(1)}, u32[]{:S(2)}, u32[]{:S(2)}) collective-permute-start(bf16[320,768]{1,0:T(8,128)(2,1)S(1)} %collective-permute-done.19.refs_3_), channel_id=1, source_target_pairs={{0,1},{1,0},{2,3},{3,2},{4,5},{5,4},{6,7},{7,6},{8,9},{9,8},{10,11... | collective-permute-start | bytes 1474568 | tf_op jit(solution)/shard_map/ppermute | solution.py:48
  67.1 6.2 %collective-permute-start.22 = (bf16[320,768]{1,0:T(8,128)(2,1)S(1)}, bf16[320,768]{1,0:T(8,128)(2,1)S(1)}, u32[]{:S(2)}, u32[]{:S(2)}) collective-permute-start(bf16[320,768]{1,0:T(8,128)(2,1)S(1)} %collective-permute-done.18.refs_2_), channel_id=1, source_target_pairs={{0,1},{1,0},{2,3},{3,2},{4,5},{5,4},{6,7},{7,6},{8,9},{9,8},{10,11... | collective-permute-start | bytes 1474568 | tf_op jit(solution)/shard_map/ppermute | solution.py:48
  77.3 11.7 %collective-permute-start.29 = (f32[160,345]{1,0:T(8,128)S(1)}, f32[160,345]{1,0:T(8,128)S(1)}, u32[]{:S(2)}, u32[]{:S(2)}) collective-permute-start(f32[160,345]{1,0:T(8,128)S(1)} %get-tuple-element.121), channel_id=1, source_target_pairs={{0,66},{1,67},{2,64},{3,65},{4,70},{5,71},{6,68},{7,69},{8,74},{9,... | collective-permute-start | bytes 662408 | tf_op jit(solution)/shard_map/ppermute | solution.py:48
  78.6 14.3 %collective-permute-start.27 = (f32[160,345]{1,0:T(8,128)S(1)}, f32[160,345]{1,0:T(8,128)S(1)}, u32[]{:S(2)}, u32[]{:S(2)}) collective-permute-start(f32[160,345]{1,0:T(8,128)S(1)} %get-tuple-element.125), channel_id=1, source_target_pairs={{0,12},{1,13},{2,14},{3,15},{4,8},{5,9},{6,10},{7,11},{8,4},{9,5},... | collective-permute-start | bytes 662408 | tf_op jit(solution)/shard_map/ppermute | solution.py:48
  80.1 11.3 %collective-permute-start.31 = (f32[160,345]{1,0:T(8,128)S(1)}, f32[160,345]{1,0:T(8,128)S(1)}, u32[]{:S(2)}, u32[]{:S(2)}) collective-permute-start(f32[160,345]{1,0:T(8,128)S(1)} %get-tuple-element.131), channel_id=1, source_target_pairs={{0,48},{1,49},{2,50},{3,51},{4,52},{5,53},{6,54},{7,55},{8,56},{9,... | collective-permute-start | bytes 662408 | tf_op jit(solution)/shard_map/ppermute | solution.py:48
  82.3 15.2 %collective-permute-start.28 = (f32[160,345]{1,0:T(8,128)S(1)}, f32[160,345]{1,0:T(8,128)S(1)}, u32[]{:S(2)}, u32[]{:S(2)}) collective-permute-start(f32[160,345]{1,0:T(8,128)S(1)} %get-tuple-element.127), channel_id=1, source_target_pairs={{0,126},{1,127},{2,124},{3,125},{4,122},{5,123},{6,120},{7,121},{8... | collective-permute-start | bytes 662408 | tf_op jit(solution)/shard_map/ppermute | solution.py:48
  89.0 9.4 %collective-permute-start.30 = (f32[160,345]{1,0:T(8,128)S(1)}, f32[160,345]{1,0:T(8,128)S(1)}, u32[]{:S(2)}, u32[]{:S(2)}) collective-permute-start(f32[160,345]{1,0:T(8,128)S(1)} %add.27), channel_id=1, source_target_pairs={{0,48},{1,49},{2,50},{3,51},{4,52},{5,53},{6,54},{7,55},{8,56},{9,... | collective-permute-start | bytes 662408 | tf_op jit(solution)/shard_map/ppermute | solution.py:48
  91.4 8.5 %collective-permute-start.32 = (f32[160,345]{1,0:T(8,128)S(1)}, f32[160,345]{1,0:T(8,128)S(1)}, u32[]{:S(2)}, u32[]{:S(2)}) collective-permute-start(f32[160,345]{1,0:T(8,128)S(1)} %add.29), channel_id=1, source_target_pairs={{0,12},{1,13},{2,14},{3,15},{4,8},{5,9},{6,10},{7,11},{8,4},{9,5},... | collective-permute-start | bytes 662408 | tf_op jit(solution)/shard_map/ppermute | solution.py:48
  93.0 8.3 %copy-start.1 = (f32[345,160]{0,1:T(8,128)S(1)}, f32[345,160]{0,1:T(8,128)}, u32[]{:S(2)}) copy-start(f32[345,160]{0,1:T(8,128)} %param.7) | copy-start | bytes 662404
  93.0 8.3 %copy-start.4 = (s32[160]{0:T(256)S(1)}, s32[160]{0:T(256)}, u32[]{:S(2)}) copy-start(s32[160]{0:T(256)} %param.6) | copy-start | bytes 1924
  93.0 8.3 %collective-permute-start.33 = (f32[160,345]{1,0:T(8,128)S(1)}, f32[160,345]{1,0:T(8,128)S(1)}, u32[]{:S(2)}, u32[]{:S(2)}) collective-permute-start(f32[160,345]{1,0:T(8,128)S(1)} %add.25), channel_id=1, source_target_pairs={{0,66},{1,67},{2,64},{3,65},{4,70},{5,71},{6,68},{7,69},{8,74},{9,... | collective-permute-start | bytes 662408 | tf_op jit(solution)/shard_map/ppermute | solution.py:48

commit v9 on v8

--- a/solution.py
+++ b/solution.py
@@ -325,13 +325,14 @@
     left_2 = [left[k] for k in second]
     left_2 += [(act_mate[k], sig_mate[k], coef_mate[k]) for k in second]
 
-    (sum_xz, sum_xyz, sum_xy, sum_yz), (rows_2, coefs_2) = partial_sums(
-        [(wide_2, 0, 320, total_2, 0), (wide_1, 0, 320, total_1, 0)], left_2, True, "second_far"
+    (sum_xyz,), (rows_2, coefs_2) = partial_sums([(wide_2, 160, 160, total_2, 160)], left_2, True, "second_farthest")
+    got_xyz = send(sum_xyz, "far", "xyz")
+    (sum_xz, sum_xy, sum_yz), _ = partial_sums(
+        [(wide_2, 0, 160, total_2, 0), (wide_1, 0, 320, total_1, 0)], (rows_2, coefs_2), True, "second_far"
     )
     part_x, part_y, part_z = send(sum_xz, "far", "z"), send(sum_xy, "far", "x"), send(sum_yz, "far", "y")
-    got_xyz = send(sum_xyz, "far", "xyz")
     (sum_x, sum_y, sum_z), _ = partial_sums(
-        [(wide_1, 320, 480, total_1, 320)], (after(rows_2, sum_xz), coefs_2), True, "second_near"
+        [(wide_1, 320, 480, total_1, 320)], (after(rows_2, sum_xz, got_xyz), coefs_2), True, "second_near"
     )
     got_x = send(after(sum_x + part_x, sum_z), "far", "x")
     got_y = send(after(sum_y + part_y, sum_z), "far", "y")

time: 102 us -> 106 us (1.039)
  waiting for transfers between devices: 33.7 us -> 36.7 us
    ppermute x34, waiting for transfers between devices: 33.7 us -> 36.7 us  [send(): return lax.ppermute(value, AXES, moves(group, dims))]
    pallas_call x5 -> x6, Pallas kernels: 21.9 us -> 22.9 us  [partial_sums(): pl.pallas_call(functools.partial(block_kernel, plan, n_in, parts, left_re...]
  transfers between devices with their start and end apart: 34 -> 34, of which waited for: 23 -> 24; matrix products, arithmetic and copies ran while one was open for 0% -> 0% of each run, Pallas kernels for 18% -> 20%
where the time goes in v9:
time: 106 us
  starting transfers between devices  42.1 us (40%)
  waiting for transfers between devices  36.7 us (35%)
  Pallas kernels  23.4 us (22%)
  local copies, waits for them, and re-layouts  2.84 us (3%)
    ppermute x34, starting transfers between devices, send(): return lax.ppermute(value, AXES, moves(group, dims))  42.1 us
    ppermute x34, waiting for transfers between devices, send(): return lax.ppermute(value, AXES, moves(group, dims))  36.7 us
    pallas_call x6, Pallas kernels, partial_sums(): pl.pallas_call(functools.partial(block_kernel, plan, n_in, parts, left_re...  22.9 us
    unnamed x10, local copies, waits for them, and re-layouts  2.84 us
  transfers between devices with their start and end apart: 34, of which 24 were waited for; matrix products, arithmetic and copies ran while one was open for 0% of the time, Pallas kernels for 20%

profile of v9, /device:TPU:0, one launch (start us, length us, event | category | flops | bytes accessed | tf_op | source)
XLA Modules:
  0.0 106.2 jit_solution(6971221241215549933)
XLA Ops:
  0.0 0.9 copy-done
  1.0 2.1 %collective-permute-start.4 = (bf16[160,768]{1,0:T(8,128)(2,1)S(1)}, bf16[160,768]{1,0:T(8,128)(2,1)S(1)}, u32[]{:S(2)}, u32[]{:S(2)}) collective-permute-start(bf16[160,768]{1,0:T(8,128)(2,1)S(1)} %split_coefs.1.refs_6_), channel_id=1, source_target_pairs={{0,2},{1,3},{2,0},{3,1},{4,6},{5,7},{6,4},{7,5},{8,10},{9,11},{10,... | collective-permute-start | bytes 737288 | tf_op jit(solution)/shard_map/ppermute | solution.py:48
  3.1 2.8 %collective-permute-start = (bf16[160,768]{1,0:T(8,128)(2,1)}, bf16[160,768]{1,0:T(8,128)(2,1)S(1)}, u32[]{:S(2)}, u32[]{:S(2)}) collective-permute-start(bf16[160,768]{1,0:T(8,128)(2,1)} %refs_0_), channel_id=1, source_target_pairs={{0,48},{1,49},{2,50},{3,51},{4,52},{5,53},{6,54},{7,55},{8,56},{9,... | collective-permute-start | bytes 737288 | tf_op jit(solution)/shard_map/ppermute | solution.py:48
  5.8 0.2 collective-permute-start.1
  6.1 3.0 %collective-permute-start.2 = (bf16[160,768]{1,0:T(8,128)(2,1)}, bf16[160,768]{1,0:T(8,128)(2,1)S(1)}, u32[]{:S(2)}, u32[]{:S(2)}) collective-permute-start(bf16[160,768]{1,0:T(8,128)(2,1)} %refs_1_), channel_id=1, source_target_pairs={{0,12},{1,13},{2,14},{3,15},{4,8},{5,9},{6,10},{7,11},{8,4},{9,5},... | collective-permute-start | bytes 737288 | tf_op jit(solution)/shard_map/ppermute | solution.py:48
  9.1 0.1 collective-permute-start.3
  9.2 0.9 copy-done.2
  10.2 0.9 copy-done.3
  11.2 0.8 collective-permute-done.refs_1_
  11.9 1.3 %collective-permute-done.1.refs_2_ = bf16[160,768]{1,0:T(8,128)(2,1)S(1)} collective-permute-done((bf16[160,768]{1,0:T(8,128)(2,1)}, bf16[160,768]{1,0:T(8,128)(2,1)S(1)}, u32[]{:S(2)}, u32[]{:S(2)}) %collective-permute-start.1) | collective-permute-done | bytes 245792 | tf_op jit(solution)/shard_map/ppermute | solution.py:48
  13.2 1.3 %collective-permute-done.2.refs_4_ = bf16[160,768]{1,0:T(8,128)(2,1)S(1)} collective-permute-done((bf16[160,768]{1,0:T(8,128)(2,1)}, bf16[160,768]{1,0:T(8,128)(2,1)S(1)}, u32[]{:S(2)}, u32[]{:S(2)}) %collective-permute-start.2) | collective-permute-done | bytes 245792 | tf_op jit(solution)/shard_map/ppermute | solution.py:48
  14.5 1.5 %collective-permute-done.3.refs_5_ = bf16[160,768]{1,0:T(8,128)(2,1)S(1)} collective-permute-done((bf16[160,768]{1,0:T(8,128)(2,1)}, bf16[160,768]{1,0:T(8,128)(2,1)S(1)}, u32[]{:S(2)}, u32[]{:S(2)}) %collective-permute-start.3) | collective-permute-done | bytes 245792 | tf_op jit(solution)/shard_map/ppermute | solution.py:48
  15.9 0.2 pairs.1
  16.1 1.8 %collective-permute-start.9 = (bf16[320,768]{1,0:T(8,128)(2,1)S(1)}, bf16[320,768]{1,0:T(8,128)(2,1)S(1)}, u32[]{:S(2)}, u32[]{:S(2)}) collective-permute-start(bf16[320,768]{1,0:T(8,128)(2,1)S(1)} %get-tuple-element.103.refs_4_.refs_2_.refs_9_), channel_id=1, source_target_pairs={{0,16},{1,17},{2,18},{3,19},{4,20},{5,21},{6,22},{7,23},{8,24},{9,... | collective-permute-start | bytes 1474568 | tf_op jit(solution)/shard_map/ppermute | solution.py:48
  17.9 0.3 collective-permute-start.6
  18.2 0.4 collective-permute-start.8
  18.6 1.2 %collective-permute-start.5 = (bf16[320,768]{1,0:T(8,128)(2,1)S(1)}, bf16[320,768]{1,0:T(8,128)(2,1)S(1)}, u32[]{:S(2)}, u32[]{:S(2)}) collective-permute-start(bf16[320,768]{1,0:T(8,128)(2,1)S(1)} %get-tuple-element.78.refs_0_.refs_18_), channel_id=1, source_target_pairs={{0,12},{1,13},{2,14},{3,15},{4,8},{5,9},{6,10},{7,11},{8,4},{9,5},... | collective-permute-start | bytes 1474568 | tf_op jit(solution)/shard_map/ppermute | solution.py:48
  19.8 3.8 %collective-permute-start.7 = (bf16[320,768]{1,0:T(8,128)(2,1)S(1)}, bf16[320,768]{1,0:T(8,128)(2,1)S(1)}, u32[]{:S(2)}, u32[]{:S(2)}) collective-permute-start(bf16[320,768]{1,0:T(8,128)(2,1)S(1)} %get-tuple-element.88.refs_19_), channel_id=1, source_target_pairs={{0,66},{1,67},{2,64},{3,65},{4,70},{5,71},{6,68},{7,69},{8,74},{9,... | collective-permute-start | bytes 1474568 | tf_op jit(solution)/shard_map/ppermute | solution.py:48
  23.6 3.6 %collective-permute-done.9.refs_5_.refs_4_ = bf16[320,768]{1,0:T(8,128)(2,1)S(1)} collective-permute-done((bf16[320,768]{1,0:T(8,128)(2,1)S(1)}, bf16[320,768]{1,0:T(8,128)(2,1)S(1)}, u32[]{:S(2)}, u32[]{:S(2)}) %collective-permute-start.9) | collective-permute-done | bytes 491552 | tf_op jit(solution)/shard_map/ppermute | solution.py:48
  27.1 1.4 %collective-permute-done.6.refs_3_.refs_1_.refs_5_.refs_0_ = bf16[320,768]{1,0:T(8,128)(2,1)S(1)} collective-permute-done((bf16[320,768]{1,0:T(8,128)(2,1)S(1)}, bf16[320,768]{1,0:T(8,128)(2,1)S(1)}, u32[]{:S(2)}, u32[]{:S(2)}) %collective-permute-start.6) | collective-permute-done | bytes 491552 | tf_op jit(solution)/shard_map/ppermute | solution.py:48
  28.5 0.2 collective-permute-done.8.refs_3_.refs_8_
  28.8 1.6 %collective-permute-done.5.refs_1_.refs_14_ = bf16[320,768]{1,0:T(8,128)(2,1)S(1)} collective-permute-done((bf16[320,768]{1,0:T(8,128)(2,1)S(1)}, bf16[320,768]{1,0:T(8,128)(2,1)S(1)}, u32[]{:S(2)}, u32[]{:S(2)}) %collective-permute-start.5) | collective-permute-done | bytes 491552 | tf_op jit(solution)/shard_map/ppermute | solution.py:48
  30.3 1.8 %collective-permute-done.7.refs_17_ = bf16[320,768]{1,0:T(8,128)(2,1)S(1)} collective-permute-done((bf16[320,768]{1,0:T(8,128)(2,1)S(1)}, bf16[320,768]{1,0:T(8,128)(2,1)S(1)}, u32[]{:S(2)}, u32[]{:S(2)}) %collective-permute-start.7) | collective-permute-done | bytes 491552 | tf_op jit(solution)/shard_map/ppermute | solution.py:48
  32.2 1.1 %collective-permute-start.14 = (bf16[320,768]{1,0:T(8,128)(2,1)S(1)}, bf16[320,768]{1,0:T(8,128)(2,1)S(1)}, u32[]{:S(2)}, u32[]{:S(2)}) collective-permute-start(bf16[320,768]{1,0:T(8,128)(2,1)S(1)} %get-tuple-element.103.refs_4_.refs_2_.refs_9_), channel_id=1, source_target_pairs={{0,4},{1,5},{2,6},{3,7},{4,0},{5,1},{6,2},{7,3},{8,12},{9,13},{10,... | collective-permute-start | bytes 1474568 | tf_op jit(solution)/shard_map/ppermute | solution.py:48
  33.3 0.4 collective-permute-start.13
  33.7 1.0 collective-permute-start.12
  34.8 3.0 %collective-permute-start.10 = (bf16[320,768]{1,0:T(8,128)(2,1)S(1)}, bf16[320,768]{1,0:T(8,128)(2,1)S(1)}, u32[]{:S(2)}, u32[]{:S(2)}) collective-permute-start(bf16[320,768]{1,0:T(8,128)(2,1)S(1)} %get-tuple-element.85), channel_id=1, source_target_pairs={{0,66},{1,67},{2,64},{3,65},{4,70},{5,71},{6,68},{7,69},{8,74},{9,... | collective-permute-start | bytes 1474568 | tf_op jit(solution)/shard_map/ppermute | solution.py:48
  37.8 0.2 four.1
  38.0 3.8 %collective-permute-done.14.refs_6_ = bf16[320,768]{1,0:T(8,128)(2,1)S(1)} collective-permute-done((bf16[320,768]{1,0:T(8,128)(2,1)S(1)}, bf16[320,768]{1,0:T(8,128)(2,1)S(1)}, u32[]{:S(2)}, u32[]{:S(2)}) %collective-permute-start.14) | collective-permute-done | bytes 491552 | tf_op jit(solution)/shard_map/ppermute | solution.py:48
  41.9 0.6 collective-permute-done.13.refs_3_.refs_1_
  42.5 1.4 %collective-permute-done.12.refs_15_ = bf16[320,768]{1,0:T(8,128)(2,1)S(1)} collective-permute-done((bf16[320,768]{1,0:T(8,128)(2,1)S(1)}, bf16[320,768]{1,0:T(8,128)(2,1)S(1)}, u32[]{:S(2)}, u32[]{:S(2)}) %collective-permute-start.12) | collective-permute-done | bytes 491552 | tf_op jit(solution)/shard_map/ppermute | solution.py:48
  43.8 1.1 %collective-permute-done.10.refs_16_ = bf16[320,768]{1,0:T(8,128)(2,1)S(1)} collective-permute-done((bf16[320,768]{1,0:T(8,128)(2,1)S(1)}, bf16[320,768]{1,0:T(8,128)(2,1)S(1)}, u32[]{:S(2)}, u32[]{:S(2)}) %collective-permute-start.10) | collective-permute-done | bytes 491552 | tf_op jit(solution)/shard_map/ppermute | solution.py:48
  44.9 1.7 %collective-permute-done.11.refs_7_ = bf16[320,768]{1,0:T(8,128)(2,1)S(1)} collective-permute-done((bf16[320,768]{1,0:T(8,128)(2,1)S(1)}, bf16[320,768]{1,0:T(8,128)(2,1)S(1)}, u32[]{:S(2)}, u32[]{:S(2)}) %collective-permute-start.11) | collective-permute-done | bytes 491552 | tf_op jit(solution)/shard_map/ppermute | solution.py:48
  46.7 0.5 collective-permute-start.16
  47.2 1.3 %collective-permute-done.15.refs_13_ = bf16[320,768]{1,0:T(8,128)(2,1)S(1)} collective-permute-done((bf16[320,768]{1,0:T(8,128)(2,1)S(1)}, bf16[320,768]{1,0:T(8,128)(2,1)S(1)}, u32[]{:S(2)}, u32[]{:S(2)}) %collective-permute-start.15) | collective-permute-done | bytes 491552 | tf_op jit(solution)/shard_map/ppermute | solution.py:48
  48.5 0.7 collective-permute-done.16.refs_11_.refs_7_
  49.2 0.7 collective-permute-done.17.refs_12_
  50.1 0.7 collective-permute-start.20
  50.8 2.6 %collective-permute-start.26 = (bf16[320,768]{1,0:T(8,128)(2,1)S(1)}, bf16[320,768]{1,0:T(8,128)(2,1)S(1)}, u32[]{:S(2)}, u32[]{:S(2)}) collective-permute-start(bf16[320,768]{1,0:T(8,128)(2,1)S(1)} %collective-permute-done.7.refs_17_), channel_id=1, source_target_pairs={{0,48},{1,49},{2,50},{3,51},{4,52},{5,53},{6,54},{7,55},{8,56},{9,... | collective-permute-start | bytes 1474568 | tf_op jit(solution)/shard_map/ppermute | solution.py:48
  53.4 0.9 collective-permute-start.18
  54.3 1.0 collective-permute-done.21.refs_10_.refs_6_
  55.3 1.2 %collective-permute-start.25 = (bf16[320,768]{1,0:T(8,128)(2,1)S(1)}, bf16[320,768]{1,0:T(8,128)(2,1)S(1)}, u32[]{:S(2)}, u32[]{:S(2)}) collective-permute-start(bf16[320,768]{1,0:T(8,128)(2,1)S(1)} %get-tuple-element.112), channel_id=1, source_target_pairs={{0,66},{1,67},{2,64},{3,65},{4,70},{5,71},{6,68},{7,69},{8,74},{9,... | collective-permute-start | bytes 1474568 | tf_op jit(solution)/shard_map/ppermute | solution.py:48
  56.5 10.0 %early.1 = (f32[960,384]{1,0:T(8,128)S(1)}, bf16[1600,1536]{1,0:T(8,128)(2,1)S(1)}, bf16[1600,768]{1,0:T(8,128)(2,1)S(1)}, bf16[960,1536]{1,0:T(8,128)(2,1)S(1)}) custom-call(bf16[320,768]{1,0:T(8,128)(2,1)S(1)} %get-tuple-element.79.refs_2_.refs_0_, bf16[320,768]{1,0:T(8,128)(2,1)S(1)} %get-tuple-element.90.refs_2_.refs_1_, ...), custom_call_target="tpu_custom_call" | custom-call | flops 8294400000 | bytes 1000000 | tf_op jit(solution)/shard_map/early/pallas_call | solution.py:209
  66.6 0.5 collective-permute-start.23
  67.1 0.3 collective-permute-start.22
  67.4 2.4 %collective-permute-done.25.refs_0_ = bf16[320,768]{1,0:T(8,128)(2,1)S(1)} collective-permute-done((bf16[320,768]{1,0:T(8,128)(2,1)S(1)}, bf16[320,768]{1,0:T(8,128)(2,1)S(1)}, u32[]{:S(2)}, u32[]{:S(2)}) %collective-permute-start.25) | collective-permute-done | bytes 491552 | tf_op jit(solution)/shard_map/ppermute | solution.py:48
  69.8 3.5 %early_right.1 = (f32[320,384]{1,0:T(8,128)S(1)}, bf16[320,1536]{1,0:T(8,128)(2,1)S(1)}) custom-call(bf16[320,768]{1,0:T(8,128)(2,1)S(1)} %collective-permute-done.25.refs_0_, bf16[320,768]{1,0:T(8,128)(2,1)S(1)} %collective-permute-done.26.refs_1_, bf16[1600,1536]{1,0:T(8,128)(2,1)S(1)} %get-tuple-element.115.refs_2_, ...), custom_call_target="tpu_custom_call" | custom-call | flops 2764800000 | bytes 1000000 | tf_op jit(solution)/shard_map/early_right/pallas_call | solution.py:209
  73.3 1.5 %second_farthest.1 = (f32[160,345]{1,0:T(8,128)S(1)}, bf16[960,1536]{1,0:T(8,128)(2,1)S(1)}, bf16[960,768]{1,0:T(8,128)(2,1)S(1)}) custom-call(bf16[320,768]{1,0:T(8,128)(2,1)S(1)} %collective-permute-done.6.refs_3_.refs_1_.refs_5_.refs_0_, bf16[320,768]{1,0:T(8,128)(2,1)S(1)} %collective-permute-done.13.refs_3_.refs_1_, ...), custom_call_target="tpu_custom_call" | custom-call | flops 829440000 | bytes 1000000 | tf_op jit(solution)/shard_map/second_farthest/pallas_call | solution.py:209
  74.8 3.9 %collective-permute-start.27 = (f32[160,345]{1,0:T(8,128)S(1)}, f32[160,345]{1,0:T(8,128)S(1)}, u32[]{:S(2)}, u32[]{:S(2)}) collective-permute-start(f32[160,345]{1,0:T(8,128)S(1)} %get-tuple-element.123), channel_id=1, source_target_pairs={{0,126},{1,127},{2,124},{3,125},{4,122},{5,123},{6,120},{7,121},{8... | collective-permute-start | bytes 662408 | tf_op jit(solution)/shard_map/ppermute | solution.py:48
  78.7 3.4 %second_far.1 = (f32[160,345]{1,0:T(8,128)S(1)}, f32[160,345]{1,0:T(8,128)S(1)}, f32[160,345]{1,0:T(8,128)S(1)}) custom-call(bf16[960,1536]{1,0:T(8,128)(2,1)S(1)} %get-tuple-element.127.refs_0_, bf16[960,768]{1,0:T(8,128)(2,1)S(1)} %get-tuple-element.120.refs_1_, bf16[320,1536]{1,0:T(8,128)(2,1)S(1)} %get-tuple-element.117.refs_11_.refs_2_, ...), custom_call_target="tpu_custom_call" | custom-call | flops 2488320000 | bytes 1000000 | tf_op jit(solution)/shard_map/second_far/pallas_call | solution.py:209
  82.1 1.9 %collective-permute-start.28 = (f32[160,345]{1,0:T(8,128)S(1)}, f32[160,345]{1,0:T(8,128)S(1)}, u32[]{:S(2)}, u32[]{:S(2)}) collective-permute-start(f32[160,345]{1,0:T(8,128)S(1)} %get-tuple-element.126), channel_id=1, source_target_pairs={{0,12},{1,13},{2,14},{3,15},{4,8},{5,9},{6,10},{7,11},{8,4},{9,5},... | collective-permute-start | bytes 662408 | tf_op jit(solution)/shard_map/ppermute | solution.py:48
  84.0 2.0 %collective-permute-start.29 = (f32[160,345]{1,0:T(8,128)S(1)}, f32[160,345]{1,0:T(8,128)S(1)}, u32[]{:S(2)}, u32[]{:S(2)}) collective-permute-start(f32[160,345]{1,0:T(8,128)S(1)} %get-tuple-element.122), channel_id=1, source_target_pairs={{0,66},{1,67},{2,64},{3,65},{4,70},{5,71},{6,68},{7,69},{8,74},{9,... | collective-permute-start | bytes 662408 | tf_op jit(solution)/shard_map/ppermute | solution.py:48
  86.0 1.0 collective-permute-start.31
  87.0 0.6 collective-permute-done.27
  87.6 3.0 %second_near.1 = (f32[160,345]{1,0:T(8,128)S(1)}, f32[160,345]{1,0:T(8,128)S(1)}, f32[160,345]{1,0:T(8,128)S(1)}) custom-call(bf16[960,1536]{1,0:T(8,128)(2,1)S(1)} %get-tuple-element.127.refs_0_, bf16[960,768]{1,0:T(8,128)(2,1)S(1)} %get-tuple-element.120.refs_1_, bf16[960,1536]{1,0:T(8,128)(2,1)S(1)} %get-tuple-element.121.refs_4_.refs_2_, ...), custom_call_target="tpu_custom_call" | custom-call | flops 2488320000 | bytes 1000000 | tf_op jit(solution)/shard_map/second_near/pallas_call | solution.py:209
  90.6 2.1 %collective-permute-done.29 = f32[160,345]{1,0:T(8,128)S(1)} collective-permute-done((f32[160,345]{1,0:T(8,128)S(1)}, f32[160,345]{1,0:T(8,128)S(1)}, u32[]{:S(2)}, u32[]{:S(2)}) %collective-permute-start.29) | collective-permute-done | bytes 220832 | tf_op jit(solution)/shard_map/ppermute | solution.py:48
  92.8 2.3 %collective-permute-start.30 = (f32[160,345]{1,0:T(8,128)S(1)}, f32[160,345]{1,0:T(8,128)S(1)}, u32[]{:S(2)}, u32[]{:S(2)}) collective-permute-start(f32[160,345]{1,0:T(8,128)S(1)} %add.27), channel_id=1, source_target_pairs={{0,48},{1,49},{2,50},{3,51},{4,52},{5,53},{6,54},{7,55},{8,56},{9,... | collective-permute-start | bytes 662408 | tf_op jit(solution)/shard_map/ppermute | solution.py:48
  95.2 1.5 %collective-permute-start.32 = (f32[160,345]{1,0:T(8,128)S(1)}, f32[160,345]{1,0:T(8,128)S(1)}, u32[]{:S(2)}, u32[]{:S(2)}) collective-permute-start(f32[160,345]{1,0:T(8,128)S(1)} %add.29), channel_id=1, source_target_pairs={{0,12},{1,13},{2,14},{3,15},{4,8},{5,9},{6,10},{7,11},{8,4},{9,5},... | collective-permute-start | bytes 662408 | tf_op jit(solution)/shard_map/ppermute | solution.py:48
  96.8 1.3 %collective-permute-start.33 = (f32[160,345]{1,0:T(8,128)S(1)}, f32[160,345]{1,0:T(8,128)S(1)}, u32[]{:S(2)}, u32[]{:S(2)}) collective-permute-start(f32[160,345]{1,0:T(8,128)S(1)} %add.25), channel_id=1, source_target_pairs={{0,66},{1,67},{2,64},{3,65},{4,70},{5,71},{6,68},{7,69},{8,74},{9,... | collective-permute-start | bytes 662408 | tf_op jit(solution)/shard_map/ppermute | solution.py:48
  98.1 1.5 %second_here.1 = f32[160,345]{1,0:T(8,128)S(1)} custom-call(bf16[960,1536]{1,0:T(8,128)(2,1)S(1)} %get-tuple-element.127.refs_0_, bf16[960,768]{1,0:T(8,128)(2,1)S(1)} %get-tuple-element.120.refs_1_, bf16[960,1536]{1,0:T(8,128)(2,1)S(1)} %get-tuple-element.121.refs_4_.refs_2_, f32[960,384]{1,0:T(8,128)S(1)} %get-tuple-element.107.refs_5_.refs_3_), custom_call_target="tpu_custom_call" | custom-call | flops 829440000 | bytes 1000000 | tf_op jit(solution)/shard_map/second_here/pallas_call | solution.py:209
  99.6 1.6 %collective-permute-done.30 = f32[160,345]{1,0:T(8,128)S(1)} collective-permute-done((f32[160,345]{1,0:T(8,128)S(1)}, f32[160,345]{1,0:T(8,128)S(1)}, u32[]{:S(2)}, u32[]{:S(2)}) %collective-permute-start.30) | collective-permute-done | bytes 220832 | tf_op jit(solution)/shard_map/ppermute | solution.py:48
  101.2 2.8 %collective-permute-done.32 = f32[160,345]{1,0:T(8,128)S(1)} collective-permute-done((f32[160,345]{1,0:T(8,128)S(1)}, f32[160,345]{1,0:T(8,128)S(1)}, u32[]{:S(2)}, u32[]{:S(2)}) %collective-permute-start.32) | collective-permute-done | bytes 220832 | tf_op jit(solution)/shard_map/ppermute | solution.py:48
  104.0 1.3 %collective-permute-done.33 = f32[160,345]{1,0:T(8,128)S(1)} collective-permute-done((f32[160,345]{1,0:T(8,128)S(1)}, f32[160,345]{1,0:T(8,128)S(1)}, u32[]{:S(2)}, u32[]{:S(2)}) %collective-permute-start.33) | collective-permute-done | bytes 220832 | tf_op jit(solution)/shard_map/ppermute | solution.py:48
  105.3 0.8 add_bitcast_fusion
  (29 shorter events, 0.6 us)
Async XLA Ops:
  0.0 0.9 copy-start
  1.0 10.1 %collective-permute-start.4 = (bf16[160,768]{1,0:T(8,128)(2,1)S(1)}, bf16[160,768]{1,0:T(8,128)(2,1)S(1)}, u32[]{:S(2)}, u32[]{:S(2)}) collective-permute-start(bf16[160,768]{1,0:T(8,128)(2,1)S(1)} %split_coefs.1.refs_6_), channel_id=1, source_target_pairs={{0,2},{1,3},{2,0},{3,1},{4,6},{5,7},{6,4},{7,5},{8,10},{9,11},{10,... | collective-permute-start | bytes 737288 | tf_op jit(solution)/shard_map/ppermute | solution.py:48
  3.1 8.8 %collective-permute-start = (bf16[160,768]{1,0:T(8,128)(2,1)}, bf16[160,768]{1,0:T(8,128)(2,1)S(1)}, u32[]{:S(2)}, u32[]{:S(2)}) collective-permute-start(bf16[160,768]{1,0:T(8,128)(2,1)} %refs_0_), channel_id=1, source_target_pairs={{0,48},{1,49},{2,50},{3,51},{4,52},{5,53},{6,54},{7,55},{8,56},{9,... | collective-permute-start | bytes 737288 | tf_op jit(solution)/shard_map/ppermute | solution.py:48
  5.8 7.3 %collective-permute-start.1 = (bf16[160,768]{1,0:T(8,128)(2,1)}, bf16[160,768]{1,0:T(8,128)(2,1)S(1)}, u32[]{:S(2)}, u32[]{:S(2)}) collective-permute-start(bf16[160,768]{1,0:T(8,128)(2,1)} %refs_0_), channel_id=1, source_target_pairs={{0,16},{1,17},{2,18},{3,19},{4,20},{5,21},{6,22},{7,23},{8,24},{9,... | collective-permute-start | bytes 737288 | tf_op jit(solution)/shard_map/ppermute | solution.py:48
  6.1 8.4 %collective-permute-start.2 = (bf16[160,768]{1,0:T(8,128)(2,1)}, bf16[160,768]{1,0:T(8,128)(2,1)S(1)}, u32[]{:S(2)}, u32[]{:S(2)}) collective-permute-start(bf16[160,768]{1,0:T(8,128)(2,1)} %refs_1_), channel_id=1, source_target_pairs={{0,12},{1,13},{2,14},{3,15},{4,8},{5,9},{6,10},{7,11},{8,4},{9,5},... | collective-permute-start | bytes 737288 | tf_op jit(solution)/shard_map/ppermute | solution.py:48
  9.1 6.8 %collective-permute-start.3 = (bf16[160,768]{1,0:T(8,128)(2,1)}, bf16[160,768]{1,0:T(8,128)(2,1)S(1)}, u32[]{:S(2)}, u32[]{:S(2)}) collective-permute-start(bf16[160,768]{1,0:T(8,128)(2,1)} %refs_1_), channel_id=1, source_target_pairs={{0,4},{1,5},{2,6},{3,7},{4,0},{5,1},{6,2},{7,3},{8,12},{9,13},{10,... | collective-permute-start | bytes 737288 | tf_op jit(solution)/shard_map/ppermute | solution.py:48
  9.2 0.9 copy-start.2
  10.2 0.9 copy-start.3
  16.1 11.1 %collective-permute-start.9 = (bf16[320,768]{1,0:T(8,128)(2,1)S(1)}, bf16[320,768]{1,0:T(8,128)(2,1)S(1)}, u32[]{:S(2)}, u32[]{:S(2)}) collective-permute-start(bf16[320,768]{1,0:T(8,128)(2,1)S(1)} %get-tuple-element.103.refs_4_.refs_2_.refs_9_), channel_id=1, source_target_pairs={{0,16},{1,17},{2,18},{3,19},{4,20},{5,21},{6,22},{7,23},{8,24},{9,... | collective-permute-start | bytes 1474568 | tf_op jit(solution)/shard_map/ppermute | solution.py:48
  17.9 10.6 %collective-permute-start.6 = (bf16[320,768]{1,0:T(8,128)(2,1)S(1)}, bf16[320,768]{1,0:T(8,128)(2,1)S(1)}, u32[]{:S(2)}, u32[]{:S(2)}) collective-permute-start(bf16[320,768]{1,0:T(8,128)(2,1)S(1)} %get-tuple-element.79.refs_2_.refs_0_), channel_id=1, source_target_pairs={{0,4},{1,5},{2,6},{3,7},{4,0},{5,1},{6,2},{7,3},{8,12},{9,13},{10,... | collective-permute-start | bytes 1474568 | tf_op jit(solution)/shard_map/ppermute | solution.py:48
  18.2 10.5 %collective-permute-start.8 = (bf16[320,768]{1,0:T(8,128)(2,1)S(1)}, bf16[320,768]{1,0:T(8,128)(2,1)S(1)}, u32[]{:S(2)}, u32[]{:S(2)}) collective-permute-start(bf16[320,768]{1,0:T(8,128)(2,1)S(1)} %get-tuple-element.90.refs_2_.refs_1_), channel_id=1, source_target_pairs={{0,2},{1,3},{2,0},{3,1},{4,6},{5,7},{6,4},{7,5},{8,10},{9,11},{10,... | collective-permute-start | bytes 1474568 | tf_op jit(solution)/shard_map/ppermute | solution.py:48
  18.6 11.7 %collective-permute-start.5 = (bf16[320,768]{1,0:T(8,128)(2,1)S(1)}, bf16[320,768]{1,0:T(8,128)(2,1)S(1)}, u32[]{:S(2)}, u32[]{:S(2)}) collective-permute-start(bf16[320,768]{1,0:T(8,128)(2,1)S(1)} %get-tuple-element.78.refs_0_.refs_18_), channel_id=1, source_target_pairs={{0,12},{1,13},{2,14},{3,15},{4,8},{5,9},{6,10},{7,11},{8,4},{9,5},... | collective-permute-start | bytes 1474568 | tf_op jit(solution)/shard_map/ppermute | solution.py:48
  19.8 12.4 %collective-permute-start.7 = (bf16[320,768]{1,0:T(8,128)(2,1)S(1)}, bf16[320,768]{1,0:T(8,128)(2,1)S(1)}, u32[]{:S(2)}, u32[]{:S(2)}) collective-permute-start(bf16[320,768]{1,0:T(8,128)(2,1)S(1)} %get-tuple-element.88.refs_19_), channel_id=1, source_target_pairs={{0,66},{1,67},{2,64},{3,65},{4,70},{5,71},{6,68},{7,69},{8,74},{9,... | collective-permute-start | bytes 1474568 | tf_op jit(solution)/shard_map/ppermute | solution.py:48
  32.2 9.7 %collective-permute-start.14 = (bf16[320,768]{1,0:T(8,128)(2,1)S(1)}, bf16[320,768]{1,0:T(8,128)(2,1)S(1)}, u32[]{:S(2)}, u32[]{:S(2)}) collective-permute-start(bf16[320,768]{1,0:T(8,128)(2,1)S(1)} %get-tuple-element.103.refs_4_.refs_2_.refs_9_), channel_id=1, source_target_pairs={{0,4},{1,5},{2,6},{3,7},{4,0},{5,1},{6,2},{7,3},{8,12},{9,13},{10,... | collective-permute-start | bytes 1474568 | tf_op jit(solution)/shard_map/ppermute | solution.py:48
  33.3 9.2 %collective-permute-start.13 = (bf16[320,768]{1,0:T(8,128)(2,1)S(1)}, bf16[320,768]{1,0:T(8,128)(2,1)S(1)}, u32[]{:S(2)}, u32[]{:S(2)}) collective-permute-start(bf16[320,768]{1,0:T(8,128)(2,1)S(1)} %get-tuple-element.90.refs_2_.refs_1_), channel_id=1, source_target_pairs={{0,16},{1,17},{2,18},{3,19},{4,20},{5,21},{6,22},{7,23},{8,24},{9,... | collective-permute-start | bytes 1474568 | tf_op jit(solution)/shard_map/ppermute | solution.py:48
  33.7 10.2 %collective-permute-start.12 = (bf16[320,768]{1,0:T(8,128)(2,1)S(1)}, bf16[320,768]{1,0:T(8,128)(2,1)S(1)}, u32[]{:S(2)}, u32[]{:S(2)}) collective-permute-start(bf16[320,768]{1,0:T(8,128)(2,1)S(1)} %get-tuple-element.88.refs_19_), channel_id=1, source_target_pairs={{0,48},{1,49},{2,50},{3,51},{4,52},{5,53},{6,54},{7,55},{8,56},{9,... | collective-permute-start | bytes 1474568 | tf_op jit(solution)/shard_map/ppermute | solution.py:48
  34.8 10.1 %collective-permute-start.10 = (bf16[320,768]{1,0:T(8,128)(2,1)S(1)}, bf16[320,768]{1,0:T(8,128)(2,1)S(1)}, u32[]{:S(2)}, u32[]{:S(2)}) collective-permute-start(bf16[320,768]{1,0:T(8,128)(2,1)S(1)} %get-tuple-element.85), channel_id=1, source_target_pairs={{0,66},{1,67},{2,64},{3,65},{4,70},{5,71},{6,68},{7,69},{8,74},{9,... | collective-permute-start | bytes 1474568 | tf_op jit(solution)/shard_map/ppermute | solution.py:48
  37.8 8.8 %collective-permute-start.11 = (bf16[320,768]{1,0:T(8,128)(2,1)S(1)}, bf16[320,768]{1,0:T(8,128)(2,1)S(1)}, u32[]{:S(2)}, u32[]{:S(2)}) collective-permute-start(bf16[320,768]{1,0:T(8,128)(2,1)S(1)} %get-tuple-element.86), channel_id=1, source_target_pairs={{0,2},{1,3},{2,0},{3,1},{4,6},{5,7},{6,4},{7,5},{8,10},{9,11},{10,... | collective-permute-start | bytes 1474568 | tf_op jit(solution)/shard_map/ppermute | solution.py:48
  46.7 1.9 %collective-permute-start.15 = (bf16[320,768]{1,0:T(8,128)(2,1)S(1)}, bf16[320,768]{1,0:T(8,128)(2,1)S(1)}, u32[]{:S(2)}, u32[]{:S(2)}) collective-permute-start(bf16[320,768]{1,0:T(8,128)(2,1)S(1)} %collective-permute-done.11.refs_7_), channel_id=1, source_target_pairs={{0,1},{1,0},{2,3},{3,2},{4,5},{5,4},{6,7},{7,6},{8,9},{9,8},{10,11... | collective-permute-start | bytes 1474568 | tf_op jit(solution)/shard_map/ppermute | solution.py:48
  46.7 2.6 %collective-permute-start.16 = (bf16[320,768]{1,0:T(8,128)(2,1)S(1)}, bf16[320,768]{1,0:T(8,128)(2,1)S(1)}, u32[]{:S(2)}, u32[]{:S(2)}) collective-permute-start(bf16[320,768]{1,0:T(8,128)(2,1)S(1)} %collective-permute-done.13.refs_3_.refs_1_), channel_id=1, source_target_pairs={{0,1},{1,0},{2,3},{3,2},{4,5},{5,4},{6,7},{7,6},{8,9},{9,8},{10,11... | collective-permute-start | bytes 1474568 | tf_op jit(solution)/shard_map/ppermute | solution.py:48
  47.2 2.8 %collective-permute-start.17 = (bf16[320,768]{1,0:T(8,128)(2,1)S(1)}, bf16[320,768]{1,0:T(8,128)(2,1)S(1)}, u32[]{:S(2)}, u32[]{:S(2)}) collective-permute-start(bf16[320,768]{1,0:T(8,128)(2,1)S(1)} %collective-permute-done.14.refs_6_), channel_id=1, source_target_pairs={{0,1},{1,0},{2,3},{3,2},{4,5},{5,4},{6,7},{7,6},{8,9},{9,8},{10,11... | collective-permute-start | bytes 1474568 | tf_op jit(solution)/shard_map/ppermute | solution.py:48
  49.9 5.4 %collective-permute-start.21 = (bf16[640,2304]{1,0:T(8,128)(2,1)S(1)}, bf16[640,2304]{1,0:T(8,128)(2,1)S(1)}, u32[]{:S(2)}, u32[]{:S(2)}) collective-permute-start(bf16[640,2304]{1,0:T(8,128)(2,1)S(1)} %four.1), channel_id=1, source_target_pairs={{0,1},{1,0},{2,3},{3,2},{4,5},{5,4},{6,7},{7,6},{8,9},{9,8},{10,11... | collective-permute-start | bytes 8847368 | tf_op jit(solution)/shard_map/ppermute | solution.py:48
  50.1 16.4 %collective-permute-start.20 = (bf16[320,768]{1,0:T(8,128)(2,1)S(1)}, bf16[320,768]{1,0:T(8,128)(2,1)S(1)}, u32[]{:S(2)}, u32[]{:S(2)}) collective-permute-start(bf16[320,768]{1,0:T(8,128)(2,1)S(1)} %collective-permute-done.8.refs_3_.refs_8_), channel_id=1, source_target_pairs={{0,16},{1,17},{2,18},{3,19},{4,20},{5,21},{6,22},{7,23},{8,24},{9,... | collective-permute-start | bytes 1474568 | tf_op jit(solution)/shard_map/ppermute | solution.py:48
  50.7 15.9 %collective-permute-start.19 = (bf16[320,768]{1,0:T(8,128)(2,1)S(1)}, bf16[320,768]{1,0:T(8,128)(2,1)S(1)}, u32[]{:S(2)}, u32[]{:S(2)}) collective-permute-start(bf16[320,768]{1,0:T(8,128)(2,1)S(1)} %get-tuple-element.99), channel_id=1, source_target_pairs={{0,2},{1,3},{2,0},{3,1},{4,6},{5,7},{6,4},{7,5},{8,10},{9,11},{10,... | collective-permute-start | bytes 1474568 | tf_op jit(solution)/shard_map/ppermute | solution.py:48
  50.8 16.7 %collective-permute-start.26 = (bf16[320,768]{1,0:T(8,128)(2,1)S(1)}, bf16[320,768]{1,0:T(8,128)(2,1)S(1)}, u32[]{:S(2)}, u32[]{:S(2)}) collective-permute-start(bf16[320,768]{1,0:T(8,128)(2,1)S(1)} %collective-permute-done.7.refs_17_), channel_id=1, source_target_pairs={{0,48},{1,49},{2,50},{3,51},{4,52},{5,53},{6,54},{7,55},{8,56},{9,... | collective-permute-start | bytes 1474568 | tf_op jit(solution)/shard_map/ppermute | solution.py:48
  53.4 13.7 %collective-permute-start.18 = (bf16[320,768]{1,0:T(8,128)(2,1)S(1)}, bf16[320,768]{1,0:T(8,128)(2,1)S(1)}, u32[]{:S(2)}, u32[]{:S(2)}) collective-permute-start(bf16[320,768]{1,0:T(8,128)(2,1)S(1)} %collective-permute-done.9.refs_5_.refs_4_), channel_id=1, source_target_pairs={{0,4},{1,5},{2,6},{3,7},{4,0},{5,1},{6,2},{7,3},{8,12},{9,13},{10,... | collective-permute-start | bytes 1474568 | tf_op jit(solution)/shard_map/ppermute | solution.py:48
  55.3 14.5 %collective-permute-start.25 = (bf16[320,768]{1,0:T(8,128)(2,1)S(1)}, bf16[320,768]{1,0:T(8,128)(2,1)S(1)}, u32[]{:S(2)}, u32[]{:S(2)}) collective-permute-start(bf16[320,768]{1,0:T(8,128)(2,1)S(1)} %get-tuple-element.112), channel_id=1, source_target_pairs={{0,66},{1,67},{2,64},{3,65},{4,70},{5,71},{6,68},{7,69},{8,74},{9,... | collective-permute-start | bytes 1474568 | tf_op jit(solution)/shard_map/ppermute | solution.py:48
  66.5 6.8 %collective-permute-start.24 = (bf16[320,768]{1,0:T(8,128)(2,1)S(1)}, bf16[320,768]{1,0:T(8,128)(2,1)S(1)}, u32[]{:S(2)}, u32[]{:S(2)}) collective-permute-start(bf16[320,768]{1,0:T(8,128)(2,1)S(1)} %collective-permute-done.20.refs_4_), channel_id=1, source_target_pairs={{0,1},{1,0},{2,3},{3,2},{4,5},{5,4},{6,7},{7,6},{8,9},{9,8},{10,11... | collective-permute-start | bytes 1474568 | tf_op jit(solution)/shard_map/ppermute | solution.py:48
  66.6 6.7 %collective-permute-start.23 = (bf16[320,768]{1,0:T(8,128)(2,1)S(1)}, bf16[320,768]{1,0:T(8,128)(2,1)S(1)}, u32[]{:S(2)}, u32[]{:S(2)}) collective-permute-start(bf16[320,768]{1,0:T(8,128)(2,1)S(1)} %collective-permute-done.19.refs_3_), channel_id=1, source_target_pairs={{0,1},{1,0},{2,3},{3,2},{4,5},{5,4},{6,7},{7,6},{8,9},{9,8},{10,11... | collective-permute-start | bytes 1474568 | tf_op jit(solution)/shard_map/ppermute | solution.py:48
  67.1 6.2 %collective-permute-start.22 = (bf16[320,768]{1,0:T(8,128)(2,1)S(1)}, bf16[320,768]{1,0:T(8,128)(2,1)S(1)}, u32[]{:S(2)}, u32[]{:S(2)}) collective-permute-start(bf16[320,768]{1,0:T(8,128)(2,1)S(1)} %collective-permute-done.18.refs_2_), channel_id=1, source_target_pairs={{0,1},{1,0},{2,3},{3,2},{4,5},{5,4},{6,7},{7,6},{8,9},{9,8},{10,11... | collective-permute-start | bytes 1474568 | tf_op jit(solution)/shard_map/ppermute | solution.py:48
  74.8 12.8 %collective-permute-start.27 = (f32[160,345]{1,0:T(8,128)S(1)}, f32[160,345]{1,0:T(8,128)S(1)}, u32[]{:S(2)}, u32[]{:S(2)}) collective-permute-start(f32[160,345]{1,0:T(8,128)S(1)} %get-tuple-element.123), channel_id=1, source_target_pairs={{0,126},{1,127},{2,124},{3,125},{4,122},{5,123},{6,120},{7,121},{8... | collective-permute-start | bytes 662408 | tf_op jit(solution)/shard_map/ppermute | solution.py:48
  82.1 14.6 %collective-permute-start.28 = (f32[160,345]{1,0:T(8,128)S(1)}, f32[160,345]{1,0:T(8,128)S(1)}, u32[]{:S(2)}, u32[]{:S(2)}) collective-permute-start(f32[160,345]{1,0:T(8,128)S(1)} %get-tuple-element.126), channel_id=1, source_target_pairs={{0,12},{1,13},{2,14},{3,15},{4,8},{5,9},{6,10},{7,11},{8,4},{9,5},... | collective-permute-start | bytes 662408 | tf_op jit(solution)/shard_map/ppermute | solution.py:48
  84.0 8.8 %collective-permute-start.29 = (f32[160,345]{1,0:T(8,128)S(1)}, f32[160,345]{1,0:T(8,128)S(1)}, u32[]{:S(2)}, u32[]{:S(2)}) collective-permute-start(f32[160,345]{1,0:T(8,128)S(1)} %get-tuple-element.122), channel_id=1, source_target_pairs={{0,66},{1,67},{2,64},{3,65},{4,70},{5,71},{6,68},{7,69},{8,74},{9,... | collective-permute-start | bytes 662408 | tf_op jit(solution)/shard_map/ppermute | solution.py:48
  86.0 9.1 %collective-permute-start.31 = (f32[160,345]{1,0:T(8,128)S(1)}, f32[160,345]{1,0:T(8,128)S(1)}, u32[]{:S(2)}, u32[]{:S(2)}) collective-permute-start(f32[160,345]{1,0:T(8,128)S(1)} %get-tuple-element.131), channel_id=1, source_target_pairs={{0,48},{1,49},{2,50},{3,51},{4,52},{5,53},{6,54},{7,55},{8,56},{9,... | collective-permute-start | bytes 662408 | tf_op jit(solution)/shard_map/ppermute | solution.py:48
  92.8 8.4 %collective-permute-start.30 = (f32[160,345]{1,0:T(8,128)S(1)}, f32[160,345]{1,0:T(8,128)S(1)}, u32[]{:S(2)}, u32[]{:S(2)}) collective-permute-start(f32[160,345]{1,0:T(8,128)S(1)} %add.27), channel_id=1, source_target_pairs={{0,48},{1,49},{2,50},{3,51},{4,52},{5,53},{6,54},{7,55},{8,56},{9,... | collective-permute-start | bytes 662408 | tf_op jit(solution)/shard_map/ppermute | solution.py:48
  95.2 8.8 %collective-permute-start.32 = (f32[160,345]{1,0:T(8,128)S(1)}, f32[160,345]{1,0:T(8,128)S(1)}, u32[]{:S(2)}, u32[]{:S(2)}) collective-permute-start(f32[160,345]{1,0:T(8,128)S(1)} %add.29), channel_id=1, source_target_pairs={{0,12},{1,13},{2,14},{3,15},{4,8},{5,9},{6,10},{7,11},{8,4},{9,5},... | collective-permute-start | bytes 662408 | tf_op jit(solution)/shard_map/ppermute | solution.py:48
  96.7 8.6 %copy-start.1 = (f32[345,160]{0,1:T(8,128)S(1)}, f32[345,160]{0,1:T(8,128)}, u32[]{:S(2)}) copy-start(f32[345,160]{0,1:T(8,128)} %param.7) | copy-start | bytes 662404
  96.7 8.6 %copy-start.4 = (s32[160]{0:T(256)S(1)}, s32[160]{0:T(256)}, u32[]{:S(2)}) copy-start(s32[160]{0:T(256)} %param.6) | copy-start | bytes 1924
  96.8 8.6 %collective-permute-start.33 = (f32[160,345]{1,0:T(8,128)S(1)}, f32[160,345]{1,0:T(8,128)S(1)}, u32[]{:S(2)}, u32[]{:S(2)}) collective-permute-start(f32[160,345]{1,0:T(8,128)S(1)} %add.25), channel_id=1, source_target_pairs={{0,66},{1,67},{2,64},{3,65},{4,70},{5,71},{6,68},{7,69},{8,74},{9,... | collective-permute-start | bytes 662408 | tf_op jit(solution)/shard_map/ppermute | solution.py:48
